TPU v7x, 32 devices: a whole 2x2x4 slice. The times are simulated.
32 devices in a mesh: req: 16 (over z, y, x), head: 2 (over core).
Axes of the slice: x: 2, y: 2, z: 4, core: 2. Of those that a mesh axis runs over, the one named last changes fastest.
Arguments:
- hidden_in: bfloat16 [768, 1536], P('req', 'head'), may hold values from -6 to 6
- norm_gain: float32 [1536], replicated, may hold values from 0.5 to 1.5
- proj_gate: bfloat16 [1536, 3072], P(None, 'head'), may hold values from -0.15625 to 0.15625
- proj_inner: bfloat16 [1536, 3072], P(None, 'head'), may hold values from -0.15625 to 0.15625
- proj_ssm: bfloat16 [1536, 256], P(None, 'head'), may hold values from -0.15625 to 0.15625
- proj_step: bfloat16 [1536, 48], P(None, 'head'), may hold values from -0.15625 to 0.15625
- step_bias: float32 [48], P('head'), may hold values from -6 to -1
- decay_log: float32 [48], P('head'), may hold values from 0 to 2.77
- skip_gain: float32 [48], P('head'), may hold values from 0.5 to 1.5
- conv_inner: bfloat16 [4, 3072], P(None, 'head'), may hold values from -3 to 3
- conv_inner_bias: float32 [3072], P('head'), may hold values from -3 to 3
- conv_ssm: bfloat16 [4, 256], replicated, may hold values from -3 to 3
- conv_ssm_bias: float32 [256], replicated, may hold values from -3 to 3
- gate_gain: float32 [3072], P('head'), may hold values from 0.5 to 1.5
- proj_out: bfloat16 [3072, 1536], P('head'), may hold values from -0.109375 to 0.109375
- states_in: bfloat16 [96, 48, 64, 128], P('req', 'head'), may hold values from -6 to 6
- edge_inner: bfloat16 [96, 3, 3072], P('req', None, 'head'), may hold values from -6 to 6
- edge_ssm: bfloat16 [96, 3, 256], P('req'), may hold values from -6 to 6
- draft_lengths: int32 [96], P('req'), may hold values from 1 to 8, as said below
- accepted: int32 [96], P('req'), may hold values from 0 to 8, as said below
- destination: int32 [96], P('req'), may hold values from 0 to 95, as said below
Outputs:
- hidden_out: bfloat16 [768, 1536], P('req', 'head')
- kept_state: bfloat16 [96, 48, 64, 128], P('req', 'head')
- kept_edge_inner: bfloat16 [96, 3, 3072], P('req', None, 'head')
- kept_edge_ssm: bfloat16 [96, 3, 256], P('req')
Inputs may be any that keep to these rules, and one draw needn't show every extreme that they name: `draft_lengths`: in every draw some request has a draft of 8 tokens. accepted[r] <= draft_lengths[r]; in every draw some request accepts none and some accepts 8. `destination`: a permutation of the 96 output rows; row d lies on index d // 6 of req; a request on index i of req goes to index (i + k) mod 16 for some k of 0 .. 7; the 6 requests of one index use 6 different k, the same set of k on every index, so every index receives exactly one request from each of 6 senders.
All inputs are finite; a program needn't handle non-finite values.
Results may differ from a plain program's by a relative error of at most 0.015.
Values may be sent and summed in bfloat16 or wider, within the bound.
No kernel may reach another device: no remote copies, remote signals or barrier semaphores. Data moves between devices by JAX's collectives and lax.ppermute only.
A program may use at most 128 MiB of HBM per device.

v0:
```python
import jax
import jax.numpy as jnp
from jax import lax
from jax.sharding import PartitionSpec as P

HEAD_DIM = 64
NSTATE = 128
KCONV = 4
DRAFT = 8
WINDOW = 8
DINNER = 3072


epsilon = 1e-05


def passed_along(array, axis, by):
    length = lax.axis_size(axis)
    return lax.ppermute(array, axis, [(i, (i + by) % length) for i in range(length)])


def causal_conv(edge, rows, weight, bias):
    full = jnp.concatenate([edge, rows], axis=1)
    total = jnp.zeros(rows.shape, jnp.float32) + bias
    for offset in range(KCONV):
        total = total + full[:, offset : offset + DRAFT, :].astype(jnp.float32) * weight[
            offset
        ].astype(jnp.float32)
    return (jax.nn.silu(total).astype(jnp.bfloat16), full)


def edge_rows(full, accepted):
    index = accepted[:, None] + jnp.arange(KCONV - 1, dtype=jnp.int32)[None, :]
    return jnp.take_along_axis(full, index[:, :, None], axis=1)


def advance(state, kept, step_now, inner_now, bmat, cmat, rates, skip_gain, accepted, position):
    state = (
        jnp.exp(step_now * rates)[:, :, None, None] * state
        + (step_now[:, :, None] * inner_now)[:, :, :, None] * bmat[:, None, None, :]
    )
    output = (
        jnp.einsum("rhpn,rn->rhp", state, cmat, precision=lax.Precision.HIGHEST)
        + skip_gain[None, :, None] * inner_now
    )
    kept = jnp.where((accepted == position + 1)[:, None, None, None], state, kept)
    return (state, kept, output)


def local(
    hidden_in,
    norm_gain,
    proj_gate,
    proj_inner,
    proj_ssm,
    proj_step,
    step_bias,
    decay_log,
    skip_gain,
    conv_inner,
    conv_inner_bias,
    conv_ssm,
    conv_ssm_bias,
    gate_gain,
    proj_out,
    states_in,
    edge_inner,
    edge_ssm,
    draft_lengths,
    accepted,
    destination,
):
    whole = lax.all_gather(hidden_in, "head", axis=1, tiled=True)
    wide = whole.astype(jnp.float32)
    normed = (
        wide * lax.rsqrt(jnp.mean(wide * wide, axis=-1, keepdims=True) + epsilon) * norm_gain
    ).astype(jnp.bfloat16)
    rows_here = normed.shape[0]
    count = states_in.shape[0]
    heads_here = states_in.shape[1]
    width_here = proj_inner.shape[1]
    gate = jnp.dot(normed, proj_gate, preferred_element_type=jnp.float32).astype(jnp.bfloat16)
    inner = jnp.dot(normed, proj_inner, preferred_element_type=jnp.float32).astype(jnp.bfloat16)
    ssm_part = jnp.dot(normed, proj_ssm, preferred_element_type=jnp.float32).astype(jnp.bfloat16)
    step_raw = jnp.dot(normed, proj_step, preferred_element_type=jnp.float32).astype(jnp.bfloat16)
    ssm_rows = lax.all_gather(ssm_part, "head", axis=1, tiled=True)
    conv_x, full_inner = causal_conv(
        edge_inner, inner.reshape(count, DRAFT, width_here), conv_inner, conv_inner_bias
    )
    conv_s, full_ssm = causal_conv(
        edge_ssm, ssm_rows.reshape(count, DRAFT, 2 * NSTATE), conv_ssm, conv_ssm_bias
    )
    live = (jnp.arange(DRAFT, dtype=jnp.int32)[None, :] < draft_lengths[:, None]).astype(
        jnp.float32
    )
    step_size = (
        jax.nn.softplus(step_raw.astype(jnp.float32).reshape(count, DRAFT, heads_here) + step_bias)
        * live[:, :, None]
    )
    rates = -jnp.exp(decay_log)
    inner_wide = conv_x.astype(jnp.float32).reshape(count, DRAFT, heads_here, HEAD_DIM)
    ssm_wide = conv_s.astype(jnp.float32)
    bmats = ssm_wide[:, :, :NSTATE]
    cmats = ssm_wide[:, :, NSTATE:]
    state = states_in.astype(jnp.float32)
    kept = jnp.where((accepted == 0)[:, None, None, None], state, jnp.zeros_like(state))
    collected = []
    for position in range(DRAFT):
        state, kept, output = advance(
            state,
            kept,
            step_size[:, position],
            inner_wide[:, position],
            bmats[:, position],
            cmats[:, position],
            rates,
            skip_gain,
            accepted,
            position,
        )
        collected.append(output)
    ssm_out = jnp.stack(collected, axis=1)
    ssm_out = ssm_out.astype(jnp.bfloat16).reshape(rows_here, width_here)
    gated = ssm_out.astype(jnp.float32) * jax.nn.silu(gate.astype(jnp.float32))
    squares = lax.psum(jnp.sum(gated * gated, axis=-1), "head")
    gated_norm = (gated * lax.rsqrt(squares[:, None] / DINNER + epsilon) * gate_gain).astype(
        jnp.bfloat16
    )
    terms = jnp.dot(gated_norm, proj_out, preferred_element_type=jnp.float32)
    totals = lax.psum(terms, "head")
    feature_width = hidden_in.shape[1]
    mine = lax.dynamic_slice_in_dim(
        totals, lax.axis_index("head") * feature_width, feature_width, 1
    )
    hidden_out = (hidden_in.astype(jnp.float32) + mine).astype(jnp.bfloat16)
    kept_local = kept.astype(jnp.bfloat16)
    keep_inner = edge_rows(full_inner, accepted)
    keep_ssm = edge_rows(full_ssm, accepted)
    peers = lax.axis_size("req")
    here = lax.axis_index("req")
    owner = destination // count
    slot = destination % count
    reach = (owner - here) % peers
    match = reach[None, :] == jnp.arange(WINDOW, dtype=jnp.int32)[:, None]
    picker = match.astype(jnp.bfloat16)

    def pick_rows(values):
        return jnp.dot(
            picker, values.reshape(count, -1), preferred_element_type=jnp.float32
        ).astype(jnp.bfloat16)

    send_state = pick_rows(kept_local)
    send_inner = pick_rows(keep_inner)
    send_ssm = pick_rows(keep_ssm)
    send_slot = jnp.sum(jnp.where(match, slot[None, :] + 1, 0), axis=1)
    got_states = []
    got_inners = []
    got_ssms = []
    got_slots = []
    for ahead in range(WINDOW):
        moved = passed_along(
            (
                send_state[ahead : ahead + 1],
                send_inner[ahead : ahead + 1],
                send_ssm[ahead : ahead + 1],
                send_slot[ahead : ahead + 1],
            ),
            "req",
            ahead,
        )
        got_states.append(moved[0])
        got_inners.append(moved[1])
        got_ssms.append(moved[2])
        got_slots.append(moved[3])
    got_state = jnp.concatenate(got_states, axis=0)
    got_inner = jnp.concatenate(got_inners, axis=0)
    got_ssm = jnp.concatenate(got_ssms, axis=0)
    got_slot = jnp.concatenate(got_slots, axis=0)
    placer = (got_slot[None, :] - 1 == jnp.arange(count, dtype=jnp.int32)[:, None]).astype(
        jnp.bfloat16
    )

    def place_rows(values, target):
        return (
            jnp.dot(placer, values, preferred_element_type=jnp.float32)
            .astype(jnp.bfloat16)
            .reshape(target)
        )

    kept_state = place_rows(got_state, states_in.shape)
    kept_edge_inner = place_rows(got_inner, edge_inner.shape)
    kept_edge_ssm = place_rows(got_ssm, edge_ssm.shape)
    return (hidden_out, kept_state, kept_edge_inner, kept_edge_ssm)


def solution(mesh):
    in_specs = (
        P("req", "head"),
        P(),
        P(None, "head"),
        P(None, "head"),
        P(None, "head"),
        P(None, "head"),
        P("head"),
        P("head"),
        P("head"),
        P(None, "head"),
        P("head"),
        P(),
        P(),
        P("head"),
        P("head", None),
        P("req", "head", None, None),
        P("req", None, "head"),
        P("req", None, None),
        P("req"),
        P("req"),
        P("req"),
    )
    out_specs = (
        P("req", "head"),
        P("req", "head", None, None),
        P("req", None, "head"),
        P("req", None, None),
    )
    return jax.shard_map(local, mesh=mesh, in_specs=in_specs, out_specs=out_specs, check_vma=False)
```

profile of v0, /device:TPU:8, one launch (start us, length us, event | category | flops | bytes accessed | tf_op | source)
XLA Modules:
  0.0 440.5 jit_solution(3972610243860089137)
XLA Ops:
  8.8 3.5 collective-permute-start.7
  16.4 2.3 all_gather.6
  19.9 1.8 all_gather.7
  23.4 4.4 collective-permute-start.31
  38.5 3.3 fusion.50
  45.6 7.0 %fusion.14 = f32[6,1,24,64]{3,1,2,0:T(1,128)S(1)} fusion(bf16[6,24,64,128]{3,2,1,0:T(8,128)(2,1)S(1)} %copy-done.1, f32[6,128]{1,0:T(8,128)} %get-tuple-element.41, f32[6,24,64]{2,1,0:T(8,128)S(1)} %get-tuple-element.24, f32[6,24]{1,0:T(8,128)S(1)} %get-tuple-element.96, bf16[6,128,1,1]{1,0,2,3:T(8,128)(2,1)} %get-tuple-element.49), kind=kOutput, calls=%fused_computation.29 | convolution fusion | flops 18874368 | bytes 2438208 | tf_op jit(solution)/shard_map/rhpn,rn->rhp/dot_general | solution.py:43
  52.8 8.3 %fusion.16 = f32[6,1,24,64]{3,1,2,0:T(1,128)S(1)} fusion(bf16[6,24,64,128]{3,2,1,0:T(8,128)(2,1)S(1)} %copy-done.1, f32[6,128]{1,0:T(8,128)} %get-tuple-element.40, f32[6,24,64]{2,1,0:T(8,128)S(1)} %get-tuple-element.23, f32[6,24]{1,0:T(8,128)S(1)} %get-tuple-element.90, f32[6,128]{1,0:T(8,128)} %get-tuple-element.41, ...), kind=kOutput, calls=%fused_computation.30 | convolution fusion | flops 22413312 | bytes 2478720 | tf_op jit(solution)/shard_map/rhpn,rn->rhp/dot_general | solution.py:43
  61.2 8.9 %fusion.13 = f32[6,1,24,64]{3,1,2,0:T(1,128)S(1)} fusion(bf16[6,24,64,128]{3,2,1,0:T(8,128)(2,1)S(1)} %copy-done.1, f32[6,128]{1,0:T(8,128)S(1)} %copy-done.19, f32[6,24,64]{2,1,0:T(8,128)S(1)} %get-tuple-element.22, f32[6,24]{1,0:T(8,128)S(1)} %get-tuple-element.91, f32[6,128]{1,0:T(8,128)S(1)} %copy-done.21, f32[6,24,64]{2,1,0:T(8,128)S(1)} %get-tuple-element.23, ...), kind=kOutput, calls=%fused_computation.27 | convolution fusion | flops 25952256 | bytes 2519232 | tf_op jit(solution)/shard_map/rhpn,rn->rhp/dot_general | solution.py:43
  70.3 11.8 %fusion.100 = f32[6,1,24,64]{3,1,2,0:T(1,128)S(1)} fusion(bf16[6,128,1,1]{1,0,2,3:T(8,128)(2,1)S(1)} %copy-done.44, bf16[6,24,64,128]{3,2,1,0:T(8,128)(2,1)S(1)} %copy-done.1, f32[6,128]{1,0:T(8,128)S(1)} %copy-done.17, f32[6,24,64]{2,1,0:T(8,128)S(1)} %get-tuple-element.21, f32[6,24]{1,0:T(8,128)S(1)} %get-tuple-element.92, f32[6,128]{1,0:T(8,128)S(1)} %copy-done.19, ...), kind=kOutput, calls=%fused_computation.191 | convolution fusion | flops 29491200 | bytes 2559744 | tf_op jit(solution)/shard_map/rhpn,rn->rhp/dot_general | solution.py:43
  82.2 14.9 %fusion.12 = f32[6,1,24,64]{3,1,2,0:T(1,128)S(1)} fusion(f32[6,128]{1,0:T(8,128)S(1)} %get-tuple-element.37, f32[6,24,64]{2,1,0:T(8,128)S(1)} %get-tuple-element.20, f32[6,24]{1,0:T(8,128)S(1)} %get-tuple-element.93, bf16[6,128,1,1]{1,0,2,3:T(8,128)(2,1)S(1)} %copy-done.43, bf16[6,24,64,128]{3,2,1,0:T(8,128)(2,1)S(1)} %copy-done.1, ...), kind=kOutput, calls=%fused_computation.24 | convolution fusion | flops 33030144 | bytes 2600256 | tf_op jit(solution)/shard_map/rhpn,rn->rhp/dot_general | solution.py:43
  97.2 16.3 %fusion.52 = f32[6,1,24,64]{3,1,2,0:T(1,128)S(1)} fusion(f32[6,128]{1,0:T(8,128)S(1)} %get-tuple-element.36, f32[6,24,64]{2,1,0:T(8,128)S(1)} %get-tuple-element.19, f32[6,24]{1,0:T(8,128)S(1)} %get-tuple-element.94, f32[6,128]{1,0:T(8,128)S(1)} %get-tuple-element.37, f32[6,24,64]{2,1,0:T(8,128)S(1)} %get-tuple-element.20, ...), kind=kOutput, calls=%fused_computation.68 | convolution fusion | flops 36569088 | bytes 2640768 | tf_op jit(solution)/shard_map/rhpn,rn->rhp/dot_general | solution.py:43
  113.6 17.7 %fusion.11 = f32[6,1,24,64]{3,1,2,0:T(1,128)S(1)} fusion(f32[6,128]{1,0:T(8,128)S(1)} %get-tuple-element.35, f32[6,24,64]{2,1,0:T(8,128)S(1)} %get-tuple-element.25, f32[6,24]{1,0:T(8,128)S(1)} %get-tuple-element.95, f32[6,128]{1,0:T(8,128)S(1)} %get-tuple-element.36, f32[6,24,64]{2,1,0:T(8,128)S(1)} %get-tuple-element.19, ...), kind=kOutput, calls=%fused_computation.21 | convolution fusion | flops 40108032 | bytes 2681280 | tf_op jit(solution)/shard_map/rhpn,rn->rhp/dot_general | solution.py:43
  131.5 19.1 %fusion.10 = f32[6,1,24,64]{3,1,2,0:T(1,128)S(1)} fusion(f32[6,128]{1,0:T(8,128)S(1)} %get-tuple-element.34, f32[6,24,64]{2,1,0:T(8,128)S(1)} %get-tuple-element.18, f32[6,24]{1,0:T(8,128)S(1)} %get-tuple-element.89, f32[6,128]{1,0:T(8,128)S(1)} %get-tuple-element.35, f32[6,24,64]{2,1,0:T(8,128)S(1)} %get-tuple-element.25, ...), kind=kOutput, calls=%fused_computation.19 | convolution fusion | flops 43646976 | bytes 2721792 | tf_op jit(solution)/shard_map/rhpn,rn->rhp/dot_general | solution.py:43
  151.6 3.5 multiply_reduce_fusion
  155.2 2.7 psum.14
  157.9 4.0 fusion.57
  164.2 16.0 %fusion.9 = bf16[6,24,64,128]{3,2,1,0:T(8,128)(2,1)S(1)} fusion(bf16[6,24,64,128]{3,2,1,0:T(8,128)(2,1)S(1)} %copy-done.1, f32[6,128]{1,0:T(8,128)S(1)} %get-tuple-element.34, f32[6,24,64]{2,1,0:T(8,128)S(1)} %copy-done.7, f32[6,24]{1,0:T(8,128)S(1)} %get-tuple-element.89, f32[6,128]{1,0:T(8,128)S(1)} %get-tuple-element.35, f32[6,24,64]{2,1,0:T(8,128)} %copy-done.14, ...), kind=kLoop, calls=%fused_computation.17 | loop fusion | flops 41287680 | bytes 5042742 | tf_op jit(solution)/shard_map/convert_element_type | solution.py:136
  187.9 4.4 collective-permute-start.29
  192.4 2.8 collective-permute-start.27
  199.1 4.3 collective-permute-start.23
  204.0 4.2 collective-permute-start.21
  209.8 5.7 %fusion.118 = (bf16[1,196608]{1,0:T(2,128)(2,1)}, bf16[1,196608]{1,0:T(2,128)(2,1)}, bf16[1,196608]{1,0:T(2,128)(2,1)}, bf16[1,196608]{1,0:T(2,128)(2,1)}, bf16[...) fusion(bf16[8,196608]{1,0:T(8,128)(2,1)S(1)} %convolution_conve, ...), kind=kLoop, calls=%fused_computation.235 | loop fusion | bytes 6291456 | tf_op jit(solution)/shard_map/slice | solution.py:163
  215.5 5.7 %concatenate.24 = s32[8]{0:T(128)} concatenate(s32[1]{0:T(128)} %collective-permute-done, s32[1]{0:T(128)} %collective-permute-done.1, s32[1]{0:T(128)} %collective-permute-done.2, s32[1]{0:T(128)} %collective-permute-done.3, s32[1]{0:T(128)} %collective-permute-done.4, s32[1]{0:T(128)} %collective-permute-done.5, s32[1]{0:T(128)} %collective-permute-done.6, s32[1]{0:T(128)} %collective-permute-done.7), dimensions={0} | concatenate | bytes 64 | tf_op jit(solution)/shard_map/concatenate | solution.py:178
  221.2 1.8 collective-permute-start.19
  223.7 3.3 collective-permute-start.15
  233.8 41.7 %collective-permute-done.17 = bf16[1,4608]{1,0:T(2,128)(2,1)} collective-permute-done((bf16[1,4608]{1,0:T(2,128)(2,1)}, bf16[1,4608]{1,0:T(2,128)(2,1)}, u32[]{:S(2)}, u32[]{:S(2)}) %collective-permute-start.17) | collective-permute-done | bytes 9248 | tf_op jit(solution)/shard_map/ppermute | solution.py:19
  275.5 72.5 %collective-permute-start.12 = (bf16[1,196608]{1,0:T(2,128)(2,1)}, bf16[1,196608]{1,0:T(2,128)(2,1)}, u32[]{:S(2)}, u32[]{:S(2)}) collective-permute-start(bf16[1,196608]{1,0:T(2,128)(2,1)} %get-tuple-element.13), channel_id=1, source_target_pairs={{0,8},{2,10},{4,12},{6,14},{8,16},{10,18},{12,20},{14,22},{16,24},... | collective-permute-start | bytes 1179656 | tf_op jit(solution)/shard_map/ppermute | solution.py:19
  357.0 7.7 %collective-permute-done.12 = bf16[1,196608]{1,0:T(2,128)(2,1)} collective-permute-done((bf16[1,196608]{1,0:T(2,128)(2,1)}, bf16[1,196608]{1,0:T(2,128)(2,1)}, u32[]{:S(2)}, u32[]{:S(2)}) %collective-permute-start.12) | collective-permute-done | bytes 393248 | tf_op jit(solution)/shard_map/ppermute | solution.py:19
  364.6 3.0 collective-permute-done.11
  369.2 46.2 %collective-permute-done.9 = bf16[1,196608]{1,0:T(2,128)(2,1)} collective-permute-done((bf16[1,196608]{1,0:T(2,128)(2,1)S(1)}, bf16[1,196608]{1,0:T(2,128)(2,1)}, u32[]{:S(2)}, u32[]{:S(2)}) %collective-permute-start.9) | collective-permute-done | bytes 393248 | tf_op jit(solution)/shard_map/ppermute | solution.py:19
  415.4 15.6 %concatenate.25 = bf16[8,196608]{1,0:T(8,128)(2,1)S(1)} concatenate(bf16[1,196608]{1,0:T(2,128)(2,1)} %collective-permute-done.8, bf16[1,196608]{1,0:T(2,128)(2,1)} %collective-permute-done.9, bf16[1,196608]{1,0:T(2,128)(2,1)} %collective-permute-done.10, bf16[1,196608]{1,0:T(2,128)(2,1)} %collective-permute-done.11, bf16[1,196608]{1,0:T(2,128)(2,1)} %collective-permute-done.12, ...), dimensions={0} | concatenate | bytes 6291456 | tf_op jit(solution)/shard_map/concatenate | solution.py:175
  431.9 1.7 copy.156
  (214 shorter events, 59.6 us)
Async XLA Ops:
  7.2 348.2 %all-reduce.2.cloned.1.call-start = ((), (), s32[]{:S(2)}) async-start(), calls=%async_computation | async-start | bytes 589824 | tf_op jit(solution)/shard_map/psum | solution.py:130
  8.8 172.2 %collective-permute-start.7 = (s32[1]{0:T(128)}, s32[1]{0:T(128)}, u32[]{:S(2)}, u32[]{:S(2)}) collective-permute-start(s32[1]{0:T(128)} %get-tuple-element.70), channel_id=1, source_target_pairs={{0,14},{2,16},{4,18},{6,20},{8,22},{10,24},{12,26},{14,28},{16,30}... | collective-permute-start | bytes 20 | tf_op jit(solution)/shard_map/ppermute | solution.py:19
  12.3 169.5 %collective-permute-start.6 = (s32[1]{0:T(128)}, s32[1]{0:T(128)}, u32[]{:S(2)}, u32[]{:S(2)}) collective-permute-start(s32[1]{0:T(128)} %get-tuple-element.71), channel_id=1, source_target_pairs={{0,12},{2,14},{4,16},{6,18},{8,20},{10,22},{12,24},{14,26},{16,28}... | collective-permute-start | bytes 20 | tf_op jit(solution)/shard_map/ppermute | solution.py:19
  12.5 170.7 %collective-permute-start.5 = (s32[1]{0:T(128)}, s32[1]{0:T(128)}, u32[]{:S(2)}, u32[]{:S(2)}) collective-permute-start(s32[1]{0:T(128)} %get-tuple-element.72), channel_id=1, source_target_pairs={{0,10},{2,12},{4,14},{6,16},{8,18},{10,20},{12,22},{14,24},{16,26}... | collective-permute-start | bytes 20 | tf_op jit(solution)/shard_map/ppermute | solution.py:19
  23.4 171.8 %collective-permute-start.31 = (bf16[1,768]{1,0:T(2,128)(2,1)}, bf16[1,768]{1,0:T(2,128)(2,1)}, u32[]{:S(2)}, u32[]{:S(2)}) collective-permute-start(bf16[1,768]{1,0:T(2,128)(2,1)} %get-tuple-element.58), channel_id=1, source_target_pairs={{0,14},{2,16},{4,18},{6,20},{8,22},{10,24},{12,26},{14,28},{16,30}... | collective-permute-start | bytes 4616 | tf_op jit(solution)/shard_map/ppermute | solution.py:19
  27.8 169.0 %collective-permute-start.30 = (bf16[1,768]{1,0:T(2,128)(2,1)}, bf16[1,768]{1,0:T(2,128)(2,1)}, u32[]{:S(2)}, u32[]{:S(2)}) collective-permute-start(bf16[1,768]{1,0:T(2,128)(2,1)} %get-tuple-element.59), channel_id=1, source_target_pairs={{0,12},{2,14},{4,16},{6,18},{8,20},{10,22},{12,24},{14,26},{16,28}... | collective-permute-start | bytes 4616 | tf_op jit(solution)/shard_map/ppermute | solution.py:19
  181.0 4.7 %collective-permute-start.4 = (s32[1]{0:T(128)}, s32[1]{0:T(128)}, u32[]{:S(2)}, u32[]{:S(2)}) collective-permute-start(s32[1]{0:T(128)} %get-tuple-element.73), channel_id=1, source_target_pairs={{0,8},{2,10},{4,12},{6,14},{8,16},{10,18},{12,20},{14,22},{16,24},... | collective-permute-start | bytes 20 | tf_op jit(solution)/shard_map/ppermute | solution.py:19
  183.3 4.6 %collective-permute-start.2 = (s32[1]{0:T(128)}, s32[1]{0:T(128)}, u32[]{:S(2)}, u32[]{:S(2)}) collective-permute-start(s32[1]{0:T(128)} %get-tuple-element.75), channel_id=1, source_target_pairs={{0,4},{2,6},{4,8},{6,10},{8,12},{10,14},{12,16},{14,18},{16,20},{1... | collective-permute-start | bytes 20 | tf_op jit(solution)/shard_map/ppermute | solution.py:19
  185.6 6.6 %collective-permute-start.1 = (s32[1]{0:T(128)}, s32[1]{0:T(128)}, u32[]{:S(2)}, u32[]{:S(2)}) collective-permute-start(s32[1]{0:T(128)} %get-tuple-element.76), channel_id=1, source_target_pairs={{0,2},{2,4},{4,6},{6,8},{8,10},{10,12},{12,14},{14,16},{16,18},{18... | collective-permute-start | bytes 20 | tf_op jit(solution)/shard_map/ppermute | solution.py:19
  186.3 6.1 %collective-permute-start = (s32[1]{0:T(128)}, s32[1]{0:T(128)}, u32[]{:S(2)}, u32[]{:S(2)}) collective-permute-start(s32[1]{0:T(128)} %get-tuple-element.77), channel_id=1, source_target_pairs={{0,0},{2,2},{4,4},{6,6},{8,8},{10,10},{12,12},{14,14},{16,16},{18,... | collective-permute-start | bytes 20 | tf_op jit(solution)/shard_map/ppermute | solution.py:19
  187.9 11.2 %collective-permute-start.29 = (bf16[1,768]{1,0:T(2,128)(2,1)}, bf16[1,768]{1,0:T(2,128)(2,1)S(1)}, u32[]{:S(2)}, u32[]{:S(2)}) collective-permute-start(bf16[1,768]{1,0:T(2,128)(2,1)} %get-tuple-element.60), channel_id=1, source_target_pairs={{0,10},{2,12},{4,14},{6,16},{8,18},{10,20},{12,22},{14,24},{16,26}... | collective-permute-start | bytes 4616 | tf_op jit(solution)/shard_map/ppermute | solution.py:19
  192.2 6.9 %collective-permute-start.28 = (bf16[1,768]{1,0:T(2,128)(2,1)}, bf16[1,768]{1,0:T(2,128)(2,1)S(1)}, u32[]{:S(2)}, u32[]{:S(2)}) collective-permute-start(bf16[1,768]{1,0:T(2,128)(2,1)} %get-tuple-element.61), channel_id=1, source_target_pairs={{0,8},{2,10},{4,12},{6,14},{8,16},{10,18},{12,20},{14,22},{16,24},... | collective-permute-start | bytes 4616 | tf_op jit(solution)/shard_map/ppermute | solution.py:19
  192.4 11.0 %collective-permute-start.27 = (bf16[1,768]{1,0:T(2,128)(2,1)S(1)}, bf16[1,768]{1,0:T(2,128)(2,1)S(1)}, u32[]{:S(2)}, u32[]{:S(2)}) collective-permute-start(bf16[1,768]{1,0:T(2,128)(2,1)S(1)} %copy-done.35), channel_id=1, source_target_pairs={{0,6},{2,8},{4,10},{6,12},{8,14},{10,16},{12,18},{14,20},{16,22},{... | collective-permute-start | bytes 4616 | tf_op jit(solution)/shard_map/ppermute | solution.py:19
  195.2 8.8 %collective-permute-start.26 = (bf16[1,768]{1,0:T(2,128)(2,1)S(1)}, bf16[1,768]{1,0:T(2,128)(2,1)S(1)}, u32[]{:S(2)}, u32[]{:S(2)}) collective-permute-start(bf16[1,768]{1,0:T(2,128)(2,1)S(1)} %copy-done.34), channel_id=1, source_target_pairs={{0,4},{2,6},{4,8},{6,10},{8,12},{10,14},{12,16},{14,18},{16,20},{1... | collective-permute-start | bytes 4616 | tf_op jit(solution)/shard_map/ppermute | solution.py:19
  196.8 11.4 %collective-permute-start.25 = (bf16[1,768]{1,0:T(2,128)(2,1)S(1)}, bf16[1,768]{1,0:T(2,128)(2,1)S(1)}, u32[]{:S(2)}, u32[]{:S(2)}) collective-permute-start(bf16[1,768]{1,0:T(2,128)(2,1)S(1)} %copy-done.33), channel_id=1, source_target_pairs={{0,2},{2,4},{4,6},{6,8},{8,10},{10,12},{12,14},{14,16},{16,18},{18... | collective-permute-start | bytes 4616 | tf_op jit(solution)/shard_map/ppermute | solution.py:19
  199.1 22.1 %collective-permute-start.24 = (bf16[1,768]{1,0:T(2,128)(2,1)S(1)}, bf16[1,768]{1,0:T(2,128)(2,1)S(1)}, u32[]{:S(2)}, u32[]{:S(2)}) collective-permute-start(bf16[1,768]{1,0:T(2,128)(2,1)S(1)} %copy-done.32), channel_id=1, source_target_pairs={{0,0},{2,2},{4,4},{6,6},{8,8},{10,10},{12,12},{14,14},{16,16},{18,... | collective-permute-start | bytes 4616 | tf_op jit(solution)/shard_map/ppermute | solution.py:19
  199.1 23.9 %collective-permute-start.23 = (bf16[1,4608]{1,0:T(2,128)(2,1)}, bf16[1,4608]{1,0:T(2,128)(2,1)}, u32[]{:S(2)}, u32[]{:S(2)}) collective-permute-start(bf16[1,4608]{1,0:T(2,128)(2,1)} %get-tuple-element.26), channel_id=1, source_target_pairs={{0,14},{2,16},{4,18},{6,20},{8,22},{10,24},{12,26},{14,28},{16,30}... | collective-permute-start | bytes 27656 | tf_op jit(solution)/shard_map/ppermute | solution.py:19
  203.4 20.3 %collective-permute-start.22 = (bf16[1,4608]{1,0:T(2,128)(2,1)}, bf16[1,4608]{1,0:T(2,128)(2,1)}, u32[]{:S(2)}, u32[]{:S(2)}) collective-permute-start(bf16[1,4608]{1,0:T(2,128)(2,1)} %get-tuple-element.27), channel_id=1, source_target_pairs={{0,12},{2,14},{4,16},{6,18},{8,20},{10,22},{12,24},{14,26},{16,28}... | collective-permute-start | bytes 27656 | tf_op jit(solution)/shard_map/ppermute | solution.py:19
  204.0 23.1 %collective-permute-start.21 = (bf16[1,4608]{1,0:T(2,128)(2,1)}, bf16[1,4608]{1,0:T(2,128)(2,1)}, u32[]{:S(2)}, u32[]{:S(2)}) collective-permute-start(bf16[1,4608]{1,0:T(2,128)(2,1)} %get-tuple-element.28), channel_id=1, source_target_pairs={{0,10},{2,12},{4,14},{6,16},{8,18},{10,20},{12,22},{14,24},{16,26}... | collective-permute-start | bytes 27656 | tf_op jit(solution)/shard_map/ppermute | solution.py:19
  208.8 18.7 %collective-permute-start.20 = (bf16[1,4608]{1,0:T(2,128)(2,1)}, bf16[1,4608]{1,0:T(2,128)(2,1)}, u32[]{:S(2)}, u32[]{:S(2)}) collective-permute-start(bf16[1,4608]{1,0:T(2,128)(2,1)} %get-tuple-element.29), channel_id=1, source_target_pairs={{0,8},{2,10},{4,12},{6,14},{8,16},{10,18},{12,20},{14,22},{16,24},... | collective-permute-start | bytes 27656 | tf_op jit(solution)/shard_map/ppermute | solution.py:19
  221.2 8.8 %collective-permute-start.19 = (bf16[1,4608]{1,0:T(2,128)(2,1)}, bf16[1,4608]{1,0:T(2,128)(2,1)}, u32[]{:S(2)}, u32[]{:S(2)}) collective-permute-start(bf16[1,4608]{1,0:T(2,128)(2,1)} %get-tuple-element.30), channel_id=1, source_target_pairs={{0,6},{2,8},{4,10},{6,12},{8,14},{10,16},{12,18},{14,20},{16,22},{... | collective-permute-start | bytes 27656 | tf_op jit(solution)/shard_map/ppermute | solution.py:19
  223.0 8.0 %collective-permute-start.18 = (bf16[1,4608]{1,0:T(2,128)(2,1)}, bf16[1,4608]{1,0:T(2,128)(2,1)}, u32[]{:S(2)}, u32[]{:S(2)}) collective-permute-start(bf16[1,4608]{1,0:T(2,128)(2,1)} %get-tuple-element.31), channel_id=1, source_target_pairs={{0,4},{2,6},{4,8},{6,10},{8,12},{10,14},{12,16},{14,18},{16,20},{1... | collective-permute-start | bytes 27656 | tf_op jit(solution)/shard_map/ppermute | solution.py:19
  223.7 126.0 %collective-permute-start.15 = (bf16[1,196608]{1,0:T(2,128)(2,1)}, bf16[1,196608]{1,0:T(2,128)(2,1)}, u32[]{:S(2)}, u32[]{:S(2)}) collective-permute-start(bf16[1,196608]{1,0:T(2,128)(2,1)} %get-tuple-element.10), channel_id=1, source_target_pairs={{0,14},{2,16},{4,18},{6,20},{8,22},{10,24},{12,26},{14,28},{16,30}... | collective-permute-start | bytes 1179656 | tf_op jit(solution)/shard_map/ppermute | solution.py:19
  227.0 122.7 %collective-permute-start.14 = (bf16[1,196608]{1,0:T(2,128)(2,1)}, bf16[1,196608]{1,0:T(2,128)(2,1)}, u32[]{:S(2)}, u32[]{:S(2)}) collective-permute-start(bf16[1,196608]{1,0:T(2,128)(2,1)} %get-tuple-element.11), channel_id=1, source_target_pairs={{0,12},{2,14},{4,16},{6,18},{8,20},{10,22},{12,24},{14,26},{16,28}... | collective-permute-start | bytes 1179656 | tf_op jit(solution)/shard_map/ppermute | solution.py:19
  227.5 123.7 %collective-permute-start.13 = (bf16[1,196608]{1,0:T(2,128)(2,1)}, bf16[1,196608]{1,0:T(2,128)(2,1)}, u32[]{:S(2)}, u32[]{:S(2)}) collective-permute-start(bf16[1,196608]{1,0:T(2,128)(2,1)} %get-tuple-element.12), channel_id=1, source_target_pairs={{0,10},{2,12},{4,14},{6,16},{8,18},{10,20},{12,22},{14,24},{16,26}... | collective-permute-start | bytes 1179656 | tf_op jit(solution)/shard_map/ppermute | solution.py:19
  230.1 45.5 %collective-permute-start.17 = (bf16[1,4608]{1,0:T(2,128)(2,1)}, bf16[1,4608]{1,0:T(2,128)(2,1)}, u32[]{:S(2)}, u32[]{:S(2)}) collective-permute-start(bf16[1,4608]{1,0:T(2,128)(2,1)} %get-tuple-element.32), channel_id=1, source_target_pairs={{0,2},{2,4},{4,6},{6,8},{8,10},{10,12},{12,14},{14,16},{16,18},{18... | collective-permute-start | bytes 27656 | tf_op jit(solution)/shard_map/ppermute | solution.py:19
  231.1 117.0 %collective-permute-start.16 = (bf16[1,4608]{1,0:T(2,128)(2,1)}, bf16[1,4608]{1,0:T(2,128)(2,1)}, u32[]{:S(2)}, u32[]{:S(2)}) collective-permute-start(bf16[1,4608]{1,0:T(2,128)(2,1)} %get-tuple-element.33), channel_id=1, source_target_pairs={{0,0},{2,2},{4,4},{6,6},{8,8},{10,10},{12,12},{14,14},{16,16},{18,... | collective-permute-start | bytes 27656 | tf_op jit(solution)/shard_map/ppermute | solution.py:19
  275.5 89.1 %collective-permute-start.12 = (bf16[1,196608]{1,0:T(2,128)(2,1)}, bf16[1,196608]{1,0:T(2,128)(2,1)}, u32[]{:S(2)}, u32[]{:S(2)}) collective-permute-start(bf16[1,196608]{1,0:T(2,128)(2,1)} %get-tuple-element.13), channel_id=1, source_target_pairs={{0,8},{2,10},{4,12},{6,14},{8,16},{10,18},{12,20},{14,22},{16,24},... | collective-permute-start | bytes 1179656 | tf_op jit(solution)/shard_map/ppermute | solution.py:19
  348.0 19.6 %collective-permute-start.11 = (bf16[1,196608]{1,0:T(2,128)(2,1)S(1)}, bf16[1,196608]{1,0:T(2,128)(2,1)}, u32[]{:S(2)}, u32[]{:S(2)}) collective-permute-start(bf16[1,196608]{1,0:T(2,128)(2,1)S(1)} %get-tuple-element.14), channel_id=1, source_target_pairs={{0,6},{2,8},{4,10},{6,12},{8,14},{10,16},{12,18},{14,20},{16,22},{... | collective-permute-start | bytes 1179656 | tf_op jit(solution)/shard_map/ppermute | solution.py:19
  349.7 19.5 %collective-permute-start.10 = (bf16[1,196608]{1,0:T(2,128)(2,1)S(1)}, bf16[1,196608]{1,0:T(2,128)(2,1)}, u32[]{:S(2)}, u32[]{:S(2)}) collective-permute-start(bf16[1,196608]{1,0:T(2,128)(2,1)S(1)} %get-tuple-element.15), channel_id=1, source_target_pairs={{0,4},{2,6},{4,8},{6,10},{8,12},{10,14},{12,16},{14,18},{16,20},{1... | collective-permute-start | bytes 1179656 | tf_op jit(solution)/shard_map/ppermute | solution.py:19
  349.7 65.7 %collective-permute-start.9 = (bf16[1,196608]{1,0:T(2,128)(2,1)S(1)}, bf16[1,196608]{1,0:T(2,128)(2,1)}, u32[]{:S(2)}, u32[]{:S(2)}) collective-permute-start(bf16[1,196608]{1,0:T(2,128)(2,1)S(1)} %get-tuple-element.16), channel_id=1, source_target_pairs={{0,2},{2,4},{4,6},{6,8},{8,10},{10,12},{12,14},{14,16},{16,18},{18... | collective-permute-start | bytes 1179656 | tf_op jit(solution)/shard_map/ppermute | solution.py:19
  351.2 64.1 %collective-permute-start.8 = (bf16[1,196608]{1,0:T(2,128)(2,1)S(1)}, bf16[1,196608]{1,0:T(2,128)(2,1)}, u32[]{:S(2)}, u32[]{:S(2)}) collective-permute-start(bf16[1,196608]{1,0:T(2,128)(2,1)S(1)} %get-tuple-element.17), channel_id=1, source_target_pairs={{0,0},{2,2},{4,4},{6,6},{8,8},{10,10},{12,12},{14,14},{16,16},{18,... | collective-permute-start | bytes 1179656 | tf_op jit(solution)/shard_map/ppermute | solution.py:19
  (48 other events, 1217.9 us)
Sparse Core Ops, SparseCore 0:
  162.1 17.9 all-reduce.1
where the time goes:
time: 443 us; the launch traced here: 440 us
  matrix products  122 us (28%)
  starting transfers between devices  120 us (27%)
  waiting for transfers between devices  101 us (23%)
  local copies, waits for them, and re-layouts  46 us (10%)
  other arithmetic  29 us (7%)
  between operations  14.8 us (3%)
  blocking collectives  6.75 us (2%)
    ppermute x32, starting transfers between devices, passed_along(): lax.ppermute(array, axis, [(i, (i + by) % length) for i in range(length)])  120 us
    dot_general x8, matrix products, advance(): jnp.einsum('rhpn,rn->rhp', state, cmat, precision=lax.Precision.HIGHEST)  104 us
    ppermute x32, waiting for transfers between devices, passed_along(): lax.ppermute(array, axis, [(i, (i + by) % length) for i in range(length)])  101 us
    convert_element_type x1, other arithmetic, local(): kept_local = kept.astype(jnp.bfloat16)  16 us
    concatenate x1, local copies, waits for them, and re-layouts, local(): got_state = jnp.concatenate(got_states, axis=0)  15.6 us
  transfers between devices with their start and end apart: 33, of which 7 were waited for; matrix products, arithmetic and copies ran while one was open for 40% of the time, Pallas kernels for 0%

commit v1 on v0

v1 whole, which is shorter than its diff:
```python
import functools

import jax
import jax.numpy as jnp
from jax import lax
from jax.experimental import pallas as pl
from jax.experimental.pallas import tpu as pltpu
from jax.sharding import PartitionSpec as P

HEAD_DIM = 64
NSTATE = 128
KCONV = 4
DRAFT = 8
WINDOW = 8
DINNER = 3072
TILE = 256
EXTRA = 2 * NSTATE

epsilon = 1e-05
HIGH = lax.Precision.HIGHEST
F32 = jnp.float32
BF16 = jnp.bfloat16


def iota(shape, axis):
    return lax.broadcasted_iota(jnp.int32, shape, axis)


def mm(a, b, precision=None):
    return jnp.dot(a, b, preferred_element_type=F32, precision=precision)


def mm_t(a, b):
    return lax.dot_general(a, b, (((1,), (1,)), ((), ())), preferred_element_type=F32)


def silu(x):
    return x * (1.0 / (1.0 + jnp.exp(-x)))


def conv_rows(rows, edges, taps, bias):
    slot = iota(rows.shape, 1)
    total = bias + taps[KCONV - 1 : KCONV] * rows
    for back in range(1, KCONV):
        mixed = jnp.where(slot >= DRAFT - back, edges, rows)
        total = total + taps[KCONV - 1 - back : KCONV - back] * pltpu.roll(mixed, back, 1)
    return total


def front_kernel(
    count,
    heads,
    ints,
    hidden,
    norm_gain,
    w_gate,
    w_inner,
    w_out,
    w_ssm,
    w_step,
    head_rows,
    taps_inner,
    bias_inner,
    taps_ssm,
    bias_ssm,
    gate_gain,
    states,
    edge_inner,
    edge_ssm,
    mine,
    theirs,
    *rest,
):
    corr = rest[:WINDOW]
    normed, acc, squares, quant, gmat, cmat, select, boxes = rest[WINDOW:]
    step = pl.program_id(0)
    last = pl.num_programs(0) - 1
    rows = count * DRAFT
    width = acc.shape[1]
    half = width // 2

    @pl.when(step == 0)
    def _():
        wide = jnp.concatenate([hidden[0], hidden[1]], axis=1).astype(F32)
        scale = lax.rsqrt(jnp.mean(wide * wide, axis=-1, keepdims=True) + epsilon)
        norm = (wide * scale * norm_gain[...]).astype(BF16)
        normed[...] = norm
        acc[...] = jnp.zeros_like(acc)
        squares[...] = jnp.zeros_like(squares)
        boxes[...] = jnp.zeros_like(boxes)
        for k in range(WINDOW):
            corr[k][...] = jnp.zeros_like(corr[k])
        row = iota((rows, rows), 0)
        col = iota((rows, rows), 1)
        request = row >> 3
        taken = jnp.zeros((rows, rows), jnp.int32)
        for r in range(count):
            taken = jnp.where(request == r, ints[1, r], taken)
        same = request == (col >> 3)
        lower = same & ((col & 7) <= (row & 7))
        before = same & ((col & 7) < taken)
        raw = mm(norm, w_step[...]).astype(BF16).astype(F32) + head_rows[0:1]
        lengths = jnp.zeros((rows, heads), jnp.int32)
        chosen = jnp.zeros((rows, heads), jnp.int32)
        hrow = iota((rows, heads), 0)
        for r in range(count):
            lengths = jnp.where((hrow >> 3) == r, ints[0, r], lengths)
            chosen = jnp.where((hrow >> 3) == r, ints[1, r], chosen)
        soft = jnp.maximum(raw, 0.0) + jnp.log1p(jnp.exp(-jnp.abs(raw)))
        size = jnp.where((hrow & 7) < lengths, soft, 0.0)
        rate = -jnp.exp(head_rows[1:2])
        cum = mm(lower.astype(F32), size, HIGH)
        upto = mm(before.astype(F32), size, HIGH)
        weight = jnp.where(
            (hrow & 7) < chosen, jnp.exp(jnp.minimum(rate * (upto - cum), 0.0)) * size, 0.0
        )
        stacked = jnp.concatenate(
            [
                rate * cum,
                size,
                weight,
                jnp.exp(rate * upto),
                jnp.broadcast_to(head_rows[2:3], (16, heads)),
            ],
            axis=0,
        )
        for part in range(3):
            piece = stacked.astype(BF16)
            quant[part] = piece
            stacked = stacked - piece.astype(F32)
        sel_rows = jnp.where(
            same & ((row & 7) < KCONV - 1),
            ((col & 7) == (row & 7) + taken - 3).astype(F32),
            0.0,
        ).astype(BF16)
        sel_edge = jnp.where(
            same & ((row & 7) < KCONV - 1),
            ((col & 7) == (row & 7) + taken + 5).astype(F32),
            0.0,
        ).astype(BF16)
        select[0] = sel_rows
        select[1] = sel_edge
        ssm = jnp.concatenate([mm(norm, w_ssm[0]), mm(norm, w_ssm[1])], axis=1).astype(BF16)
        before_ssm = edge_ssm[...].astype(F32)
        conv = conv_rows(
            ssm.astype(F32).reshape(count, DRAFT, 2 * NSTATE),
            before_ssm,
            taps_ssm[...].astype(F32),
            bias_ssm[...],
        )
        both = silu(conv).reshape(rows, 2 * NSTATE).astype(BF16)
        bmat = both[:, :NSTATE]
        cvec = both[:, NSTATE:]
        cmat[...] = cvec.astype(F32)
        pair = jnp.where(lower, mm_t(cvec, bmat), 0.0)
        fold = ((iota((rows, NSTATE), 0) & 7) == iota((rows, NSTATE), 1)).astype(F32)
        gmat[...] = mm(pair, fold, HIGH)
        kept = mm(sel_rows, ssm) + mm(
            sel_edge, before_ssm.reshape(rows, 2 * NSTATE).astype(BF16)
        )
        wide_b = bmat.astype(F32)
        place = iota((DRAFT, NSTATE), 0)
        for r in range(count):
            own = kept[r * DRAFT : (r + 1) * DRAFT]
            slot = jnp.full((DRAFT, NSTATE), (ints[3, r] + 1).astype(F32))
            packed = jnp.where(
                place < 3,
                own[:, :NSTATE],
                jnp.where(place < 6, pltpu.roll(own[:, NSTATE:], 3, 0), slot),
            )
            top = jnp.concatenate([wide_b[r * DRAFT : (r + 1) * DRAFT], packed], axis=1)
            low = jnp.concatenate([jnp.zeros((DRAFT, NSTATE), F32), slot], axis=1)
            boxes[ints[2, r]] = jnp.concatenate([top, low], axis=0).astype(BF16)
        for k in range(WINDOW):
            corr[k][:, width : width + EXTRA] = boxes[k]

    norm = normed[...]
    inner = mm(norm, w_inner[...]).astype(BF16)
    gate = mm(norm, w_gate[...]).astype(BF16).astype(F32)
    edges = edge_inner[...].astype(F32)
    conv = conv_rows(
        inner.astype(F32).reshape(count, DRAFT, TILE),
        edges,
        taps_inner[...].astype(F32),
        bias_inner[...],
    )
    x = silu(conv).reshape(rows, TILE).astype(BF16).astype(F32)
    first_head = step * (TILE // HEAD_DIM)
    spread = (
        iota((heads, TILE), 0) == first_head + (iota((heads, TILE), 1) >> 6)
    ).astype(BF16)
    expanded = mm(quant[0], spread) + mm(quant[1], spread) + mm(quant[2], spread)
    level = expanded[:rows]
    weighted = expanded[rows : 2 * rows] * x
    past = jnp.concatenate(
        [
            mm_t(cmat[r * DRAFT : (r + 1) * DRAFT].astype(BF16), states[r])
            for r in range(count)
        ],
        axis=0,
    )
    out = jnp.exp(level) * past + expanded[4 * rows : 4 * rows + 1] * x
    level3 = level.reshape(count, DRAFT, TILE)
    weighted3 = weighted.reshape(count, DRAFT, TILE)
    total = jnp.zeros((count, DRAFT, TILE), F32)
    for u in range(DRAFT):
        factor = jnp.exp(jnp.minimum(level3 - level3[:, u : u + 1], 0.0))
        share = gmat[:, u : u + 1].reshape(count, DRAFT, 1)
        total = total + share * factor * weighted3[:, u : u + 1]
    out = (out + total.reshape(rows, TILE)).astype(BF16).astype(F32)
    gated = out * silu(gate)
    squared = gated * gated
    squares[...] += squared[:, :128] + squared[:, 128:]
    acc[...] += mm((gated * gate_gain[...]).astype(BF16), w_out[...])
    delta = expanded[2 * rows : 3 * rows] * x
    decay = expanded[3 * rows : 4 * rows]
    decay_hi = decay.astype(BF16).astype(F32)
    second = mm(select[0], inner) + mm(select[1], edges.reshape(rows, TILE).astype(BF16))
    place = iota((rows, TILE), 0) & 7
    second = jnp.where(
        place == 3, decay_hi, jnp.where(place == 4, decay - decay_hi, second)
    )
    for r in range(count):
        span = slice(r * DRAFT, (r + 1) * DRAFT)
        boxes[ints[2, r]] = jnp.concatenate([delta[span], second[span]], axis=0).astype(BF16)
    here = pl.ds(pl.multiple_of(step * TILE, TILE), TILE)
    for k in range(WINDOW):
        corr[k][:, here] = boxes[k]

    @pl.when(step == last)
    def _():
        total_square = jnp.broadcast_to(
            jnp.sum(squares[...], axis=1, keepdims=True), squares.shape
        )
        mine[:, half:] = total_square
        theirs[:, half:] = total_square

        @pl.when(ints[4, 0] == 0)
        def _():
            mine[:, :half] = acc[:, :half]
            theirs[:, :half] = acc[:, half:]

        @pl.when(ints[4, 0] != 0)
        def _():
            mine[:, :half] = acc[:, half:]
            theirs[:, :half] = acc[:, :half]


def front(count, heads, width, depth, args):
    rows = count * DRAFT
    tiles = width // TILE

    def whole(shape):
        return pl.BlockSpec(shape, lambda j: (0,) * len(shape))

    in_specs = [
        pl.BlockSpec(memory_space=pltpu.SMEM),
        whole((2, rows, depth // 2)),
        whole((1, depth)),
        pl.BlockSpec((depth, TILE), lambda j: (0, j)),
        pl.BlockSpec((depth, TILE), lambda j: (0, j)),
        pl.BlockSpec((TILE, depth), lambda j: (j, 0)),
        whole((2, depth, NSTATE)),
        whole((depth, heads)),
        whole((3, heads)),
        pl.BlockSpec((KCONV, TILE), lambda j: (0, j)),
        pl.BlockSpec((1, TILE), lambda j: (0, j)),
        whole((KCONV, 2 * NSTATE)),
        whole((1, 2 * NSTATE)),
        pl.BlockSpec((1, TILE), lambda j: (0, j)),
        pl.BlockSpec((count, TILE, NSTATE), lambda j: (0, j, 0)),
        pl.BlockSpec((count, DRAFT, TILE), lambda j: (0, 0, j)),
        whole((count, DRAFT, 2 * NSTATE)),
    ]
    out_width = depth // 2 + 128
    out_shape = [jax.ShapeDtypeStruct((rows, out_width), F32)] * 2 + [
        jax.ShapeDtypeStruct((2 * DRAFT, width + EXTRA), BF16)
    ] * WINDOW
    out_specs = [whole((rows, out_width))] * 2 + [whole((2 * DRAFT, width + EXTRA))] * WINDOW
    return pl.pallas_call(
        functools.partial(front_kernel, count, heads),
        grid=(tiles,),
        in_specs=in_specs,
        out_specs=out_specs,
        out_shape=out_shape,
        scratch_shapes=[
            pltpu.VMEM((rows, depth), BF16),
            pltpu.VMEM((rows, depth), F32),
            pltpu.VMEM((rows, 128), F32),
            pltpu.VMEM((3, 4 * rows + 16, heads), BF16),
            pltpu.VMEM((rows, NSTATE), F32),
            pltpu.VMEM((rows, NSTATE), F32),
            pltpu.VMEM((2, rows, rows), BF16),
            pltpu.VMEM((WINDOW, 2 * DRAFT, TILE), BF16),
        ],
        compiler_params=pltpu.CompilerParams(
            dimension_semantics=("arbitrary",), vmem_limit_bytes=40 * 1024 * 1024
        ),
        cost_estimate=pl.CostEstimate(
            flops=2 * rows * depth * width * 3,
            bytes_accessed=3 * depth * width * 2 + count * width * NSTATE * 2,
            transcendentals=rows * width * 12,
        ),
        name="front",
    )(*args)


def merge_kernel(offsets, local_first, *refs):
    n = len(offsets)
    ints = refs[0]
    sources = refs[1 : 1 + n]
    corr = refs[1 + n : 1 + 2 * n]
    kept, out_inner, out_ssm = refs[1 + 2 * n : 4 + 2 * n]
    loaded, merged, sem_in, sem_out = refs[4 + 2 * n :]
    width = loaded.shape[1]

    def source(i):
        if local_first and i == 0:
            return sources[0].at[ints[0]]
        return sources[i].at[0]

    def fetch(i):
        return pltpu.make_async_copy(source(i), loaded.at[i], sem_in.at[i])

    for i in range(n):
        fetch(i).start()
    slots = []
    for i in range(n):
        mark = corr[i][:, width + NSTATE : width + 2 * NSTATE].astype(F32)
        slot = jnp.max(mark[DRAFT:]).astype(jnp.int32) - 1
        slots.append(slot)
        fetch(i).wait()

        @pl.when(slot >= 0)
        def _(i=i, slot=slot, mark=mark):
            ones = jnp.where(
                (iota((2 * DRAFT, NSTATE), 0) == 11) | (iota((2 * DRAFT, NSTATE), 0) == 12),
                1.0,
                0.0,
            ).astype(BF16)
            right = jnp.concatenate([corr[i][:, width : width + NSTATE], ones], axis=1)

            @pl.loop(0, width // TILE)
            def _(c):
                span = pl.ds(pl.multiple_of(c * TILE, TILE), TILE)
                both = lax.dot_general(
                    corr[i][:, span],
                    right,
                    (((0,), (0,)), ((), ())),
                    preferred_element_type=F32,
                )
                state = loaded[i, span].astype(F32)
                merged[i, span] = (both[:, NSTATE:] * state + both[:, :NSTATE]).astype(BF16)

            pltpu.make_async_copy(merged.at[i], kept.at[slot], sem_out.at[i]).start()
            rows = corr[i][:, :width].astype(F32)[DRAFT : DRAFT + 3]
            out_inner[slot] = rows.astype(BF16)
            high = pltpu.roll(mark[:DRAFT], DRAFT - 3, 0)
            out_ssm[slot] = jnp.concatenate([mark[:3], high[:3]], axis=1).astype(BF16)

    for i in range(n):

        @pl.when(slots[i] >= 0)
        def _(i=i):
            pltpu.make_async_copy(merged.at[i], kept.at[slots[i]], sem_out.at[i]).wait()


def merge(count, width, first, sources, corr):
    n = len(sources)
    hbm = pl.BlockSpec(memory_space=pl.ANY)
    vmem = pl.BlockSpec(memory_space=pltpu.VMEM)
    return pl.pallas_call(
        functools.partial(merge_kernel, tuple(range(n)), True),
        in_specs=[pl.BlockSpec(memory_space=pltpu.SMEM)] + [hbm] * n + [vmem] * n,
        out_specs=[hbm, vmem, vmem],
        out_shape=[
            jax.ShapeDtypeStruct((count, width, NSTATE), BF16),
            jax.ShapeDtypeStruct((count, KCONV - 1, width), BF16),
            jax.ShapeDtypeStruct((count, KCONV - 1, 2 * NSTATE), BF16),
        ],
        scratch_shapes=[
            pltpu.VMEM((n, width, NSTATE), BF16),
            pltpu.VMEM((n, width, NSTATE), BF16),
            pltpu.SemaphoreType.DMA((n,)),
            pltpu.SemaphoreType.DMA((n,)),
        ],
        compiler_params=pltpu.CompilerParams(vmem_limit_bytes=40 * 1024 * 1024),
        cost_estimate=pl.CostEstimate(
            flops=2 * n * width * 16 * 256,
            bytes_accessed=2 * n * width * NSTATE * 2,
            transcendentals=0,
        ),
        name="merge",
    )(first, *sources, *corr)


def passed_along(array, axis, by):
    length = lax.axis_size(axis)
    return lax.ppermute(array, axis, [(i, (i + by) % length) for i in range(length)])


def local(
    hidden_in,
    norm_gain,
    proj_gate,
    proj_inner,
    proj_ssm,
    proj_step,
    step_bias,
    decay_log,
    skip_gain,
    conv_inner,
    conv_inner_bias,
    conv_ssm,
    conv_ssm_bias,
    gate_gain,
    proj_out,
    states_in,
    edge_inner,
    edge_ssm,
    draft_lengths,
    accepted,
    destination,
):
    count, heads = states_in.shape[:2]
    depth, width = proj_inner.shape
    peers = lax.axis_size("req")
    here = lax.axis_index("req")
    side = lax.axis_index("head")
    reach = (destination // count - here) % peers
    slot = destination % count
    match = reach[None, :] == jnp.arange(WINDOW, dtype=jnp.int32)[:, None]
    index = jnp.sum(jnp.where(match, jnp.arange(count, dtype=jnp.int32)[None, :], 0), axis=1)
    flat = states_in.reshape(count, width, NSTATE)
    sources = [flat]
    for k in range(1, WINDOW):
        picked = lax.dynamic_slice_in_dim(flat, index[k], 1, 0)
        sources.append(passed_along(picked, "req", k))

    hidden = lax.all_gather(hidden_in, "head", axis=0, tiled=False)
    w_ssm = lax.all_gather(proj_ssm, "head", axis=0, tiled=False)
    ints = jnp.stack(
        [draft_lengths, accepted, reach, slot, jnp.broadcast_to(side, (count,))]
    ).astype(jnp.int32)
    pad = ((0, 0), (DRAFT - KCONV + 1, 0), (0, 0))
    results = front(
        count,
        heads,
        width,
        depth,
        (
            ints,
            hidden,
            norm_gain.reshape(1, depth),
            proj_gate,
            proj_inner,
            proj_out,
            w_ssm,
            proj_step,
            jnp.stack([step_bias, decay_log, skip_gain]),
            conv_inner,
            conv_inner_bias.reshape(1, width),
            conv_ssm,
            conv_ssm_bias.reshape(1, 2 * NSTATE),
            gate_gain.reshape(1, width),
            flat,
            jnp.pad(edge_inner, pad),
            jnp.pad(edge_ssm, pad),
        ),
    )
    mine, theirs = results[:2]
    corr = list(results[2:])
    other = passed_along(theirs, "head", 1)
    half = depth // 2
    total = mine + other
    scale = lax.rsqrt(total[:, half : half + 1] / DINNER + epsilon)
    hidden_out = (hidden_in.astype(F32) + total[:, :half] * scale).astype(BF16)
    for k in range(1, WINDOW):
        corr[k] = passed_along(corr[k], "req", k)
    kept, kept_inner, kept_ssm = merge(count, width, index[:1], sources, corr)
    return (hidden_out, kept.reshape(states_in.shape), kept_inner, kept_ssm)


def solution(mesh):
    in_specs = (
        P("req", "head"),
        P(),
        P(None, "head"),
        P(None, "head"),
        P(None, "head"),
        P(None, "head"),
        P("head"),
        P("head"),
        P("head"),
        P(None, "head"),
        P("head"),
        P(),
        P(),
        P("head"),
        P("head", None),
        P("req", "head", None, None),
        P("req", None, "head"),
        P("req", None, None),
        P("req"),
        P("req"),
        P("req"),
    )
    out_specs = (
        P("req", "head"),
        P("req", "head", None, None),
        P("req", None, "head"),
        P("req", None, None),
    )
    return jax.shard_map(local, mesh=mesh, in_specs=in_specs, out_specs=out_specs, check_vma=False)
```

time: 443 us -> 148 us (0.33)
  the two profiles are of different devices: /device:TPU:8 before, /device:TPU:0 now
where the time goes in v1:
time: 148 us
  waiting for transfers between devices  56.4 us (38%)
  starting transfers between devices  29.3 us (20%)
  Pallas kernels  21.2 us (14%)
  local copies, waits for them, and re-layouts  18.7 us (13%)
  between operations  14.3 us (10%)
  blocking collectives  4.61 us (3%)
  other arithmetic  3.06 us (2%)
    ppermute x15, waiting for transfers between devices, passed_along(): lax.ppermute(array, axis, [(i, (i + by) % length) for i in range(length)])  56.4 us
    ppermute x15, starting transfers between devices, passed_along(): lax.ppermute(array, axis, [(i, (i + by) % length) for i in range(length)])  29.3 us
    pallas_call x1, Pallas kernels, merge(): pl.pallas_call(functools.partial(merge_kernel, tuple(range(n)), True), in...  12.4 us
    unnamed x51, local copies, waits for them, and re-layouts  11 us
    pallas_call x1, Pallas kernels, front(): pl.pallas_call(functools.partial(front_kernel, count, heads), grid=(tiles...  8.78 us
    dynamic_slice x1, local copies, waits for them, and re-layouts, local(): picked = lax.dynamic_slice_in_dim(flat, index[k], 1, 0)  3.27 us
  transfers between devices with their start and end apart: 15, of which 7 were waited for; matrix products, arithmetic and copies ran while one was open for 4% of the time, Pallas kernels for 6%

profile of v1, /device:TPU:0, one launch (start us, length us, event | category | flops | bytes accessed | tf_op | source)
XLA Modules:
  0.0 147.5 jit_solution(2474426376382654959)
XLA Ops:
  0.7 1.4 fusion.5
  16.3 3.3 %constant_dynamic-slice_fusion.6 = (bf16[1,1536,128]{2,1,0:T(8,128)(2,1)}, bf16[1,1536,128]{2,1,0:T(8,128)(2,1)}, bf16[1,1536,128]{2,1,0:T(8,128)(2,1)}, bf16[1,...) fusion(bf16[6,1536,128]{2,1,0:T(8,128)(2,1)} %bitcast.20, ...), kind=kLoop, calls=%fused_computation.21 | loop fusion | bytes 5505052 | tf_op jit(solution)/shard_map/dynamic_slice | solution.py:437
  19.5 4.9 %collective-permute-start.7 = (bf16[1,1536,128]{2,1,0:T(8,128)(2,1)}, bf16[1,1536,128]{2,1,0:T(8,128)(2,1)}, u32[]{:S(2)}, u32[]{:S(2)}) collective-permute-start(bf16[1,1536,128]{2,1,0:T(8,128)(2,1)} %get-tuple-element.30), channel_id=1, source_target_pairs={{0,14},{2,16},{4,18},{6,20},{8,22},{10,24},{12,26},{14,28},{16,30}... | collective-permute-start | bytes 1179656 | tf_op jit(solution)/shard_map/ppermute | solution.py:399
  24.4 2.5 %collective-permute-start.6 = (bf16[1,1536,128]{2,1,0:T(8,128)(2,1)}, bf16[1,1536,128]{2,1,0:T(8,128)(2,1)}, u32[]{:S(2)}, u32[]{:S(2)}) collective-permute-start(bf16[1,1536,128]{2,1,0:T(8,128)(2,1)} %get-tuple-element.31), channel_id=1, source_target_pairs={{0,12},{2,14},{4,16},{6,18},{8,20},{10,22},{12,24},{14,26},{16,28}... | collective-permute-start | bytes 1179656 | tf_op jit(solution)/shard_map/ppermute | solution.py:399
  28.2 0.7 pad.8.edge_inner
  29.0 2.0 %all-gather = bf16[96,768]{1,0:T(8,128)(2,1)} all-gather(bf16[48,768]{1,0:T(8,128)(2,1)S(1)} %copy-done.16), channel_id=2, replica_groups=mesh['req'=16,'head'=2] {'head'}, dimensions={0}, use_global_device_ids=true | all-gather | bytes 221184 | tf_op jit(solution)/shard_map/all_gather | solution.py:440
  31.2 2.6 %all-gather.1 = bf16[3072,128]{1,0:T(8,128)(2,1)S(1)} all-gather(bf16[1536,128]{1,0:T(8,128)(2,1)} %param.25), channel_id=3, replica_groups=mesh['req'=16,'head'=2] {'head'}, dimensions={0}, use_global_device_ids=true | all-gather | bytes 1179648 | tf_op jit(solution)/shard_map/all_gather | solution.py:441
  34.4 1.3 stack.31.ints
  35.7 0.7 pad_maximum_fusion.head_rows
  36.4 2.3 %copy-done.1 = bf16[1536,1536]{1,0:T(8,128)(2,1)S(1)} copy-done((bf16[1536,1536]{1,0:T(8,128)(2,1)S(1)}, bf16[1536,1536]{1,0:T(8,128)(2,1)}, u32[]{:S(2)}) %copy-start.1) | copy-done | bytes 4718616
  38.7 2.3 %copy-done.2 = bf16[1536,1536]{1,0:T(8,128)(2,1)S(1)} copy-done((bf16[1536,1536]{1,0:T(8,128)(2,1)S(1)}, bf16[1536,1536]{1,0:T(8,128)(2,1)}, u32[]{:S(2)}) %copy-start.2) | copy-done | bytes 4718616
  41.1 0.9 copy-done.3
  42.0 0.9 copy-done.4
  42.9 0.7 copy-done.5
  43.6 0.7 copy-done.6
  44.3 0.7 copy-done.7
  45.0 0.7 copy-done.8
  45.7 0.7 copy-done.9
  46.4 0.7 copy-done.10
  47.1 8.8 %front.1 = (f32[48,896]{1,0:T(8,128)S(1)}, f32[48,896]{1,0:T(8,128)S(1)}, bf16[16,1792]{1,0:T(8,128)(2,1)S(1)}, bf16[16,1792]{1,0:T(8,128)(2,1)S(1)}, bf16[16,17...) custom-call(s32[5,6]{1,0:T(8,128)S(1)} %copy-done.7, ...), custom_call_target="tpu_custom_call" | custom-call | flops 679477248 | bytes 16515072 | tf_op jit(solution)/shard_map/front/pallas_call | solution.py:280
  56.6 1.0 collective-permute-start.9
  57.5 2.5 %collective-permute-start.10 = (bf16[16,1792]{1,0:T(8,128)(2,1)S(1)}, bf16[16,1792]{1,0:T(8,128)(2,1)S(1)}, u32[]{:S(2)}, u32[]{:S(2)}) collective-permute-start(bf16[16,1792]{1,0:T(8,128)(2,1)S(1)} %get-tuple-element.22), channel_id=1, source_target_pairs={{0,6},{2,8},{4,10},{6,12},{8,14},{10,16},{12,18},{14,20},{16,22},{... | collective-permute-start | bytes 172040 | tf_op jit(solution)/shard_map/ppermute | solution.py:399
  60.1 4.1 %collective-permute-done.8.refs_10_ = bf16[16,1792]{1,0:T(8,128)(2,1)S(1)} collective-permute-done((bf16[16,1792]{1,0:T(8,128)(2,1)S(1)}, bf16[16,1792]{1,0:T(8,128)(2,1)S(1)}, u32[]{:S(2)}, u32[]{:S(2)}) %collective-permute-start.8) | collective-permute-done | bytes 57376 | tf_op jit(solution)/shard_map/ppermute | solution.py:399
  64.4 2.7 %collective-permute-start.12 = (bf16[16,1792]{1,0:T(8,128)(2,1)S(1)}, bf16[16,1792]{1,0:T(8,128)(2,1)S(1)}, u32[]{:S(2)}, u32[]{:S(2)}) collective-permute-start(bf16[16,1792]{1,0:T(8,128)(2,1)S(1)} %get-tuple-element.24), channel_id=1, source_target_pairs={{0,10},{2,12},{4,14},{6,16},{8,18},{10,20},{12,22},{14,24},{16,26}... | collective-permute-start | bytes 172040 | tf_op jit(solution)/shard_map/ppermute | solution.py:399
  67.1 3.6 %collective-permute-done.11.refs_13_ = bf16[16,1792]{1,0:T(8,128)(2,1)S(1)} collective-permute-done((bf16[16,1792]{1,0:T(8,128)(2,1)S(1)}, bf16[16,1792]{1,0:T(8,128)(2,1)S(1)}, u32[]{:S(2)}, u32[]{:S(2)}) %collective-permute-start.11) | collective-permute-done | bytes 57376 | tf_op jit(solution)/shard_map/ppermute | solution.py:399
  70.7 2.4 %collective-permute-done.12.refs_14_ = bf16[16,1792]{1,0:T(8,128)(2,1)S(1)} collective-permute-done((bf16[16,1792]{1,0:T(8,128)(2,1)S(1)}, bf16[16,1792]{1,0:T(8,128)(2,1)S(1)}, u32[]{:S(2)}, u32[]{:S(2)}) %collective-permute-start.12) | collective-permute-done | bytes 57376 | tf_op jit(solution)/shard_map/ppermute | solution.py:399
  73.4 4.5 %collective-permute-done.13.refs_15_ = bf16[16,1792]{1,0:T(8,128)(2,1)S(1)} collective-permute-done((bf16[16,1792]{1,0:T(8,128)(2,1)S(1)}, bf16[16,1792]{1,0:T(8,128)(2,1)S(1)}, u32[]{:S(2)}, u32[]{:S(2)}) %collective-permute-start.13) | collective-permute-done | bytes 57376 | tf_op jit(solution)/shard_map/ppermute | solution.py:399
  78.4 17.6 %collective-permute-done.14.refs_16_ = bf16[16,1792]{1,0:T(8,128)(2,1)S(1)} collective-permute-done((bf16[16,1792]{1,0:T(8,128)(2,1)S(1)}, bf16[16,1792]{1,0:T(8,128)(2,1)S(1)}, u32[]{:S(2)}, u32[]{:S(2)}) %collective-permute-start.14) | collective-permute-done | bytes 57376 | tf_op jit(solution)/shard_map/ppermute | solution.py:399
  96.1 14.1 %collective-permute-start.2 = (bf16[1,1536,128]{2,1,0:T(8,128)(2,1)S(1)}, bf16[1,1536,128]{2,1,0:T(8,128)(2,1)S(1)}, u32[]{:S(2)}, u32[]{:S(2)}) collective-permute-start(bf16[1,1536,128]{2,1,0:T(8,128)(2,1)S(1)} %copy-done.12), channel_id=1, source_target_pairs={{0,4},{2,6},{4,8},{6,10},{8,12},{10,14},{12,16},{14,18},{16,20},{1... | collective-permute-start | bytes 1179656 | tf_op jit(solution)/shard_map/ppermute | solution.py:399
  110.3 0.7 fusion.1
  111.0 24.0 %collective-permute-done.5.refs_6_ = bf16[1,1536,128]{2,1,0:T(8,128)(2,1)S(1)} collective-permute-done((bf16[1,1536,128]{2,1,0:T(8,128)(2,1)S(1)}, bf16[1,1536,128]{2,1,0:T(8,128)(2,1)S(1)}, u32[]{:S(2)}, u32[]{:S(2)}) %collective-permute-start.5) | collective-permute-done | bytes 393248 | tf_op jit(solution)/shard_map/ppermute | solution.py:399
  135.1 12.4 %merge.1 = (bf16[6,1536,128]{2,1,0:T(8,128)(2,1)}, bf16[6,3,1536]{2,1,0:T(4,128)(2,1)}, bf16[6,3,256]{2,1,0:T(4,128)(2,1)}) custom-call(s32[1]{0:T(128)} %get-tuple-element.44.refs_0_, bf16[6,1536,128]{2,1,0:T(8,128)(2,1)S(1)} %bitcast.22, bf16[1,1536,128]{2,1,0:T(8,128)(2,1)S(1)} %collective-permute-done.1.refs_2_, ...), custom_call_target="tpu_custom_call" | custom-call | flops 100663296 | bytes 6291456 | tf_op jit(solution)/shard_map/merge/pallas_call | solution.py:372
  (68 shorter events, 4.8 us)
Async XLA Ops:
  0.6 35.8 %copy-start = (bf16[6,24,64,128]{3,2,1,0:T(8,128)(2,1)S(1)}, bf16[6,24,64,128]{3,2,1,0:T(8,128)(2,1)}, u32[]{:S(2)}) copy-start(bf16[6,24,64,128]{3,2,1,0:T(8,128)(2,1)} %param.36) | copy-start | bytes 7077892
  0.6 26.3 %copy-start.21 = (f32[1536]{0:T(1024)S(1)}, f32[1536]{0:T(1024)}, u32[]{:S(2)}) copy-start(f32[1536]{0:T(1024)} %param.22) | copy-start | bytes 18436
  0.7 26.3 %copy-start.22 = (f32[1536]{0:T(1024)S(1)}, f32[1536]{0:T(1024)}, u32[]{:S(2)}) copy-start(f32[1536]{0:T(1024)} %param.31) | copy-start | bytes 18436
  0.7 26.4 %copy-start.23 = (f32[1536]{0:T(1024)S(1)}, f32[1536]{0:T(1024)}, u32[]{:S(2)}) copy-start(f32[1536]{0:T(1024)} %param.34) | copy-start | bytes 18436
  0.7 27.0 %copy-start.20 = (bf16[6,3,256]{2,1,0:T(4,128)(2,1)S(1)}, bf16[6,3,256]{2,1,0:T(4,128)(2,1)}, u32[]{:S(2)}) copy-start(bf16[6,3,256]{2,1,0:T(4,128)(2,1)} %param.38) | copy-start | bytes 27652
  0.7 27.6 %copy-start.18 = (bf16[6,3,1536]{2,1,0:T(4,128)(2,1)S(1)}, bf16[6,3,1536]{2,1,0:T(4,128)(2,1)}, u32[]{:S(2)}) copy-start(bf16[6,3,1536]{2,1,0:T(4,128)(2,1)} %param.37) | copy-start | bytes 165892
  0.7 28.3 %copy-start.16 = (bf16[48,768]{1,0:T(8,128)(2,1)S(1)}, bf16[48,768]{1,0:T(8,128)(2,1)}, u32[]{:S(2)}) copy-start(bf16[48,768]{1,0:T(8,128)(2,1)} %param.21) | copy-start | bytes 221188
  0.7 30.3 %copy-start.19 = (bf16[1536,24]{0,1:T(8,128)(2,1)S(1)}, bf16[1536,24]{0,1:T(8,128)(2,1)}, u32[]{:S(2)}) copy-start(bf16[1536,24]{0,1:T(8,128)(2,1)} %param.26) | copy-start | bytes 221188
  2.1 26.8 %copy-start.24 = (s32[6]{0:T(128)}, s32[6]{0:T(128)S(1)}, u32[]{:S(2)}) copy-start(s32[6]{0:T(128)S(1)} %get-tuple-element.46) | copy-start | bytes 76
  19.5 76.5 %collective-permute-start.7 = (bf16[1,1536,128]{2,1,0:T(8,128)(2,1)}, bf16[1,1536,128]{2,1,0:T(8,128)(2,1)}, u32[]{:S(2)}, u32[]{:S(2)}) collective-permute-start(bf16[1,1536,128]{2,1,0:T(8,128)(2,1)} %get-tuple-element.30), channel_id=1, source_target_pairs={{0,14},{2,16},{4,18},{6,20},{8,22},{10,24},{12,26},{14,28},{16,30}... | collective-permute-start | bytes 1179656 | tf_op jit(solution)/shard_map/ppermute | solution.py:399
  24.4 85.7 %collective-permute-start.6 = (bf16[1,1536,128]{2,1,0:T(8,128)(2,1)}, bf16[1,1536,128]{2,1,0:T(8,128)(2,1)}, u32[]{:S(2)}, u32[]{:S(2)}) collective-permute-start(bf16[1,1536,128]{2,1,0:T(8,128)(2,1)} %get-tuple-element.31), channel_id=1, source_target_pairs={{0,12},{2,14},{4,16},{6,18},{8,20},{10,22},{12,24},{14,26},{16,28}... | collective-permute-start | bytes 1179656 | tf_op jit(solution)/shard_map/ppermute | solution.py:399
  36.4 2.3 %copy-start.1 = (bf16[1536,1536]{1,0:T(8,128)(2,1)S(1)}, bf16[1536,1536]{1,0:T(8,128)(2,1)}, u32[]{:S(2)}) copy-start(bf16[1536,1536]{1,0:T(8,128)(2,1)} %w_gate.1) | copy-start | bytes 14155780
  38.7 2.3 %copy-start.2 = (bf16[1536,1536]{1,0:T(8,128)(2,1)S(1)}, bf16[1536,1536]{1,0:T(8,128)(2,1)}, u32[]{:S(2)}) copy-start(bf16[1536,1536]{1,0:T(8,128)(2,1)} %w_inner.1) | copy-start | bytes 14155780
  47.1 30.8 %copy-start.15 = (bf16[1,1536,128]{2,1,0:T(8,128)(2,1)S(1)}, bf16[1,1536,128]{2,1,0:T(8,128)(2,1)}, u32[]{:S(2)}) copy-start(bf16[1,1536,128]{2,1,0:T(8,128)(2,1)} %get-tuple-element.32) | copy-start | bytes 1179652
  47.1 48.9 %copy-start.14 = (bf16[1,1536,128]{2,1,0:T(8,128)(2,1)S(1)}, bf16[1,1536,128]{2,1,0:T(8,128)(2,1)}, u32[]{:S(2)}) copy-start(bf16[1,1536,128]{2,1,0:T(8,128)(2,1)} %get-tuple-element.33) | copy-start | bytes 1179652
  47.1 48.9 %copy-start.13 = (bf16[1,1536,128]{2,1,0:T(8,128)(2,1)S(1)}, bf16[1,1536,128]{2,1,0:T(8,128)(2,1)}, u32[]{:S(2)}) copy-start(bf16[1,1536,128]{2,1,0:T(8,128)(2,1)} %get-tuple-element.34) | copy-start | bytes 1179652
  47.1 49.0 %copy-start.12 = (bf16[1,1536,128]{2,1,0:T(8,128)(2,1)S(1)}, bf16[1,1536,128]{2,1,0:T(8,128)(2,1)}, u32[]{:S(2)}) copy-start(bf16[1,1536,128]{2,1,0:T(8,128)(2,1)} %get-tuple-element.35) | copy-start | bytes 1179652
  47.1 63.1 %copy-start.11 = (bf16[1,1536,128]{2,1,0:T(8,128)(2,1)S(1)}, bf16[1,1536,128]{2,1,0:T(8,128)(2,1)}, u32[]{:S(2)}) copy-start(bf16[1,1536,128]{2,1,0:T(8,128)(2,1)} %get-tuple-element.36) | copy-start | bytes 1179652
  47.1 63.2 %copy-start.17 = (bf16[48,768]{1,0:T(8,128)(2,1)S(1)}, bf16[48,768]{1,0:T(8,128)(2,1)}, u32[]{:S(2)}) copy-start(bf16[48,768]{1,0:T(8,128)(2,1)} %param.21) | copy-start | bytes 221188
  55.9 8.3 %collective-permute-start.8 = (bf16[16,1792]{1,0:T(8,128)(2,1)S(1)}, bf16[16,1792]{1,0:T(8,128)(2,1)S(1)}, u32[]{:S(2)}, u32[]{:S(2)}) collective-permute-start(bf16[16,1792]{1,0:T(8,128)(2,1)S(1)} %get-tuple-element.20), channel_id=1, source_target_pairs={{0,2},{2,4},{4,6},{6,8},{8,10},{10,12},{12,14},{14,16},{16,18},{18... | collective-permute-start | bytes 172040 | tf_op jit(solution)/shard_map/ppermute | solution.py:399
  56.6 7.6 %collective-permute-start.9 = (bf16[16,1792]{1,0:T(8,128)(2,1)S(1)}, bf16[16,1792]{1,0:T(8,128)(2,1)S(1)}, u32[]{:S(2)}, u32[]{:S(2)}) collective-permute-start(bf16[16,1792]{1,0:T(8,128)(2,1)S(1)} %get-tuple-element.21), channel_id=1, source_target_pairs={{0,4},{2,6},{4,8},{6,10},{8,12},{10,14},{12,16},{14,18},{16,20},{1... | collective-permute-start | bytes 172040 | tf_op jit(solution)/shard_map/ppermute | solution.py:399
  57.5 6.9 %collective-permute-start.10 = (bf16[16,1792]{1,0:T(8,128)(2,1)S(1)}, bf16[16,1792]{1,0:T(8,128)(2,1)S(1)}, u32[]{:S(2)}, u32[]{:S(2)}) collective-permute-start(bf16[16,1792]{1,0:T(8,128)(2,1)S(1)} %get-tuple-element.22), channel_id=1, source_target_pairs={{0,6},{2,8},{4,10},{6,12},{8,14},{10,16},{12,18},{14,20},{16,22},{... | collective-permute-start | bytes 172040 | tf_op jit(solution)/shard_map/ppermute | solution.py:399
  64.2 31.8 %collective-permute-start = (f32[48,896]{1,0:T(8,128)S(1)}, f32[48,896]{1,0:T(8,128)S(1)}, u32[]{:S(2)}, u32[]{:S(2)}) collective-permute-start(f32[48,896]{1,0:T(8,128)S(1)} %get-tuple-element.18), channel_id=1, source_target_pairs={{0,1},{1,0},{2,3},{3,2},{4,5},{5,4},{6,7},{7,6},{8,9},{9,8},{10,11... | collective-permute-start | bytes 516104 | tf_op jit(solution)/shard_map/ppermute | solution.py:399
  64.2 6.5 %collective-permute-start.11 = (bf16[16,1792]{1,0:T(8,128)(2,1)S(1)}, bf16[16,1792]{1,0:T(8,128)(2,1)S(1)}, u32[]{:S(2)}, u32[]{:S(2)}) collective-permute-start(bf16[16,1792]{1,0:T(8,128)(2,1)S(1)} %get-tuple-element.23), channel_id=1, source_target_pairs={{0,8},{2,10},{4,12},{6,14},{8,16},{10,18},{12,20},{14,22},{16,24},... | collective-permute-start | bytes 172040 | tf_op jit(solution)/shard_map/ppermute | solution.py:399
  64.4 8.7 %collective-permute-start.12 = (bf16[16,1792]{1,0:T(8,128)(2,1)S(1)}, bf16[16,1792]{1,0:T(8,128)(2,1)S(1)}, u32[]{:S(2)}, u32[]{:S(2)}) collective-permute-start(bf16[16,1792]{1,0:T(8,128)(2,1)S(1)} %get-tuple-element.24), channel_id=1, source_target_pairs={{0,10},{2,12},{4,14},{6,16},{8,18},{10,20},{12,22},{14,24},{16,26}... | collective-permute-start | bytes 172040 | tf_op jit(solution)/shard_map/ppermute | solution.py:399
  70.7 7.2 %collective-permute-start.13 = (bf16[16,1792]{1,0:T(8,128)(2,1)S(1)}, bf16[16,1792]{1,0:T(8,128)(2,1)S(1)}, u32[]{:S(2)}, u32[]{:S(2)}) collective-permute-start(bf16[16,1792]{1,0:T(8,128)(2,1)S(1)} %get-tuple-element.25), channel_id=1, source_target_pairs={{0,12},{2,14},{4,16},{6,18},{8,20},{10,22},{12,24},{14,26},{16,28}... | collective-permute-start | bytes 172040 | tf_op jit(solution)/shard_map/ppermute | solution.py:399
  73.1 22.9 %collective-permute-start.14 = (bf16[16,1792]{1,0:T(8,128)(2,1)S(1)}, bf16[16,1792]{1,0:T(8,128)(2,1)S(1)}, u32[]{:S(2)}, u32[]{:S(2)}) collective-permute-start(bf16[16,1792]{1,0:T(8,128)(2,1)S(1)} %get-tuple-element.26), channel_id=1, source_target_pairs={{0,14},{2,16},{4,18},{6,20},{8,22},{10,24},{12,26},{14,28},{16,30}... | collective-permute-start | bytes 172040 | tf_op jit(solution)/shard_map/ppermute | solution.py:399
  77.9 57.2 %collective-permute-start.5 = (bf16[1,1536,128]{2,1,0:T(8,128)(2,1)S(1)}, bf16[1,1536,128]{2,1,0:T(8,128)(2,1)S(1)}, u32[]{:S(2)}, u32[]{:S(2)}) collective-permute-start(bf16[1,1536,128]{2,1,0:T(8,128)(2,1)S(1)} %copy-done.15), channel_id=1, source_target_pairs={{0,10},{2,12},{4,14},{6,16},{8,18},{10,20},{12,22},{14,24},{16,26}... | collective-permute-start | bytes 1179656 | tf_op jit(solution)/shard_map/ppermute | solution.py:399
  96.0 39.1 %collective-permute-start.4 = (bf16[1,1536,128]{2,1,0:T(8,128)(2,1)S(1)}, bf16[1,1536,128]{2,1,0:T(8,128)(2,1)S(1)}, u32[]{:S(2)}, u32[]{:S(2)}) collective-permute-start(bf16[1,1536,128]{2,1,0:T(8,128)(2,1)S(1)} %copy-done.14), channel_id=1, source_target_pairs={{0,8},{2,10},{4,12},{6,14},{8,16},{10,18},{12,20},{14,22},{16,24},... | collective-permute-start | bytes 1179656 | tf_op jit(solution)/shard_map/ppermute | solution.py:399
  96.0 39.1 %collective-permute-start.3 = (bf16[1,1536,128]{2,1,0:T(8,128)(2,1)S(1)}, bf16[1,1536,128]{2,1,0:T(8,128)(2,1)S(1)}, u32[]{:S(2)}, u32[]{:S(2)}) collective-permute-start(bf16[1,1536,128]{2,1,0:T(8,128)(2,1)S(1)} %copy-done.13), channel_id=1, source_target_pairs={{0,6},{2,8},{4,10},{6,12},{8,14},{10,16},{12,18},{14,20},{16,22},{... | collective-permute-start | bytes 1179656 | tf_op jit(solution)/shard_map/ppermute | solution.py:399
  96.1 39.0 %collective-permute-start.2 = (bf16[1,1536,128]{2,1,0:T(8,128)(2,1)S(1)}, bf16[1,1536,128]{2,1,0:T(8,128)(2,1)S(1)}, u32[]{:S(2)}, u32[]{:S(2)}) collective-permute-start(bf16[1,1536,128]{2,1,0:T(8,128)(2,1)S(1)} %copy-done.12), channel_id=1, source_target_pairs={{0,4},{2,6},{4,8},{6,10},{8,12},{10,14},{12,16},{14,18},{16,20},{1... | collective-permute-start | bytes 1179656 | tf_op jit(solution)/shard_map/ppermute | solution.py:399
  110.2 24.9 %collective-permute-start.1 = (bf16[1,1536,128]{2,1,0:T(8,128)(2,1)S(1)}, bf16[1,1536,128]{2,1,0:T(8,128)(2,1)S(1)}, u32[]{:S(2)}, u32[]{:S(2)}) collective-permute-start(bf16[1,1536,128]{2,1,0:T(8,128)(2,1)S(1)} %copy-done.11), channel_id=1, source_target_pairs={{0,2},{2,4},{4,6},{6,8},{8,10},{10,12},{12,14},{14,16},{16,18},{18... | collective-permute-start | bytes 1179656 | tf_op jit(solution)/shard_map/ppermute | solution.py:399
  (8 other events, 6.0 us)

commit v2 on v1

--- a/solution.py
+++ b/solution.py
@@ -50,7 +50,9 @@
 def front_kernel(
     count,
     heads,
-    ints,
+    table,
+    lengths_in,
+    accepted_in,
     hidden,
     norm_gain,
     w_gate,
@@ -71,8 +73,8 @@
     theirs,
     *rest,
 ):
-    corr = rest[:WINDOW]
-    normed, acc, squares, quant, gmat, cmat, select, boxes = rest[WINDOW:]
+    corr = rest[:count]
+    normed, acc, squares, quant, gmat, cmat, select, boxes = rest[count:]
     step = pl.program_id(0)
     last = pl.num_programs(0) - 1
     rows = count * DRAFT
@@ -87,15 +89,12 @@
         normed[...] = norm
         acc[...] = jnp.zeros_like(acc)
         squares[...] = jnp.zeros_like(squares)
-        boxes[...] = jnp.zeros_like(boxes)
-        for k in range(WINDOW):
-            corr[k][...] = jnp.zeros_like(corr[k])
         row = iota((rows, rows), 0)
         col = iota((rows, rows), 1)
         request = row >> 3
         taken = jnp.zeros((rows, rows), jnp.int32)
         for r in range(count):
-            taken = jnp.where(request == r, ints[1, r], taken)
+            taken = jnp.where(request == r, accepted_in[r], taken)
         same = request == (col >> 3)
         lower = same & ((col & 7) <= (row & 7))
         before = same & ((col & 7) < taken)
@@ -104,8 +103,8 @@
         chosen = jnp.zeros((rows, heads), jnp.int32)
         hrow = iota((rows, heads), 0)
         for r in range(count):
-            lengths = jnp.where((hrow >> 3) == r, ints[0, r], lengths)
-            chosen = jnp.where((hrow >> 3) == r, ints[1, r], chosen)
+            lengths = jnp.where((hrow >> 3) == r, lengths_in[r], lengths)
+            chosen = jnp.where((hrow >> 3) == r, accepted_in[r], chosen)
         soft = jnp.maximum(raw, 0.0) + jnp.log1p(jnp.exp(-jnp.abs(raw)))
         size = jnp.where((hrow & 7) < lengths, soft, 0.0)
         rate = -jnp.exp(head_rows[1:2])
@@ -162,7 +161,7 @@
         place = iota((DRAFT, NSTATE), 0)
         for r in range(count):
             own = kept[r * DRAFT : (r + 1) * DRAFT]
-            slot = jnp.full((DRAFT, NSTATE), (ints[3, r] + 1).astype(F32))
+            slot = jnp.full((DRAFT, NSTATE), (table[1, r] + 1).astype(F32))
             packed = jnp.where(
                 place < 3,
                 own[:, :NSTATE],
@@ -170,8 +169,8 @@
             )
             top = jnp.concatenate([wide_b[r * DRAFT : (r + 1) * DRAFT], packed], axis=1)
             low = jnp.concatenate([jnp.zeros((DRAFT, NSTATE), F32), slot], axis=1)
-            boxes[ints[2, r]] = jnp.concatenate([top, low], axis=0).astype(BF16)
-        for k in range(WINDOW):
+            boxes[table[0, r]] = jnp.concatenate([top, low], axis=0).astype(BF16)
+        for k in range(count):
             corr[k][:, width : width + EXTRA] = boxes[k]
 
     norm = normed[...]
@@ -222,9 +221,9 @@
     )
     for r in range(count):
         span = slice(r * DRAFT, (r + 1) * DRAFT)
-        boxes[ints[2, r]] = jnp.concatenate([delta[span], second[span]], axis=0).astype(BF16)
+        boxes[table[0, r]] = jnp.concatenate([delta[span], second[span]], axis=0).astype(BF16)
     here = pl.ds(pl.multiple_of(step * TILE, TILE), TILE)
-    for k in range(WINDOW):
+    for k in range(count):
         corr[k][:, here] = boxes[k]
 
     @pl.when(step == last)
@@ -235,12 +234,12 @@
         mine[:, half:] = total_square
         theirs[:, half:] = total_square
 
-        @pl.when(ints[4, 0] == 0)
+        @pl.when(table[2, 0] == 0)
         def _():
             mine[:, :half] = acc[:, :half]
             theirs[:, :half] = acc[:, half:]
 
-        @pl.when(ints[4, 0] != 0)
+        @pl.when(table[2, 0] != 0)
         def _():
             mine[:, :half] = acc[:, half:]
             theirs[:, :half] = acc[:, :half]
@@ -254,7 +253,7 @@
         return pl.BlockSpec(shape, lambda j: (0,) * len(shape))
 
     in_specs = [
-        pl.BlockSpec(memory_space=pltpu.SMEM),
+        *[pl.BlockSpec(memory_space=pltpu.SMEM)] * 3,
         whole((2, rows, depth // 2)),
         whole((1, depth)),
         pl.BlockSpec((depth, TILE), lambda j: (0, j)),
@@ -275,8 +274,8 @@
     out_width = depth // 2 + 128
     out_shape = [jax.ShapeDtypeStruct((rows, out_width), F32)] * 2 + [
         jax.ShapeDtypeStruct((2 * DRAFT, width + EXTRA), BF16)
-    ] * WINDOW
-    out_specs = [whole((rows, out_width))] * 2 + [whole((2 * DRAFT, width + EXTRA))] * WINDOW
+    ] * count
+    out_specs = [whole((rows, out_width))] * 2 + [whole((2 * DRAFT, width + EXTRA))] * count
     return pl.pallas_call(
         functools.partial(front_kernel, count, heads),
         grid=(tiles,),
@@ -291,11 +290,9 @@
             pltpu.VMEM((rows, NSTATE), F32),
             pltpu.VMEM((rows, NSTATE), F32),
             pltpu.VMEM((2, rows, rows), BF16),
-            pltpu.VMEM((WINDOW, 2 * DRAFT, TILE), BF16),
+            pltpu.VMEM((count, 2 * DRAFT, TILE), BF16),
         ],
-        compiler_params=pltpu.CompilerParams(
-            dimension_semantics=("arbitrary",), vmem_limit_bytes=40 * 1024 * 1024
-        ),
+        compiler_params=pltpu.CompilerParams(dimension_semantics=("arbitrary",)),
         cost_estimate=pl.CostEstimate(
             flops=2 * rows * depth * width * 3,
             bytes_accessed=3 * depth * width * 2 + count * width * NSTATE * 2,
@@ -305,93 +302,145 @@
     )(*args)
 
 
-def merge_kernel(offsets, local_first, *refs):
-    n = len(offsets)
-    ints = refs[0]
-    sources = refs[1 : 1 + n]
-    corr = refs[1 + n : 1 + 2 * n]
-    kept, out_inner, out_ssm = refs[1 + 2 * n : 4 + 2 * n]
-    loaded, merged, sem_in, sem_out = refs[4 + 2 * n :]
-    width = loaded.shape[1]
-
-    def source(i):
-        if local_first and i == 0:
-            return sources[0].at[ints[0]]
-        return sources[i].at[0]
-
-    def fetch(i):
-        return pltpu.make_async_copy(source(i), loaded.at[i], sem_in.at[i])
-
-    for i in range(n):
-        fetch(i).start()
-    slots = []
-    for i in range(n):
-        mark = corr[i][:, width + NSTATE : width + 2 * NSTATE].astype(F32)
-        slot = jnp.max(mark[DRAFT:]).astype(jnp.int32) - 1
-        slots.append(slot)
-        fetch(i).wait()
-
-        @pl.when(slot >= 0)
-        def _(i=i, slot=slot, mark=mark):
-            ones = jnp.where(
-                (iota((2 * DRAFT, NSTATE), 0) == 11) | (iota((2 * DRAFT, NSTATE), 0) == 12),
-                1.0,
-                0.0,
-            ).astype(BF16)
-            right = jnp.concatenate([corr[i][:, width : width + NSTATE], ones], axis=1)
-
-            @pl.loop(0, width // TILE)
-            def _(c):
-                span = pl.ds(pl.multiple_of(c * TILE, TILE), TILE)
-                both = lax.dot_general(
-                    corr[i][:, span],
-                    right,
-                    (((0,), (0,)), ((), ())),
-                    preferred_element_type=F32,
-                )
-                state = loaded[i, span].astype(F32)
-                merged[i, span] = (both[:, NSTATE:] * state + both[:, :NSTATE]).astype(BF16)
-
-            pltpu.make_async_copy(merged.at[i], kept.at[slot], sem_out.at[i]).start()
-            rows = corr[i][:, :width].astype(F32)[DRAFT : DRAFT + 3]
-            out_inner[slot] = rows.astype(BF16)
+def pick_kernel(count, peers, destination, states, *outs):
+    picked = outs[:count]
+    table, branch, sems = outs[count:]
+    here = lax.axis_index("req")
+    reach = [
+        lax.rem(lax.div(destination[r], count) - here + peers, peers) for r in range(count)
+    ]
+    rank = []
+    for r in range(count):
+        below = [(reach[q] < reach[r]).astype(jnp.int32) for q in range(count) if q != r]
+        rank.append(sum(below))
+        table[0, r] = rank[r]
+        table[1, r] = lax.rem(destination[r], count)
+        table[2, r] = lax.axis_index("head")
+    copies = []
+    for j in range(count):
+        source = sum((rank[r] == j).astype(jnp.int32) * r for r in range(count))
+        copy = pltpu.make_async_copy(states.at[source], picked[j].at[0], sems.at[j])
+        copy.start()
+        copies.append(copy)
+    low = jnp.int32(0)
+    run = jnp.int32(1)
+    for b in range(WINDOW):
+        found = sum((reach[r] == b).astype(jnp.int32) for r in range(count))
+        run = run * found
+        low = low + run
+    high = WINDOW * (WINDOW - 1) // 2 - sum(reach) - low
+    branch[0] = lax.div(low * (2 * WINDOW - 1 - low), 2) + high - low - 1
+    for copy in copies:
+        copy.wait()
+
+
+def pick(count, width, peers, destination, states):
+    hbm = pl.BlockSpec(memory_space=pl.ANY)
+    smem = pl.BlockSpec(memory_space=pltpu.SMEM)
+    return pl.pallas_call(
+        functools.partial(pick_kernel, count, peers),
+        in_specs=[smem, hbm],
+        out_specs=[hbm] * count + [smem] * 2,
+        out_shape=[jax.ShapeDtypeStruct((1, width, NSTATE), BF16)] * count
+        + [
+            jax.ShapeDtypeStruct((3, count), jnp.int32),
+            jax.ShapeDtypeStruct((1,), jnp.int32),
+        ],
+        scratch_shapes=[pltpu.SemaphoreType.DMA((count,))],
+        name="pick",
+    )(destination, states)
+
+
+MERGE_PARTS = 3
+
+
+def merge_kernel(count, final, *refs):
+    source = refs[0]
+    corr = refs[1]
+    n = 2 + (count - 1 if final else 0)
+    others = refs[2:n]
+    refs = refs[n:]
+    if len(refs) == (8 if final else 6):
+        refs = refs[1:]
+    kept = refs[0]
+    loaded, merged, sem_in, sem_out = refs[-4:]
+    width = loaded.shape[0]
+    part = width // MERGE_PARTS
+
+    def span(c):
+        return slice(c * part, (c + 1) * part)
+
+    def fetch(c):
+        return pltpu.make_async_copy(source.at[0, span(c)], loaded.at[span(c)], sem_in.at[c])
+
+    def mark_of(ref):
+        mark = ref[:, width + NSTATE : width + 2 * NSTATE].astype(F32)
+        return mark, jnp.max(mark[DRAFT:]).astype(jnp.int32) - 1
+
+    for c in range(MERGE_PARTS):
+        fetch(c).start()
+    slot = mark_of(corr)[1]
+
+    def put(c):
+        return pltpu.make_async_copy(
+            merged.at[span(c)], kept.at[slot, span(c)], sem_out.at[c]
+        )
+
+    line = iota((2 * DRAFT, NSTATE), 0)
+    ones = jnp.where((line == 11) | (line == 12), 1.0, 0.0).astype(BF16)
+    right = jnp.concatenate([corr[:, width : width + NSTATE], ones], axis=1)
+    for c in range(MERGE_PARTS):
+        both = lax.dot_general(
+            corr[:, span(c)], right, (((0,), (0,)), ((), ())), preferred_element_type=F32
+        )
+        fetch(c).wait()
+        state = loaded[span(c)].astype(F32)
+        merged[span(c)] = (both[:, NSTATE:] * state + both[:, :NSTATE]).astype(BF16)
+        put(c).start()
+    if final:
+        out_inner, out_ssm = refs[1:3]
+        for ref in (corr, *others):
+            mark, target = mark_of(ref)
+            rows = ref[:, :width].astype(F32)[DRAFT : DRAFT + 3]
+            out_inner[target] = rows.astype(BF16)
             high = pltpu.roll(mark[:DRAFT], DRAFT - 3, 0)
-            out_ssm[slot] = jnp.concatenate([mark[:3], high[:3]], axis=1).astype(BF16)
-
-    for i in range(n):
-
-        @pl.when(slots[i] >= 0)
-        def _(i=i):
-            pltpu.make_async_copy(merged.at[i], kept.at[slots[i]], sem_out.at[i]).wait()
-
-
-def merge(count, width, first, sources, corr):
-    n = len(sources)
+            out_ssm[target] = jnp.concatenate([mark[:3], high[:3]], axis=1).astype(BF16)
+    for c in range(MERGE_PARTS):
+        put(c).wait()
+
+
+def merge(count, width, kept, source, corr, others=()):
     hbm = pl.BlockSpec(memory_space=pl.ANY)
     vmem = pl.BlockSpec(memory_space=pltpu.VMEM)
-    return pl.pallas_call(
-        functools.partial(merge_kernel, tuple(range(n)), True),
-        in_specs=[pl.BlockSpec(memory_space=pltpu.SMEM)] + [hbm] * n + [vmem] * n,
-        out_specs=[hbm, vmem, vmem],
-        out_shape=[
-            jax.ShapeDtypeStruct((count, width, NSTATE), BF16),
+    final = len(others) > 0
+    inputs = [source, corr, *others] + ([] if kept is None else [kept])
+    out_shape = [jax.ShapeDtypeStruct((count, width, NSTATE), BF16)]
+    if final:
+        out_shape += [
             jax.ShapeDtypeStruct((count, KCONV - 1, width), BF16),
             jax.ShapeDtypeStruct((count, KCONV - 1, 2 * NSTATE), BF16),
+        ]
+    return pl.pallas_call(
+        functools.partial(merge_kernel, count, final),
+        in_specs=[hbm]
+        + [vmem] * (1 + len(others))
+        + ([] if kept is None else [hbm]),
+        out_specs=[hbm] + [vmem] * (len(out_shape) - 1),
+        out_shape=out_shape,
+        input_output_aliases={} if kept is None else {len(inputs) - 1: 0},
+        scratch_shapes=[
+            pltpu.VMEM((width, NSTATE), BF16),
+            pltpu.VMEM((width, NSTATE), BF16),
+            pltpu.SemaphoreType.DMA((MERGE_PARTS,)),
+            pltpu.SemaphoreType.DMA((MERGE_PARTS,)),
         ],
-        scratch_shapes=[
-            pltpu.VMEM((n, width, NSTATE), BF16),
-            pltpu.VMEM((n, width, NSTATE), BF16),
-            pltpu.SemaphoreType.DMA((n,)),
-            pltpu.SemaphoreType.DMA((n,)),
-        ],
-        compiler_params=pltpu.CompilerParams(vmem_limit_bytes=40 * 1024 * 1024),
         cost_estimate=pl.CostEstimate(
-            flops=2 * n * width * 16 * 256,
-            bytes_accessed=2 * n * width * NSTATE * 2,
+            flops=2 * width * 16 * 256,
+            bytes_accessed=2 * width * NSTATE * 2,
             transcendentals=0,
         ),
         name="merge",
-    )(first, *sources, *corr)
+    )(*inputs)
 
 
 def passed_along(array, axis, by):
@@ -425,59 +474,121 @@
     count, heads = states_in.shape[:2]
     depth, width = proj_inner.shape
     peers = lax.axis_size("req")
-    here = lax.axis_index("req")
-    side = lax.axis_index("head")
-    reach = (destination // count - here) % peers
-    slot = destination % count
-    match = reach[None, :] == jnp.arange(WINDOW, dtype=jnp.int32)[:, None]
-    index = jnp.sum(jnp.where(match, jnp.arange(count, dtype=jnp.int32)[None, :], 0), axis=1)
     flat = states_in.reshape(count, width, NSTATE)
-    sources = [flat]
-    for k in range(1, WINDOW):
-        picked = lax.dynamic_slice_in_dim(flat, index[k], 1, 0)
-        sources.append(passed_along(picked, "req", k))
-
-    hidden = lax.all_gather(hidden_in, "head", axis=0, tiled=False)
-    w_ssm = lax.all_gather(proj_ssm, "head", axis=0, tiled=False)
-    ints = jnp.stack(
-        [draft_lengths, accepted, reach, slot, jnp.broadcast_to(side, (count,))]
-    ).astype(jnp.int32)
-    pad = ((0, 0), (DRAFT - KCONV + 1, 0), (0, 0))
-    results = front(
-        count,
-        heads,
-        width,
-        depth,
+    results = pick(count, width, peers, destination, flat)
+    picked = list(results[:count])
+    table, branch = results[count:]
+    half = depth // 2
+    given = (
+        norm_gain,
+        proj_gate,
+        proj_inner,
+        proj_out,
+        proj_step,
+        step_bias,
+        decay_log,
+        skip_gain,
+        conv_inner,
+        conv_inner_bias,
+        conv_ssm,
+        conv_ssm_bias,
+        gate_gain,
+        flat,
+        edge_inner,
+        edge_ssm,
+        draft_lengths,
+        accepted,
+    )
+
+    def layer(table, hidden_in, proj_ssm, given):
         (
-            ints,
-            hidden,
-            norm_gain.reshape(1, depth),
+            norm_gain,
             proj_gate,
             proj_inner,
             proj_out,
-            w_ssm,
             proj_step,
-            jnp.stack([step_bias, decay_log, skip_gain]),
+            step_bias,
+            decay_log,
+            skip_gain,
             conv_inner,
-            conv_inner_bias.reshape(1, width),
+            conv_inner_bias,
             conv_ssm,
-            conv_ssm_bias.reshape(1, 2 * NSTATE),
-            gate_gain.reshape(1, width),
+            conv_ssm_bias,
+            gate_gain,
             flat,
-            jnp.pad(edge_inner, pad),
-            jnp.pad(edge_ssm, pad),
-        ),
+            edge_inner,
+            edge_ssm,
+            draft_lengths,
+            accepted,
+        ) = given
+        pad = ((0, 0), (DRAFT - KCONV + 1, 0), (0, 0))
+        return front(
+            count,
+            heads,
+            width,
+            depth,
+            (
+                table,
+                draft_lengths,
+                accepted,
+                lax.all_gather(hidden_in, "head", axis=0, tiled=False),
+                norm_gain.reshape(1, depth),
+                proj_gate,
+                proj_inner,
+                proj_out,
+                lax.all_gather(proj_ssm, "head", axis=0, tiled=False),
+                proj_step,
+                jnp.stack([step_bias, decay_log, skip_gain]),
+                conv_inner,
+                conv_inner_bias.reshape(1, width),
+                conv_ssm,
+                conv_ssm_bias.reshape(1, 2 * NSTATE),
+                gate_gain.reshape(1, width),
+                flat,
+                jnp.pad(edge_inner, pad),
+                jnp.pad(edge_ssm, pad),
+            ),
+        )
+
+    def run(offsets, operands):
+        table, picked, hidden_in, proj_ssm, given = operands
+        results = layer(table, hidden_in, proj_ssm, given)
+        mine, theirs = results[:2]
+        corr = list(results[2:])
+        arrived = list(picked)
+        for j, k in enumerate(offsets):
+            if k > 0:
+                state = picked[j]
+                if j == 0:
+                    state, corr[j] = lax.optimization_barrier((state, corr[j]))
+                arrived[j] = passed_along(state, "req", k)
+        pair = lax.all_gather(theirs, "head", axis=0, tiled=False)
+        other = jnp.where(lax.axis_index("head") == 0, pair[1], pair[0])
+        total = mine + other
+        scale = lax.rsqrt(total[:, half : half + 1] / DINNER + epsilon)
+        hidden_out = (hidden_in.astype(F32) + total[:, :half] * scale).astype(BF16)
+        for j, k in enumerate(offsets):
+            if k > 0:
+                arrived[j], corr[j] = lax.optimization_barrier((arrived[j], corr[j]))
+                corr[j] = passed_along(corr[j], "req", k)
+        kept = None
+        for j in range(count - 1):
+            (kept,) = merge(count, width, kept, arrived[j], corr[j])
+        kept, kept_inner, kept_ssm = merge(
+            count, width, kept, arrived[-1], corr[-1], tuple(corr[:-1])
+        )
+        return hidden_out, kept, kept_inner, kept_ssm
+
+    sets = [
+        tuple(k for k in range(WINDOW) if k not in (low, high))
+        for low in range(WINDOW)
+        for high in range(low + 1, WINDOW)
+    ]
+    hidden_out, kept, kept_inner, kept_ssm = lax.switch(
+        branch[0],
+        [functools.partial(run, offsets) for offsets in sets],
+        (table, picked, hidden_in, proj_ssm, given),
     )
-    mine, theirs = results[:2]
-    corr = list(results[2:])
-    other = passed_along(theirs, "head", 1)
-    half = depth // 2
-    total = mine + other
-    scale = lax.rsqrt(total[:, half : half + 1] / DINNER + epsilon)
-    hidden_out = (hidden_in.astype(F32) + total[:, :half] * scale).astype(BF16)
-    for k in range(1, WINDOW):
-        corr[k] = passed_along(corr[k], "req", k)
-    kept, kept_inner, kept_ssm = merge(count, width, index[:1], sources, corr)
     return (hidden_out, kept.reshape(states_in.shape), kept_inner, kept_ssm)
 
 

time: 148 us -> 202 us (1.36)
  the two profiles are of different devices: /device:TPU:0 before, /device:TPU:22 now
where the time goes in v2:
time: 202 us; the launch traced here: 200 us
  Pallas kernels  92.7 us (46%)
  loops' own time  36.9 us (18%)
  waiting for transfers between devices  22.4 us (11%)
  starting transfers between devices  22 us (11%)
  local copies, waits for them, and re-layouts  11.6 us (6%)
  blocking collectives  9.96 us (5%)
  other arithmetic  2.42 us (1%)
    pallas_call x1, Pallas kernels, pick(): pl.pallas_call(functools.partial(pick_kernel, count, peers), in_specs=[sm...  62.2 us
    unnamed x1, loops' own time  36.9 us
    ppermute x10, waiting for transfers between devices, passed_along(): lax.ppermute(array, axis, [(i, (i + by) % length) for i in range(length)])  22.4 us
    ppermute x10, starting transfers between devices, passed_along(): lax.ppermute(array, axis, [(i, (i + by) % length) for i in range(length)])  22 us
    pallas_call x6, Pallas kernels, merge(): pl.pallas_call(functools.partial(merge_kernel, count, final), in_specs=[h...  19.1 us
    pallas_call x1, Pallas kernels, front(): pl.pallas_call(functools.partial(front_kernel, count, heads), grid=(tiles...  11.3 us
    all_gather x1, blocking collectives, layer(): lax.all_gather(proj_ssm, 'head', axis=0, tiled=False)  4.28 us
  transfers between devices with their start and end apart: 10, of which 3 were waited for; matrix products, arithmetic and copies ran while one was open for 5% of the time, Pallas kernels for 13%

profile of v2, /device:TPU:22, one launch (start us, length us, event | category | flops | bytes accessed | tf_op | source)
XLA Modules:
  0.0 199.9 jit_solution(17419788740676076931)
XLA Ops:
  0.7 62.2 %pick.1 = (bf16[1,1536,128]{2,1,0:T(8,128)(2,1)S(1)}, bf16[1,1536,128]{2,1,0:T(8,128)(2,1)}, bf16[1,1536,128]{2,1,0:T(8,128)(2,1)}, bf16[1,1536,128]{2,1,0:T(8,1...) custom-call(s32[6]{0:T(128)} %destination.1, ...), custom_call_target="tpu_custom_call" | custom-call | tf_op jit(solution)/shard_map/pick/pallas_call | solution.py:340
  63.6 135.1 %conditional.4 = (bf16[6,1536,128]{2,1,0:T(8,128)(2,1)}, bf16[6,3,1536]{2,1,0:T(4,128)(2,1)}, bf16[6,3,256]{2,1,0:T(4,128)(2,1)}, bf16[48,768]{1,0:T(8,128)(2,1)S(1)}) conditional(s32[]{:T(128)} %bitcast.169, (bf16[1,1536,128]{2,1,0:T(8,128)(2,1)}, bf16[48,768]{1,0:T(8,128)(2,1)}, f32[1536]{0:T(1024)S(1)}, ...), branch_computations={%region_0.1_spmd, %region_1.2_spmd, %region_2.3_spmd, %region_3.4_... | conditional | flops 755208448 | bytes 46478348
  89.7 1.6 collective-permute-start.136
  91.4 1.7 collective-permute-start.140
  93.0 2.5 %collective-permute-start.142 = (bf16[1,1536,128]{2,1,0:T(8,128)(2,1)}, bf16[1,1536,128]{2,1,0:T(8,128)(2,1)}, u32[]{:S(2)}, u32[]{:S(2)}) collective-permute-start(bf16[1,1536,128]{2,1,0:T(8,128)(2,1)} %get-tuple-element.2163), channel_id=1, source_target_pairs={{0,10},{2,12},{4,14},{6,16},{8,18},{10,20},{12,22},{14,24},{16,26}... | collective-permute-start | bytes 1179656 | tf_op jit(solution)/shard_map/cond/branch_12_fun/ppermute | solution.py:448
  95.6 2.5 %collective-permute-start.134 = (bf16[1,1536,128]{2,1,0:T(8,128)(2,1)}, bf16[1,1536,128]{2,1,0:T(8,128)(2,1)S(1)}, u32[]{:S(2)}, u32[]{:S(2)}) collective-permute-start(bf16[1,1536,128]{2,1,0:T(8,128)(2,1)} %get-tuple-element.2128), channel_id=1, source_target_pairs={{0,12},{2,14},{4,16},{6,18},{8,20},{10,22},{12,24},{14,26},{16,28}... | collective-permute-start | bytes 1179656 | tf_op jit(solution)/shard_map/cond/branch_12_fun/ppermute | solution.py:448
  98.1 3.4 %all-gather.36 = bf16[96,768]{1,0:T(8,128)(2,1)} all-gather(bf16[48,768]{1,0:T(8,128)(2,1)} %get-tuple-element.2132), channel_id=38, replica_groups=mesh['req'=16,'head'=2] {'head'}, dimensions={0}, use_global_device_ids=true | all-gather | bytes 221184 | tf_op jit(solution)/shard_map/cond/branch_12_fun/all_gather | solution.py:534
  101.5 4.3 %all-gather.37 = bf16[3072,128]{1,0:T(8,128)(2,1)} all-gather(bf16[1536,128]{1,0:T(8,128)(2,1)} %get-tuple-element.2137), channel_id=39, replica_groups=mesh['req'=16,'head'=2] {'head'}, dimensions={0}, use_global_device_ids=true | all-gather | bytes 1179648 | tf_op jit(solution)/shard_map/cond/branch_12_fun/all_gather | solution.py:539
  105.8 1.8 copy.205.w_step
  107.6 1.6 pad.138.edge_inner
  109.2 1.3 pad.139.edge_ssm
  111.1 1.3 reshape.344.bias_inner
  112.4 1.3 reshape.346.gate_gain
  113.7 1.3 pad_maximum_fusion.12.head_rows
  115.0 11.3 %front.40 = (f32[48,896]{1,0:T(8,128)}, f32[48,896]{1,0:T(8,128)}, bf16[16,1792]{1,0:T(8,128)(2,1)}, bf16[16,1792]{1,0:T(8,128)(2,1)}, bf16[16,1792]{1,0:T(8,128...) custom-call(s32[3,6]{1,0:T(4,128)S(1)} %get-tuple-element.2129.table, ...), custom_call_target="tpu_custom_call" | custom-call | flops 679477248 | bytes 16515072 | tf_op jit(solution)/shard_map/cond/branch_12_fun/front/pallas_call | solution.py:279
  126.3 2.3 %all-gather.38 = f32[96,896]{1,0:T(8,128)S(1)} all-gather(f32[48,896]{1,0:T(8,128)} %get-tuple-element.2175), channel_id=40, replica_groups=mesh['req'=16,'head'=2] {'head'}, dimensions={0}, use_global_device_ids=true | all-gather | bytes 516096 | tf_op jit(solution)/shard_map/cond/branch_12_fun/all_gather | solution.py:565
  128.6 1.0 fusion.72
  129.6 1.1 collective-permute-start.137
  130.8 0.6 collective-permute-start.139
  131.4 4.3 %collective-permute-done.140.refs_0_ = bf16[1,1536,128]{2,1,0:T(8,128)(2,1)} collective-permute-done((bf16[1,1536,128]{2,1,0:T(8,128)(2,1)}, bf16[1,1536,128]{2,1,0:T(8,128)(2,1)}, u32[]{:S(2)}, u32[]{:S(2)}) %collective-permute-start.140) | collective-permute-done | bytes 393248 | tf_op jit(solution)/shard_map/cond/branch_12_fun/ppermute | solution.py:448
  135.7 16.5 %collective-permute-done.142.refs_0_ = bf16[1,1536,128]{2,1,0:T(8,128)(2,1)} collective-permute-done((bf16[1,1536,128]{2,1,0:T(8,128)(2,1)}, bf16[1,1536,128]{2,1,0:T(8,128)(2,1)}, u32[]{:S(2)}, u32[]{:S(2)}) %collective-permute-start.142) | collective-permute-done | bytes 393248 | tf_op jit(solution)/shard_map/cond/branch_12_fun/ppermute | solution.py:448
  152.3 7.6 %collective-permute-start.143 = (bf16[16,1792]{1,0:T(8,128)(2,1)}, bf16[16,1792]{1,0:T(8,128)(2,1)S(1)}, u32[]{:S(2)}, u32[]{:S(2)}) collective-permute-start(bf16[16,1792]{1,0:T(8,128)(2,1)} %get-tuple-element.2165), channel_id=1, source_target_pairs={{0,10},{2,12},{4,14},{6,16},{8,18},{10,20},{12,22},{14,24},{16,26}... | collective-permute-start | bytes 172040 | tf_op jit(solution)/shard_map/cond/branch_12_fun/ppermute | solution.py:448
  159.9 1.5 collective-permute-done.134.refs_0_
  161.3 4.2 %collective-permute-start.135 = (bf16[16,1792]{1,0:T(8,128)(2,1)}, bf16[16,1792]{1,0:T(8,128)(2,1)S(1)}, u32[]{:S(2)}, u32[]{:S(2)}) collective-permute-start(bf16[16,1792]{1,0:T(8,128)(2,1)} %get-tuple-element.2152), channel_id=1, source_target_pairs={{0,12},{2,14},{4,16},{6,18},{8,20},{10,22},{12,24},{14,26},{16,28}... | collective-permute-start | bytes 172040 | tf_op jit(solution)/shard_map/cond/branch_12_fun/ppermute | solution.py:448
  165.7 2.9 %merge.240.refs_2_ = bf16[6,1536,128]{2,1,0:T(8,128)(2,1)} custom-call(bf16[1,1536,128]{2,1,0:T(8,128)(2,1)S(1)} %get-tuple-element.2170.refs_0_, bf16[16,1792]{1,0:T(8,128)(2,1)} %get-tuple-element.2153.refs_1_.refs_2_), custom_call_target="tpu_custom_call" | custom-call | flops 12582912 | bytes 786432 | tf_op jit(solution)/shard_map/cond/branch_12_fun/merge/pallas_call | solution.py:423
  169.2 3.1 %merge.241.refs_2_ = bf16[6,1536,128]{2,1,0:T(8,128)(2,1)} custom-call(bf16[1,1536,128]{2,1,0:T(8,128)(2,1)} %collective-permute-done.136.refs_0_, bf16[16,1792]{1,0:T(8,128)(2,1)} %copy-done.108, bf16[6,1536,128]{2,1,0:T(8,128)(2,1)} %merge.240.refs_2_), custom_call_target="tpu_custom_call", output_to_operand_aliasing={{}: (2, {})} | custom-call | flops 12582912 | bytes 786432 | tf_op jit(solution)/shard_map/cond/branch_12_fun/merge/pallas_call | solution.py:423
  172.3 0.6 copy-done.136
  172.9 3.1 %merge.242.refs_2_ = bf16[6,1536,128]{2,1,0:T(8,128)(2,1)} custom-call(bf16[1,1536,128]{2,1,0:T(8,128)(2,1)} %collective-permute-done.138.refs_0_, bf16[16,1792]{1,0:T(8,128)(2,1)} %copy-done.136, bf16[6,1536,128]{2,1,0:T(8,128)(2,1)} %merge.241.refs_2_), custom_call_target="tpu_custom_call", output_to_operand_aliasing={{}: (2, {})} | custom-call | flops 12582912 | bytes 786432 | tf_op jit(solution)/shard_map/cond/branch_12_fun/merge/pallas_call | solution.py:423
  176.7 3.1 %merge.243.refs_2_ = bf16[6,1536,128]{2,1,0:T(8,128)(2,1)} custom-call(bf16[1,1536,128]{2,1,0:T(8,128)(2,1)} %collective-permute-done.140.refs_0_, bf16[16,1792]{1,0:T(8,128)(2,1)} %copy-done.164, bf16[6,1536,128]{2,1,0:T(8,128)(2,1)} %merge.242.refs_2_), custom_call_target="tpu_custom_call", output_to_operand_aliasing={{}: (2, {})} | custom-call | flops 12582912 | bytes 786432 | tf_op jit(solution)/shard_map/cond/branch_12_fun/merge/pallas_call | solution.py:423
  180.4 3.1 %merge.244.refs_7_ = bf16[6,1536,128]{2,1,0:T(8,128)(2,1)} custom-call(bf16[1,1536,128]{2,1,0:T(8,128)(2,1)} %collective-permute-done.142.refs_0_, bf16[16,1792]{1,0:T(8,128)(2,1)} %copy-done.192, bf16[6,1536,128]{2,1,0:T(8,128)(2,1)} %merge.243.refs_2_), custom_call_target="tpu_custom_call", output_to_operand_aliasing={{}: (2, {})} | custom-call | flops 12582912 | bytes 786432 | tf_op jit(solution)/shard_map/cond/branch_12_fun/merge/pallas_call | solution.py:423
  184.1 3.9 %merge.245 = (bf16[6,1536,128]{2,1,0:T(8,128)(2,1)}, bf16[6,3,1536]{2,1,0:T(4,128)(2,1)}, bf16[6,3,256]{2,1,0:T(4,128)(2,1)}) custom-call(bf16[1,1536,128]{2,1,0:T(8,128)(2,1)} %copy-done.38, bf16[16,1792]{1,0:T(8,128)(2,1)} %copy-done.228, bf16[16,1792]{1,0:T(8,128)(2,1)} %get-tuple-element.2153.refs_1_.refs_2_, ...), custom_call_target="tpu_custom_call", output_to_operand_aliasing={{0}: (7, {})} | custom-call | flops 12582912 | bytes 786432 | tf_op jit(solution)/shard_map/cond/branch_12_fun/merge/pallas_call | solution.py:423
  198.7 0.6 copy-done.215
  (36 shorter events, 3.4 us)
Async XLA Ops:
  0.6 62.9 %copy-start = (bf16[6,24,64,128]{3,2,1,0:T(8,128)(2,1)S(1)}, bf16[6,24,64,128]{3,2,1,0:T(8,128)(2,1)}, u32[]{:S(2)}) copy-start(bf16[6,24,64,128]{3,2,1,0:T(8,128)(2,1)} %param.64) | copy-start | bytes 7077892
  0.6 62.9 %copy-start.30 = (f32[1536]{0:T(1024)S(1)}, f32[1536]{0:T(1024)}, u32[]{:S(2)}) copy-start(f32[1536]{0:T(1024)} %param.50) | copy-start | bytes 18436
  0.7 62.9 %copy-start.29 = (bf16[4,1536]{1,0:T(4,128)(2,1)S(1)}, bf16[4,1536]{1,0:T(4,128)(2,1)}, u32[]{:S(2)}) copy-start(bf16[4,1536]{1,0:T(4,128)(2,1)} %param.58) | copy-start | bytes 36868
  0.7 62.9 %copy-start.31 = (bf16[4,256]{1,0:T(4,128)(2,1)S(1)}, bf16[4,256]{1,0:T(4,128)(2,1)}, u32[]{:S(2)}) copy-start(bf16[4,256]{1,0:T(4,128)(2,1)} %param.60) | copy-start | bytes 6148
  0.7 62.9 %copy-start.32 = (f32[256]{0:T(256)S(1)}, f32[256]{0:T(256)}, u32[]{:S(2)}) copy-start(f32[256]{0:T(256)} %param.61) | copy-start | bytes 3076
  89.7 39.9 %collective-permute-start.136 = (bf16[1,1536,128]{2,1,0:T(8,128)(2,1)}, bf16[1,1536,128]{2,1,0:T(8,128)(2,1)}, u32[]{:S(2)}, u32[]{:S(2)}) collective-permute-start(bf16[1,1536,128]{2,1,0:T(8,128)(2,1)} %get-tuple-element.2154), channel_id=1, source_target_pairs={{0,4},{2,6},{4,8},{6,10},{8,12},{10,14},{12,16},{14,18},{16,20},{1... | collective-permute-start | bytes 1179656 | tf_op jit(solution)/shard_map/cond/branch_12_fun/ppermute | solution.py:448
  91.3 39.5 %collective-permute-start.138 = (bf16[1,1536,128]{2,1,0:T(8,128)(2,1)}, bf16[1,1536,128]{2,1,0:T(8,128)(2,1)}, u32[]{:S(2)}, u32[]{:S(2)}) collective-permute-start(bf16[1,1536,128]{2,1,0:T(8,128)(2,1)} %get-tuple-element.2157), channel_id=1, source_target_pairs={{0,6},{2,8},{4,10},{6,12},{8,14},{10,16},{12,18},{14,20},{16,22},{... | collective-permute-start | bytes 1179656 | tf_op jit(solution)/shard_map/cond/branch_12_fun/ppermute | solution.py:448
  91.4 44.4 %collective-permute-start.140 = (bf16[1,1536,128]{2,1,0:T(8,128)(2,1)}, bf16[1,1536,128]{2,1,0:T(8,128)(2,1)}, u32[]{:S(2)}, u32[]{:S(2)}) collective-permute-start(bf16[1,1536,128]{2,1,0:T(8,128)(2,1)} %get-tuple-element.2160), channel_id=1, source_target_pairs={{0,8},{2,10},{4,12},{6,14},{8,16},{10,18},{12,20},{14,22},{16,24},... | collective-permute-start | bytes 1179656 | tf_op jit(solution)/shard_map/cond/branch_12_fun/ppermute | solution.py:448
  93.0 59.2 %collective-permute-start.142 = (bf16[1,1536,128]{2,1,0:T(8,128)(2,1)}, bf16[1,1536,128]{2,1,0:T(8,128)(2,1)}, u32[]{:S(2)}, u32[]{:S(2)}) collective-permute-start(bf16[1,1536,128]{2,1,0:T(8,128)(2,1)} %get-tuple-element.2163), channel_id=1, source_target_pairs={{0,10},{2,12},{4,14},{6,16},{8,18},{10,20},{12,22},{14,24},{16,26}... | collective-permute-start | bytes 1179656 | tf_op jit(solution)/shard_map/cond/branch_12_fun/ppermute | solution.py:448
  95.6 65.8 %collective-permute-start.134 = (bf16[1,1536,128]{2,1,0:T(8,128)(2,1)}, bf16[1,1536,128]{2,1,0:T(8,128)(2,1)S(1)}, u32[]{:S(2)}, u32[]{:S(2)}) collective-permute-start(bf16[1,1536,128]{2,1,0:T(8,128)(2,1)} %get-tuple-element.2128), channel_id=1, source_target_pairs={{0,12},{2,14},{4,16},{6,18},{8,20},{10,22},{12,24},{14,26},{16,28}... | collective-permute-start | bytes 1179656 | tf_op jit(solution)/shard_map/cond/branch_12_fun/ppermute | solution.py:448
  115.0 50.6 %copy-start.13 = (bf16[48,768]{1,0:T(8,128)(2,1)S(1)}, bf16[48,768]{1,0:T(8,128)(2,1)}, u32[]{:S(2)}) copy-start(bf16[48,768]{1,0:T(8,128)(2,1)} %get-tuple-element.2132) | copy-start | bytes 221188
  129.6 38.9 %collective-permute-start.137 = (bf16[16,1792]{1,0:T(8,128)(2,1)}, bf16[16,1792]{1,0:T(8,128)(2,1)S(1)}, u32[]{:S(2)}, u32[]{:S(2)}) collective-permute-start(bf16[16,1792]{1,0:T(8,128)(2,1)} %get-tuple-element.2156), channel_id=1, source_target_pairs={{0,4},{2,6},{4,8},{6,10},{8,12},{10,14},{12,16},{14,18},{16,20},{1... | collective-permute-start | bytes 172040 | tf_op jit(solution)/shard_map/cond/branch_12_fun/ppermute | solution.py:448
  130.8 41.5 %collective-permute-start.139 = (bf16[16,1792]{1,0:T(8,128)(2,1)}, bf16[16,1792]{1,0:T(8,128)(2,1)S(1)}, u32[]{:S(2)}, u32[]{:S(2)}) collective-permute-start(bf16[16,1792]{1,0:T(8,128)(2,1)} %get-tuple-element.2159), channel_id=1, source_target_pairs={{0,6},{2,8},{4,10},{6,12},{8,14},{10,16},{12,18},{14,20},{16,22},{... | collective-permute-start | bytes 172040 | tf_op jit(solution)/shard_map/cond/branch_12_fun/ppermute | solution.py:448
  135.7 40.3 %collective-permute-start.141 = (bf16[16,1792]{1,0:T(8,128)(2,1)}, bf16[16,1792]{1,0:T(8,128)(2,1)S(1)}, u32[]{:S(2)}, u32[]{:S(2)}) collective-permute-start(bf16[16,1792]{1,0:T(8,128)(2,1)} %get-tuple-element.2162), channel_id=1, source_target_pairs={{0,8},{2,10},{4,12},{6,14},{8,16},{10,18},{12,20},{14,22},{16,24},... | collective-permute-start | bytes 172040 | tf_op jit(solution)/shard_map/cond/branch_12_fun/ppermute | solution.py:448
  152.3 27.5 %collective-permute-start.143 = (bf16[16,1792]{1,0:T(8,128)(2,1)}, bf16[16,1792]{1,0:T(8,128)(2,1)S(1)}, u32[]{:S(2)}, u32[]{:S(2)}) collective-permute-start(bf16[16,1792]{1,0:T(8,128)(2,1)} %get-tuple-element.2165), channel_id=1, source_target_pairs={{0,10},{2,12},{4,14},{6,16},{8,18},{10,20},{12,22},{14,24},{16,26}... | collective-permute-start | bytes 172040 | tf_op jit(solution)/shard_map/cond/branch_12_fun/ppermute | solution.py:448
  161.3 11.0 %copy-start.38 = (bf16[1,1536,128]{2,1,0:T(8,128)(2,1)}, bf16[1,1536,128]{2,1,0:T(8,128)(2,1)S(1)}, u32[]{:S(2)}) copy-start(bf16[1,1536,128]{2,1,0:T(8,128)(2,1)S(1)} %collective-permute-done.134.refs_0_) | copy-start | bytes 1179652
  161.3 22.1 %collective-permute-start.135 = (bf16[16,1792]{1,0:T(8,128)(2,1)}, bf16[16,1792]{1,0:T(8,128)(2,1)S(1)}, u32[]{:S(2)}, u32[]{:S(2)}) collective-permute-start(bf16[16,1792]{1,0:T(8,128)(2,1)} %get-tuple-element.2152), channel_id=1, source_target_pairs={{0,12},{2,14},{4,16},{6,18},{8,20},{10,22},{12,24},{14,26},{16,28}... | collective-permute-start | bytes 172040 | tf_op jit(solution)/shard_map/cond/branch_12_fun/ppermute | solution.py:448
  168.6 0.6 copy-start.108
  172.3 0.6 copy-start.136
  176.0 0.6 copy-start.164
  179.7 0.6 copy-start.192
  183.5 0.6 copy-start.228
  198.7 0.6 copy-start.215

commit v3 on v1

v3 whole, which is shorter than its diff:
```python
import functools

import jax
import jax.numpy as jnp
from jax import lax
from jax.experimental import pallas as pl
from jax.experimental.pallas import tpu as pltpu
from jax.sharding import PartitionSpec as P

HEAD_DIM = 64
NSTATE = 128
KCONV = 4
DRAFT = 8
WINDOW = 8
DINNER = 3072
TILE = 256
EXTRA = NSTATE
PLANE = 4
RAW = (7, 6, 5)
PARTS = 3
SMALL = pl.CostEstimate(flops=1024, bytes_accessed=1024, transcendentals=0)

epsilon = 1e-05
HIGH = lax.Precision.HIGHEST
F32 = jnp.float32
BF16 = jnp.bfloat16


def iota(shape, axis):
    return lax.broadcasted_iota(jnp.int32, shape, axis)


def mm(a, b, precision=None):
    return jnp.dot(a, b, preferred_element_type=F32, precision=precision)


def mm_t(a, b):
    return lax.dot_general(a, b, (((1,), (1,)), ((), ())), preferred_element_type=F32)


def silu(x):
    return x * (1.0 / (1.0 + jnp.exp(-x)))


def conv_rows(rows, edges, taps, bias):
    slot = iota(rows.shape, 1)
    total = bias + taps[KCONV - 1 : KCONV] * rows
    for back in range(1, KCONV):
        mixed = jnp.where(slot >= DRAFT - back, edges, rows)
        total = total + taps[KCONV - 1 - back : KCONV - back] * pltpu.roll(mixed, back, 1)
    return total


def front_kernel(
    count,
    heads,
    table,
    lengths_in,
    accepted_in,
    hidden,
    vectors,
    w_gate,
    w_inner,
    w_out,
    w_ssm,
    w_step,
    head_rows,
    taps_inner,
    vector_tile,
    taps_ssm,
    bias_ssm,
    states,
    edge_inner,
    edge_ssm,
    mine,
    theirs,
    *rest,
):
    corr = rest[:WINDOW]
    normed, acc, squares, quant, gmat, cmat, select, boxes, edge_pad = rest[WINDOW:]
    step = pl.program_id(0)
    last = pl.num_programs(0) - 1
    rows = count * DRAFT
    width = acc.shape[1]
    half = width // 2

    @pl.when(step == 0)
    def _():
        wide = jnp.concatenate([hidden[0], hidden[1]], axis=1).astype(F32)
        scale = lax.rsqrt(jnp.mean(wide * wide, axis=-1, keepdims=True) + epsilon)
        norm = (wide * scale * vectors[0:1]).astype(BF16)
        normed[...] = norm
        acc[...] = jnp.zeros_like(acc)
        squares[...] = jnp.zeros_like(squares)
        boxes[...] = jnp.zeros_like(boxes)
        edge_pad[...] = jnp.zeros_like(edge_pad)
        edge_pad[:, DRAFT - KCONV + 1 :] = edge_ssm[...].astype(F32)
        row = iota((rows, rows), 0)
        col = iota((rows, rows), 1)
        request = row >> 3
        taken = jnp.zeros((rows, rows), jnp.int32)
        for r in range(count):
            taken = jnp.where(request == r, accepted_in[r], taken)
        same = request == (col >> 3)
        lower = same & ((col & 7) <= (row & 7))
        before = same & ((col & 7) < taken)
        raw = mm_t(norm, w_step[...]).astype(BF16).astype(F32) + head_rows[0:1]
        lengths = jnp.zeros((rows, heads), jnp.int32)
        chosen = jnp.zeros((rows, heads), jnp.int32)
        hrow = iota((rows, heads), 0)
        for r in range(count):
            lengths = jnp.where((hrow >> 3) == r, lengths_in[r], lengths)
            chosen = jnp.where((hrow >> 3) == r, accepted_in[r], chosen)
        soft = jnp.maximum(raw, 0.0) + jnp.log1p(jnp.exp(-jnp.abs(raw)))
        size = jnp.where((hrow & 7) < lengths, soft, 0.0)
        rate = -jnp.exp(head_rows[1:2])
        cum = mm(lower.astype(F32), size, HIGH)
        upto = mm(before.astype(F32), size, HIGH)
        weight = jnp.where(
            (hrow & 7) < chosen, jnp.exp(jnp.minimum(rate * (upto - cum), 0.0)) * size, 0.0
        )
        stacked = jnp.concatenate(
            [
                rate * cum,
                size,
                weight,
                jnp.exp(rate * upto),
                jnp.broadcast_to(head_rows[2:3], (16, heads)),
            ],
            axis=0,
        )
        for part in range(3):
            piece = stacked.astype(BF16)
            quant[part] = piece
            stacked = stacked - piece.astype(F32)
        sel_rows = jnp.where(
            same & ((row & 7) < KCONV - 1),
            ((col & 7) == (row & 7) + taken - 3).astype(F32),
            0.0,
        ).astype(BF16)
        sel_edge = jnp.where(
            same & ((row & 7) < KCONV - 1),
            ((col & 7) == (row & 7) + taken + 5).astype(F32),
            0.0,
        ).astype(BF16)
        select[0] = sel_rows
        select[1] = sel_edge
        ssm = jnp.concatenate([mm(norm, w_ssm[0]), mm(norm, w_ssm[1])], axis=1).astype(BF16)
        before_ssm = edge_pad[...]
        conv = conv_rows(
            ssm.astype(F32).reshape(count, DRAFT, 2 * NSTATE),
            before_ssm,
            taps_ssm[...].astype(F32),
            bias_ssm[...],
        )
        both = silu(conv).reshape(rows, 2 * NSTATE).astype(BF16)
        bmat = both[:, :NSTATE]
        cvec = both[:, NSTATE:]
        cmat[...] = cvec.astype(F32)
        pair = jnp.where(lower, mm_t(cvec, bmat), 0.0)
        fold = ((iota((rows, NSTATE), 0) & 7) == iota((rows, NSTATE), 1)).astype(F32)
        gmat[...] = mm(pair, fold, HIGH)
        kept = mm(sel_rows, ssm) + mm(
            sel_edge, before_ssm.reshape(rows, 2 * NSTATE).astype(BF16)
        )
        wide_b = bmat.astype(F32)
        place = iota((DRAFT, NSTATE), 0)
        for r in range(count):
            own = kept[r * DRAFT : (r + 1) * DRAFT]
            packed = jnp.where(
                place < 3,
                own[:, :NSTATE],
                jnp.where(
                    place < 6,
                    pltpu.roll(own[:, NSTATE:], 3, 0),
                    jnp.full((DRAFT, NSTATE), (table[1, r] + 1).astype(F32)),
                ),
            )
            boxes[table[0, r], :, :NSTATE] = jnp.concatenate(
                [wide_b[r * DRAFT : (r + 1) * DRAFT], packed], axis=0
            ).astype(BF16)
        for k in range(WINDOW):
            corr[k][:, width:] = boxes[k, :, :NSTATE]

    norm = normed[...]
    inner = mm(norm, w_inner[...]).astype(BF16)
    gate = mm(norm, w_gate[...]).astype(BF16).astype(F32)
    edge_pad[:, DRAFT - KCONV + 1 :] = edge_inner[...].astype(F32)
    edges = edge_pad[...]
    conv = conv_rows(
        inner.astype(F32).reshape(count, DRAFT, TILE),
        edges,
        taps_inner[...].astype(F32),
        vector_tile[1:2],
    )
    x = silu(conv).reshape(rows, TILE).astype(BF16).astype(F32)
    first_head = step * (TILE // HEAD_DIM)
    spread = (
        iota((heads, TILE), 0) == first_head + (iota((heads, TILE), 1) >> 6)
    ).astype(BF16)
    expanded = mm(quant[0], spread) + mm(quant[1], spread) + mm(quant[2], spread)
    level = expanded[:rows]
    weighted = expanded[rows : 2 * rows] * x
    past = jnp.concatenate(
        [
            mm_t(cmat[r * DRAFT : (r + 1) * DRAFT].astype(BF16), states[r])
            for r in range(count)
        ],
        axis=0,
    )
    out = jnp.exp(level) * past + expanded[4 * rows : 4 * rows + 1] * x
    level3 = level.reshape(count, DRAFT, TILE)
    weighted3 = weighted.reshape(count, DRAFT, TILE)
    total = jnp.zeros((count, DRAFT, TILE), F32)
    for u in range(DRAFT):
        factor = jnp.exp(jnp.minimum(level3 - level3[:, u : u + 1], 0.0))
        share = gmat[:, u : u + 1].reshape(count, DRAFT, 1)
        total = total + share * factor * weighted3[:, u : u + 1]
    out = (out + total.reshape(rows, TILE)).astype(BF16).astype(F32)
    gated = out * silu(gate)
    squared = gated * gated
    squares[...] += squared[:, :128] + squared[:, 128:]
    acc[...] += mm((gated * vector_tile[2:3]).astype(BF16), w_out[...])
    delta = expanded[2 * rows : 3 * rows] * x
    decay = expanded[3 * rows : 4 * rows]
    decay_hi = decay.astype(BF16).astype(F32)
    second = mm(select[0], inner) + mm(select[1], edges.reshape(rows, TILE).astype(BF16))
    place = iota((rows, TILE), 0) & 7
    second = jnp.where(
        place == 3, decay_hi, jnp.where(place == 4, decay - decay_hi, second)
    )
    for r in range(count):
        span = slice(r * DRAFT, (r + 1) * DRAFT)
        boxes[table[0, r]] = jnp.concatenate([delta[span], second[span]], axis=0).astype(BF16)
    here = pl.ds(pl.multiple_of(step * TILE, TILE), TILE)
    for k in range(WINDOW):
        corr[k][:, here] = boxes[k]

    @pl.when(step == last)
    def _():
        total_square = jnp.broadcast_to(
            jnp.sum(squares[...], axis=1, keepdims=True), squares.shape
        )
        mine[:, half:] = total_square
        theirs[:, half:] = total_square

        @pl.when(table[2, 0] == 0)
        def _():
            mine[:, :half] = acc[:, :half]
            theirs[:, :half] = acc[:, half:]

        @pl.when(table[2, 0] != 0)
        def _():
            mine[:, :half] = acc[:, half:]
            theirs[:, :half] = acc[:, :half]


def front(count, heads, width, depth, args):
    rows = count * DRAFT
    tiles = width // TILE

    def whole(shape):
        return pl.BlockSpec(shape, lambda j: (0,) * len(shape))

    in_specs = [
        *[pl.BlockSpec(memory_space=pltpu.SMEM)] * 3,
        whole((2, rows, depth // 2)),
        whole((3, depth)),
        pl.BlockSpec((depth, TILE), lambda j: (0, j)),
        pl.BlockSpec((depth, TILE), lambda j: (0, j)),
        pl.BlockSpec((TILE, depth), lambda j: (j, 0)),
        whole((2, depth, NSTATE)),
        whole((heads, depth)),
        whole((3, heads)),
        pl.BlockSpec((KCONV, TILE), lambda j: (0, j)),
        pl.BlockSpec((3, TILE), lambda j: (0, j)),
        whole((KCONV, 2 * NSTATE)),
        whole((1, 2 * NSTATE)),
        pl.BlockSpec((count, TILE, NSTATE), lambda j: (0, j, 0)),
        pl.BlockSpec((count, KCONV - 1, TILE), lambda j: (0, 0, j)),
        whole((count, KCONV - 1, 2 * NSTATE)),
    ]
    out_width = depth // 2 + 128
    out_shape = [jax.ShapeDtypeStruct((rows, out_width), F32)] * 2 + [
        jax.ShapeDtypeStruct((2 * DRAFT, width + EXTRA), BF16)
    ] * WINDOW
    out_specs = [whole((rows, out_width))] * 2 + [whole((2 * DRAFT, width + EXTRA))] * WINDOW
    return pl.pallas_call(
        functools.partial(front_kernel, count, heads),
        grid=(tiles,),
        in_specs=in_specs,
        out_specs=out_specs,
        out_shape=out_shape,
        scratch_shapes=[
            pltpu.VMEM((rows, depth), BF16),
            pltpu.VMEM((rows, depth), F32),
            pltpu.VMEM((rows, 128), F32),
            pltpu.VMEM((3, 4 * rows + 16, heads), BF16),
            pltpu.VMEM((rows, NSTATE), F32),
            pltpu.VMEM((rows, NSTATE), F32),
            pltpu.VMEM((2, rows, rows), BF16),
            pltpu.VMEM((WINDOW, 2 * DRAFT, TILE), BF16),
            pltpu.VMEM((count, DRAFT, TILE), F32),
        ],
        compiler_params=pltpu.CompilerParams(dimension_semantics=("arbitrary",)),
        cost_estimate=SMALL,
        name="front",
    )(*args)


def pick_kernel(count, peers, destination, states, *outs):
    picked = outs[: len(RAW)]
    table, sems = outs[len(RAW) :]
    here = lax.axis_index("req")
    reach = [
        lax.rem(lax.div(destination[r], count) - here + peers, peers) for r in range(count)
    ]
    index = []
    for k in range(WINDOW):
        index.append(sum((reach[r] == k).astype(jnp.int32) * r for r in range(count)))
        table[3, k] = index[k]
    copies = []
    for n, k in enumerate(RAW):
        copy = pltpu.make_async_copy(states.at[index[k]], picked[n], sems.at[n])
        copy.start()
        copies.append(copy)
    for r in range(count):
        table[0, r] = reach[r]
        table[1, r] = lax.rem(destination[r], count)
        table[2, r] = lax.axis_index("head")
    for copy in copies:
        copy.wait()


def in_hbm():
    return pl.BlockSpec(memory_space=pl.ANY)


def in_vmem():
    return pl.BlockSpec(memory_space=pltpu.VMEM)


def in_smem():
    return pl.BlockSpec(memory_space=pltpu.SMEM)


def pick(count, width, peers, destination, states):
    return pl.pallas_call(
        functools.partial(pick_kernel, count, peers),
        in_specs=[in_smem(), in_hbm()],
        out_specs=[in_vmem()] * len(RAW) + [in_smem()],
        out_shape=[jax.ShapeDtypeStruct((width, NSTATE), BF16)] * len(RAW)
        + [jax.ShapeDtypeStruct((4, max(count, WINDOW)), jnp.int32)],
        scratch_shapes=[pltpu.SemaphoreType.DMA((len(RAW),))],
        cost_estimate=SMALL,
        name="pick",
    )(destination, states)


def advance(corr, state, out):
    width = state.shape[0]
    line = iota((2 * DRAFT, NSTATE), 0)
    bmat = jnp.where(line < DRAFT, corr[:, width:].astype(F32), 0.0)
    ones = jnp.where((line == 11) | (line == 12), 1.0, 0.0)
    right = jnp.concatenate([bmat, ones], axis=1).astype(BF16)
    part = width // PARTS
    for c in range(PARTS):
        span = slice(c * part, (c + 1) * part)
        both = lax.dot_general(
            corr[:, span], right, (((0,), (0,)), ((), ())), preferred_element_type=F32
        )
        out[span] = (both[:, NSTATE:] * state[span].astype(F32) + both[:, :NSTATE]).astype(BF16)


def tail_rows(width):
    pairs = (width // NSTATE + 2) // 2
    return pairs, pairs * 2 * DRAFT


def column():
    return lax.rem(lax.axis_index("req"), PLANE)


def finish_kernel(offsets, aside, *refs):
    n = len(offsets)
    table, states = refs[:2]
    corr = refs[2 : 2 + n]
    outs = refs[2 + n : 2 + 2 * n]
    loaded, sems = refs[-2:]
    width = loaded.shape[1]
    pairs, _ = tail_rows(width)
    copies = []
    for i, k in enumerate(offsets):
        copy = pltpu.make_async_copy(states.at[table[3, k]], loaded.at[i], sems.at[i])
        copy.start()
        copies.append(copy)
    for i in range(n):
        low = corr[i][...].astype(F32)[DRAFT:]
        low = jnp.concatenate(
            [low, jnp.zeros((DRAFT, 2 * pairs * NSTATE - low.shape[1]), F32)], axis=1
        )
        for t in range(pairs):
            block = jnp.concatenate(
                [
                    low[:, t * NSTATE : (t + 1) * NSTATE],
                    low[:, (t + pairs) * NSTATE : (t + pairs + 1) * NSTATE],
                ],
                axis=0,
            )
            outs[i][width + t * 2 * DRAFT : width + (t + 1) * 2 * DRAFT] = block.astype(BF16)
        copies[i].wait()
        advance(corr[i], loaded.at[i], outs[i])
    if aside:
        other = refs[2 + 2 * n]

        @pl.when(column() == 3)
        def _():
            other[...] = outs[offsets.index(1)][...]

        @pl.when(column() != 3)
        def _():
            other[...] = outs[offsets.index(3)][...]


def finish(offsets, aside, table, states, corr):
    n = len(offsets)
    width = states.shape[1]
    shape = jax.ShapeDtypeStruct((width + tail_rows(width)[1], NSTATE), BF16)
    outs = n + (1 if aside else 0)
    return pl.pallas_call(
        functools.partial(finish_kernel, offsets, aside),
        in_specs=[in_smem(), in_hbm()] + [in_vmem()] * n,
        out_specs=[in_vmem()] * outs,
        out_shape=[shape] * outs,
        scratch_shapes=[
            pltpu.VMEM((n, width, NSTATE), BF16),
            pltpu.SemaphoreType.DMA((n,)),
        ],
        cost_estimate=SMALL,
        name="finish",
    )(table, states, *[corr[k] for k in offsets])


def mark_of(low):
    return jnp.max(low[6:7]).astype(jnp.int32) - 1


def merge_kernel(table, states, raw7, raw6, raw5, raw5_aside, *refs):
    corr = refs[:4]
    kept, loaded, merged, sem_in, sem_out = refs[4:]
    width = loaded.shape[1]

    def fetch(i, source):
        return pltpu.make_async_copy(source, loaded.at[i], sem_in.at[i])

    fetch(0, states.at[table[3, 0]]).start()
    fetch(1, raw7).start()
    fetch(2, raw6).start()

    @pl.when(column() == 0)
    def _():
        fetch(3, raw5_aside).start()

    @pl.when(column() != 0)
    def _():
        fetch(3, raw5).start()

    slots = [mark_of(ref[:, width:].astype(F32)[DRAFT:]) for ref in corr]

    def put(i):
        return pltpu.make_async_copy(merged.at[i], kept.at[slots[i]], sem_out.at[i])

    for i in range(4):
        fetch(i, raw7).wait()

        @pl.when(slots[i] >= 0)
        def _(i=i):
            advance(corr[i], loaded.at[i], merged.at[i])
            put(i).start()

    for i in range(4):

        @pl.when(slots[i] >= 0)
        def _(i=i):
            put(i).wait()


def merge(count, table, states, raws, corr):
    width = states.shape[1]
    return pl.pallas_call(
        merge_kernel,
        in_specs=[in_smem()] + [in_hbm()] * 5 + [in_vmem()] * 4,
        out_specs=in_hbm(),
        out_shape=jax.ShapeDtypeStruct((count, width, NSTATE), BF16),
        scratch_shapes=[
            pltpu.VMEM((4, width, NSTATE), BF16),
            pltpu.VMEM((4, width, NSTATE), BF16),
            pltpu.SemaphoreType.DMA((4,)),
            pltpu.SemaphoreType.DMA((4,)),
        ],
        cost_estimate=SMALL,
        name="merge",
    )(table, states, *raws, *corr)


def place_kernel(first, second, third, fourth, aside, *refs):
    corr = refs[:4]
    _, kept, out_inner, out_ssm, loaded, sem_in, sem_out = refs[4:]
    width = out_inner.shape[2]
    pairs, _ = tail_rows(width)

    def fetch(i, source):
        return pltpu.make_async_copy(source, loaded.at[i], sem_in.at[i])

    fetch(3, fourth).start()
    fetch(1, second).start()
    for i, source, turned in ((0, first, 0), (2, third, 1)):

        @pl.when(column() == turned)
        def _(i=i):
            fetch(i, aside).start()

        @pl.when(column() != turned)
        def _(i=i, source=source):
            fetch(i, source).start()

    def write_edges(slot, inner, low):
        out_inner[slot] = inner[: KCONV - 1].astype(BF16)
        high = pltpu.roll(low, DRAFT - 3, 0)
        out_ssm[slot] = jnp.concatenate([low[:3], high[:3]], axis=1).astype(BF16)

    for ref in corr:
        low = ref[...].astype(F32)[DRAFT:]
        slot = mark_of(low[:, width:])

        @pl.when(slot >= 0)
        def _(slot=slot, low=low):
            write_edges(slot, low[:, :width], low[:, width:])

    def put(i, slot):
        return pltpu.make_async_copy(
            loaded.at[i, pl.ds(0, width)], kept.at[slot], sem_out.at[i]
        )

    slots = []
    for i in (3, 1, 2, 0):
        fetch(i, fourth).wait()
        parts = [
            loaded[i, width + t * 2 * DRAFT : width + (t + 1) * 2 * DRAFT].astype(F32)
            for t in range(pairs)
        ]
        lows = [part[:DRAFT] for part in parts] + [part[DRAFT:] for part in parts]
        tiles = width // NSTATE
        slot = mark_of(lows[tiles])
        slots.append((i, slot))

        @pl.when(slot >= 0)
        def _(i=i, slot=slot, lows=lows):
            put(i, slot).start()
            write_edges(slot, jnp.concatenate(lows[:tiles], axis=1), lows[tiles])

    for i, slot in slots:

        @pl.when(slot >= 0)
        def _(i=i, slot=slot):
            put(i, slot).wait()


def place(count, width, messages, corr, kept):
    rows = width + tail_rows(width)[1]
    return pl.pallas_call(
        place_kernel,
        in_specs=[in_hbm()] * 5 + [in_vmem()] * 4 + [in_hbm()],
        out_specs=[in_hbm(), in_vmem(), in_vmem()],
        out_shape=[
            jax.ShapeDtypeStruct((count, width, NSTATE), BF16),
            jax.ShapeDtypeStruct((count, KCONV - 1, width), BF16),
            jax.ShapeDtypeStruct((count, KCONV - 1, 2 * NSTATE), BF16),
        ],
        input_output_aliases={9: 0},
        scratch_shapes=[
            pltpu.VMEM((4, rows, NSTATE), BF16),
            pltpu.SemaphoreType.DMA((4,)),
            pltpu.SemaphoreType.DMA((4,)),
        ],
        cost_estimate=SMALL,
        name="place",
    )(*messages, *corr, kept)


def moved(array, by, columns=range(PLANE)):
    length = lax.axis_size("req")
    pairs = [(i, (i + by[i % PLANE]) % length) for i in range(length) if i % PLANE in columns]
    return lax.ppermute(array, "req", pairs)


def local(
    hidden_in,
    norm_gain,
    proj_gate,
    proj_inner,
    proj_ssm,
    proj_step,
    step_bias,
    decay_log,
    skip_gain,
    conv_inner,
    conv_inner_bias,
    conv_ssm,
    conv_ssm_bias,
    gate_gain,
    proj_out,
    states_in,
    edge_inner,
    edge_ssm,
    draft_lengths,
    accepted,
    destination,
):
    count, heads = states_in.shape[:2]
    depth, width = proj_inner.shape
    peers = lax.axis_size("req")
    flat = states_in.reshape(count, width, NSTATE)
    raw7, raw6, raw5, table = pick(count, width, peers, destination, flat)
    raw5_z = moved(raw5, [8] * PLANE, (3,))
    raw7 = moved(raw7, [7] * PLANE)
    raw6 = moved(raw6, [6] * PLANE)
    raw5 = moved(raw5, [5] * PLANE, (0, 1, 2))
    results = front(
        count,
        heads,
        width,
        depth,
        (
            table,
            draft_lengths,
            accepted,
            lax.all_gather(hidden_in, "head", axis=0, tiled=False),
            jnp.stack([norm_gain, conv_inner_bias, gate_gain]),
            proj_gate,
            proj_inner,
            proj_out,
            lax.all_gather(proj_ssm, "head", axis=0, tiled=False),
            proj_step.T,
            jnp.stack([step_bias, decay_log, skip_gain]),
            conv_inner,
            jnp.stack([norm_gain, conv_inner_bias, gate_gain]),
            conv_ssm,
            conv_ssm_bias.reshape(1, 2 * NSTATE),
            flat,
            edge_inner,
            edge_ssm,
        ),
    )
    mine, theirs = results[:2]
    corr = list(results[2:])
    (fourth,) = finish((4,), False, table, flat, corr)
    fourth = moved(fourth, [4] * PLANE)
    first, second, third, aside = finish((1, 2, 3), True, table, flat, corr)

    pair = lax.all_gather(theirs, "head", axis=0, tiled=False)
    other = jnp.where(lax.axis_index("head") == 0, pair[1], pair[0])
    total = mine + other
    half = depth // 2
    scale = lax.rsqrt(total[:, half : half + 1] / DINNER + epsilon)
    hidden_out = (hidden_in.astype(F32) + total[:, :half] * scale).astype(BF16)

    raw7, raw6, raw5, raw5_z, fourth, aside, third, second, first, *late = (
        lax.optimization_barrier(
            (raw7, raw6, raw5, raw5_z, fourth, aside, third, second, first, *corr[5:])
        )
    )
    corr[5:] = late
    raw5_turned = moved(raw5_z, [-3] * PLANE, (3,))
    aside = moved(aside, [4] * PLANE, (2, 3))
    third = moved(third, [3] * PLANE, (0, 1, 3))
    second = moved(second, [2] * PLANE)
    turned = moved(aside, [0, 0, -1, -3], (2, 3))
    third, first = lax.optimization_barrier((third, first))
    first = moved(first, [1] * PLANE, (0, 1, 2))
    raw5_turned, corr[7] = lax.optimization_barrier((raw5_turned, corr[7]))
    corr[7] = moved(corr[7], [7] * PLANE)
    corr[7], corr[6] = lax.optimization_barrier((corr[7], corr[6]))
    corr[6] = moved(corr[6], [6] * PLANE)
    corr[6], corr[5] = lax.optimization_barrier((corr[6], corr[5]))
    corr[5] = moved(corr[5], [5] * PLANE)
    sent = [corr[0], corr[7], corr[6], corr[5]]
    kept = merge(count, table, flat, (raw7, raw6, raw5, raw5_turned), sent)
    kept, kept_inner, kept_ssm = place(
        count, width, (first, second, third, fourth, turned), sent, kept
    )
    return (hidden_out, kept.reshape(states_in.shape), kept_inner, kept_ssm)


def solution(mesh):
    in_specs = (
        P("req", "head"),
        P(),
        P(None, "head"),
        P(None, "head"),
        P(None, "head"),
        P(None, "head"),
        P("head"),
        P("head"),
        P("head"),
        P(None, "head"),
        P("head"),
        P(),
        P(),
        P("head"),
        P("head", None),
        P("req", "head", None, None),
        P("req", None, "head"),
        P("req", None, None),
        P("req"),
        P("req"),
        P("req"),
    )
    out_specs = (
        P("req", "head"),
        P("req", "head", None, None),
        P("req", None, "head"),
        P("req", None, None),
    )
    return jax.shard_map(local, mesh=mesh, in_specs=in_specs, out_specs=out_specs, check_vma=False)
```

time: 148 us -> 159 us (1.074)
  waiting for transfers between devices: 56.4 us -> 77.9 us
  local copies, waits for them, and re-layouts: 18.7 us -> 5.1 us
  between operations: 14.3 us -> 0.9 us
  Pallas kernels: 21.2 us -> 30.6 us
  blocking collectives: 4.61 us -> 9.82 us
    ppermute x15 -> x14, waiting for transfers between devices: 56.4 us -> 77.9 us  [moved(): return lax.ppermute(array, 'req', pairs)]
    unnamed x51 -> x36, local copies, waits for them, and re-layouts: 11 us -> 2.99 us
    pallas_call x1 -> x5, Pallas kernels: 12.4 us -> 18.5 us  [the longest x2 7.52 us: finish(): pl.pallas_call(functools.partial(finish_kernel, offsets, aside), in_specs...]
    all_gather x2 -> x3, blocking collectives: 4.61 us -> 9.82 us  [the longest x1 4.07 us: local(): lax.all_gather(proj_ssm, 'head', axis=0, tiled=False)]
    pallas_call x1, Pallas kernels: 8.78 us -> 12.1 us  [front(): pl.pallas_call(functools.partial(front_kernel, count, heads), grid=(tiles...]
    dynamic_slice x1 -> x0, local copies, waits for them, and re-layouts: 3.27 us -> none  [local(): picked = lax.dynamic_slice_in_dim(flat, index[k], 1, 0)]
    ppermute x15 -> x14, starting transfers between devices: 29.3 us -> 30.5 us  [moved(): return lax.ppermute(array, 'req', pairs)]
  transfers between devices with their start and end apart: 15 -> 14, of which waited for: 7 -> 6; matrix products, arithmetic and copies ran while one was open for 4% -> 1% of each run, Pallas kernels for 6% -> 6%
where the time goes in v3:
time: 159 us
  waiting for transfers between devices  77.9 us (49%)
  Pallas kernels  30.6 us (19%)
  starting transfers between devices  30.5 us (19%)
  blocking collectives  9.82 us (6%)
  local copies, waits for them, and re-layouts  5.1 us (3%)
  other arithmetic  3.68 us (2%)
    ppermute x14, waiting for transfers between devices, moved(): return lax.ppermute(array, 'req', pairs)  77.9 us
    ppermute x14, starting transfers between devices, moved(): return lax.ppermute(array, 'req', pairs)  30.5 us
    pallas_call x1, Pallas kernels, front(): pl.pallas_call(functools.partial(front_kernel, count, heads), grid=(tiles...  12.1 us
    pallas_call x2, Pallas kernels, finish(): pl.pallas_call(functools.partial(finish_kernel, offsets, aside), in_specs...  7.52 us
    pallas_call x1, Pallas kernels, merge(): pl.pallas_call(merge_kernel, in_specs=[in_smem()] + [in_hbm()] * 5 + [in_...  4.37 us
    all_gather x1, blocking collectives, local(): lax.all_gather(proj_ssm, 'head', axis=0, tiled=False)  4.07 us
    all_gather x1, blocking collectives, local(): lax.all_gather(hidden_in, 'head', axis=0, tiled=False)  3.7 us
    pallas_call x1, Pallas kernels, place(): pl.pallas_call(place_kernel, in_specs=[in_hbm()] * 5 + [in_vmem()] * 4 +...  3.6 us
  transfers between devices with their start and end apart: 14, of which 6 were waited for; matrix products, arithmetic and copies ran while one was open for 1% of the time, Pallas kernels for 6%

profile of v3, /device:TPU:0, one launch (start us, length us, event | category | flops | bytes accessed | tf_op | source)
XLA Modules:
  0.0 158.6 jit_solution(17747034668183112467)
XLA Ops:
  0.6 0.7 stack.28
  2.7 3.7 %all-gather = bf16[96,768]{1,0:T(8,128)(2,1)} all-gather(bf16[48,768]{1,0:T(8,128)(2,1)} %param.21), channel_id=2, replica_groups=mesh['req'=16,'head'=2] {'head'}, dimensions={0}, use_global_device_ids=true | all-gather | bytes 221184 | tf_op jit(solution)/shard_map/all_gather | solution.py:638
  6.4 4.1 %all-gather.1 = bf16[3072,128]{1,0:T(8,128)(2,1)} all-gather(bf16[1536,128]{1,0:T(8,128)(2,1)} %param.25), channel_id=3, replica_groups=mesh['req'=16,'head'=2] {'head'}, dimensions={0}, use_global_device_ids=true | all-gather | bytes 1179648 | tf_op jit(solution)/shard_map/all_gather | solution.py:643
  10.5 3.0 %pick.1 = (bf16[1536,128]{1,0:T(8,128)(2,1)}, bf16[1536,128]{1,0:T(8,128)(2,1)}, bf16[1536,128]{1,0:T(8,128)(2,1)}, s32[4,8]{1,0:T(4,128)}) custom-call(s32[6]{0:T(128)} %destination.1, bf16[6,1536,128]{2,1,0:T(8,128)(2,1)} %bitcast.9), custom_call_target="tpu_custom_call" | custom-call | flops 1024 | bytes 1024 | tf_op jit(solution)/shard_map/pick/pallas_call | solution.py:348
  13.5 1.3 pad_maximum_fusion.1.head_rows
  15.4 12.1 %front.1 = (f32[48,896]{1,0:T(8,128)}, f32[48,896]{1,0:T(8,128)}, bf16[16,1664]{1,0:T(8,128)(2,1)}, bf16[16,1664]{1,0:T(8,128)(2,1)}, bf16[16,1664]{1,0:T(8,128)...) custom-call(s32[4,8]{1,0:T(4,128)} %get-tuple-element.45.table.refs_, ...), custom_call_target="tpu_custom_call" | custom-call | flops 1024 | bytes 1024 | tf_op jit(solution)/shard_map/front/pallas_call | solution.py:288
  27.6 3.1 %finish.2 = bf16[1648,128]{1,0:T(8,128)(2,1)} custom-call(s32[4,8]{1,0:T(4,128)} %get-tuple-element.45.table.refs_0_, bf16[6,1536,128]{2,1,0:T(8,128)(2,1)} %bitcast.11, bf16[16,1664]{1,0:T(8,128)(2,1)} %get-tuple-element.51.refs_2_), custom_call_target="tpu_custom_call" | custom-call | flops 1024 | bytes 1024 | tf_op jit(solution)/shard_map/finish/pallas_call | solution.py:430
  30.7 3.0 %collective-permute-start.4 = (bf16[1648,128]{1,0:T(8,128)(2,1)}, bf16[1648,128]{1,0:T(8,128)(2,1)S(1)}, u32[]{:S(2)}, u32[]{:S(2)}) collective-permute-start(bf16[1648,128]{1,0:T(8,128)(2,1)} %finish.2), channel_id=1, source_target_pairs={{0,8},{2,10},{4,12},{6,14},{8,16},{10,18},{12,20},{14,22},{16,24},... | collective-permute-start | bytes 1265672 | tf_op jit(solution)/shard_map/ppermute | solution.py:594
  33.7 3.5 %collective-permute-start = (bf16[1536,128]{1,0:T(8,128)(2,1)}, bf16[1536,128]{1,0:T(8,128)(2,1)S(1)}, u32[]{:S(2)}, u32[]{:S(2)}) collective-permute-start(bf16[1536,128]{1,0:T(8,128)(2,1)} %get-tuple-element.48), channel_id=1, source_target_pairs={{0,14},{2,16},{4,18},{6,20},{8,22},{10,24},{12,26},{14,28},{16,30}... | collective-permute-start | bytes 1179656 | tf_op jit(solution)/shard_map/ppermute | solution.py:594
  37.1 1.2 collective-permute-start.1
  39.0 2.6 %collective-permute-start.2 = (bf16[1536,128]{1,0:T(8,128)(2,1)S(1)}, bf16[1536,128]{1,0:T(8,128)(2,1)S(1)}, u32[]{:S(2)}, u32[]{:S(2)}) collective-permute-start(bf16[1536,128]{1,0:T(8,128)(2,1)S(1)} %copy-done.14), channel_id=1, source_target_pairs={{0,10},{2,12},{4,14},{8,18},{10,20},{12,22},{16,26},{18,28},{20,30... | collective-permute-start | bytes 1179656 | tf_op jit(solution)/shard_map/ppermute | solution.py:594
  41.6 4.4 %finish.3 = (bf16[1648,128]{1,0:T(8,128)(2,1)}, bf16[1648,128]{1,0:T(8,128)(2,1)}, bf16[1648,128]{1,0:T(8,128)(2,1)}, bf16[1648,128]{1,0:T(8,128)(2,1)}) custom-call(s32[4,8]{1,0:T(4,128)} %get-tuple-element.45.table.refs_0_, bf16[6,1536,128]{2,1,0:T(8,128)(2,1)} %bitcast.12, bf16[16,1664]{1,0:T(8,128)(2,1)} %get-tuple-element.52.refs_2_, ...), custom_call_target="tpu_custom_call" | custom-call | flops 1024 | bytes 1024 | tf_op jit(solution)/shard_map/finish/pallas_call | solution.py:430
  46.1 34.5 %collective-permute-done.raw7 = bf16[1536,128]{1,0:T(8,128)(2,1)S(1)} collective-permute-done((bf16[1536,128]{1,0:T(8,128)(2,1)}, bf16[1536,128]{1,0:T(8,128)(2,1)S(1)}, u32[]{:S(2)}, u32[]{:S(2)}) %collective-permute-start) | collective-permute-done | bytes 393248 | tf_op jit(solution)/shard_map/ppermute | solution.py:594
  80.6 8.5 %collective-permute-done.1.raw6 = bf16[1536,128]{1,0:T(8,128)(2,1)S(1)} collective-permute-done((bf16[1536,128]{1,0:T(8,128)(2,1)S(1)}, bf16[1536,128]{1,0:T(8,128)(2,1)S(1)}, u32[]{:S(2)}, u32[]{:S(2)}) %collective-permute-start.1) | collective-permute-done | bytes 393248 | tf_op jit(solution)/shard_map/ppermute | solution.py:594
  89.1 11.8 %collective-permute-start.5 = (bf16[1648,128]{1,0:T(8,128)(2,1)}, bf16[1648,128]{1,0:T(8,128)(2,1)S(1)}, u32[]{:S(2)}, u32[]{:S(2)}) collective-permute-start(bf16[1648,128]{1,0:T(8,128)(2,1)} %get-tuple-element.62), channel_id=1, source_target_pairs={{0,6},{2,8},{6,12},{8,14},{10,16},{14,20},{16,22},{18,24},{22,28},... | collective-permute-start | bytes 1265672 | tf_op jit(solution)/shard_map/ppermute | solution.py:594
  100.9 1.4 collective-permute-start.8
  102.3 1.3 collective-permute-start.10
  103.6 2.1 %all-gather.2 = f32[96,896]{1,0:T(8,128)S(1)} all-gather(f32[48,896]{1,0:T(8,128)S(1)} %copy-done.13), channel_id=4, replica_groups=mesh['req'=16,'head'=2] {'head'}, dimensions={0}, use_global_device_ids=true | all-gather | bytes 516096 | tf_op jit(solution)/shard_map/all_gather | solution.py:661
  105.7 22.4 %collective-permute-done.10.raw5_aside = bf16[1536,128]{1,0:T(8,128)(2,1)S(1)} collective-permute-done((bf16[1536,128]{1,0:T(8,128)(2,1)S(1)}, bf16[1536,128]{1,0:T(8,128)(2,1)S(1)}, u32[]{:S(2)}, u32[]{:S(2)}) %collective-permute-start.10) | collective-permute-done | bytes 393248 | tf_op jit(solution)/shard_map/ppermute | solution.py:594
  128.1 0.7 copy-done.8
  128.9 1.3 collective-permute-start.6
  130.2 1.3 collective-permute-start.9
  131.5 1.0 fusion
  132.5 1.6 %collective-permute-done.11.refs_1_ = bf16[16,1664]{1,0:T(8,128)(2,1)S(1)} collective-permute-done((bf16[16,1664]{1,0:T(8,128)(2,1)S(1)}, bf16[16,1664]{1,0:T(8,128)(2,1)S(1)}, u32[]{:S(2)}, u32[]{:S(2)}) %collective-permute-start.11) | collective-permute-done | bytes 53280 | tf_op jit(solution)/shard_map/ppermute | solution.py:594
  134.1 1.6 collective-permute-start.12
  135.7 5.5 %collective-permute-done.12.refs_2_ = bf16[16,1664]{1,0:T(8,128)(2,1)S(1)} collective-permute-done((bf16[16,1664]{1,0:T(8,128)(2,1)S(1)}, bf16[16,1664]{1,0:T(8,128)(2,1)S(1)}, u32[]{:S(2)}, u32[]{:S(2)}) %collective-permute-start.12) | collective-permute-done | bytes 53280 | tf_op jit(solution)/shard_map/ppermute | solution.py:594
  141.3 0.9 collective-permute-start.13
  142.2 0.7 fusion.2
  142.9 5.4 %collective-permute-done.13.refs_3_ = bf16[16,1664]{1,0:T(8,128)(2,1)S(1)} collective-permute-done((bf16[16,1664]{1,0:T(8,128)(2,1)}, bf16[16,1664]{1,0:T(8,128)(2,1)S(1)}, u32[]{:S(2)}, u32[]{:S(2)}) %collective-permute-start.13) | collective-permute-done | bytes 53280 | tf_op jit(solution)/shard_map/ppermute | solution.py:594
  148.9 4.4 %merge.1.refs_4_ = bf16[6,1536,128]{2,1,0:T(8,128)(2,1)} custom-call(s32[4,8]{1,0:T(4,128)} %get-tuple-element.45.table.refs_0_, bf16[6,1536,128]{2,1,0:T(8,128)(2,1)} %bitcast.13, bf16[1536,128]{1,0:T(8,128)(2,1)} %copy-done.5, bf16[1536,128]{1,0:T(8,128)(2,1)} %copy-done.6, bf16[1536,128]{1,0:T(8,128)(2,1)} %copy-done.7, bf16[1536,128]{1,0:T(8,128)(2,1)} %copy-done.8, ...), custom_call_target="tpu_custom_call" | custom-call | flops 1024 | bytes 1024 | tf_op jit(solution)/shard_map/merge/pallas_call | solution.py:490
  154.2 0.8 copy-done.4
  155.0 3.6 %place.1 = (bf16[6,1536,128]{2,1,0:T(8,128)(2,1)}, bf16[6,3,1536]{2,1,0:T(4,128)(2,1)}, bf16[6,3,256]{2,1,0:T(4,128)(2,1)}) custom-call(bf16[1648,128]{1,0:T(8,128)(2,1)} %copy-done.3, bf16[1648,128]{1,0:T(8,128)(2,1)} %copy-done.2, bf16[1648,128]{1,0:T(8,128)(2,1)} %copy-done.1, bf16[1648,128]{1,0:T(8,128)(2,1)} %copy-done, ...), custom_call_target="tpu_custom_call", output_to_operand_aliasing={{0}: (9, {})} | custom-call | flops 1024 | bytes 1024 | tf_op jit(solution)/shard_map/place/pallas_call | solution.py:571
  (49 shorter events, 4.3 us)
Async XLA Ops:
  15.4 21.7 %copy-start.15 = (bf16[1536,128]{1,0:T(8,128)(2,1)S(1)}, bf16[1536,128]{1,0:T(8,128)(2,1)}, u32[]{:S(2)}) copy-start(bf16[1536,128]{1,0:T(8,128)(2,1)} %get-tuple-element.49) | copy-start | bytes 1179652
  15.4 22.9 %copy-start.14 = (bf16[1536,128]{1,0:T(8,128)(2,1)S(1)}, bf16[1536,128]{1,0:T(8,128)(2,1)}, u32[]{:S(2)}) copy-start(bf16[1536,128]{1,0:T(8,128)(2,1)} %get-tuple-element.50) | copy-start | bytes 1179652
  27.6 76.1 %copy-start.13 = (f32[48,896]{1,0:T(8,128)S(1)}, f32[48,896]{1,0:T(8,128)}, u32[]{:S(2)}) copy-start(f32[48,896]{1,0:T(8,128)} %get-tuple-element.47) | copy-start | bytes 516100
  27.6 100.6 %copy-start.17 = (bf16[16,1664]{1,0:T(8,128)(2,1)S(1)}, bf16[16,1664]{1,0:T(8,128)(2,1)}, u32[]{:S(2)}) copy-start(bf16[16,1664]{1,0:T(8,128)(2,1)} %get-tuple-element.72) | copy-start | bytes 159748
  27.6 106.5 %copy-start.16 = (bf16[16,1664]{1,0:T(8,128)(2,1)S(1)}, bf16[16,1664]{1,0:T(8,128)(2,1)}, u32[]{:S(2)}) copy-start(bf16[16,1664]{1,0:T(8,128)(2,1)} %get-tuple-element.75) | copy-start | bytes 159748
  27.6 114.6 %copy-start.9 = (bf16[48,768]{1,0:T(8,128)(2,1)S(1)}, bf16[48,768]{1,0:T(8,128)(2,1)}, u32[]{:S(2)}) copy-start(bf16[48,768]{1,0:T(8,128)(2,1)} %param.21) | copy-start | bytes 221188
  30.7 58.4 %collective-permute-start.4 = (bf16[1648,128]{1,0:T(8,128)(2,1)}, bf16[1648,128]{1,0:T(8,128)(2,1)S(1)}, u32[]{:S(2)}, u32[]{:S(2)}) collective-permute-start(bf16[1648,128]{1,0:T(8,128)(2,1)} %finish.2), channel_id=1, source_target_pairs={{0,8},{2,10},{4,12},{6,14},{8,16},{10,18},{12,20},{14,22},{16,24},... | collective-permute-start | bytes 1265672 | tf_op jit(solution)/shard_map/ppermute | solution.py:594
  33.7 46.9 %collective-permute-start = (bf16[1536,128]{1,0:T(8,128)(2,1)}, bf16[1536,128]{1,0:T(8,128)(2,1)S(1)}, u32[]{:S(2)}, u32[]{:S(2)}) collective-permute-start(bf16[1536,128]{1,0:T(8,128)(2,1)} %get-tuple-element.48), channel_id=1, source_target_pairs={{0,14},{2,16},{4,18},{6,20},{8,22},{10,24},{12,26},{14,28},{16,30}... | collective-permute-start | bytes 1179656 | tf_op jit(solution)/shard_map/ppermute | solution.py:594
  37.1 51.9 %collective-permute-start.1 = (bf16[1536,128]{1,0:T(8,128)(2,1)S(1)}, bf16[1536,128]{1,0:T(8,128)(2,1)S(1)}, u32[]{:S(2)}, u32[]{:S(2)}) collective-permute-start(bf16[1536,128]{1,0:T(8,128)(2,1)S(1)} %copy-done.15), channel_id=1, source_target_pairs={{0,12},{2,14},{4,16},{6,18},{8,20},{10,22},{12,24},{14,26},{16,28}... | collective-permute-start | bytes 1179656 | tf_op jit(solution)/shard_map/ppermute | solution.py:594
  38.3 50.8 %collective-permute-start.3 = (bf16[1536,128]{1,0:T(8,128)(2,1)S(1)}, bf16[1536,128]{1,0:T(8,128)(2,1)S(1)}, u32[]{:S(2)}, u32[]{:S(2)}) collective-permute-start(bf16[1536,128]{1,0:T(8,128)(2,1)S(1)} %copy-done.14), channel_id=1, source_target_pairs={{6,22},{14,30},{22,6},{30,14},{7,23},{15,31},{23,7},{31,15}} | collective-permute-start | bytes 1179656 | tf_op jit(solution)/shard_map/ppermute | solution.py:594
  39.0 50.1 %collective-permute-start.2 = (bf16[1536,128]{1,0:T(8,128)(2,1)S(1)}, bf16[1536,128]{1,0:T(8,128)(2,1)S(1)}, u32[]{:S(2)}, u32[]{:S(2)}) collective-permute-start(bf16[1536,128]{1,0:T(8,128)(2,1)S(1)} %copy-done.14), channel_id=1, source_target_pairs={{0,10},{2,12},{4,14},{8,18},{10,20},{12,22},{16,26},{18,28},{20,30... | collective-permute-start | bytes 1179656 | tf_op jit(solution)/shard_map/ppermute | solution.py:594
  80.6 67.7 %copy-start.5 = (bf16[1536,128]{1,0:T(8,128)(2,1)}, bf16[1536,128]{1,0:T(8,128)(2,1)S(1)}, u32[]{:S(2)}) copy-start(bf16[1536,128]{1,0:T(8,128)(2,1)S(1)} %collective-permute-done.raw7) | copy-start | bytes 1179652
  89.1 59.2 %copy-start.6 = (bf16[1536,128]{1,0:T(8,128)(2,1)}, bf16[1536,128]{1,0:T(8,128)(2,1)S(1)}, u32[]{:S(2)}) copy-start(bf16[1536,128]{1,0:T(8,128)(2,1)S(1)} %collective-permute-done.1.raw6) | copy-start | bytes 1179652
  89.1 59.2 %copy-start.7 = (bf16[1536,128]{1,0:T(8,128)(2,1)}, bf16[1536,128]{1,0:T(8,128)(2,1)S(1)}, u32[]{:S(2)}) copy-start(bf16[1536,128]{1,0:T(8,128)(2,1)S(1)} %collective-permute-done.2.raw5) | copy-start | bytes 1179652
  89.1 64.3 %copy-start = (bf16[1648,128]{1,0:T(8,128)(2,1)}, bf16[1648,128]{1,0:T(8,128)(2,1)S(1)}, u32[]{:S(2)}) copy-start(bf16[1648,128]{1,0:T(8,128)(2,1)S(1)} %collective-permute-done.4.fourth) | copy-start | bytes 1265668
  89.1 39.8 %collective-permute-start.5 = (bf16[1648,128]{1,0:T(8,128)(2,1)}, bf16[1648,128]{1,0:T(8,128)(2,1)S(1)}, u32[]{:S(2)}, u32[]{:S(2)}) collective-permute-start(bf16[1648,128]{1,0:T(8,128)(2,1)} %get-tuple-element.62), channel_id=1, source_target_pairs={{0,6},{2,8},{6,12},{8,14},{10,16},{14,20},{16,22},{18,24},{22,28},... | collective-permute-start | bytes 1265672 | tf_op jit(solution)/shard_map/ppermute | solution.py:594
  100.9 29.3 %collective-permute-start.8 = (bf16[1648,128]{1,0:T(8,128)(2,1)}, bf16[1648,128]{1,0:T(8,128)(2,1)}, u32[]{:S(2)}, u32[]{:S(2)}) collective-permute-start(bf16[1648,128]{1,0:T(8,128)(2,1)} %get-tuple-element.68), channel_id=1, source_target_pairs={{4,12},{6,14},{12,20},{14,22},{20,28},{22,30},{28,4},{30,6},{5,13}... | collective-permute-start | bytes 1265672 | tf_op jit(solution)/shard_map/ppermute | solution.py:594
  102.3 25.8 %collective-permute-start.10 = (bf16[1536,128]{1,0:T(8,128)(2,1)S(1)}, bf16[1536,128]{1,0:T(8,128)(2,1)S(1)}, u32[]{:S(2)}, u32[]{:S(2)}) collective-permute-start(bf16[1536,128]{1,0:T(8,128)(2,1)S(1)} %collective-permute-done.3), channel_id=1, source_target_pairs={{6,0},{14,8},{22,16},{30,24},{7,1},{15,9},{23,17},{31,25}} | collective-permute-start | bytes 1179656 | tf_op jit(solution)/shard_map/ppermute | solution.py:594
  105.7 47.6 %collective-permute-start.7 = (bf16[1648,128]{1,0:T(8,128)(2,1)}, bf16[1648,128]{1,0:T(8,128)(2,1)S(1)}, u32[]{:S(2)}, u32[]{:S(2)}) collective-permute-start(bf16[1648,128]{1,0:T(8,128)(2,1)} %get-tuple-element.65), channel_id=1, source_target_pairs={{0,4},{2,6},{4,8},{6,10},{8,12},{10,14},{12,16},{14,18},{16,20},{1... | collective-permute-start | bytes 1265672 | tf_op jit(solution)/shard_map/ppermute | solution.py:594
  128.1 0.7 copy-start.8
  128.1 5.9 %collective-permute-start.11 = (bf16[16,1664]{1,0:T(8,128)(2,1)S(1)}, bf16[16,1664]{1,0:T(8,128)(2,1)S(1)}, u32[]{:S(2)}, u32[]{:S(2)}) collective-permute-start(bf16[16,1664]{1,0:T(8,128)(2,1)S(1)} %copy-done.17), channel_id=1, source_target_pairs={{0,14},{2,16},{4,18},{6,20},{8,22},{10,24},{12,26},{14,28},{16,30}... | collective-permute-start | bytes 159752 | tf_op jit(solution)/shard_map/ppermute | solution.py:594
  128.9 24.5 %copy-start.1 = (bf16[1648,128]{1,0:T(8,128)(2,1)}, bf16[1648,128]{1,0:T(8,128)(2,1)S(1)}, u32[]{:S(2)}) copy-start(bf16[1648,128]{1,0:T(8,128)(2,1)S(1)} %collective-permute-done.5.third) | copy-start | bytes 1265668
  128.9 24.4 %collective-permute-start.6 = (bf16[1648,128]{1,0:T(8,128)(2,1)}, bf16[1648,128]{1,0:T(8,128)(2,1)S(1)}, u32[]{:S(2)}, u32[]{:S(2)}) collective-permute-start(bf16[1648,128]{1,0:T(8,128)(2,1)} %get-tuple-element.64), channel_id=1, source_target_pairs={{0,2},{2,4},{4,6},{8,10},{10,12},{12,14},{16,18},{18,20},{20,22},{... | collective-permute-start | bytes 1265672 | tf_op jit(solution)/shard_map/ppermute | solution.py:594
  130.2 23.1 %collective-permute-start.9 = (bf16[1648,128]{1,0:T(8,128)(2,1)}, bf16[1648,128]{1,0:T(8,128)(2,1)S(1)}, u32[]{:S(2)}, u32[]{:S(2)}) collective-permute-start(bf16[1648,128]{1,0:T(8,128)(2,1)} %collective-permute-done.8), channel_id=1, source_target_pairs={{4,2},{6,0},{12,10},{14,8},{20,18},{22,16},{28,26},{30,24},{5,3},{... | collective-permute-start | bytes 1265672 | tf_op jit(solution)/shard_map/ppermute | solution.py:594
  134.1 14.2 %copy-start.10 = (bf16[16,1664]{1,0:T(8,128)(2,1)}, bf16[16,1664]{1,0:T(8,128)(2,1)S(1)}, u32[]{:S(2)}) copy-start(bf16[16,1664]{1,0:T(8,128)(2,1)S(1)} %collective-permute-done.11.refs_1_) | copy-start | bytes 159748
  134.1 7.2 %collective-permute-start.12 = (bf16[16,1664]{1,0:T(8,128)(2,1)S(1)}, bf16[16,1664]{1,0:T(8,128)(2,1)S(1)}, u32[]{:S(2)}, u32[]{:S(2)}) collective-permute-start(bf16[16,1664]{1,0:T(8,128)(2,1)S(1)} %copy-done.16), channel_id=1, source_target_pairs={{0,12},{2,14},{4,16},{6,18},{8,20},{10,22},{12,24},{14,26},{16,28}... | collective-permute-start | bytes 159752 | tf_op jit(solution)/shard_map/ppermute | solution.py:594
  141.3 7.1 %copy-start.11 = (bf16[16,1664]{1,0:T(8,128)(2,1)}, bf16[16,1664]{1,0:T(8,128)(2,1)S(1)}, u32[]{:S(2)}) copy-start(bf16[16,1664]{1,0:T(8,128)(2,1)S(1)} %collective-permute-done.12.refs_2_) | copy-start | bytes 159748
  141.3 7.0 %collective-permute-start.13 = (bf16[16,1664]{1,0:T(8,128)(2,1)}, bf16[16,1664]{1,0:T(8,128)(2,1)S(1)}, u32[]{:S(2)}, u32[]{:S(2)}) collective-permute-start(bf16[16,1664]{1,0:T(8,128)(2,1)} %get-tuple-element.78), channel_id=1, source_target_pairs={{0,10},{2,12},{4,14},{6,16},{8,18},{10,20},{12,22},{14,24},{16,26}... | collective-permute-start | bytes 159752 | tf_op jit(solution)/shard_map/ppermute | solution.py:594
  148.3 0.6 copy-start.12
  153.3 0.8 copy-start.2
  153.3 0.9 copy-start.3
  154.2 0.8 copy-start.4

commit v4 on v3

--- a/solution.py
+++ b/solution.py
@@ -16,9 +16,10 @@
 TILE = 256
 EXTRA = NSTATE
 PLANE = 4
-RAW = (7, 6, 5)
+RAW = (4, 5, 6, 7)
 PARTS = 3
 SMALL = pl.CostEstimate(flops=1024, bytes_accessed=1024, transcendentals=0)
+STEP = pl.CostEstimate(flops=1024, bytes_accessed=40_000_000, transcendentals=0)
 
 epsilon = 1e-05
 HIGH = lax.Precision.HIGHEST
@@ -381,7 +382,7 @@
     return lax.rem(lax.axis_index("req"), PLANE)
 
 
-def finish_kernel(offsets, aside, *refs):
+def finish_kernel(offsets, *refs):
     n = len(offsets)
     table, states = refs[:2]
     corr = refs[2 : 2 + n]
@@ -410,28 +411,17 @@
             outs[i][width + t * 2 * DRAFT : width + (t + 1) * 2 * DRAFT] = block.astype(BF16)
         copies[i].wait()
         advance(corr[i], loaded.at[i], outs[i])
-    if aside:
-        other = refs[2 + 2 * n]
-
-        @pl.when(column() == 3)
-        def _():
-            other[...] = outs[offsets.index(1)][...]
-
-        @pl.when(column() != 3)
-        def _():
-            other[...] = outs[offsets.index(3)][...]
-
-
-def finish(offsets, aside, table, states, corr):
+
+
+def finish(offsets, table, states, corr):
     n = len(offsets)
     width = states.shape[1]
     shape = jax.ShapeDtypeStruct((width + tail_rows(width)[1], NSTATE), BF16)
-    outs = n + (1 if aside else 0)
     return pl.pallas_call(
-        functools.partial(finish_kernel, offsets, aside),
+        functools.partial(finish_kernel, offsets),
         in_specs=[in_smem(), in_hbm()] + [in_vmem()] * n,
-        out_specs=[in_vmem()] * outs,
-        out_shape=[shape] * outs,
+        out_specs=[in_vmem()] * n,
+        out_shape=[shape] * n,
         scratch_shapes=[
             pltpu.VMEM((n, width, NSTATE), BF16),
             pltpu.SemaphoreType.DMA((n,)),
@@ -445,84 +435,119 @@
     return jnp.max(low[6:7]).astype(jnp.int32) - 1
 
 
-def merge_kernel(table, states, raw7, raw6, raw5, raw5_aside, *refs):
-    corr = refs[:4]
-    kept, loaded, merged, sem_in, sem_out = refs[4:]
-    width = loaded.shape[1]
-
-    def fetch(i, source):
-        return pltpu.make_async_copy(source, loaded.at[i], sem_in.at[i])
-
-    fetch(0, states.at[table[3, 0]]).start()
-    fetch(1, raw7).start()
-    fetch(2, raw6).start()
-
-    @pl.when(column() == 0)
-    def _():
-        fetch(3, raw5_aside).start()
-
-    @pl.when(column() != 0)
-    def _():
-        fetch(3, raw5).start()
-
+def merge_kernel(table, states, *refs):
+    n = 1 + len(RAW)
+    raws = refs[: n - 1]
+    turned = refs[n - 1]
+    corr = refs[n : 2 * n]
+    _, kept, loaded, merged, sem_in, sem_out = refs[2 * n :]
+    width = loaded.shape[0]
+    own = pltpu.make_async_copy(states.at[table[3, 0]], loaded, sem_in)
+    own.start()
     slots = [mark_of(ref[:, width:].astype(F32)[DRAFT:]) for ref in corr]
 
     def put(i):
         return pltpu.make_async_copy(merged.at[i], kept.at[slots[i]], sem_out.at[i])
 
-    for i in range(4):
-        fetch(i, raw7).wait()
+    for i in range(n):
+        if i == 0:
+            own.wait()
 
         @pl.when(slots[i] >= 0)
         def _(i=i):
-            advance(corr[i], loaded.at[i], merged.at[i])
+            if i == 0:
+                advance(corr[i], loaded, merged.at[i])
+            elif RAW[i - 1] == 5:
+
+                @pl.when(column() == 0)
+                def _():
+                    advance(corr[i], turned, merged.at[i])
+
+                @pl.when(column() != 0)
+                def _():
+                    advance(corr[i], raws[i - 1], merged.at[i])
+
+            else:
+                advance(corr[i], raws[i - 1], merged.at[i])
             put(i).start()
 
-    for i in range(4):
+    for i in range(n):
 
         @pl.when(slots[i] >= 0)
         def _(i=i):
             put(i).wait()
 
 
-def merge(count, table, states, raws, corr):
+def merge(count, table, states, raws, turned, corr, kept):
     width = states.shape[1]
+    n = 1 + len(RAW)
     return pl.pallas_call(
         merge_kernel,
-        in_specs=[in_smem()] + [in_hbm()] * 5 + [in_vmem()] * 4,
+        in_specs=[in_smem(), in_hbm()] + [in_vmem()] * (2 * n) + [in_hbm()],
         out_specs=in_hbm(),
         out_shape=jax.ShapeDtypeStruct((count, width, NSTATE), BF16),
         scratch_shapes=[
-            pltpu.VMEM((4, width, NSTATE), BF16),
-            pltpu.VMEM((4, width, NSTATE), BF16),
-            pltpu.SemaphoreType.DMA((4,)),
-            pltpu.SemaphoreType.DMA((4,)),
+            pltpu.VMEM((width, NSTATE), BF16),
+            pltpu.VMEM((n, width, NSTATE), BF16),
+            pltpu.SemaphoreType.DMA,
+            pltpu.SemaphoreType.DMA((n,)),
         ],
-        cost_estimate=SMALL,
+        input_output_aliases={2 + 2 * n: 0},
+        cost_estimate=STEP,
         name="merge",
-    )(table, states, *raws, *corr)
-
-
-def place_kernel(first, second, third, fourth, aside, *refs):
-    corr = refs[:4]
-    _, kept, out_inner, out_ssm, loaded, sem_in, sem_out = refs[4:]
+    )(table, states, *raws, turned, *corr, kept)
+
+
+def halves(ref, width):
+    parts = [
+        ref[row : row + 2 * DRAFT].astype(F32)
+        for row in range(width, ref.shape[0], 2 * DRAFT)
+    ]
+    return [part[:DRAFT] for part in parts] + [part[DRAFT:] for part in parts]
+
+
+def place_kernel(width, message, *refs):
+    kept, sem = refs[-2:]
+    slot = mark_of(halves(message, width)[width // NSTATE])
+
+    @pl.when(slot >= 0)
+    def _():
+        copy = pltpu.make_async_copy(message.at[pl.ds(0, width)], kept.at[slot], sem)
+        copy.start()
+        copy.wait()
+
+
+def place(count, width, message, kept=None):
+    return pl.pallas_call(
+        functools.partial(place_kernel, width),
+        in_specs=[in_vmem()] + ([] if kept is None else [in_hbm()]),
+        out_specs=in_hbm(),
+        out_shape=jax.ShapeDtypeStruct((count, width, NSTATE), BF16),
+        input_output_aliases={} if kept is None else {1: 0},
+        scratch_shapes=[pltpu.SemaphoreType.DMA],
+        cost_estimate=STEP,
+        name="place",
+    )(message, *([] if kept is None else [kept]))
+
+
+def close_kernel(n, *refs):
+    messages = refs[:n]
+    corr = refs[n : n + 1 + len(RAW)]
+    _, kept, out_inner, out_ssm, sem = refs[n + 1 + len(RAW) :]
     width = out_inner.shape[2]
-    pairs, _ = tail_rows(width)
-
-    def fetch(i, source):
-        return pltpu.make_async_copy(source, loaded.at[i], sem_in.at[i])
-
-    fetch(3, fourth).start()
-    fetch(1, second).start()
-    for i, source, turned in ((0, first, 0), (2, third, 1)):
-
-        @pl.when(column() == turned)
-        def _(i=i):
-            fetch(i, aside).start()
-
-        @pl.when(column() != turned)
-        def _(i=i, source=source):
-            fetch(i, source).start()
+    tiles = width // NSTATE
+    marks = []
+    for ref in messages:
+        lows = halves(ref, width)
+        marks.append((mark_of(lows[tiles]), lows))
+    last = marks[0][0]
+
+    def put():
+        return pltpu.make_async_copy(messages[0].at[pl.ds(0, width)], kept.at[last], sem)
+
+    @pl.when(last >= 0)
+    def _():
+        put().start()
 
     def write_edges(slot, inner, low):
         out_inner[slot] = inner[: KCONV - 1].astype(BF16)
@@ -537,60 +562,38 @@
         def _(slot=slot, low=low):
             write_edges(slot, low[:, :width], low[:, width:])
 
-    def put(i, slot):
-        return pltpu.make_async_copy(
-            loaded.at[i, pl.ds(0, width)], kept.at[slot], sem_out.at[i]
-        )
-
-    slots = []
-    for i in (3, 1, 2, 0):
-        fetch(i, fourth).wait()
-        parts = [
-            loaded[i, width + t * 2 * DRAFT : width + (t + 1) * 2 * DRAFT].astype(F32)
-            for t in range(pairs)
-        ]
-        lows = [part[:DRAFT] for part in parts] + [part[DRAFT:] for part in parts]
-        tiles = width // NSTATE
-        slot = mark_of(lows[tiles])
-        slots.append((i, slot))
+    for slot, lows in marks:
 
         @pl.when(slot >= 0)
-        def _(i=i, slot=slot, lows=lows):
-            put(i, slot).start()
+        def _(slot=slot, lows=lows):
             write_edges(slot, jnp.concatenate(lows[:tiles], axis=1), lows[tiles])
 
-    for i, slot in slots:
-
-        @pl.when(slot >= 0)
-        def _(i=i, slot=slot):
-            put(i, slot).wait()
-
-
-def place(count, width, messages, corr, kept):
-    rows = width + tail_rows(width)[1]
+    @pl.when(last >= 0)
+    def _():
+        put().wait()
+
+
+def close(count, width, messages, corr, kept):
+    n = len(messages)
     return pl.pallas_call(
-        place_kernel,
-        in_specs=[in_hbm()] * 5 + [in_vmem()] * 4 + [in_hbm()],
+        functools.partial(close_kernel, n),
+        in_specs=[in_vmem()] * (n + len(corr)) + [in_hbm()],
         out_specs=[in_hbm(), in_vmem(), in_vmem()],
         out_shape=[
             jax.ShapeDtypeStruct((count, width, NSTATE), BF16),
             jax.ShapeDtypeStruct((count, KCONV - 1, width), BF16),
             jax.ShapeDtypeStruct((count, KCONV - 1, 2 * NSTATE), BF16),
         ],
-        input_output_aliases={9: 0},
-        scratch_shapes=[
-            pltpu.VMEM((4, rows, NSTATE), BF16),
-            pltpu.SemaphoreType.DMA((4,)),
-            pltpu.SemaphoreType.DMA((4,)),
-        ],
+        input_output_aliases={n + len(corr): 0},
+        scratch_shapes=[pltpu.SemaphoreType.DMA],
         cost_estimate=SMALL,
-        name="place",
+        name="close",
     )(*messages, *corr, kept)
 
 
-def moved(array, by, columns=range(PLANE)):
+def moved(array, by, columns=tuple(range(PLANE))):
     length = lax.axis_size("req")
-    pairs = [(i, (i + by[i % PLANE]) % length) for i in range(length) if i % PLANE in columns]
+    pairs = [(i, (i + by) % length) for i in range(length) if i % PLANE in columns]
     return lax.ppermute(array, "req", pairs)
 
 
@@ -621,11 +624,13 @@
     depth, width = proj_inner.shape
     peers = lax.axis_size("req")
     flat = states_in.reshape(count, width, NSTATE)
-    raw7, raw6, raw5, table = pick(count, width, peers, destination, flat)
-    raw5_z = moved(raw5, [8] * PLANE, (3,))
-    raw7 = moved(raw7, [7] * PLANE)
-    raw6 = moved(raw6, [6] * PLANE)
-    raw5 = moved(raw5, [5] * PLANE, (0, 1, 2))
+    *raws, table = pick(count, width, peers, destination, flat)
+    raw5_z = moved(raws[1], 8, (3,))
+    raws = [
+        moved(raw, k, (0, 1, 2) if k == 5 else (0, 1, 2, 3)) for raw, k in zip(raws, RAW)
+    ]
+    table, ready, ready_ssm = lax.optimization_barrier((table, hidden_in, proj_ssm))
+    vectors = jnp.stack([norm_gain, conv_inner_bias, gate_gain])
     results = front(
         count,
         heads,
@@ -635,16 +640,16 @@
             table,
             draft_lengths,
             accepted,
-            lax.all_gather(hidden_in, "head", axis=0, tiled=False),
-            jnp.stack([norm_gain, conv_inner_bias, gate_gain]),
+            lax.all_gather(ready, "head", axis=0, tiled=False),
+            vectors,
             proj_gate,
             proj_inner,
             proj_out,
-            lax.all_gather(proj_ssm, "head", axis=0, tiled=False),
+            lax.all_gather(ready_ssm, "head", axis=0, tiled=False),
             proj_step.T,
             jnp.stack([step_bias, decay_log, skip_gain]),
             conv_inner,
-            jnp.stack([norm_gain, conv_inner_bias, gate_gain]),
+            vectors,
             conv_ssm,
             conv_ssm_bias.reshape(1, 2 * NSTATE),
             flat,
@@ -654,9 +659,7 @@
     )
     mine, theirs = results[:2]
     corr = list(results[2:])
-    (fourth,) = finish((4,), False, table, flat, corr)
-    fourth = moved(fourth, [4] * PLANE)
-    first, second, third, aside = finish((1, 2, 3), True, table, flat, corr)
+    first, second, third = finish((1, 2, 3), table, flat, corr)
 
     pair = lax.all_gather(theirs, "head", axis=0, tiled=False)
     other = jnp.where(lax.axis_index("head") == 0, pair[1], pair[0])
@@ -665,30 +668,26 @@
     scale = lax.rsqrt(total[:, half : half + 1] / DINNER + epsilon)
     hidden_out = (hidden_in.astype(F32) + total[:, :half] * scale).astype(BF16)
 
-    raw7, raw6, raw5, raw5_z, fourth, aside, third, second, first, *late = (
-        lax.optimization_barrier(
-            (raw7, raw6, raw5, raw5_z, fourth, aside, third, second, first, *corr[5:])
-        )
+    raw4, raw5, raw6, raw7 = raws
+    raw5_z, third = lax.optimization_barrier((raw5_z, third))
+    turned = moved(raw5_z, -3, (3,))
+    raw4, third = lax.optimization_barrier((raw4, third))
+    third = moved(third, 3)
+    raw5, second = lax.optimization_barrier((raw5, second))
+    second = moved(second, 2)
+    raw6, first = lax.optimization_barrier((raw6, first))
+    first = moved(first, 1)
+    raw7, *late = lax.optimization_barrier((raw7, *corr[4:]))
+    corr[7] = moved(late[3], 7)
+    raw4, raw5, raw6, raw7, raw5_z, *late = lax.optimization_barrier(
+        (raw4, raw5, raw6, raw7, raw5_z, *late[:3])
     )
-    corr[5:] = late
-    raw5_turned = moved(raw5_z, [-3] * PLANE, (3,))
-    aside = moved(aside, [4] * PLANE, (2, 3))
-    third = moved(third, [3] * PLANE, (0, 1, 3))
-    second = moved(second, [2] * PLANE)
-    turned = moved(aside, [0, 0, -1, -3], (2, 3))
-    third, first = lax.optimization_barrier((third, first))
-    first = moved(first, [1] * PLANE, (0, 1, 2))
-    raw5_turned, corr[7] = lax.optimization_barrier((raw5_turned, corr[7]))
-    corr[7] = moved(corr[7], [7] * PLANE)
-    corr[7], corr[6] = lax.optimization_barrier((corr[7], corr[6]))
-    corr[6] = moved(corr[6], [6] * PLANE)
-    corr[6], corr[5] = lax.optimization_barrier((corr[6], corr[5]))
-    corr[5] = moved(corr[5], [5] * PLANE)
-    sent = [corr[0], corr[7], corr[6], corr[5]]
-    kept = merge(count, table, flat, (raw7, raw6, raw5, raw5_turned), sent)
-    kept, kept_inner, kept_ssm = place(
-        count, width, (first, second, third, fourth, turned), sent, kept
-    )
+    corr[4:7] = [moved(array, k) for array, k in zip(late, (4, 5, 6))]
+    sent = [corr[0], *corr[4:]]
+    kept = place(count, width, third)
+    kept = place(count, width, second, kept)
+    kept = merge(count, table, flat, (raw4, raw5, raw6, raw7), turned, sent, kept)
+    kept, kept_inner, kept_ssm = close(count, width, (first, second, third), sent, kept)
     return (hidden_out, kept.reshape(states_in.shape), kept_inner, kept_ssm)
 
 

time: 159 us -> 133 us (0.84); the launches traced: 159 us -> 131 us
  waiting for transfers between devices: 77.9 us -> 3.09 us
  starting transfers between devices: 30.5 us -> 84.9 us
  local copies, waits for them, and re-layouts: 5.1 us -> 1.63 us
  blocking collectives: 9.82 us -> 6.56 us
    ppermute x14 -> x13, waiting for transfers between devices: 77.9 us -> 3.09 us  [moved(): return lax.ppermute(array, 'req', pairs)]
    ppermute x14 -> x13, starting transfers between devices: 30.5 us -> 84.9 us  [moved(): return lax.ppermute(array, 'req', pairs)]
    all_gather x2, blocking collectives: 7.77 us -> 4.52 us  [the longest x1 2.49 us: local(): lax.all_gather(ready_ssm, 'head', axis=0, tiled=False)]
    another operation x3, local copies, waits for them, and re-layouts: 2.1 us -> 0.02 us  [local(): vectors = jnp.stack([norm_gain, conv_inner_bias, gate_gain])]
    pallas_call x4 -> x5, Pallas kernels: 15.5 us -> 15.2 us  [the longest x1 4.55 us: merge(): pl.pallas_call(merge_kernel, in_specs=[in_smem(), in_hbm()] + [in_vmem()]...]
  transfers between devices with their start and end apart: 14 -> 13, of which waited for: 6 -> 2; matrix products, arithmetic and copies ran while one was open for 1% -> 2% of each run, Pallas kernels for 6% -> 19%
where the time goes in v4:
time: 133 us; the launch traced here: 131 us
  starting transfers between devices  84.9 us (64%)
  Pallas kernels  30.7 us (23%)
  blocking collectives  6.56 us (5%)
  waiting for transfers between devices  3.09 us (2%)
  other arithmetic  3 us (2%)
  local copies, waits for them, and re-layouts  1.63 us (1%)
    ppermute x13, starting transfers between devices, moved(): return lax.ppermute(array, 'req', pairs)  84.9 us
    pallas_call x1, Pallas kernels, front(): pl.pallas_call(functools.partial(front_kernel, count, heads), grid=(tiles...  12.1 us
    pallas_call x1, Pallas kernels, merge(): pl.pallas_call(merge_kernel, in_specs=[in_smem(), in_hbm()] + [in_vmem()]...  4.55 us
    pallas_call x1, Pallas kernels, finish(): pl.pallas_call(functools.partial(finish_kernel, offsets), in_specs=[in_sm...  4.02 us
    pallas_call x2, Pallas kernels, place(): pl.pallas_call(functools.partial(place_kernel, width), in_specs=[in_vmem(...  3.76 us
    pallas_call x1, Pallas kernels, pick(): pl.pallas_call(functools.partial(pick_kernel, count, peers), in_specs=[in...  3.42 us
    ppermute x13, waiting for transfers between devices, moved(): return lax.ppermute(array, 'req', pairs)  3.09 us
    pallas_call x1, Pallas kernels, close(): pl.pallas_call(functools.partial(close_kernel, n), in_specs=[in_vmem()] *...  2.84 us
  transfers between devices with their start and end apart: 13, of which 2 were waited for; matrix products, arithmetic and copies ran while one was open for 2% of the time, Pallas kernels for 19%

profile of v4, /device:TPU:0, one launch (start us, length us, event | category | flops | bytes accessed | tf_op | source)
XLA Modules:
  0.0 130.9 jit_solution(15678570275952606903)
XLA Ops:
  0.7 3.4 %pick.1 = (bf16[1536,128]{1,0:T(8,128)(2,1)}, bf16[1536,128]{1,0:T(8,128)(2,1)}, bf16[1536,128]{1,0:T(8,128)(2,1)}, bf16[1536,128]{1,0:T(8,128)(2,1)}, s32[4,8]{1,0:T(4,128)}) custom-call(s32[6]{0:T(128)} %destination.1, bf16[6,1536,128]{2,1,0:T(8,128)(2,1)} %bitcast.9), custom_call_target="tpu_custom_call" | custom-call | flops 1024 | bytes 1024 | tf_op jit(solution)/shard_map/pick/pallas_call | solution.py:349
  4.1 0.7 collective-permute-start.5
  4.8 5.9 %collective-permute-start.2 = (bf16[1536,128]{1,0:T(8,128)(2,1)}, bf16[1536,128]{1,0:T(8,128)(2,1)S(1)}, u32[]{:S(2)}, u32[]{:S(2)}) collective-permute-start(bf16[1536,128]{1,0:T(8,128)(2,1)} %get-tuple-element.60), channel_id=1, source_target_pairs={{0,10},{2,12},{4,14},{8,18},{10,20},{12,22},{16,26},{18,28},{20,30... | collective-permute-start | bytes 1179656 | tf_op jit(solution)/shard_map/ppermute | solution.py:597
  10.7 4.1 %collective-permute-start = (bf16[1536,128]{1,0:T(8,128)(2,1)}, bf16[1536,128]{1,0:T(8,128)(2,1)S(1)}, u32[]{:S(2)}, u32[]{:S(2)}) collective-permute-start(bf16[1536,128]{1,0:T(8,128)(2,1)} %get-tuple-element.54), channel_id=1, source_target_pairs={{0,12},{2,14},{4,16},{6,18},{8,20},{10,22},{12,24},{14,26},{16,28}... | collective-permute-start | bytes 1179656 | tf_op jit(solution)/shard_map/ppermute | solution.py:597
  14.8 1.6 %collective-permute-start.4 = (bf16[1536,128]{1,0:T(8,128)(2,1)}, bf16[1536,128]{1,0:T(8,128)(2,1)S(1)}, u32[]{:S(2)}, u32[]{:S(2)}) collective-permute-start(bf16[1536,128]{1,0:T(8,128)(2,1)} %get-tuple-element.63), channel_id=1, source_target_pairs={{0,8},{2,10},{4,12},{6,14},{8,16},{10,18},{12,20},{14,22},{16,24},... | collective-permute-start | bytes 1179656 | tf_op jit(solution)/shard_map/ppermute | solution.py:597
  16.5 0.6 pad_maximum_fusion.vectors.vector_tile
  17.1 2.5 %all-gather.1 = bf16[3072,128]{1,0:T(8,128)(2,1)} all-gather(bf16[1536,128]{1,0:T(8,128)(2,1)S(1)} %copy-done.8), channel_id=3, replica_groups=mesh['req'=16,'head'=2] {'head'}, dimensions={0}, use_global_device_ids=true | all-gather | bytes 1179648 | tf_op jit(solution)/shard_map/all_gather | solution.py:648
  19.6 0.6 pad_maximum_fusion.1.head_rows
  20.2 2.0 %all-gather = bf16[96,768]{1,0:T(8,128)(2,1)} all-gather(bf16[48,768]{1,0:T(8,128)(2,1)S(1)} %copy-done.9), channel_id=2, replica_groups=mesh['req'=16,'head'=2] {'head'}, dimensions={0}, use_global_device_ids=true | all-gather | bytes 221184 | tf_op jit(solution)/shard_map/all_gather | solution.py:643
  22.3 12.1 %front.1 = (f32[48,896]{1,0:T(8,128)}, f32[48,896]{1,0:T(8,128)}, bf16[16,1664]{1,0:T(8,128)(2,1)}, bf16[16,1664]{1,0:T(8,128)(2,1)}, bf16[16,1664]{1,0:T(8,128)...) custom-call(s32[4,8]{1,0:T(4,128)} %get-tuple-element.49.table.refs_, ...), custom_call_target="tpu_custom_call" | custom-call | flops 1024 | bytes 1024 | tf_op jit(solution)/shard_map/front/pallas_call | solution.py:289
  34.4 4.0 %finish.1 = (bf16[1648,128]{1,0:T(8,128)(2,1)}, bf16[1648,128]{1,0:T(8,128)(2,1)}, bf16[1648,128]{1,0:T(8,128)(2,1)}) custom-call(s32[4,8]{1,0:T(4,128)} %get-tuple-element.49.table.refs_0_, bf16[6,1536,128]{2,1,0:T(8,128)(2,1)} %bitcast.11, bf16[16,1664]{1,0:T(8,128)(2,1)} %get-tuple-element.55.refs_2_, bf16[16,1664]{1,0:T(8,128)(2,1)} %get-tuple-element.56.refs_3_, ...), custom_call_target="tpu_custom_call" | custom-call | flops 1024 | bytes 1024 | tf_op jit(solution)/shard_map/finish/pallas_call | solution.py:420
  38.4 2.5 %collective-permute-done.4.refs_0_ = bf16[1536,128]{1,0:T(8,128)(2,1)S(1)} collective-permute-done((bf16[1536,128]{1,0:T(8,128)(2,1)}, bf16[1536,128]{1,0:T(8,128)(2,1)S(1)}, u32[]{:S(2)}, u32[]{:S(2)}) %collective-permute-start.4) | collective-permute-done | bytes 393248 | tf_op jit(solution)/shard_map/ppermute | solution.py:597
  40.9 39.0 %collective-permute-start.6 = (bf16[1648,128]{1,0:T(8,128)(2,1)}, bf16[1648,128]{1,0:T(8,128)(2,1)S(1)}, u32[]{:S(2)}, u32[]{:S(2)}) collective-permute-start(bf16[1648,128]{1,0:T(8,128)(2,1)} %get-tuple-element.66), channel_id=1, source_target_pairs={{0,6},{2,8},{4,10},{6,12},{8,14},{10,16},{12,18},{14,20},{16,22},{... | collective-permute-start | bytes 1265672 | tf_op jit(solution)/shard_map/ppermute | solution.py:597
  80.0 2.0 %all-gather.2 = f32[96,896]{1,0:T(8,128)S(1)} all-gather(f32[48,896]{1,0:T(8,128)S(1)} %copy-done.13), channel_id=4, replica_groups=mesh['req'=16,'head'=2] {'head'}, dimensions={0}, use_global_device_ids=true | all-gather | bytes 516096 | tf_op jit(solution)/shard_map/all_gather | solution.py:664
  82.0 1.3 collective-permute-start.12
  83.3 7.8 %collective-permute-start.1 = (bf16[1648,128]{1,0:T(8,128)(2,1)}, bf16[1648,128]{1,0:T(8,128)(2,1)S(1)}, u32[]{:S(2)}, u32[]{:S(2)}) collective-permute-start(bf16[1648,128]{1,0:T(8,128)(2,1)} %get-tuple-element.59), channel_id=1, source_target_pairs={{0,2},{2,4},{4,6},{6,8},{8,10},{10,12},{12,14},{14,16},{16,18},{18... | collective-permute-start | bytes 1265672 | tf_op jit(solution)/shard_map/ppermute | solution.py:597
  91.1 0.9 fusion
  92.1 0.1 collective-permute-start.11
  92.2 0.1 fusion.5
  92.3 19.5 %collective-permute-start.8 = (bf16[16,1664]{1,0:T(8,128)(2,1)}, bf16[16,1664]{1,0:T(8,128)(2,1)}, u32[]{:S(2)}, u32[]{:S(2)}) collective-permute-start(bf16[16,1664]{1,0:T(8,128)(2,1)} %get-tuple-element.81), channel_id=1, source_target_pairs={{0,8},{2,10},{4,12},{6,14},{8,16},{10,18},{12,20},{14,22},{16,24},... | collective-permute-start | bytes 159752 | tf_op jit(solution)/shard_map/ppermute | solution.py:597
  111.8 1.9 %place.2.refs_0_ = bf16[6,1536,128]{2,1,0:T(8,128)(2,1)} custom-call(bf16[1648,128]{1,0:T(8,128)(2,1)} %copy-done), custom_call_target="tpu_custom_call" | custom-call | flops 1024 | bytes 40000000 | tf_op jit(solution)/shard_map/place/pallas_call | solution.py:521
  113.7 0.1 collective-permute-start.9
  113.8 4.9 %collective-permute-start.10 = (bf16[16,1664]{1,0:T(8,128)(2,1)}, bf16[16,1664]{1,0:T(8,128)(2,1)S(1)}, u32[]{:S(2)}, u32[]{:S(2)}) collective-permute-start(bf16[16,1664]{1,0:T(8,128)(2,1)} %get-tuple-element.83), channel_id=1, source_target_pairs={{0,12},{2,14},{4,16},{6,18},{8,20},{10,22},{12,24},{14,26},{16,28}... | collective-permute-start | bytes 159752 | tf_op jit(solution)/shard_map/ppermute | solution.py:597
  118.7 0.7 fusion.2
  119.5 1.9 %place.3.refs_10_ = bf16[6,1536,128]{2,1,0:T(8,128)(2,1)} custom-call(bf16[1648,128]{1,0:T(8,128)(2,1)} %copy-done.1, bf16[6,1536,128]{2,1,0:T(8,128)(2,1)} %place.2.refs_0_), custom_call_target="tpu_custom_call", output_to_operand_aliasing={{}: (1, {})} | custom-call | flops 1024 | bytes 40000000 | tf_op jit(solution)/shard_map/place/pallas_call | solution.py:521
  121.4 0.6 collective-permute-done.9.refs_7_.refs_5_
  122.0 0.6 copy-done.11
  122.6 0.0 copy-done.12
  122.6 0.2 copy-done.7
  122.8 4.6 %merge.1.refs_8_ = bf16[6,1536,128]{2,1,0:T(8,128)(2,1)} custom-call(s32[4,8]{1,0:T(4,128)} %get-tuple-element.49.table.refs_0_, bf16[6,1536,128]{2,1,0:T(8,128)(2,1)} %bitcast.12, bf16[1536,128]{1,0:T(8,128)(2,1)} %copy-done.5, bf16[1536,128]{1,0:T(8,128)(2,1)} %copy-done.3, bf16[1536,128]{1,0:T(8,128)(2,1)} %copy-done.4, ...), custom_call_target="tpu_custom_call", output_to_operand_aliasing={{}: (12, {})} | custom-call | flops 1024 | bytes 40000000 | tf_op jit(solution)/shard_map/merge/pallas_call | solution.py:484
  127.3 0.7 copy-done.2
  128.1 2.8 %close.1 = (bf16[6,1536,128]{2,1,0:T(8,128)(2,1)}, bf16[6,3,1536]{2,1,0:T(4,128)(2,1)}, bf16[6,3,256]{2,1,0:T(4,128)(2,1)}) custom-call(bf16[1648,128]{1,0:T(8,128)(2,1)} %copy-done.2, bf16[1648,128]{1,0:T(8,128)(2,1)} %copy-done.1, bf16[1648,128]{1,0:T(8,128)(2,1)} %copy-done, ...), custom_call_target="tpu_custom_call", output_to_operand_aliasing={{0}: (8, {})} | custom-call | flops 1024 | bytes 1024 | tf_op jit(solution)/shard_map/close/pallas_call | solution.py:578
  (54 shorter events, 0.1 us)
Async XLA Ops:
  0.6 15.8 %copy-start.14 = (f32[1536]{0:T(1024)S(1)}, f32[1536]{0:T(1024)}, u32[]{:S(2)}) copy-start(f32[1536]{0:T(1024)} %param.22) | copy-start | bytes 18436
  0.6 15.8 %copy-start.15 = (f32[1536]{0:T(1024)S(1)}, f32[1536]{0:T(1024)}, u32[]{:S(2)}) copy-start(f32[1536]{0:T(1024)} %param.31) | copy-start | bytes 18436
  0.7 15.8 %copy-start.16 = (f32[1536]{0:T(1024)S(1)}, f32[1536]{0:T(1024)}, u32[]{:S(2)}) copy-start(f32[1536]{0:T(1024)} %param.34) | copy-start | bytes 18436
  0.7 19.6 %copy-start.9 = (bf16[48,768]{1,0:T(8,128)(2,1)S(1)}, bf16[48,768]{1,0:T(8,128)(2,1)}, u32[]{:S(2)}) copy-start(bf16[48,768]{1,0:T(8,128)(2,1)} %param.21) | copy-start | bytes 221188
  0.7 16.4 %copy-start.8 = (bf16[1536,128]{1,0:T(8,128)(2,1)S(1)}, bf16[1536,128]{1,0:T(8,128)(2,1)}, u32[]{:S(2)}) copy-start(bf16[1536,128]{1,0:T(8,128)(2,1)} %param.25) | copy-start | bytes 1179652
  0.7 18.9 %copy-start.17 = (f32[24]{0:T(128)S(1)}, f32[24]{0:T(128)}, u32[]{:S(2)}) copy-start(f32[24]{0:T(128)} %param.29) | copy-start | bytes 292
  0.7 18.9 %copy-start.18 = (f32[24]{0:T(128)S(1)}, f32[24]{0:T(128)}, u32[]{:S(2)}) copy-start(f32[24]{0:T(128)} %param.28) | copy-start | bytes 292
  0.7 18.9 %copy-start.19 = (f32[24]{0:T(128)S(1)}, f32[24]{0:T(128)}, u32[]{:S(2)}) copy-start(f32[24]{0:T(128)} %param.27) | copy-start | bytes 292
  4.1 34.3 %collective-permute-start.5 = (bf16[1536,128]{1,0:T(8,128)(2,1)}, bf16[1536,128]{1,0:T(8,128)(2,1)S(1)}, u32[]{:S(2)}, u32[]{:S(2)}) collective-permute-start(bf16[1536,128]{1,0:T(8,128)(2,1)} %get-tuple-element.60), channel_id=1, source_target_pairs={{6,22},{14,30},{22,6},{30,14},{7,23},{15,31},{23,7},{31,15}} | collective-permute-start | bytes 1179656 | tf_op jit(solution)/shard_map/ppermute | solution.py:597
  4.8 33.6 %collective-permute-start.2 = (bf16[1536,128]{1,0:T(8,128)(2,1)}, bf16[1536,128]{1,0:T(8,128)(2,1)S(1)}, u32[]{:S(2)}, u32[]{:S(2)}) collective-permute-start(bf16[1536,128]{1,0:T(8,128)(2,1)} %get-tuple-element.60), channel_id=1, source_target_pairs={{0,10},{2,12},{4,14},{8,18},{10,20},{12,22},{16,26},{18,28},{20,30... | collective-permute-start | bytes 1179656 | tf_op jit(solution)/shard_map/ppermute | solution.py:597
  10.7 71.3 %collective-permute-start = (bf16[1536,128]{1,0:T(8,128)(2,1)}, bf16[1536,128]{1,0:T(8,128)(2,1)S(1)}, u32[]{:S(2)}, u32[]{:S(2)}) collective-permute-start(bf16[1536,128]{1,0:T(8,128)(2,1)} %get-tuple-element.54), channel_id=1, source_target_pairs={{0,12},{2,14},{4,16},{6,18},{8,20},{10,22},{12,24},{14,26},{16,28}... | collective-permute-start | bytes 1179656 | tf_op jit(solution)/shard_map/ppermute | solution.py:597
  14.8 26.1 %collective-permute-start.4 = (bf16[1536,128]{1,0:T(8,128)(2,1)}, bf16[1536,128]{1,0:T(8,128)(2,1)S(1)}, u32[]{:S(2)}, u32[]{:S(2)}) collective-permute-start(bf16[1536,128]{1,0:T(8,128)(2,1)} %get-tuple-element.63), channel_id=1, source_target_pairs={{0,8},{2,10},{4,12},{6,14},{8,16},{10,18},{12,20},{14,22},{16,24},... | collective-permute-start | bytes 1179656 | tf_op jit(solution)/shard_map/ppermute | solution.py:597
  16.4 75.6 %collective-permute-start.7 = (bf16[1536,128]{1,0:T(8,128)(2,1)}, bf16[1536,128]{1,0:T(8,128)(2,1)S(1)}, u32[]{:S(2)}, u32[]{:S(2)}) collective-permute-start(bf16[1536,128]{1,0:T(8,128)(2,1)} %get-tuple-element.71), channel_id=1, source_target_pairs={{0,14},{2,16},{4,18},{6,20},{8,22},{10,24},{12,26},{14,28},{16,30}... | collective-permute-start | bytes 1179656 | tf_op jit(solution)/shard_map/ppermute | solution.py:597
  34.3 45.6 %copy-start.13 = (f32[48,896]{1,0:T(8,128)S(1)}, f32[48,896]{1,0:T(8,128)}, u32[]{:S(2)}) copy-start(f32[48,896]{1,0:T(8,128)} %get-tuple-element.53) | copy-start | bytes 516100
  38.4 82.9 %copy-start.3 = (bf16[1536,128]{1,0:T(8,128)(2,1)}, bf16[1536,128]{1,0:T(8,128)(2,1)S(1)}, u32[]{:S(2)}) copy-start(bf16[1536,128]{1,0:T(8,128)(2,1)S(1)} %collective-permute-done.2.refs_1_) | copy-start | bytes 1179652
  38.4 2.5 %copy-start.20 = (bf16[1536,128]{1,0:T(8,128)(2,1)}, bf16[1536,128]{1,0:T(8,128)(2,1)S(1)}, u32[]{:S(2)}) copy-start(bf16[1536,128]{1,0:T(8,128)(2,1)S(1)} %collective-permute-done.5) | copy-start | bytes 1179652
  40.9 80.4 %copy-start.5 = (bf16[1536,128]{1,0:T(8,128)(2,1)}, bf16[1536,128]{1,0:T(8,128)(2,1)S(1)}, u32[]{:S(2)}) copy-start(bf16[1536,128]{1,0:T(8,128)(2,1)S(1)} %collective-permute-done.4.refs_0_) | copy-start | bytes 1179652
  40.9 51.3 %collective-permute-start.6 = (bf16[1648,128]{1,0:T(8,128)(2,1)}, bf16[1648,128]{1,0:T(8,128)(2,1)S(1)}, u32[]{:S(2)}, u32[]{:S(2)}) collective-permute-start(bf16[1648,128]{1,0:T(8,128)(2,1)} %get-tuple-element.66), channel_id=1, source_target_pairs={{0,6},{2,8},{4,10},{6,12},{8,14},{10,16},{12,18},{14,20},{16,22},{... | collective-permute-start | bytes 1265672 | tf_op jit(solution)/shard_map/ppermute | solution.py:597
  80.0 33.8 %collective-permute-start.3 = (bf16[1648,128]{1,0:T(8,128)(2,1)}, bf16[1648,128]{1,0:T(8,128)(2,1)S(1)}, u32[]{:S(2)}, u32[]{:S(2)}) collective-permute-start(bf16[1648,128]{1,0:T(8,128)(2,1)} %get-tuple-element.62), channel_id=1, source_target_pairs={{0,4},{2,6},{4,8},{6,10},{8,12},{10,14},{12,16},{14,18},{16,20},{1... | collective-permute-start | bytes 1265672 | tf_op jit(solution)/shard_map/ppermute | solution.py:597
  82.0 39.3 %copy-start.4 = (bf16[1536,128]{1,0:T(8,128)(2,1)}, bf16[1536,128]{1,0:T(8,128)(2,1)S(1)}, u32[]{:S(2)}) copy-start(bf16[1536,128]{1,0:T(8,128)(2,1)S(1)} %collective-permute-done.refs_2_) | copy-start | bytes 1179652
  82.0 39.9 %collective-permute-start.12 = (bf16[1536,128]{1,0:T(8,128)(2,1)}, bf16[1536,128]{1,0:T(8,128)(2,1)S(1)}, u32[]{:S(2)}, u32[]{:S(2)}) collective-permute-start(bf16[1536,128]{1,0:T(8,128)(2,1)} %copy-done.20), channel_id=1, source_target_pairs={{6,0},{14,8},{22,16},{30,24},{7,1},{15,9},{23,17},{31,25}} | collective-permute-start | bytes 1179656 | tf_op jit(solution)/shard_map/ppermute | solution.py:597
  83.3 44.0 %collective-permute-start.1 = (bf16[1648,128]{1,0:T(8,128)(2,1)}, bf16[1648,128]{1,0:T(8,128)(2,1)S(1)}, u32[]{:S(2)}, u32[]{:S(2)}) collective-permute-start(bf16[1648,128]{1,0:T(8,128)(2,1)} %get-tuple-element.59), channel_id=1, source_target_pairs={{0,2},{2,4},{4,6},{6,8},{8,10},{10,12},{12,14},{14,16},{16,18},{18... | collective-permute-start | bytes 1265672 | tf_op jit(solution)/shard_map/ppermute | solution.py:597
  92.1 29.9 %copy-start.6 = (bf16[1536,128]{1,0:T(8,128)(2,1)}, bf16[1536,128]{1,0:T(8,128)(2,1)S(1)}, u32[]{:S(2)}) copy-start(bf16[1536,128]{1,0:T(8,128)(2,1)S(1)} %collective-permute-done.7.refs_3_) | copy-start | bytes 1179652
  92.1 21.6 %collective-permute-start.11 = (bf16[16,1664]{1,0:T(8,128)(2,1)}, bf16[16,1664]{1,0:T(8,128)(2,1)S(1)}, u32[]{:S(2)}, u32[]{:S(2)}) collective-permute-start(bf16[16,1664]{1,0:T(8,128)(2,1)} %get-tuple-element.84), channel_id=1, source_target_pairs={{0,14},{2,16},{4,18},{6,20},{8,22},{10,24},{12,26},{14,28},{16,30}... | collective-permute-start | bytes 159752 | tf_op jit(solution)/shard_map/ppermute | solution.py:597
  92.3 19.5 %copy-start = (bf16[1648,128]{1,0:T(8,128)(2,1)}, bf16[1648,128]{1,0:T(8,128)(2,1)S(1)}, u32[]{:S(2)}) copy-start(bf16[1648,128]{1,0:T(8,128)(2,1)S(1)} %collective-permute-done.6.message.refs_2_) | copy-start | bytes 1265668
  92.3 29.1 %collective-permute-start.8 = (bf16[16,1664]{1,0:T(8,128)(2,1)}, bf16[16,1664]{1,0:T(8,128)(2,1)}, u32[]{:S(2)}, u32[]{:S(2)}) collective-permute-start(bf16[16,1664]{1,0:T(8,128)(2,1)} %get-tuple-element.81), channel_id=1, source_target_pairs={{0,8},{2,10},{4,12},{6,14},{8,16},{10,18},{12,20},{14,22},{16,24},... | collective-permute-start | bytes 159752 | tf_op jit(solution)/shard_map/ppermute | solution.py:597
  113.7 7.7 %copy-start.10 = (bf16[16,1664]{1,0:T(8,128)(2,1)}, bf16[16,1664]{1,0:T(8,128)(2,1)S(1)}, u32[]{:S(2)}) copy-start(bf16[16,1664]{1,0:T(8,128)(2,1)S(1)} %collective-permute-done.11.refs_9_.refs_7_) | copy-start | bytes 159748
  113.7 8.2 %collective-permute-start.9 = (bf16[16,1664]{1,0:T(8,128)(2,1)}, bf16[16,1664]{1,0:T(8,128)(2,1)S(1)}, u32[]{:S(2)}, u32[]{:S(2)}) collective-permute-start(bf16[16,1664]{1,0:T(8,128)(2,1)} %get-tuple-element.82), channel_id=1, source_target_pairs={{0,10},{2,12},{4,14},{6,16},{8,18},{10,20},{12,22},{14,24},{16,26}... | collective-permute-start | bytes 159752 | tf_op jit(solution)/shard_map/ppermute | solution.py:597
  113.8 5.7 %copy-start.1 = (bf16[1648,128]{1,0:T(8,128)(2,1)}, bf16[1648,128]{1,0:T(8,128)(2,1)S(1)}, u32[]{:S(2)}) copy-start(bf16[1648,128]{1,0:T(8,128)(2,1)S(1)} %collective-permute-done.3.message.refs_1_) | copy-start | bytes 1265668
  113.8 8.2 %collective-permute-start.10 = (bf16[16,1664]{1,0:T(8,128)(2,1)}, bf16[16,1664]{1,0:T(8,128)(2,1)S(1)}, u32[]{:S(2)}, u32[]{:S(2)}) collective-permute-start(bf16[16,1664]{1,0:T(8,128)(2,1)} %get-tuple-element.83), channel_id=1, source_target_pairs={{0,12},{2,14},{4,16},{6,18},{8,20},{10,22},{12,24},{14,26},{16,28}... | collective-permute-start | bytes 159752 | tf_op jit(solution)/shard_map/ppermute | solution.py:597
  122.0 0.8 copy-start.7
  127.3 0.8 copy-start.2
  (2 other events, 1.2 us)

commit v5 on v4

--- a/solution.py
+++ b/solution.py
@@ -15,11 +15,10 @@
 DINNER = 3072
 TILE = 256
 EXTRA = NSTATE
-PLANE = 4
-RAW = (4, 5, 6, 7)
+RAW = (7,)
 PARTS = 3
 SMALL = pl.CostEstimate(flops=1024, bytes_accessed=1024, transcendentals=0)
-STEP = pl.CostEstimate(flops=1024, bytes_accessed=40_000_000, transcendentals=0)
+STEP = pl.CostEstimate(flops=1024, bytes_accessed=8_000_000, transcendentals=0)
 
 epsilon = 1e-05
 HIGH = lax.Precision.HIGHEST
@@ -378,10 +377,6 @@
     return pairs, pairs * 2 * DRAFT
 
 
-def column():
-    return lax.rem(lax.axis_index("req"), PLANE)
-
-
 def finish_kernel(offsets, *refs):
     n = len(offsets)
     table, states = refs[:2]
@@ -438,9 +433,8 @@
 def merge_kernel(table, states, *refs):
     n = 1 + len(RAW)
     raws = refs[: n - 1]
-    turned = refs[n - 1]
-    corr = refs[n : 2 * n]
-    _, kept, loaded, merged, sem_in, sem_out = refs[2 * n :]
+    corr = refs[n - 1 : 2 * n - 1]
+    _, kept, loaded, merged, sem_in, sem_out = refs[2 * n - 1 :]
     width = loaded.shape[0]
     own = pltpu.make_async_copy(states.at[table[3, 0]], loaded, sem_in)
     own.start()
@@ -455,20 +449,7 @@
 
         @pl.when(slots[i] >= 0)
         def _(i=i):
-            if i == 0:
-                advance(corr[i], loaded, merged.at[i])
-            elif RAW[i - 1] == 5:
-
-                @pl.when(column() == 0)
-                def _():
-                    advance(corr[i], turned, merged.at[i])
-
-                @pl.when(column() != 0)
-                def _():
-                    advance(corr[i], raws[i - 1], merged.at[i])
-
-            else:
-                advance(corr[i], raws[i - 1], merged.at[i])
+            advance(corr[i], raws[i - 1] if i > 0 else loaded, merged.at[i])
             put(i).start()
 
     for i in range(n):
@@ -478,12 +459,12 @@
             put(i).wait()
 
 
-def merge(count, table, states, raws, turned, corr, kept):
+def merge(count, table, states, raws, corr, kept):
     width = states.shape[1]
     n = 1 + len(RAW)
     return pl.pallas_call(
         merge_kernel,
-        in_specs=[in_smem(), in_hbm()] + [in_vmem()] * (2 * n) + [in_hbm()],
+        in_specs=[in_smem(), in_hbm()] + [in_vmem()] * (2 * n - 1) + [in_hbm()],
         out_specs=in_hbm(),
         out_shape=jax.ShapeDtypeStruct((count, width, NSTATE), BF16),
         scratch_shapes=[
@@ -492,10 +473,10 @@
             pltpu.SemaphoreType.DMA,
             pltpu.SemaphoreType.DMA((n,)),
         ],
-        input_output_aliases={2 + 2 * n: 0},
-        cost_estimate=STEP,
+        input_output_aliases={1 + 2 * n: 0},
+        cost_estimate=SMALL,
         name="merge",
-    )(table, states, *raws, turned, *corr, kept)
+    )(table, states, *raws, *corr, kept)
 
 
 def halves(ref, width):
@@ -591,10 +572,9 @@
     )(*messages, *corr, kept)
 
 
-def moved(array, by, columns=tuple(range(PLANE))):
+def moved(array, by):
     length = lax.axis_size("req")
-    pairs = [(i, (i + by) % length) for i in range(length) if i % PLANE in columns]
-    return lax.ppermute(array, "req", pairs)
+    return lax.ppermute(array, "req", [(i, (i + by) % length) for i in range(length)])
 
 
 def local(
@@ -625,10 +605,7 @@
     peers = lax.axis_size("req")
     flat = states_in.reshape(count, width, NSTATE)
     *raws, table = pick(count, width, peers, destination, flat)
-    raw5_z = moved(raws[1], 8, (3,))
-    raws = [
-        moved(raw, k, (0, 1, 2) if k == 5 else (0, 1, 2, 3)) for raw, k in zip(raws, RAW)
-    ]
+    raws = [moved(raw, k) for raw, k in zip(raws, RAW)]
     table, ready, ready_ssm = lax.optimization_barrier((table, hidden_in, proj_ssm))
     vectors = jnp.stack([norm_gain, conv_inner_bias, gate_gain])
     results = front(
@@ -659,7 +636,16 @@
     )
     mine, theirs = results[:2]
     corr = list(results[2:])
-    first, second, third = finish((1, 2, 3), table, flat, corr)
+    sixth, fifth, fourth, third = finish((6, 5, 4, 3), table, flat, corr)
+    raw7, corr[7], sixth, fifth, fourth, third, later = lax.optimization_barrier(
+        (raws[0], corr[7], sixth, fifth, fourth, third, table)
+    )
+    sixth = moved(sixth, 6)
+    fifth = moved(fifth, 5)
+    fourth = moved(fourth, 4)
+    third = moved(third, 3)
+    corr[7] = moved(corr[7], 7)
+    second, first = finish((2, 1), later, flat, corr)
 
     pair = lax.all_gather(theirs, "head", axis=0, tiled=False)
     other = jnp.where(lax.axis_index("head") == 0, pair[1], pair[0])
@@ -668,26 +654,22 @@
     scale = lax.rsqrt(total[:, half : half + 1] / DINNER + epsilon)
     hidden_out = (hidden_in.astype(F32) + total[:, :half] * scale).astype(BF16)
 
-    raw4, raw5, raw6, raw7 = raws
-    raw5_z, third = lax.optimization_barrier((raw5_z, third))
-    turned = moved(raw5_z, -3, (3,))
-    raw4, third = lax.optimization_barrier((raw4, third))
-    third = moved(third, 3)
-    raw5, second = lax.optimization_barrier((raw5, second))
+    sixth, fourth, corr[7], second = lax.optimization_barrier(
+        (sixth, fourth, corr[7], second)
+    )
     second = moved(second, 2)
-    raw6, first = lax.optimization_barrier((raw6, first))
+    fifth, third, first = lax.optimization_barrier((fifth, third, first))
     first = moved(first, 1)
-    raw7, *late = lax.optimization_barrier((raw7, *corr[4:]))
-    corr[7] = moved(late[3], 7)
-    raw4, raw5, raw6, raw7, raw5_z, *late = lax.optimization_barrier(
-        (raw4, raw5, raw6, raw7, raw5_z, *late[:3])
-    )
-    corr[4:7] = [moved(array, k) for array, k in zip(late, (4, 5, 6))]
-    sent = [corr[0], *corr[4:]]
-    kept = place(count, width, third)
+    sent = [corr[0], corr[7]]
+    kept = place(count, width, sixth)
+    kept = place(count, width, fourth, kept)
+    kept = merge(count, table, flat, [raw7], sent, kept)
+    kept = place(count, width, fifth, kept)
+    kept = place(count, width, third, kept)
     kept = place(count, width, second, kept)
-    kept = merge(count, table, flat, (raw4, raw5, raw6, raw7), turned, sent, kept)
-    kept, kept_inner, kept_ssm = close(count, width, (first, second, third), sent, kept)
+    kept, kept_inner, kept_ssm = close(
+        count, width, (first, second, third, fourth, fifth, sixth), sent, kept
+    )
     return (hidden_out, kept.reshape(states_in.shape), kept_inner, kept_ssm)
 
 

time: 133 us -> 125 us (0.940)
  starting transfers between devices: 84.9 us -> 21.4 us
  waiting for transfers between devices: 3.09 us -> 52.8 us
  Pallas kernels: 30.7 us -> 37.7 us
    ppermute x13 -> x8, starting transfers between devices: 84.9 us -> 21.4 us  [moved(): lax.ppermute(array, 'req', [(i, (i + by) % length) for i in range(length)])]
    ppermute x13 -> x8, waiting for transfers between devices: 3.09 us -> 52.8 us  [moved(): lax.ppermute(array, 'req', [(i, (i + by) % length) for i in range(length)])]
    pallas_call x2 -> x5, Pallas kernels: 3.76 us -> 8.66 us  [place(): pl.pallas_call(functools.partial(place_kernel, width), in_specs=[in_vmem(...]
    pallas_call x1 -> x2, Pallas kernels: 4.02 us -> 8.09 us  [finish(): pl.pallas_call(functools.partial(finish_kernel, offsets), in_specs=[in_sm...]
  transfers between devices with their start and end apart: 13 -> 8, of which waited for: 2 -> 4; matrix products, arithmetic and copies ran while one was open for 2% -> 2% of each run, Pallas kernels for 19% -> 26%
where the time goes in v5:
time: 125 us; the launch traced here: 124 us
  waiting for transfers between devices  52.8 us (42%)
  Pallas kernels  37.7 us (30%)
  starting transfers between devices  21.4 us (17%)
  blocking collectives  6.57 us (5%)
  other arithmetic  3.03 us (2%)
  local copies, waits for them, and re-layouts  1.59 us (1%)
    ppermute x8, waiting for transfers between devices, moved(): lax.ppermute(array, 'req', [(i, (i + by) % length) for i in range(length)])  52.8 us
    ppermute x8, starting transfers between devices, moved(): lax.ppermute(array, 'req', [(i, (i + by) % length) for i in range(length)])  21.4 us
    pallas_call x1, Pallas kernels, front(): pl.pallas_call(functools.partial(front_kernel, count, heads), grid=(tiles...  12.1 us
    pallas_call x5, Pallas kernels, place(): pl.pallas_call(functools.partial(place_kernel, width), in_specs=[in_vmem(...  8.66 us
    pallas_call x2, Pallas kernels, finish(): pl.pallas_call(functools.partial(finish_kernel, offsets), in_specs=[in_sm...  8.09 us
    pallas_call x1, Pallas kernels, merge(): pl.pallas_call(merge_kernel, in_specs=[in_smem(), in_hbm()] + [in_vmem()]...  3.64 us
    pallas_call x1, Pallas kernels, pick(): pl.pallas_call(functools.partial(pick_kernel, count, peers), in_specs=[in...  2.65 us
    pallas_call x1, Pallas kernels, close(): pl.pallas_call(functools.partial(close_kernel, n), in_specs=[in_vmem()] *...  2.63 us
  transfers between devices with their start and end apart: 8, of which 4 were waited for; matrix products, arithmetic and copies ran while one was open for 2% of the time, Pallas kernels for 26%

profile of v5, /device:TPU:0, one launch (start us, length us, event | category | flops | bytes accessed | tf_op | source)
XLA Modules:
  0.0 124.0 jit_solution(1499120384213252496)
XLA Ops:
  0.7 2.6 %pick.1 = (bf16[1536,128]{1,0:T(8,128)(2,1)}, s32[4,8]{1,0:T(4,128)}) custom-call(s32[6]{0:T(128)} %destination.1, bf16[6,1536,128]{2,1,0:T(8,128)(2,1)} %bitcast.10), custom_call_target="tpu_custom_call" | custom-call | flops 1024 | bytes 1024 | tf_op jit(solution)/shard_map/pick/pallas_call | solution.py:348
  3.4 5.0 %collective-permute-start = (bf16[1536,128]{1,0:T(8,128)(2,1)}, bf16[1536,128]{1,0:T(8,128)(2,1)S(1)}, u32[]{:S(2)}, u32[]{:S(2)}) collective-permute-start(bf16[1536,128]{1,0:T(8,128)(2,1)} %get-tuple-element.48), channel_id=1, source_target_pairs={{0,14},{2,16},{4,18},{6,20},{8,22},{10,24},{12,26},{14,28},{16,30}... | collective-permute-start | bytes 1179656 | tf_op jit(solution)/shard_map/ppermute | solution.py:577
  8.4 2.0 %all-gather = bf16[96,768]{1,0:T(8,128)(2,1)} all-gather(bf16[48,768]{1,0:T(8,128)(2,1)S(1)} %copy-done.8), channel_id=2, replica_groups=mesh['req'=16,'head'=2] {'head'}, dimensions={0}, use_global_device_ids=true | all-gather | bytes 221184 | tf_op jit(solution)/shard_map/all_gather | solution.py:620
  10.5 0.6 pad_maximum_fusion.1.head_rows
  11.1 2.5 %all-gather.1 = bf16[3072,128]{1,0:T(8,128)(2,1)} all-gather(bf16[1536,128]{1,0:T(8,128)(2,1)S(1)} %copy-done.7), channel_id=3, replica_groups=mesh['req'=16,'head'=2] {'head'}, dimensions={0}, use_global_device_ids=true | all-gather | bytes 1179648 | tf_op jit(solution)/shard_map/all_gather | solution.py:625
  13.5 0.6 pad_maximum_fusion.vectors.vector_tile
  14.2 12.1 %front.1 = (f32[48,896]{1,0:T(8,128)}, f32[48,896]{1,0:T(8,128)}, bf16[16,1664]{1,0:T(8,128)(2,1)}, bf16[16,1664]{1,0:T(8,128)(2,1)}, bf16[16,1664]{1,0:T(8,128)...) custom-call(s32[4,8]{1,0:T(4,128)} %get-tuple-element.60.table.refs_, ...), custom_call_target="tpu_custom_call" | custom-call | flops 1024 | bytes 1024 | tf_op jit(solution)/shard_map/front/pallas_call | solution.py:288
  26.3 4.6 %finish.2 = (bf16[1648,128]{1,0:T(8,128)(2,1)}, bf16[1648,128]{1,0:T(8,128)(2,1)}, bf16[1648,128]{1,0:T(8,128)(2,1)}, bf16[1648,128]{1,0:T(8,128)(2,1)}) custom-call(s32[4,8]{1,0:T(4,128)} %get-tuple-element.60.table.refs_0_, bf16[6,1536,128]{2,1,0:T(8,128)(2,1)} %bitcast.12, bf16[16,1664]{1,0:T(8,128)(2,1)} %get-tuple-element.50.refs_2_, ...), custom_call_target="tpu_custom_call" | custom-call | flops 1024 | bytes 1024 | tf_op jit(solution)/shard_map/finish/pallas_call | solution.py:415
  30.8 1.7 %collective-permute-start.1 = (bf16[1648,128]{1,0:T(8,128)(2,1)}, bf16[1648,128]{1,0:T(8,128)(2,1)S(1)}, u32[]{:S(2)}, u32[]{:S(2)}) collective-permute-start(bf16[1648,128]{1,0:T(8,128)(2,1)} %get-tuple-element.58), channel_id=1, source_target_pairs={{0,10},{2,12},{4,14},{6,16},{8,18},{10,20},{12,22},{14,24},{16,26}... | collective-permute-start | bytes 1265672 | tf_op jit(solution)/shard_map/ppermute | solution.py:577
  32.5 3.4 %collective-permute-start.2 = (bf16[1648,128]{1,0:T(8,128)(2,1)}, bf16[1648,128]{1,0:T(8,128)(2,1)S(1)}, u32[]{:S(2)}, u32[]{:S(2)}) collective-permute-start(bf16[1648,128]{1,0:T(8,128)(2,1)} %get-tuple-element.59), channel_id=1, source_target_pairs={{0,6},{2,8},{4,10},{6,12},{8,14},{10,16},{12,18},{14,20},{16,22},{... | collective-permute-start | bytes 1265672 | tf_op jit(solution)/shard_map/ppermute | solution.py:577
  35.9 0.3 collective-permute-start.4
  36.1 2.5 %collective-permute-start.5 = (bf16[1648,128]{1,0:T(8,128)(2,1)}, bf16[1648,128]{1,0:T(8,128)(2,1)S(1)}, u32[]{:S(2)}, u32[]{:S(2)}) collective-permute-start(bf16[1648,128]{1,0:T(8,128)(2,1)} %get-tuple-element.66), channel_id=1, source_target_pairs={{0,8},{2,10},{4,12},{6,14},{8,16},{10,18},{12,20},{14,22},{16,24},... | collective-permute-start | bytes 1265672 | tf_op jit(solution)/shard_map/ppermute | solution.py:577
  38.6 0.1 collective-permute-start.6
  38.7 2.0 %all-gather.2 = f32[96,896]{1,0:T(8,128)S(1)} all-gather(f32[48,896]{1,0:T(8,128)S(1)} %copy-done.10), channel_id=4, replica_groups=mesh['req'=16,'head'=2] {'head'}, dimensions={0}, use_global_device_ids=true | all-gather | bytes 516096 | tf_op jit(solution)/shard_map/all_gather | solution.py:650
  40.8 3.5 %finish.3 = (bf16[1648,128]{1,0:T(8,128)(2,1)}, bf16[1648,128]{1,0:T(8,128)(2,1)}) custom-call(s32[4,8]{1,0:T(4,128)} %get-tuple-element.60.table.refs_0_, bf16[6,1536,128]{2,1,0:T(8,128)(2,1)} %bitcast.13, bf16[16,1664]{1,0:T(8,128)(2,1)} %get-tuple-element.61.refs_2_, bf16[16,1664]{1,0:T(8,128)(2,1)} %get-tuple-element.62.refs_3_), custom_call_target="tpu_custom_call" | custom-call | flops 1024 | bytes 1024 | tf_op jit(solution)/shard_map/finish/pallas_call | solution.py:415
  44.3 45.9 %collective-permute-done.1.message.refs_4_ = bf16[1648,128]{1,0:T(8,128)(2,1)S(1)} collective-permute-done((bf16[1648,128]{1,0:T(8,128)(2,1)}, bf16[1648,128]{1,0:T(8,128)(2,1)S(1)}, u32[]{:S(2)}, u32[]{:S(2)}) %collective-permute-start.1) | collective-permute-done | bytes 421920 | tf_op jit(solution)/shard_map/ppermute | solution.py:577
  90.2 0.7 collective-permute-done.4.message.refs_5_
  90.9 8.5 %collective-permute-start.7 = (bf16[1648,128]{1,0:T(8,128)(2,1)}, bf16[1648,128]{1,0:T(8,128)(2,1)S(1)}, u32[]{:S(2)}, u32[]{:S(2)}) collective-permute-start(bf16[1648,128]{1,0:T(8,128)(2,1)} %get-tuple-element.69), channel_id=1, source_target_pairs={{0,4},{2,6},{4,8},{6,10},{8,12},{10,14},{12,16},{14,18},{16,20},{1... | collective-permute-start | bytes 1265672 | tf_op jit(solution)/shard_map/ppermute | solution.py:577
  99.5 1.0 fusion
  100.4 0.1 fusion.5
  100.6 0.7 fusion.2
  101.3 1.9 %place.5.refs_0_ = bf16[6,1536,128]{2,1,0:T(8,128)(2,1)} custom-call(bf16[1648,128]{1,0:T(8,128)(2,1)} %copy-done), custom_call_target="tpu_custom_call" | custom-call | flops 1024 | bytes 8000000 | tf_op jit(solution)/shard_map/place/pallas_call | solution.py:502
  103.2 1.1 place.6.refs_3_
  104.4 3.6 %merge.1.refs_0_ = bf16[6,1536,128]{2,1,0:T(8,128)(2,1)} custom-call(s32[4,8]{1,0:T(4,128)} %get-tuple-element.60.table.refs_0_, bf16[6,1536,128]{2,1,0:T(8,128)(2,1)} %bitcast.14, bf16[1536,128]{1,0:T(8,128)(2,1)} %copy-done.6, bf16[16,1664]{1,0:T(8,128)(2,1)} %get-tuple-element.74.refs_1_.refs_6_, ...), custom_call_target="tpu_custom_call", output_to_operand_aliasing={{}: (5, {})} | custom-call | flops 1024 | bytes 1024 | tf_op jit(solution)/shard_map/merge/pallas_call | solution.py:465
  108.0 1.9 %place.7.refs_0_ = bf16[6,1536,128]{2,1,0:T(8,128)(2,1)} custom-call(bf16[1648,128]{1,0:T(8,128)(2,1)} %copy-done.1, bf16[6,1536,128]{2,1,0:T(8,128)(2,1)} %merge.1.refs_0_), custom_call_target="tpu_custom_call", output_to_operand_aliasing={{}: (1, {})} | custom-call | flops 1024 | bytes 8000000 | tf_op jit(solution)/shard_map/place/pallas_call | solution.py:502
  109.9 1.9 %place.8.refs_0_ = bf16[6,1536,128]{2,1,0:T(8,128)(2,1)} custom-call(bf16[1648,128]{1,0:T(8,128)(2,1)} %copy-done.2, bf16[6,1536,128]{2,1,0:T(8,128)(2,1)} %place.7.refs_0_), custom_call_target="tpu_custom_call", output_to_operand_aliasing={{}: (1, {})} | custom-call | flops 1024 | bytes 8000000 | tf_op jit(solution)/shard_map/place/pallas_call | solution.py:502
  111.8 5.3 %collective-permute-done.7.message.refs_1_ = bf16[1648,128]{1,0:T(8,128)(2,1)S(1)} collective-permute-done((bf16[1648,128]{1,0:T(8,128)(2,1)}, bf16[1648,128]{1,0:T(8,128)(2,1)S(1)}, u32[]{:S(2)}, u32[]{:S(2)}) %collective-permute-start.7) | collective-permute-done | bytes 421920 | tf_op jit(solution)/shard_map/ppermute | solution.py:577
  117.1 0.8 copy-done.4
  117.8 1.9 %place.9.refs_8_ = bf16[6,1536,128]{2,1,0:T(8,128)(2,1)} custom-call(bf16[1648,128]{1,0:T(8,128)(2,1)} %copy-done.4, bf16[6,1536,128]{2,1,0:T(8,128)(2,1)} %place.8.refs_0_), custom_call_target="tpu_custom_call", output_to_operand_aliasing={{}: (1, {})} | custom-call | flops 1024 | bytes 8000000 | tf_op jit(solution)/shard_map/place/pallas_call | solution.py:502
  119.7 0.9 collective-permute-done.3.refs_0_
  120.6 0.7 copy-done.5
  121.4 2.6 %close.1 = (bf16[6,1536,128]{2,1,0:T(8,128)(2,1)}, bf16[6,3,1536]{2,1,0:T(4,128)(2,1)}, bf16[6,3,256]{2,1,0:T(4,128)(2,1)}) custom-call(bf16[1648,128]{1,0:T(8,128)(2,1)} %copy-done.5, bf16[1648,128]{1,0:T(8,128)(2,1)} %copy-done.4, bf16[1648,128]{1,0:T(8,128)(2,1)} %copy-done.2, bf16[1648,128]{1,0:T(8,128)(2,1)} %copy-done.3, ...), custom_call_target="tpu_custom_call", output_to_operand_aliasing={{0}: (8, {})} | custom-call | flops 1024 | bytes 1024 | tf_op jit(solution)/shard_map/close/pallas_call | solution.py:559
  (42 shorter events, 0.1 us)
Async XLA Ops:
  0.6 7.7 %copy-start.11 = (f32[1536]{0:T(1024)S(1)}, f32[1536]{0:T(1024)}, u32[]{:S(2)}) copy-start(f32[1536]{0:T(1024)} %param.22) | copy-start | bytes 18436
  0.6 7.7 %copy-start.12 = (f32[1536]{0:T(1024)S(1)}, f32[1536]{0:T(1024)}, u32[]{:S(2)}) copy-start(f32[1536]{0:T(1024)} %param.31) | copy-start | bytes 18436
  0.7 7.7 %copy-start.13 = (f32[1536]{0:T(1024)S(1)}, f32[1536]{0:T(1024)}, u32[]{:S(2)}) copy-start(f32[1536]{0:T(1024)} %param.34) | copy-start | bytes 18436
  0.7 7.7 %copy-start.8 = (bf16[48,768]{1,0:T(8,128)(2,1)S(1)}, bf16[48,768]{1,0:T(8,128)(2,1)}, u32[]{:S(2)}) copy-start(bf16[48,768]{1,0:T(8,128)(2,1)} %param.21) | copy-start | bytes 221188
  0.7 10.4 %copy-start.7 = (bf16[1536,128]{1,0:T(8,128)(2,1)S(1)}, bf16[1536,128]{1,0:T(8,128)(2,1)}, u32[]{:S(2)}) copy-start(bf16[1536,128]{1,0:T(8,128)(2,1)} %param.25) | copy-start | bytes 1179652
  0.7 9.8 %copy-start.14 = (f32[24]{0:T(128)S(1)}, f32[24]{0:T(128)}, u32[]{:S(2)}) copy-start(f32[24]{0:T(128)} %param.29) | copy-start | bytes 292
  0.7 9.8 %copy-start.15 = (f32[24]{0:T(128)S(1)}, f32[24]{0:T(128)}, u32[]{:S(2)}) copy-start(f32[24]{0:T(128)} %param.28) | copy-start | bytes 292
  0.7 9.7 %copy-start.16 = (f32[24]{0:T(128)S(1)}, f32[24]{0:T(128)}, u32[]{:S(2)}) copy-start(f32[24]{0:T(128)} %param.27) | copy-start | bytes 292
  3.4 27.5 %collective-permute-start = (bf16[1536,128]{1,0:T(8,128)(2,1)}, bf16[1536,128]{1,0:T(8,128)(2,1)S(1)}, u32[]{:S(2)}, u32[]{:S(2)}) collective-permute-start(bf16[1536,128]{1,0:T(8,128)(2,1)} %get-tuple-element.48), channel_id=1, source_target_pairs={{0,14},{2,16},{4,18},{6,20},{8,22},{10,24},{12,26},{14,28},{16,30}... | collective-permute-start | bytes 1179656 | tf_op jit(solution)/shard_map/ppermute | solution.py:577
  26.2 12.4 %copy-start.17 = (bf16[16,1664]{1,0:T(8,128)(2,1)S(1)}, bf16[16,1664]{1,0:T(8,128)(2,1)}, u32[]{:S(2)}) copy-start(bf16[16,1664]{1,0:T(8,128)(2,1)} %get-tuple-element.67) | copy-start | bytes 159748
  26.2 12.5 %copy-start.10 = (f32[48,896]{1,0:T(8,128)S(1)}, f32[48,896]{1,0:T(8,128)}, u32[]{:S(2)}) copy-start(f32[48,896]{1,0:T(8,128)} %get-tuple-element.47) | copy-start | bytes 516100
  30.8 72.3 %copy-start.6 = (bf16[1536,128]{1,0:T(8,128)(2,1)}, bf16[1536,128]{1,0:T(8,128)(2,1)S(1)}, u32[]{:S(2)}) copy-start(bf16[1536,128]{1,0:T(8,128)(2,1)S(1)} %collective-permute-done.refs_0_) | copy-start | bytes 1179652
  30.8 59.3 %collective-permute-start.1 = (bf16[1648,128]{1,0:T(8,128)(2,1)}, bf16[1648,128]{1,0:T(8,128)(2,1)S(1)}, u32[]{:S(2)}, u32[]{:S(2)}) collective-permute-start(bf16[1648,128]{1,0:T(8,128)(2,1)} %get-tuple-element.58), channel_id=1, source_target_pairs={{0,10},{2,12},{4,14},{6,16},{8,18},{10,20},{12,22},{14,24},{16,26}... | collective-permute-start | bytes 1265672 | tf_op jit(solution)/shard_map/ppermute | solution.py:577
  32.5 57.7 %collective-permute-start.2 = (bf16[1648,128]{1,0:T(8,128)(2,1)}, bf16[1648,128]{1,0:T(8,128)(2,1)S(1)}, u32[]{:S(2)}, u32[]{:S(2)}) collective-permute-start(bf16[1648,128]{1,0:T(8,128)(2,1)} %get-tuple-element.59), channel_id=1, source_target_pairs={{0,6},{2,8},{4,10},{6,12},{8,14},{10,16},{12,18},{14,20},{16,22},{... | collective-permute-start | bytes 1265672 | tf_op jit(solution)/shard_map/ppermute | solution.py:577
  35.9 55.1 %collective-permute-start.4 = (bf16[1648,128]{1,0:T(8,128)(2,1)}, bf16[1648,128]{1,0:T(8,128)(2,1)S(1)}, u32[]{:S(2)}, u32[]{:S(2)}) collective-permute-start(bf16[1648,128]{1,0:T(8,128)(2,1)} %get-tuple-element.65), channel_id=1, source_target_pairs={{0,12},{2,14},{4,16},{6,18},{8,20},{10,22},{12,24},{14,26},{16,28}... | collective-permute-start | bytes 1265672 | tf_op jit(solution)/shard_map/ppermute | solution.py:577
  36.1 54.8 %collective-permute-start.5 = (bf16[1648,128]{1,0:T(8,128)(2,1)}, bf16[1648,128]{1,0:T(8,128)(2,1)S(1)}, u32[]{:S(2)}, u32[]{:S(2)}) collective-permute-start(bf16[1648,128]{1,0:T(8,128)(2,1)} %get-tuple-element.66), channel_id=1, source_target_pairs={{0,8},{2,10},{4,12},{6,14},{8,16},{10,18},{12,20},{14,22},{16,24},... | collective-permute-start | bytes 1265672 | tf_op jit(solution)/shard_map/ppermute | solution.py:577
  38.6 51.6 %collective-permute-start.6 = (bf16[16,1664]{1,0:T(8,128)(2,1)S(1)}, bf16[16,1664]{1,0:T(8,128)(2,1)S(1)}, u32[]{:S(2)}, u32[]{:S(2)}) collective-permute-start(bf16[16,1664]{1,0:T(8,128)(2,1)S(1)} %copy-done.17), channel_id=1, source_target_pairs={{0,14},{2,16},{4,18},{6,20},{8,22},{10,24},{12,26},{14,28},{16,30}... | collective-permute-start | bytes 159752 | tf_op jit(solution)/shard_map/ppermute | solution.py:577
  90.2 14.2 %copy-start.1 = (bf16[1648,128]{1,0:T(8,128)(2,1)}, bf16[1648,128]{1,0:T(8,128)(2,1)S(1)}, u32[]{:S(2)}) copy-start(bf16[1648,128]{1,0:T(8,128)(2,1)S(1)} %collective-permute-done.1.message.refs_4_) | copy-start | bytes 1265668
  90.2 17.8 %copy-start.2 = (bf16[1648,128]{1,0:T(8,128)(2,1)}, bf16[1648,128]{1,0:T(8,128)(2,1)S(1)}, u32[]{:S(2)}) copy-start(bf16[1648,128]{1,0:T(8,128)(2,1)S(1)} %collective-permute-done.2.message.refs_2_) | copy-start | bytes 1265668
  90.2 14.2 %copy-start.9 = (bf16[16,1664]{1,0:T(8,128)(2,1)}, bf16[16,1664]{1,0:T(8,128)(2,1)S(1)}, u32[]{:S(2)}) copy-start(bf16[16,1664]{1,0:T(8,128)(2,1)S(1)} %collective-permute-done.6.refs_2_.refs_7_) | copy-start | bytes 159748
  90.9 10.3 %copy-start = (bf16[1648,128]{1,0:T(8,128)(2,1)}, bf16[1648,128]{1,0:T(8,128)(2,1)S(1)}, u32[]{:S(2)}) copy-start(bf16[1648,128]{1,0:T(8,128)(2,1)S(1)} %collective-permute-done.4.message.refs_5_) | copy-start | bytes 1265668
  90.9 12.2 %copy-start.3 = (bf16[1648,128]{1,0:T(8,128)(2,1)}, bf16[1648,128]{1,0:T(8,128)(2,1)S(1)}, u32[]{:S(2)}) copy-start(bf16[1648,128]{1,0:T(8,128)(2,1)S(1)} %collective-permute-done.5.message.refs_3_) | copy-start | bytes 1265668
  90.9 26.1 %collective-permute-start.7 = (bf16[1648,128]{1,0:T(8,128)(2,1)}, bf16[1648,128]{1,0:T(8,128)(2,1)S(1)}, u32[]{:S(2)}, u32[]{:S(2)}) collective-permute-start(bf16[1648,128]{1,0:T(8,128)(2,1)} %get-tuple-element.69), channel_id=1, source_target_pairs={{0,4},{2,6},{4,8},{6,10},{8,12},{10,14},{12,16},{14,18},{16,20},{1... | collective-permute-start | bytes 1265672 | tf_op jit(solution)/shard_map/ppermute | solution.py:577
  99.5 21.2 %collective-permute-start.3 = (bf16[1648,128]{1,0:T(8,128)(2,1)}, bf16[1648,128]{1,0:T(8,128)(2,1)S(1)}, u32[]{:S(2)}, u32[]{:S(2)}) collective-permute-start(bf16[1648,128]{1,0:T(8,128)(2,1)} %get-tuple-element.64), channel_id=1, source_target_pairs={{0,2},{2,4},{4,6},{6,8},{8,10},{10,12},{12,14},{14,16},{16,18},{18... | collective-permute-start | bytes 1265672 | tf_op jit(solution)/shard_map/ppermute | solution.py:577
  117.1 0.8 copy-start.4
  120.6 0.8 copy-start.5

commit v6 on v5

--- a/solution.py
+++ b/solution.py
@@ -15,7 +15,7 @@
 DINNER = 3072
 TILE = 256
 EXTRA = NSTATE
-RAW = (7,)
+RAW = (6, 7)
 PARTS = 3
 SMALL = pl.CostEstimate(flops=1024, bytes_accessed=1024, transcendentals=0)
 STEP = pl.CostEstimate(flops=1024, bytes_accessed=8_000_000, transcendentals=0)
@@ -636,16 +636,16 @@
     )
     mine, theirs = results[:2]
     corr = list(results[2:])
-    sixth, fifth, fourth, third = finish((6, 5, 4, 3), table, flat, corr)
-    raw7, corr[7], sixth, fifth, fourth, third, later = lax.optimization_barrier(
-        (raws[0], corr[7], sixth, fifth, fourth, third, table)
-    )
-    sixth = moved(sixth, 6)
+    fifth, fourth, third, second = finish((5, 4, 3, 2), table, flat, corr)
+    *raws, corr[7], fifth, fourth, third, second, later = lax.optimization_barrier(
+        (*raws, corr[7], fifth, fourth, third, second, table)
+    )
     fifth = moved(fifth, 5)
     fourth = moved(fourth, 4)
     third = moved(third, 3)
+    second = moved(second, 2)
     corr[7] = moved(corr[7], 7)
-    second, first = finish((2, 1), later, flat, corr)
+    (first,) = finish((1,), later, flat, corr)
 
     pair = lax.all_gather(theirs, "head", axis=0, tiled=False)
     other = jnp.where(lax.axis_index("head") == 0, pair[1], pair[0])
@@ -654,21 +654,19 @@
     scale = lax.rsqrt(total[:, half : half + 1] / DINNER + epsilon)
     hidden_out = (hidden_in.astype(F32) + total[:, :half] * scale).astype(BF16)
 
-    sixth, fourth, corr[7], second = lax.optimization_barrier(
-        (sixth, fourth, corr[7], second)
-    )
-    second = moved(second, 2)
-    fifth, third, first = lax.optimization_barrier((fifth, third, first))
+    fifth, fourth, third, second, corr[7], corr[6], first = lax.optimization_barrier(
+        (fifth, fourth, third, second, corr[7], corr[6], first)
+    )
     first = moved(first, 1)
-    sent = [corr[0], corr[7]]
-    kept = place(count, width, sixth)
+    corr[6] = moved(corr[6], 6)
+    sent = [corr[0], *corr[6:]]
+    kept = place(count, width, fifth)
     kept = place(count, width, fourth, kept)
-    kept = merge(count, table, flat, [raw7], sent, kept)
-    kept = place(count, width, fifth, kept)
     kept = place(count, width, third, kept)
     kept = place(count, width, second, kept)
+    kept = merge(count, table, flat, raws, sent, kept)
     kept, kept_inner, kept_ssm = close(
-        count, width, (first, second, third, fourth, fifth, sixth), sent, kept
+        count, width, (first, second, third, fourth, fifth), sent, kept
     )
     return (hidden_out, kept.reshape(states_in.shape), kept_inner, kept_ssm)
 

time: 125 us -> 126 us (level)
  the two profiles are of different devices: /device:TPU:0 before, /device:TPU:3 now
where the time goes in v6:
time: 126 us; the launch traced here: 125 us
  waiting for transfers between devices  45.2 us (36%)
  Pallas kernels  36.2 us (29%)
  starting transfers between devices  29 us (23%)
  blocking collectives  9.96 us (8%)
  other arithmetic  2.23 us (2%)
  local copies, waits for them, and re-layouts  1.47 us (1%)
    ppermute x9, waiting for transfers between devices, moved(): lax.ppermute(array, 'req', [(i, (i + by) % length) for i in range(length)])  45.2 us
    ppermute x9, starting transfers between devices, moved(): lax.ppermute(array, 'req', [(i, (i + by) % length) for i in range(length)])  29 us
    pallas_call x1, Pallas kernels, front(): pl.pallas_call(functools.partial(front_kernel, count, heads), grid=(tiles...  12.1 us
    pallas_call x2, Pallas kernels, finish(): pl.pallas_call(functools.partial(finish_kernel, offsets), in_specs=[in_sm...  7.58 us
    pallas_call x4, Pallas kernels, place(): pl.pallas_call(functools.partial(place_kernel, width), in_specs=[in_vmem(...  6.79 us
    all_gather x1, blocking collectives, local(): pair = lax.all_gather(theirs, 'head', axis=0, tiled=False)  4.55 us
    pallas_call x1, Pallas kernels, merge(): pl.pallas_call(merge_kernel, in_specs=[in_smem(), in_hbm()] + [in_vmem()]...  4.17 us
    pallas_call x1, Pallas kernels, pick(): pl.pallas_call(functools.partial(pick_kernel, count, peers), in_specs=[in...  2.95 us
  transfers between devices with their start and end apart: 9, of which 4 were waited for; matrix products, arithmetic and copies ran while one was open for 2% of the time, Pallas kernels for 24%

profile of v6, /device:TPU:3, one launch (start us, length us, event | category | flops | bytes accessed | tf_op | source)
XLA Modules:
  0.0 125.1 jit_solution(3483854470956719835)
XLA Ops:
  0.7 3.0 %pick.1 = (bf16[1536,128]{1,0:T(8,128)(2,1)}, bf16[1536,128]{1,0:T(8,128)(2,1)}, s32[4,8]{1,0:T(4,128)}) custom-call(s32[6]{0:T(128)} %destination.1, bf16[6,1536,128]{2,1,0:T(8,128)(2,1)} %bitcast.10), custom_call_target="tpu_custom_call" | custom-call | flops 1024 | bytes 1024 | tf_op jit(solution)/shard_map/pick/pallas_call | solution.py:348
  3.7 2.3 %collective-permute-start = (bf16[1536,128]{1,0:T(8,128)(2,1)}, bf16[1536,128]{1,0:T(8,128)(2,1)S(1)}, u32[]{:S(2)}, u32[]{:S(2)}) collective-permute-start(bf16[1536,128]{1,0:T(8,128)(2,1)} %get-tuple-element.48), channel_id=1, source_target_pairs={{0,12},{2,14},{4,16},{6,18},{8,20},{10,22},{12,24},{14,26},{16,28}... | collective-permute-start | bytes 1179656 | tf_op jit(solution)/shard_map/ppermute | solution.py:577
  6.0 2.3 %collective-permute-start.1 = (bf16[1536,128]{1,0:T(8,128)(2,1)}, bf16[1536,128]{1,0:T(8,128)(2,1)S(1)}, u32[]{:S(2)}, u32[]{:S(2)}) collective-permute-start(bf16[1536,128]{1,0:T(8,128)(2,1)} %get-tuple-element.49), channel_id=1, source_target_pairs={{0,14},{2,16},{4,18},{6,20},{8,22},{10,24},{12,26},{14,28},{16,30}... | collective-permute-start | bytes 1179656 | tf_op jit(solution)/shard_map/ppermute | solution.py:577
  8.3 2.9 %all-gather = bf16[96,768]{1,0:T(8,128)(2,1)} all-gather(bf16[48,768]{1,0:T(8,128)(2,1)S(1)} %copy-done.8), channel_id=2, replica_groups=mesh['req'=16,'head'=2] {'head'}, dimensions={0}, use_global_device_ids=true | all-gather | bytes 221184 | tf_op jit(solution)/shard_map/all_gather | solution.py:620
  11.3 0.6 pad_maximum_fusion.1.head_rows
  11.9 2.5 %all-gather.1 = bf16[3072,128]{1,0:T(8,128)(2,1)} all-gather(bf16[1536,128]{1,0:T(8,128)(2,1)S(1)} %copy-done.7), channel_id=3, replica_groups=mesh['req'=16,'head'=2] {'head'}, dimensions={0}, use_global_device_ids=true | all-gather | bytes 1179648 | tf_op jit(solution)/shard_map/all_gather | solution.py:625
  14.4 0.6 pad_maximum_fusion.vectors.vector_tile
  15.0 12.1 %front.1 = (f32[48,896]{1,0:T(8,128)}, f32[48,896]{1,0:T(8,128)}, bf16[16,1664]{1,0:T(8,128)(2,1)}, bf16[16,1664]{1,0:T(8,128)(2,1)}, bf16[16,1664]{1,0:T(8,128)...) custom-call(s32[4,8]{1,0:T(4,128)} %get-tuple-element.65.table.refs_, ...), custom_call_target="tpu_custom_call" | custom-call | flops 1024 | bytes 1024 | tf_op jit(solution)/shard_map/front/pallas_call | solution.py:288
  27.1 4.6 %finish.2 = (bf16[1648,128]{1,0:T(8,128)(2,1)}, bf16[1648,128]{1,0:T(8,128)(2,1)}, bf16[1648,128]{1,0:T(8,128)(2,1)}, bf16[1648,128]{1,0:T(8,128)(2,1)}) custom-call(s32[4,8]{1,0:T(4,128)} %get-tuple-element.65.table.refs_0_, bf16[6,1536,128]{2,1,0:T(8,128)(2,1)} %bitcast.12, bf16[16,1664]{1,0:T(8,128)(2,1)} %get-tuple-element.51.refs_2_, ...), custom_call_target="tpu_custom_call" | custom-call | flops 1024 | bytes 1024 | tf_op jit(solution)/shard_map/finish/pallas_call | solution.py:415
  31.7 0.9 collective-permute-done.refs_0_
  32.6 8.7 %collective-permute-done.1.refs_1_ = bf16[1536,128]{1,0:T(8,128)(2,1)S(1)} collective-permute-done((bf16[1536,128]{1,0:T(8,128)(2,1)}, bf16[1536,128]{1,0:T(8,128)(2,1)S(1)}, u32[]{:S(2)}, u32[]{:S(2)}) %collective-permute-start.1) | collective-permute-done | bytes 393248 | tf_op jit(solution)/shard_map/ppermute | solution.py:577
  41.3 1.3 %collective-permute-start.2 = (bf16[1648,128]{1,0:T(8,128)(2,1)}, bf16[1648,128]{1,0:T(8,128)(2,1)S(1)}, u32[]{:S(2)}, u32[]{:S(2)}) collective-permute-start(bf16[1648,128]{1,0:T(8,128)(2,1)} %get-tuple-element.59), channel_id=1, source_target_pairs={{0,10},{2,12},{4,14},{6,16},{8,18},{10,20},{12,22},{14,24},{16,26}... | collective-permute-start | bytes 1265672 | tf_op jit(solution)/shard_map/ppermute | solution.py:577
  42.6 0.0 collective-permute-start.3
  42.6 4.2 %collective-permute-start.4 = (bf16[1648,128]{1,0:T(8,128)(2,1)}, bf16[1648,128]{1,0:T(8,128)(2,1)S(1)}, u32[]{:S(2)}, u32[]{:S(2)}) collective-permute-start(bf16[1648,128]{1,0:T(8,128)(2,1)} %get-tuple-element.61), channel_id=1, source_target_pairs={{0,6},{2,8},{4,10},{6,12},{8,14},{10,16},{12,18},{14,20},{16,22},{... | collective-permute-start | bytes 1265672 | tf_op jit(solution)/shard_map/ppermute | solution.py:577
  46.7 13.2 %collective-permute-start.5 = (bf16[1648,128]{1,0:T(8,128)(2,1)}, bf16[1648,128]{1,0:T(8,128)(2,1)S(1)}, u32[]{:S(2)}, u32[]{:S(2)}) collective-permute-start(bf16[1648,128]{1,0:T(8,128)(2,1)} %get-tuple-element.62), channel_id=1, source_target_pairs={{0,4},{2,6},{4,8},{6,10},{8,12},{10,14},{12,16},{14,18},{16,20},{1... | collective-permute-start | bytes 1265672 | tf_op jit(solution)/shard_map/ppermute | solution.py:577
  60.0 5.7 %collective-permute-start.6 = (bf16[16,1664]{1,0:T(8,128)(2,1)S(1)}, bf16[16,1664]{1,0:T(8,128)(2,1)S(1)}, u32[]{:S(2)}, u32[]{:S(2)}) collective-permute-start(bf16[16,1664]{1,0:T(8,128)(2,1)S(1)} %copy-done.19), channel_id=1, source_target_pairs={{0,14},{2,16},{4,18},{6,20},{8,22},{10,24},{12,26},{14,28},{16,30}... | collective-permute-start | bytes 159752 | tf_op jit(solution)/shard_map/ppermute | solution.py:577
  65.6 4.5 %all-gather.2 = f32[96,896]{1,0:T(8,128)S(1)} all-gather(f32[48,896]{1,0:T(8,128)S(1)} %copy-done.12), channel_id=4, replica_groups=mesh['req'=16,'head'=2] {'head'}, dimensions={0}, use_global_device_ids=true | all-gather | bytes 516096 | tf_op jit(solution)/shard_map/all_gather | solution.py:650
  70.2 3.0 %finish.3 = bf16[1648,128]{1,0:T(8,128)(2,1)} custom-call(s32[4,8]{1,0:T(4,128)} %get-tuple-element.65.table.refs_0_, bf16[6,1536,128]{2,1,0:T(8,128)(2,1)} %bitcast.13, bf16[16,1664]{1,0:T(8,128)(2,1)} %get-tuple-element.66.refs_2_), custom_call_target="tpu_custom_call" | custom-call | flops 1024 | bytes 1024 | tf_op jit(solution)/shard_map/finish/pallas_call | solution.py:415
  73.2 29.5 %collective-permute-done.6.refs_4_.refs_7_ = bf16[16,1664]{1,0:T(8,128)(2,1)S(1)} collective-permute-done((bf16[16,1664]{1,0:T(8,128)(2,1)S(1)}, bf16[16,1664]{1,0:T(8,128)(2,1)S(1)}, u32[]{:S(2)}, u32[]{:S(2)}) %collective-permute-start.6) | collective-permute-done | bytes 53280 | tf_op jit(solution)/shard_map/ppermute | solution.py:577
  102.8 0.1 collective-permute-start.7
  102.9 0.1 fusion.5
  103.0 0.1 collective-permute-start.8
  103.1 0.8 fusion.2
  103.9 1.1 place.4.refs_0_
  105.1 1.9 %place.5.refs_0_ = bf16[6,1536,128]{2,1,0:T(8,128)(2,1)} custom-call(bf16[1648,128]{1,0:T(8,128)(2,1)} %copy-done.1, bf16[6,1536,128]{2,1,0:T(8,128)(2,1)} %place.4.refs_0_), custom_call_target="tpu_custom_call", output_to_operand_aliasing={{}: (1, {})} | custom-call | flops 1024 | bytes 8000000 | tf_op jit(solution)/shard_map/place/pallas_call | solution.py:502
  107.0 1.9 %place.6.refs_0_ = bf16[6,1536,128]{2,1,0:T(8,128)(2,1)} custom-call(bf16[1648,128]{1,0:T(8,128)(2,1)} %copy-done.2, bf16[6,1536,128]{2,1,0:T(8,128)(2,1)} %place.5.refs_0_), custom_call_target="tpu_custom_call", output_to_operand_aliasing={{}: (1, {})} | custom-call | flops 1024 | bytes 8000000 | tf_op jit(solution)/shard_map/place/pallas_call | solution.py:502
  108.9 1.9 %place.7.refs_5_ = bf16[6,1536,128]{2,1,0:T(8,128)(2,1)} custom-call(bf16[1648,128]{1,0:T(8,128)(2,1)} %copy-done.3, bf16[6,1536,128]{2,1,0:T(8,128)(2,1)} %place.6.refs_0_), custom_call_target="tpu_custom_call", output_to_operand_aliasing={{}: (1, {})} | custom-call | flops 1024 | bytes 8000000 | tf_op jit(solution)/shard_map/place/pallas_call | solution.py:502
  110.8 6.1 %collective-permute-done.8.refs_3_.refs_6_ = bf16[16,1664]{1,0:T(8,128)(2,1)S(1)} collective-permute-done((bf16[16,1664]{1,0:T(8,128)(2,1)}, bf16[16,1664]{1,0:T(8,128)(2,1)S(1)}, u32[]{:S(2)}, u32[]{:S(2)}) %collective-permute-start.8) | collective-permute-done | bytes 53280 | tf_op jit(solution)/shard_map/ppermute | solution.py:577
  116.9 0.6 copy-done.10
  117.5 4.2 %merge.1.refs_8_ = bf16[6,1536,128]{2,1,0:T(8,128)(2,1)} custom-call(s32[4,8]{1,0:T(4,128)} %get-tuple-element.65.table.refs_0_, bf16[6,1536,128]{2,1,0:T(8,128)(2,1)} %bitcast.14, bf16[1536,128]{1,0:T(8,128)(2,1)} %copy-done.5, bf16[1536,128]{1,0:T(8,128)(2,1)} %copy-done.6, ...), custom_call_target="tpu_custom_call", output_to_operand_aliasing={{}: (7, {})} | custom-call | flops 1024 | bytes 1024 | tf_op jit(solution)/shard_map/merge/pallas_call | solution.py:465
  121.7 0.8 copy-done.4
  122.4 2.6 %close.1 = (bf16[6,1536,128]{2,1,0:T(8,128)(2,1)}, bf16[6,3,1536]{2,1,0:T(4,128)(2,1)}, bf16[6,3,256]{2,1,0:T(4,128)(2,1)}) custom-call(bf16[1648,128]{1,0:T(8,128)(2,1)} %copy-done.4, bf16[1648,128]{1,0:T(8,128)(2,1)} %copy-done.3, bf16[1648,128]{1,0:T(8,128)(2,1)} %copy-done.2, bf16[1648,128]{1,0:T(8,128)(2,1)} %copy-done.1, ...), custom_call_target="tpu_custom_call", output_to_operand_aliasing={{0}: (8, {})} | custom-call | flops 1024 | bytes 1024 | tf_op jit(solution)/shard_map/close/pallas_call | solution.py:559
  (47 shorter events, 0.1 us)
Async XLA Ops:
  0.6 7.6 %copy-start.13 = (f32[1536]{0:T(1024)S(1)}, f32[1536]{0:T(1024)}, u32[]{:S(2)}) copy-start(f32[1536]{0:T(1024)} %param.22) | copy-start | bytes 18436
  0.6 7.6 %copy-start.14 = (f32[1536]{0:T(1024)S(1)}, f32[1536]{0:T(1024)}, u32[]{:S(2)}) copy-start(f32[1536]{0:T(1024)} %param.31) | copy-start | bytes 18436
  0.7 7.6 %copy-start.15 = (f32[1536]{0:T(1024)S(1)}, f32[1536]{0:T(1024)}, u32[]{:S(2)}) copy-start(f32[1536]{0:T(1024)} %param.34) | copy-start | bytes 18436
  0.7 7.7 %copy-start.8 = (bf16[48,768]{1,0:T(8,128)(2,1)S(1)}, bf16[48,768]{1,0:T(8,128)(2,1)}, u32[]{:S(2)}) copy-start(bf16[48,768]{1,0:T(8,128)(2,1)} %param.21) | copy-start | bytes 221188
  0.7 11.2 %copy-start.7 = (bf16[1536,128]{1,0:T(8,128)(2,1)S(1)}, bf16[1536,128]{1,0:T(8,128)(2,1)}, u32[]{:S(2)}) copy-start(bf16[1536,128]{1,0:T(8,128)(2,1)} %param.25) | copy-start | bytes 1179652
  0.7 10.6 %copy-start.16 = (f32[24]{0:T(128)S(1)}, f32[24]{0:T(128)}, u32[]{:S(2)}) copy-start(f32[24]{0:T(128)} %param.29) | copy-start | bytes 292
  0.7 10.6 %copy-start.17 = (f32[24]{0:T(128)S(1)}, f32[24]{0:T(128)}, u32[]{:S(2)}) copy-start(f32[24]{0:T(128)} %param.28) | copy-start | bytes 292
  0.7 10.6 %copy-start.18 = (f32[24]{0:T(128)S(1)}, f32[24]{0:T(128)}, u32[]{:S(2)}) copy-start(f32[24]{0:T(128)} %param.27) | copy-start | bytes 292
  3.7 28.9 %collective-permute-start = (bf16[1536,128]{1,0:T(8,128)(2,1)}, bf16[1536,128]{1,0:T(8,128)(2,1)S(1)}, u32[]{:S(2)}, u32[]{:S(2)}) collective-permute-start(bf16[1536,128]{1,0:T(8,128)(2,1)} %get-tuple-element.48), channel_id=1, source_target_pairs={{0,12},{2,14},{4,16},{6,18},{8,20},{10,22},{12,24},{14,26},{16,28}... | collective-permute-start | bytes 1179656 | tf_op jit(solution)/shard_map/ppermute | solution.py:577
  6.0 35.3 %collective-permute-start.1 = (bf16[1536,128]{1,0:T(8,128)(2,1)}, bf16[1536,128]{1,0:T(8,128)(2,1)S(1)}, u32[]{:S(2)}, u32[]{:S(2)}) collective-permute-start(bf16[1536,128]{1,0:T(8,128)(2,1)} %get-tuple-element.49), channel_id=1, source_target_pairs={{0,14},{2,16},{4,18},{6,20},{8,22},{10,24},{12,26},{14,28},{16,30}... | collective-permute-start | bytes 1179656 | tf_op jit(solution)/shard_map/ppermute | solution.py:577
  27.1 32.9 %copy-start.19 = (bf16[16,1664]{1,0:T(8,128)(2,1)S(1)}, bf16[16,1664]{1,0:T(8,128)(2,1)}, u32[]{:S(2)}) copy-start(bf16[16,1664]{1,0:T(8,128)(2,1)} %get-tuple-element.63) | copy-start | bytes 159748
  27.1 38.6 %copy-start.12 = (f32[48,896]{1,0:T(8,128)S(1)}, f32[48,896]{1,0:T(8,128)}, u32[]{:S(2)}) copy-start(f32[48,896]{1,0:T(8,128)} %get-tuple-element.47) | copy-start | bytes 516100
  27.1 75.8 %copy-start.11 = (f32[48,896]{1,0:T(8,128)S(1)}, f32[48,896]{1,0:T(8,128)}, u32[]{:S(2)}) copy-start(f32[48,896]{1,0:T(8,128)} %get-tuple-element.46) | copy-start | bytes 516100
  32.6 72.5 %copy-start.5 = (bf16[1536,128]{1,0:T(8,128)(2,1)}, bf16[1536,128]{1,0:T(8,128)(2,1)S(1)}, u32[]{:S(2)}) copy-start(bf16[1536,128]{1,0:T(8,128)(2,1)S(1)} %collective-permute-done.refs_0_) | copy-start | bytes 1179652
  41.3 63.8 %copy-start.6 = (bf16[1536,128]{1,0:T(8,128)(2,1)}, bf16[1536,128]{1,0:T(8,128)(2,1)S(1)}, u32[]{:S(2)}) copy-start(bf16[1536,128]{1,0:T(8,128)(2,1)S(1)} %collective-permute-done.1.refs_1_) | copy-start | bytes 1179652
  41.3 61.4 %collective-permute-start.2 = (bf16[1648,128]{1,0:T(8,128)(2,1)}, bf16[1648,128]{1,0:T(8,128)(2,1)S(1)}, u32[]{:S(2)}, u32[]{:S(2)}) collective-permute-start(bf16[1648,128]{1,0:T(8,128)(2,1)} %get-tuple-element.59), channel_id=1, source_target_pairs={{0,10},{2,12},{4,14},{6,16},{8,18},{10,20},{12,22},{14,24},{16,26}... | collective-permute-start | bytes 1265672 | tf_op jit(solution)/shard_map/ppermute | solution.py:577
  42.6 60.2 %collective-permute-start.3 = (bf16[1648,128]{1,0:T(8,128)(2,1)}, bf16[1648,128]{1,0:T(8,128)(2,1)S(1)}, u32[]{:S(2)}, u32[]{:S(2)}) collective-permute-start(bf16[1648,128]{1,0:T(8,128)(2,1)} %get-tuple-element.60), channel_id=1, source_target_pairs={{0,8},{2,10},{4,12},{6,14},{8,16},{10,18},{12,20},{14,22},{16,24},... | collective-permute-start | bytes 1265672 | tf_op jit(solution)/shard_map/ppermute | solution.py:577
  42.6 60.2 %collective-permute-start.4 = (bf16[1648,128]{1,0:T(8,128)(2,1)}, bf16[1648,128]{1,0:T(8,128)(2,1)S(1)}, u32[]{:S(2)}, u32[]{:S(2)}) collective-permute-start(bf16[1648,128]{1,0:T(8,128)(2,1)} %get-tuple-element.61), channel_id=1, source_target_pairs={{0,6},{2,8},{4,10},{6,12},{8,14},{10,16},{12,18},{14,20},{16,22},{... | collective-permute-start | bytes 1265672 | tf_op jit(solution)/shard_map/ppermute | solution.py:577
  46.7 56.0 %collective-permute-start.5 = (bf16[1648,128]{1,0:T(8,128)(2,1)}, bf16[1648,128]{1,0:T(8,128)(2,1)S(1)}, u32[]{:S(2)}, u32[]{:S(2)}) collective-permute-start(bf16[1648,128]{1,0:T(8,128)(2,1)} %get-tuple-element.62), channel_id=1, source_target_pairs={{0,4},{2,6},{4,8},{6,10},{8,12},{10,14},{12,16},{14,18},{16,20},{1... | collective-permute-start | bytes 1265672 | tf_op jit(solution)/shard_map/ppermute | solution.py:577
  60.0 42.8 %collective-permute-start.6 = (bf16[16,1664]{1,0:T(8,128)(2,1)S(1)}, bf16[16,1664]{1,0:T(8,128)(2,1)S(1)}, u32[]{:S(2)}, u32[]{:S(2)}) collective-permute-start(bf16[16,1664]{1,0:T(8,128)(2,1)S(1)} %copy-done.19), channel_id=1, source_target_pairs={{0,14},{2,16},{4,18},{6,20},{8,22},{10,24},{12,26},{14,28},{16,30}... | collective-permute-start | bytes 159752 | tf_op jit(solution)/shard_map/ppermute | solution.py:577
  102.7 4.3 %copy-start.9 = (bf16[16,1664]{1,0:T(8,128)(2,1)}, bf16[16,1664]{1,0:T(8,128)(2,1)S(1)}, u32[]{:S(2)}) copy-start(bf16[16,1664]{1,0:T(8,128)(2,1)S(1)} %collective-permute-done.6.refs_4_.refs_7_) | copy-start | bytes 159748
  102.7 1.2 copy-start
  102.7 2.4 %copy-start.1 = (bf16[1648,128]{1,0:T(8,128)(2,1)}, bf16[1648,128]{1,0:T(8,128)(2,1)S(1)}, u32[]{:S(2)}) copy-start(bf16[1648,128]{1,0:T(8,128)(2,1)S(1)} %collective-permute-done.3.message.refs_3_) | copy-start | bytes 1265668
  102.8 4.3 %copy-start.2 = (bf16[1648,128]{1,0:T(8,128)(2,1)}, bf16[1648,128]{1,0:T(8,128)(2,1)S(1)}, u32[]{:S(2)}) copy-start(bf16[1648,128]{1,0:T(8,128)(2,1)S(1)} %collective-permute-done.4.message.refs_2_) | copy-start | bytes 1265668
  102.8 4.2 %copy-start.3 = (bf16[1648,128]{1,0:T(8,128)(2,1)}, bf16[1648,128]{1,0:T(8,128)(2,1)S(1)}, u32[]{:S(2)}) copy-start(bf16[1648,128]{1,0:T(8,128)(2,1)S(1)} %collective-permute-done.5.message.refs_1_) | copy-start | bytes 1265668
  102.8 18.9 %collective-permute-start.7 = (bf16[1648,128]{1,0:T(8,128)(2,1)}, bf16[1648,128]{1,0:T(8,128)(2,1)S(1)}, u32[]{:S(2)}, u32[]{:S(2)}) collective-permute-start(bf16[1648,128]{1,0:T(8,128)(2,1)} %finish.3), channel_id=1, source_target_pairs={{0,2},{2,4},{4,6},{6,8},{8,10},{10,12},{12,14},{14,16},{16,18},{18... | collective-permute-start | bytes 1265672 | tf_op jit(solution)/shard_map/ppermute | solution.py:577
  103.0 13.9 %collective-permute-start.8 = (bf16[16,1664]{1,0:T(8,128)(2,1)}, bf16[16,1664]{1,0:T(8,128)(2,1)S(1)}, u32[]{:S(2)}, u32[]{:S(2)}) collective-permute-start(bf16[16,1664]{1,0:T(8,128)(2,1)} %get-tuple-element.73), channel_id=1, source_target_pairs={{0,12},{2,14},{4,16},{6,18},{8,20},{10,22},{12,24},{14,26},{16,28}... | collective-permute-start | bytes 159752 | tf_op jit(solution)/shard_map/ppermute | solution.py:577
  116.9 0.6 copy-start.10
  121.7 0.8 copy-start.4

commit v7 on v6

--- a/solution.py
+++ b/solution.py
@@ -15,7 +15,7 @@
 DINNER = 3072
 TILE = 256
 EXTRA = NSTATE
-RAW = (6, 7)
+RAW = (7, 2)
 PARTS = 3
 SMALL = pl.CostEstimate(flops=1024, bytes_accessed=1024, transcendentals=0)
 STEP = pl.CostEstimate(flops=1024, bytes_accessed=8_000_000, transcendentals=0)
@@ -636,14 +636,14 @@
     )
     mine, theirs = results[:2]
     corr = list(results[2:])
-    fifth, fourth, third, second = finish((5, 4, 3, 2), table, flat, corr)
-    *raws, corr[7], fifth, fourth, third, second, later = lax.optimization_barrier(
-        (*raws, corr[7], fifth, fourth, third, second, table)
-    )
+    sixth, fifth, fourth, third = finish((6, 5, 4, 3), table, flat, corr)
+    *raws, corr[7], sixth, fifth, fourth, third, later = lax.optimization_barrier(
+        (*raws, corr[7], sixth, fifth, fourth, third, table)
+    )
+    sixth = moved(sixth, 6)
     fifth = moved(fifth, 5)
     fourth = moved(fourth, 4)
     third = moved(third, 3)
-    second = moved(second, 2)
     corr[7] = moved(corr[7], 7)
     (first,) = finish((1,), later, flat, corr)
 
@@ -654,19 +654,19 @@
     scale = lax.rsqrt(total[:, half : half + 1] / DINNER + epsilon)
     hidden_out = (hidden_in.astype(F32) + total[:, :half] * scale).astype(BF16)
 
-    fifth, fourth, third, second, corr[7], corr[6], first = lax.optimization_barrier(
-        (fifth, fourth, third, second, corr[7], corr[6], first)
-    )
+    sixth, fifth, fourth, third, corr[7], corr[2], first = lax.optimization_barrier(
+        (sixth, fifth, fourth, third, corr[7], corr[2], first)
+    )
+    corr[2] = moved(corr[2], 2)
     first = moved(first, 1)
-    corr[6] = moved(corr[6], 6)
-    sent = [corr[0], *corr[6:]]
-    kept = place(count, width, fifth)
+    sent = [corr[0], *(corr[k] for k in RAW)]
+    kept = place(count, width, sixth)
+    kept = place(count, width, fifth, kept)
     kept = place(count, width, fourth, kept)
     kept = place(count, width, third, kept)
-    kept = place(count, width, second, kept)
     kept = merge(count, table, flat, raws, sent, kept)
     kept, kept_inner, kept_ssm = close(
-        count, width, (first, second, third, fourth, fifth), sent, kept
+        count, width, (first, third, fourth, fifth, sixth), sent, kept
     )
     return (hidden_out, kept.reshape(states_in.shape), kept_inner, kept_ssm)
 

time: 126 us -> 118 us (0.937)
  the two profiles are of different devices: /device:TPU:3 before, /device:TPU:2 now
where the time goes in v7:
time: 118 us; the launch traced here: 117 us
  waiting for transfers between devices  48.2 us (41%)
  Pallas kernels  36.5 us (31%)
  starting transfers between devices  20.8 us (18%)
  blocking collectives  6.57 us (6%)
  other arithmetic  2.1 us (2%)
  local copies, waits for them, and re-layouts  1.47 us (1%)
    ppermute x9, waiting for transfers between devices, moved(): lax.ppermute(array, 'req', [(i, (i + by) % length) for i in range(length)])  48.2 us
    ppermute x9, starting transfers between devices, moved(): lax.ppermute(array, 'req', [(i, (i + by) % length) for i in range(length)])  20.8 us
    pallas_call x1, Pallas kernels, front(): pl.pallas_call(functools.partial(front_kernel, count, heads), grid=(tiles...  12.1 us
    pallas_call x2, Pallas kernels, finish(): pl.pallas_call(functools.partial(finish_kernel, offsets), in_specs=[in_sm...  7.59 us
    pallas_call x4, Pallas kernels, place(): pl.pallas_call(functools.partial(place_kernel, width), in_specs=[in_vmem(...  7.53 us
    pallas_call x1, Pallas kernels, merge(): pl.pallas_call(merge_kernel, in_specs=[in_smem(), in_hbm()] + [in_vmem()]...  3.34 us
    pallas_call x1, Pallas kernels, close(): pl.pallas_call(functools.partial(close_kernel, n), in_specs=[in_vmem()] *...  3.07 us
    pallas_call x1, Pallas kernels, pick(): pl.pallas_call(functools.partial(pick_kernel, count, peers), in_specs=[in...  2.95 us
  transfers between devices with their start and end apart: 9, of which 3 were waited for; matrix products, arithmetic and copies ran while one was open for 2% of the time, Pallas kernels for 26%

profile of v7, /device:TPU:2, one launch (start us, length us, event | category | flops | bytes accessed | tf_op | source)
XLA Modules:
  0.0 116.7 jit_solution(114232080622373072)
XLA Ops:
  0.7 3.0 %pick.1 = (bf16[1536,128]{1,0:T(8,128)(2,1)}, bf16[1536,128]{1,0:T(8,128)(2,1)}, s32[4,8]{1,0:T(4,128)}) custom-call(s32[6]{0:T(128)} %destination.1, bf16[6,1536,128]{2,1,0:T(8,128)(2,1)} %bitcast.10), custom_call_target="tpu_custom_call" | custom-call | flops 1024 | bytes 1024 | tf_op jit(solution)/shard_map/pick/pallas_call | solution.py:348
  3.7 2.6 %collective-permute-start = (bf16[1536,128]{1,0:T(8,128)(2,1)}, bf16[1536,128]{1,0:T(8,128)(2,1)S(1)}, u32[]{:S(2)}, u32[]{:S(2)}) collective-permute-start(bf16[1536,128]{1,0:T(8,128)(2,1)} %get-tuple-element.48), channel_id=1, source_target_pairs={{0,14},{2,16},{4,18},{6,20},{8,22},{10,24},{12,26},{14,28},{16,30}... | collective-permute-start | bytes 1179656 | tf_op jit(solution)/shard_map/ppermute | solution.py:577
  6.3 1.5 %collective-permute-start.1 = (bf16[1536,128]{1,0:T(8,128)(2,1)}, bf16[1536,128]{1,0:T(8,128)(2,1)S(1)}, u32[]{:S(2)}, u32[]{:S(2)}) collective-permute-start(bf16[1536,128]{1,0:T(8,128)(2,1)} %get-tuple-element.49), channel_id=1, source_target_pairs={{0,4},{2,6},{4,8},{6,10},{8,12},{10,14},{12,16},{14,18},{16,20},{1... | collective-permute-start | bytes 1179656 | tf_op jit(solution)/shard_map/ppermute | solution.py:577
  7.9 2.0 %all-gather = bf16[96,768]{1,0:T(8,128)(2,1)} all-gather(bf16[48,768]{1,0:T(8,128)(2,1)S(1)} %copy-done.8), channel_id=2, replica_groups=mesh['req'=16,'head'=2] {'head'}, dimensions={0}, use_global_device_ids=true | all-gather | bytes 221184 | tf_op jit(solution)/shard_map/all_gather | solution.py:620
  9.9 0.6 pad_maximum_fusion.1.head_rows
  10.5 2.5 %all-gather.1 = bf16[3072,128]{1,0:T(8,128)(2,1)} all-gather(bf16[1536,128]{1,0:T(8,128)(2,1)S(1)} %copy-done.7), channel_id=3, replica_groups=mesh['req'=16,'head'=2] {'head'}, dimensions={0}, use_global_device_ids=true | all-gather | bytes 1179648 | tf_op jit(solution)/shard_map/all_gather | solution.py:625
  13.0 0.6 pad_maximum_fusion.vectors.vector_tile
  13.7 12.1 %front.1 = (f32[48,896]{1,0:T(8,128)}, f32[48,896]{1,0:T(8,128)}, bf16[16,1664]{1,0:T(8,128)(2,1)}, bf16[16,1664]{1,0:T(8,128)(2,1)}, bf16[16,1664]{1,0:T(8,128)...) custom-call(s32[4,8]{1,0:T(4,128)} %get-tuple-element.65.table.refs_, ...), custom_call_target="tpu_custom_call" | custom-call | flops 1024 | bytes 1024 | tf_op jit(solution)/shard_map/front/pallas_call | solution.py:288
  25.7 4.6 %finish.2 = (bf16[1648,128]{1,0:T(8,128)(2,1)}, bf16[1648,128]{1,0:T(8,128)(2,1)}, bf16[1648,128]{1,0:T(8,128)(2,1)}, bf16[1648,128]{1,0:T(8,128)(2,1)}) custom-call(s32[4,8]{1,0:T(4,128)} %get-tuple-element.65.table.refs_0_, bf16[6,1536,128]{2,1,0:T(8,128)(2,1)} %bitcast.12, bf16[16,1664]{1,0:T(8,128)(2,1)} %get-tuple-element.51.refs_2_, ...), custom_call_target="tpu_custom_call" | custom-call | flops 1024 | bytes 1024 | tf_op jit(solution)/shard_map/finish/pallas_call | solution.py:415
  30.3 4.0 %collective-permute-done.refs_0_ = bf16[1536,128]{1,0:T(8,128)(2,1)S(1)} collective-permute-done((bf16[1536,128]{1,0:T(8,128)(2,1)}, bf16[1536,128]{1,0:T(8,128)(2,1)S(1)}, u32[]{:S(2)}, u32[]{:S(2)}) %collective-permute-start) | collective-permute-done | bytes 393248 | tf_op jit(solution)/shard_map/ppermute | solution.py:577
  34.3 0.0 collective-permute-done.1.refs_1_
  34.3 0.1 collective-permute-start.2
  34.4 0.8 collective-permute-start.3
  35.2 0.5 collective-permute-start.4
  35.7 1.9 %collective-permute-start.5 = (bf16[1648,128]{1,0:T(8,128)(2,1)}, bf16[1648,128]{1,0:T(8,128)(2,1)S(1)}, u32[]{:S(2)}, u32[]{:S(2)}) collective-permute-start(bf16[1648,128]{1,0:T(8,128)(2,1)} %get-tuple-element.62), channel_id=1, source_target_pairs={{0,6},{2,8},{4,10},{6,12},{8,14},{10,16},{12,18},{14,20},{16,22},{... | collective-permute-start | bytes 1265672 | tf_op jit(solution)/shard_map/ppermute | solution.py:577
  37.6 2.9 %collective-permute-start.6 = (bf16[16,1664]{1,0:T(8,128)(2,1)S(1)}, bf16[16,1664]{1,0:T(8,128)(2,1)S(1)}, u32[]{:S(2)}, u32[]{:S(2)}) collective-permute-start(bf16[16,1664]{1,0:T(8,128)(2,1)S(1)} %copy-done.19), channel_id=1, source_target_pairs={{0,14},{2,16},{4,18},{6,20},{8,22},{10,24},{12,26},{14,28},{16,30}... | collective-permute-start | bytes 159752 | tf_op jit(solution)/shard_map/ppermute | solution.py:577
  40.5 2.0 %all-gather.2 = f32[96,896]{1,0:T(8,128)S(1)} all-gather(f32[48,896]{1,0:T(8,128)S(1)} %copy-done.12), channel_id=4, replica_groups=mesh['req'=16,'head'=2] {'head'}, dimensions={0}, use_global_device_ids=true | all-gather | bytes 516096 | tf_op jit(solution)/shard_map/all_gather | solution.py:650
  42.5 3.0 %finish.3 = bf16[1648,128]{1,0:T(8,128)(2,1)} custom-call(s32[4,8]{1,0:T(4,128)} %get-tuple-element.65.table.refs_0_, bf16[6,1536,128]{2,1,0:T(8,128)(2,1)} %bitcast.13, bf16[16,1664]{1,0:T(8,128)(2,1)} %get-tuple-element.66.refs_2_), custom_call_target="tpu_custom_call" | custom-call | flops 1024 | bytes 1024 | tf_op jit(solution)/shard_map/finish/pallas_call | solution.py:415
  45.5 38.4 %collective-permute-done.6.refs_3_.refs_6_ = bf16[16,1664]{1,0:T(8,128)(2,1)S(1)} collective-permute-done((bf16[16,1664]{1,0:T(8,128)(2,1)S(1)}, bf16[16,1664]{1,0:T(8,128)(2,1)S(1)}, u32[]{:S(2)}, u32[]{:S(2)}) %collective-permute-start.6) | collective-permute-done | bytes 53280 | tf_op jit(solution)/shard_map/ppermute | solution.py:577
  84.0 10.5 %collective-permute-start.7 = (bf16[1648,128]{1,0:T(8,128)(2,1)}, bf16[1648,128]{1,0:T(8,128)(2,1)S(1)}, u32[]{:S(2)}, u32[]{:S(2)}) collective-permute-start(bf16[1648,128]{1,0:T(8,128)(2,1)} %finish.3), channel_id=1, source_target_pairs={{0,2},{2,4},{4,6},{6,8},{8,10},{10,12},{12,14},{14,16},{16,18},{18... | collective-permute-start | bytes 1265672 | tf_op jit(solution)/shard_map/ppermute | solution.py:577
  94.6 0.1 fusion.5
  94.7 0.1 collective-permute-start.8
  94.7 0.7 fusion.2
  95.5 1.9 %place.4.refs_0_ = bf16[6,1536,128]{2,1,0:T(8,128)(2,1)} custom-call(bf16[1648,128]{1,0:T(8,128)(2,1)} %copy-done), custom_call_target="tpu_custom_call" | custom-call | flops 1024 | bytes 8000000 | tf_op jit(solution)/shard_map/place/pallas_call | solution.py:502
  97.4 1.9 %place.5.refs_0_ = bf16[6,1536,128]{2,1,0:T(8,128)(2,1)} custom-call(bf16[1648,128]{1,0:T(8,128)(2,1)} %copy-done.1, bf16[6,1536,128]{2,1,0:T(8,128)(2,1)} %place.4.refs_0_), custom_call_target="tpu_custom_call", output_to_operand_aliasing={{}: (1, {})} | custom-call | flops 1024 | bytes 8000000 | tf_op jit(solution)/shard_map/place/pallas_call | solution.py:502
  99.3 1.9 %place.6.refs_0_ = bf16[6,1536,128]{2,1,0:T(8,128)(2,1)} custom-call(bf16[1648,128]{1,0:T(8,128)(2,1)} %copy-done.2, bf16[6,1536,128]{2,1,0:T(8,128)(2,1)} %place.5.refs_0_), custom_call_target="tpu_custom_call", output_to_operand_aliasing={{}: (1, {})} | custom-call | flops 1024 | bytes 8000000 | tf_op jit(solution)/shard_map/place/pallas_call | solution.py:502
  101.2 1.9 %place.7.refs_5_ = bf16[6,1536,128]{2,1,0:T(8,128)(2,1)} custom-call(bf16[1648,128]{1,0:T(8,128)(2,1)} %copy-done.3, bf16[6,1536,128]{2,1,0:T(8,128)(2,1)} %place.6.refs_0_), custom_call_target="tpu_custom_call", output_to_operand_aliasing={{}: (1, {})} | custom-call | flops 1024 | bytes 8000000 | tf_op jit(solution)/shard_map/place/pallas_call | solution.py:502
  103.1 5.8 %collective-permute-done.8.refs_4_.refs_7_ = bf16[16,1664]{1,0:T(8,128)(2,1)S(1)} collective-permute-done((bf16[16,1664]{1,0:T(8,128)(2,1)}, bf16[16,1664]{1,0:T(8,128)(2,1)S(1)}, u32[]{:S(2)}, u32[]{:S(2)}) %collective-permute-start.8) | collective-permute-done | bytes 53280 | tf_op jit(solution)/shard_map/ppermute | solution.py:577
  108.9 0.6 copy-done.10
  109.5 3.3 %merge.1.refs_8_ = bf16[6,1536,128]{2,1,0:T(8,128)(2,1)} custom-call(s32[4,8]{1,0:T(4,128)} %get-tuple-element.65.table.refs_0_, bf16[6,1536,128]{2,1,0:T(8,128)(2,1)} %bitcast.14, bf16[1536,128]{1,0:T(8,128)(2,1)} %copy-done.5, bf16[1536,128]{1,0:T(8,128)(2,1)} %copy-done.6, ...), custom_call_target="tpu_custom_call", output_to_operand_aliasing={{}: (7, {})} | custom-call | flops 1024 | bytes 1024 | tf_op jit(solution)/shard_map/merge/pallas_call | solution.py:465
  112.9 0.8 copy-done.4
  113.6 3.1 %close.1 = (bf16[6,1536,128]{2,1,0:T(8,128)(2,1)}, bf16[6,3,1536]{2,1,0:T(4,128)(2,1)}, bf16[6,3,256]{2,1,0:T(4,128)(2,1)}) custom-call(bf16[1648,128]{1,0:T(8,128)(2,1)} %copy-done.4, bf16[1648,128]{1,0:T(8,128)(2,1)} %copy-done.3, bf16[1648,128]{1,0:T(8,128)(2,1)} %copy-done.2, bf16[1648,128]{1,0:T(8,128)(2,1)} %copy-done.1, ...), custom_call_target="tpu_custom_call", output_to_operand_aliasing={{0}: (8, {})} | custom-call | flops 1024 | bytes 1024 | tf_op jit(solution)/shard_map/close/pallas_call | solution.py:559
  (47 shorter events, 0.1 us)
Async XLA Ops:
  0.6 7.2 %copy-start.13 = (f32[1536]{0:T(1024)S(1)}, f32[1536]{0:T(1024)}, u32[]{:S(2)}) copy-start(f32[1536]{0:T(1024)} %param.22) | copy-start | bytes 18436
  0.6 7.2 %copy-start.14 = (f32[1536]{0:T(1024)S(1)}, f32[1536]{0:T(1024)}, u32[]{:S(2)}) copy-start(f32[1536]{0:T(1024)} %param.31) | copy-start | bytes 18436
  0.7 7.2 %copy-start.15 = (f32[1536]{0:T(1024)S(1)}, f32[1536]{0:T(1024)}, u32[]{:S(2)}) copy-start(f32[1536]{0:T(1024)} %param.34) | copy-start | bytes 18436
  0.7 7.2 %copy-start.8 = (bf16[48,768]{1,0:T(8,128)(2,1)S(1)}, bf16[48,768]{1,0:T(8,128)(2,1)}, u32[]{:S(2)}) copy-start(bf16[48,768]{1,0:T(8,128)(2,1)} %param.21) | copy-start | bytes 221188
  0.7 9.9 %copy-start.7 = (bf16[1536,128]{1,0:T(8,128)(2,1)S(1)}, bf16[1536,128]{1,0:T(8,128)(2,1)}, u32[]{:S(2)}) copy-start(bf16[1536,128]{1,0:T(8,128)(2,1)} %param.25) | copy-start | bytes 1179652
  0.7 9.2 %copy-start.16 = (f32[24]{0:T(128)S(1)}, f32[24]{0:T(128)}, u32[]{:S(2)}) copy-start(f32[24]{0:T(128)} %param.29) | copy-start | bytes 292
  0.7 9.2 %copy-start.17 = (f32[24]{0:T(128)S(1)}, f32[24]{0:T(128)}, u32[]{:S(2)}) copy-start(f32[24]{0:T(128)} %param.28) | copy-start | bytes 292
  0.7 9.2 %copy-start.18 = (f32[24]{0:T(128)S(1)}, f32[24]{0:T(128)}, u32[]{:S(2)}) copy-start(f32[24]{0:T(128)} %param.27) | copy-start | bytes 292
  3.7 30.7 %collective-permute-start = (bf16[1536,128]{1,0:T(8,128)(2,1)}, bf16[1536,128]{1,0:T(8,128)(2,1)S(1)}, u32[]{:S(2)}, u32[]{:S(2)}) collective-permute-start(bf16[1536,128]{1,0:T(8,128)(2,1)} %get-tuple-element.48), channel_id=1, source_target_pairs={{0,14},{2,16},{4,18},{6,20},{8,22},{10,24},{12,26},{14,28},{16,30}... | collective-permute-start | bytes 1179656 | tf_op jit(solution)/shard_map/ppermute | solution.py:577
  6.3 28.1 %collective-permute-start.1 = (bf16[1536,128]{1,0:T(8,128)(2,1)}, bf16[1536,128]{1,0:T(8,128)(2,1)S(1)}, u32[]{:S(2)}, u32[]{:S(2)}) collective-permute-start(bf16[1536,128]{1,0:T(8,128)(2,1)} %get-tuple-element.49), channel_id=1, source_target_pairs={{0,4},{2,6},{4,8},{6,10},{8,12},{10,14},{12,16},{14,18},{16,20},{1... | collective-permute-start | bytes 1179656 | tf_op jit(solution)/shard_map/ppermute | solution.py:577
  25.7 11.9 %copy-start.19 = (bf16[16,1664]{1,0:T(8,128)(2,1)S(1)}, bf16[16,1664]{1,0:T(8,128)(2,1)}, u32[]{:S(2)}) copy-start(bf16[16,1664]{1,0:T(8,128)(2,1)} %get-tuple-element.63) | copy-start | bytes 159748
  25.7 14.7 %copy-start.12 = (f32[48,896]{1,0:T(8,128)S(1)}, f32[48,896]{1,0:T(8,128)}, u32[]{:S(2)}) copy-start(f32[48,896]{1,0:T(8,128)} %get-tuple-element.47) | copy-start | bytes 516100
  25.7 68.8 %copy-start.11 = (f32[48,896]{1,0:T(8,128)S(1)}, f32[48,896]{1,0:T(8,128)}, u32[]{:S(2)}) copy-start(f32[48,896]{1,0:T(8,128)} %get-tuple-element.46) | copy-start | bytes 516100
  34.3 63.0 %copy-start.5 = (bf16[1536,128]{1,0:T(8,128)(2,1)}, bf16[1536,128]{1,0:T(8,128)(2,1)S(1)}, u32[]{:S(2)}) copy-start(bf16[1536,128]{1,0:T(8,128)(2,1)S(1)} %collective-permute-done.refs_0_) | copy-start | bytes 1179652
  34.3 63.0 %copy-start.6 = (bf16[1536,128]{1,0:T(8,128)(2,1)}, bf16[1536,128]{1,0:T(8,128)(2,1)S(1)}, u32[]{:S(2)}) copy-start(bf16[1536,128]{1,0:T(8,128)(2,1)S(1)} %collective-permute-done.1.refs_1_) | copy-start | bytes 1179652
  34.3 49.6 %collective-permute-start.2 = (bf16[1648,128]{1,0:T(8,128)(2,1)}, bf16[1648,128]{1,0:T(8,128)(2,1)S(1)}, u32[]{:S(2)}, u32[]{:S(2)}) collective-permute-start(bf16[1648,128]{1,0:T(8,128)(2,1)} %get-tuple-element.59), channel_id=1, source_target_pairs={{0,12},{2,14},{4,16},{6,18},{8,20},{10,22},{12,24},{14,26},{16,28}... | collective-permute-start | bytes 1265672 | tf_op jit(solution)/shard_map/ppermute | solution.py:577
  34.4 49.5 %collective-permute-start.3 = (bf16[1648,128]{1,0:T(8,128)(2,1)}, bf16[1648,128]{1,0:T(8,128)(2,1)S(1)}, u32[]{:S(2)}, u32[]{:S(2)}) collective-permute-start(bf16[1648,128]{1,0:T(8,128)(2,1)} %get-tuple-element.60), channel_id=1, source_target_pairs={{0,10},{2,12},{4,14},{6,16},{8,18},{10,20},{12,22},{14,24},{16,26}... | collective-permute-start | bytes 1265672 | tf_op jit(solution)/shard_map/ppermute | solution.py:577
  35.2 48.8 %collective-permute-start.4 = (bf16[1648,128]{1,0:T(8,128)(2,1)}, bf16[1648,128]{1,0:T(8,128)(2,1)S(1)}, u32[]{:S(2)}, u32[]{:S(2)}) collective-permute-start(bf16[1648,128]{1,0:T(8,128)(2,1)} %get-tuple-element.61), channel_id=1, source_target_pairs={{0,8},{2,10},{4,12},{6,14},{8,16},{10,18},{12,20},{14,22},{16,24},... | collective-permute-start | bytes 1265672 | tf_op jit(solution)/shard_map/ppermute | solution.py:577
  35.7 48.3 %collective-permute-start.5 = (bf16[1648,128]{1,0:T(8,128)(2,1)}, bf16[1648,128]{1,0:T(8,128)(2,1)S(1)}, u32[]{:S(2)}, u32[]{:S(2)}) collective-permute-start(bf16[1648,128]{1,0:T(8,128)(2,1)} %get-tuple-element.62), channel_id=1, source_target_pairs={{0,6},{2,8},{4,10},{6,12},{8,14},{10,16},{12,18},{14,20},{16,22},{... | collective-permute-start | bytes 1265672 | tf_op jit(solution)/shard_map/ppermute | solution.py:577
  37.6 46.3 %collective-permute-start.6 = (bf16[16,1664]{1,0:T(8,128)(2,1)S(1)}, bf16[16,1664]{1,0:T(8,128)(2,1)S(1)}, u32[]{:S(2)}, u32[]{:S(2)}) collective-permute-start(bf16[16,1664]{1,0:T(8,128)(2,1)S(1)} %copy-done.19), channel_id=1, source_target_pairs={{0,14},{2,16},{4,18},{6,20},{8,22},{10,24},{12,26},{14,28},{16,30}... | collective-permute-start | bytes 159752 | tf_op jit(solution)/shard_map/ppermute | solution.py:577
  83.9 15.3 %copy-start.9 = (bf16[16,1664]{1,0:T(8,128)(2,1)}, bf16[16,1664]{1,0:T(8,128)(2,1)S(1)}, u32[]{:S(2)}) copy-start(bf16[16,1664]{1,0:T(8,128)(2,1)S(1)} %collective-permute-done.6.refs_3_.refs_6_) | copy-start | bytes 159748
  84.0 11.5 %copy-start = (bf16[1648,128]{1,0:T(8,128)(2,1)}, bf16[1648,128]{1,0:T(8,128)(2,1)S(1)}, u32[]{:S(2)}) copy-start(bf16[1648,128]{1,0:T(8,128)(2,1)S(1)} %collective-permute-done.2.message.refs_4_) | copy-start | bytes 1265668
  84.0 13.4 %copy-start.1 = (bf16[1648,128]{1,0:T(8,128)(2,1)}, bf16[1648,128]{1,0:T(8,128)(2,1)S(1)}, u32[]{:S(2)}) copy-start(bf16[1648,128]{1,0:T(8,128)(2,1)S(1)} %collective-permute-done.3.message.refs_3_) | copy-start | bytes 1265668
  84.0 15.3 %copy-start.2 = (bf16[1648,128]{1,0:T(8,128)(2,1)}, bf16[1648,128]{1,0:T(8,128)(2,1)S(1)}, u32[]{:S(2)}) copy-start(bf16[1648,128]{1,0:T(8,128)(2,1)S(1)} %collective-permute-done.4.message.refs_2_) | copy-start | bytes 1265668
  84.0 15.3 %copy-start.3 = (bf16[1648,128]{1,0:T(8,128)(2,1)}, bf16[1648,128]{1,0:T(8,128)(2,1)S(1)}, u32[]{:S(2)}) copy-start(bf16[1648,128]{1,0:T(8,128)(2,1)S(1)} %collective-permute-done.5.message.refs_1_) | copy-start | bytes 1265668
  84.0 28.8 %collective-permute-start.7 = (bf16[1648,128]{1,0:T(8,128)(2,1)}, bf16[1648,128]{1,0:T(8,128)(2,1)S(1)}, u32[]{:S(2)}, u32[]{:S(2)}) collective-permute-start(bf16[1648,128]{1,0:T(8,128)(2,1)} %finish.3), channel_id=1, source_target_pairs={{0,2},{2,4},{4,6},{6,8},{8,10},{10,12},{12,14},{14,16},{16,18},{18... | collective-permute-start | bytes 1265672 | tf_op jit(solution)/shard_map/ppermute | solution.py:577
  94.7 14.2 %collective-permute-start.8 = (bf16[16,1664]{1,0:T(8,128)(2,1)}, bf16[16,1664]{1,0:T(8,128)(2,1)S(1)}, u32[]{:S(2)}, u32[]{:S(2)}) collective-permute-start(bf16[16,1664]{1,0:T(8,128)(2,1)} %get-tuple-element.74), channel_id=1, source_target_pairs={{0,4},{2,6},{4,8},{6,10},{8,12},{10,14},{12,16},{14,18},{16,20},{1... | collective-permute-start | bytes 159752 | tf_op jit(solution)/shard_map/ppermute | solution.py:577
  108.9 0.6 copy-start.10
  112.8 0.8 copy-start.4

commit v8 on v7

--- a/solution.py
+++ b/solution.py
@@ -18,7 +18,6 @@
 RAW = (7, 2)
 PARTS = 3
 SMALL = pl.CostEstimate(flops=1024, bytes_accessed=1024, transcendentals=0)
-STEP = pl.CostEstimate(flops=1024, bytes_accessed=8_000_000, transcendentals=0)
 
 epsilon = 1e-05
 HIGH = lax.Precision.HIGHEST
@@ -373,8 +372,9 @@
 
 
 def tail_rows(width):
-    pairs = (width // NSTATE + 2) // 2
-    return pairs, pairs * 2 * DRAFT
+    tiles = width // NSTATE
+    groups = tiles // 2 + 1
+    return groups, (groups + groups % 2) * DRAFT
 
 
 def finish_kernel(offsets, *refs):
@@ -384,7 +384,7 @@
     outs = refs[2 + n : 2 + 2 * n]
     loaded, sems = refs[-2:]
     width = loaded.shape[1]
-    pairs, _ = tail_rows(width)
+    groups, _ = tail_rows(width)
     copies = []
     for i, k in enumerate(offsets):
         copy = pltpu.make_async_copy(states.at[table[3, k]], loaded.at[i], sems.at[i])
@@ -392,18 +392,18 @@
         copies.append(copy)
     for i in range(n):
         low = corr[i][...].astype(F32)[DRAFT:]
-        low = jnp.concatenate(
-            [low, jnp.zeros((DRAFT, 2 * pairs * NSTATE - low.shape[1]), F32)], axis=1
-        )
-        for t in range(pairs):
-            block = jnp.concatenate(
-                [
-                    low[:, t * NSTATE : (t + 1) * NSTATE],
-                    low[:, (t + pairs) * NSTATE : (t + pairs + 1) * NSTATE],
-                ],
-                axis=0,
-            )
-            outs[i][width + t * 2 * DRAFT : width + (t + 1) * 2 * DRAFT] = block.astype(BF16)
+        half = iota((DRAFT, NSTATE), 0) < DRAFT // 2
+        tiles = [low[:, t * NSTATE : (t + 1) * NSTATE] for t in range(width // NSTATE + 1)]
+        packed = [
+            jnp.where(half, tiles[2 * g], pltpu.roll(tiles[2 * g + 1], DRAFT // 2, 0))
+            for g in range(groups - 1)
+        ]
+        packed.append(tiles[-1])
+        if groups % 2:
+            packed.append(jnp.zeros((DRAFT, NSTATE), F32))
+        for g in range(0, len(packed), 2):
+            block = jnp.concatenate(packed[g : g + 2], axis=0)
+            outs[i][width + g * DRAFT : width + (g + 2) * DRAFT] = block.astype(BF16)
         copies[i].wait()
         advance(corr[i], loaded.at[i], outs[i])
 
@@ -430,41 +430,42 @@
     return jnp.max(low[6:7]).astype(jnp.int32) - 1
 
 
-def merge_kernel(table, states, *refs):
-    n = 1 + len(RAW)
-    raws = refs[: n - 1]
-    corr = refs[n - 1 : 2 * n - 1]
-    _, kept, loaded, merged, sem_in, sem_out = refs[2 * n - 1 :]
+def merge_kernel(own, *refs):
+    table, states = refs[:2]
+    raw = refs[2]
+    corr = refs[3 : 4 + own]
+    _, kept, loaded, merged, sem_in, sem_out = refs[4 + own :]
     width = loaded.shape[0]
-    own = pltpu.make_async_copy(states.at[table[3, 0]], loaded, sem_in)
-    own.start()
+    if own:
+        copy = pltpu.make_async_copy(states.at[table[3, 0]], loaded, sem_in)
+        copy.start()
     slots = [mark_of(ref[:, width:].astype(F32)[DRAFT:]) for ref in corr]
 
     def put(i):
         return pltpu.make_async_copy(merged.at[i], kept.at[slots[i]], sem_out.at[i])
 
-    for i in range(n):
-        if i == 0:
-            own.wait()
+    for i in range(1 + own):
+        if i == 1:
+            copy.wait()
 
         @pl.when(slots[i] >= 0)
         def _(i=i):
-            advance(corr[i], raws[i - 1] if i > 0 else loaded, merged.at[i])
+            advance(corr[i], loaded if i == 1 else raw, merged.at[i])
             put(i).start()
 
-    for i in range(n):
+    for i in range(1 + own):
 
         @pl.when(slots[i] >= 0)
         def _(i=i):
             put(i).wait()
 
 
-def merge(count, table, states, raws, corr, kept):
+def merge(count, table, states, raw, corr, kept):
     width = states.shape[1]
-    n = 1 + len(RAW)
+    n = len(corr)
     return pl.pallas_call(
-        merge_kernel,
-        in_specs=[in_smem(), in_hbm()] + [in_vmem()] * (2 * n - 1) + [in_hbm()],
+        functools.partial(merge_kernel, n - 1),
+        in_specs=[in_smem(), in_hbm()] + [in_vmem()] * (1 + n) + [in_hbm()],
         out_specs=in_hbm(),
         out_shape=jax.ShapeDtypeStruct((count, width, NSTATE), BF16),
         scratch_shapes=[
@@ -473,62 +474,48 @@
             pltpu.SemaphoreType.DMA,
             pltpu.SemaphoreType.DMA((n,)),
         ],
-        input_output_aliases={1 + 2 * n: 0},
+        input_output_aliases={3 + n: 0},
         cost_estimate=SMALL,
         name="merge",
-    )(table, states, *raws, *corr, kept)
+    )(table, states, raw, *corr, kept)
 
 
 def halves(ref, width):
-    parts = [
-        ref[row : row + 2 * DRAFT].astype(F32)
-        for row in range(width, ref.shape[0], 2 * DRAFT)
-    ]
-    return [part[:DRAFT] for part in parts] + [part[DRAFT:] for part in parts]
-
-
-def place_kernel(width, message, *refs):
-    kept, sem = refs[-2:]
-    slot = mark_of(halves(message, width)[width // NSTATE])
-
-    @pl.when(slot >= 0)
-    def _():
-        copy = pltpu.make_async_copy(message.at[pl.ds(0, width)], kept.at[slot], sem)
-        copy.start()
-        copy.wait()
-
-
-def place(count, width, message, kept=None):
-    return pl.pallas_call(
-        functools.partial(place_kernel, width),
-        in_specs=[in_vmem()] + ([] if kept is None else [in_hbm()]),
-        out_specs=in_hbm(),
-        out_shape=jax.ShapeDtypeStruct((count, width, NSTATE), BF16),
-        input_output_aliases={} if kept is None else {1: 0},
-        scratch_shapes=[pltpu.SemaphoreType.DMA],
-        cost_estimate=STEP,
-        name="place",
-    )(message, *([] if kept is None else [kept]))
-
-
-def close_kernel(n, *refs):
+    groups, _ = tail_rows(width)
+    tiles = []
+    for row in range(width, ref.shape[0], 2 * DRAFT):
+        block = ref[row : row + 2 * DRAFT].astype(F32)
+        for part in (block[:DRAFT], block[DRAFT:]):
+            if len(tiles) < 2 * (groups - 1):
+                tiles += [part, pltpu.roll(part, DRAFT // 2, 0)]
+            else:
+                tiles.append(part)
+    return tiles[: 2 * groups - 1]
+
+
+def place_kernel(n, earlier, *refs):
     messages = refs[:n]
-    corr = refs[n : n + 1 + len(RAW)]
-    _, kept, out_inner, out_ssm, sem = refs[n + 1 + len(RAW) :]
+    out = len(refs) - 4
+    corr = refs[n : out - 3 * earlier]
+    kept, out_inner, out_ssm, sems = refs[out:]
     width = out_inner.shape[2]
     tiles = width // NSTATE
-    marks = []
-    for ref in messages:
-        lows = halves(ref, width)
-        marks.append((mark_of(lows[tiles]), lows))
-    last = marks[0][0]
-
-    def put():
-        return pltpu.make_async_copy(messages[0].at[pl.ds(0, width)], kept.at[last], sem)
-
-    @pl.when(last >= 0)
-    def _():
-        put().start()
+    if earlier:
+        out_inner[...] = refs[out - 2][...]
+        out_ssm[...] = refs[out - 1][...]
+    lows = [halves(ref, width) for ref in messages]
+    slots = [mark_of(low[tiles]) for low in lows]
+
+    def put(i):
+        return pltpu.make_async_copy(
+            messages[i].at[pl.ds(0, width)], kept.at[slots[i]], sems.at[i]
+        )
+
+    for i in range(n):
+
+        @pl.when(slots[i] >= 0)
+        def _(i=i):
+            put(i).start()
 
     def write_edges(slot, inner, low):
         out_inner[slot] = inner[: KCONV - 1].astype(BF16)
@@ -543,33 +530,37 @@
         def _(slot=slot, low=low):
             write_edges(slot, low[:, :width], low[:, width:])
 
-    for slot, lows in marks:
-
-        @pl.when(slot >= 0)
-        def _(slot=slot, lows=lows):
-            write_edges(slot, jnp.concatenate(lows[:tiles], axis=1), lows[tiles])
-
-    @pl.when(last >= 0)
-    def _():
-        put().wait()
-
-
-def close(count, width, messages, corr, kept):
+    for i in range(n):
+
+        @pl.when(slots[i] >= 0)
+        def _(i=i):
+            write_edges(slots[i], jnp.concatenate(lows[i][:tiles], axis=1), lows[i][tiles])
+
+    for i in range(n):
+
+        @pl.when(slots[i] >= 0)
+        def _(i=i):
+            put(i).wait()
+
+
+def place(count, width, messages, corr, earlier=()):
     n = len(messages)
+    inputs = [*messages, *corr]
     return pl.pallas_call(
-        functools.partial(close_kernel, n),
-        in_specs=[in_vmem()] * (n + len(corr)) + [in_hbm()],
+        functools.partial(place_kernel, n, 1 if earlier else 0),
+        in_specs=[in_vmem()] * len(inputs)
+        + ([in_hbm(), in_vmem(), in_vmem()] if earlier else []),
         out_specs=[in_hbm(), in_vmem(), in_vmem()],
         out_shape=[
             jax.ShapeDtypeStruct((count, width, NSTATE), BF16),
             jax.ShapeDtypeStruct((count, KCONV - 1, width), BF16),
             jax.ShapeDtypeStruct((count, KCONV - 1, 2 * NSTATE), BF16),
         ],
-        input_output_aliases={n + len(corr): 0},
-        scratch_shapes=[pltpu.SemaphoreType.DMA],
+        input_output_aliases={len(inputs): 0} if earlier else {},
+        scratch_shapes=[pltpu.SemaphoreType.DMA((n,))],
         cost_estimate=SMALL,
-        name="close",
-    )(*messages, *corr, kept)
+        name="place",
+    )(*inputs, *earlier)
 
 
 def moved(array, by):
@@ -659,14 +650,13 @@
     )
     corr[2] = moved(corr[2], 2)
     first = moved(first, 1)
-    sent = [corr[0], *(corr[k] for k in RAW)]
-    kept = place(count, width, sixth)
-    kept = place(count, width, fifth, kept)
-    kept = place(count, width, fourth, kept)
-    kept = place(count, width, third, kept)
-    kept = merge(count, table, flat, raws, sent, kept)
-    kept, kept_inner, kept_ssm = close(
-        count, width, (first, third, fourth, fifth, sixth), sent, kept
+    kept, edges, edges_ssm = place(
+        count, width, (sixth, fifth, fourth, third), (corr[0], corr[7])
+    )
+    kept = merge(count, table, flat, raws[0], (corr[7], corr[0]), kept)
+    kept = merge(count, table, flat, raws[1], (corr[2],), kept)
+    kept, kept_inner, kept_ssm = place(
+        count, width, (first,), (corr[2],), (kept, edges, edges_ssm)
     )
     return (hidden_out, kept.reshape(states_in.shape), kept_inner, kept_ssm)
 

time: 118 us -> 113 us (0.958)
  the two profiles are of different devices: /device:TPU:2 before, /device:TPU:0 now
where the time goes in v8:
time: 113 us; the launch traced here: 112 us
  waiting for transfers between devices  46.7 us (41%)
  Pallas kernels  33.7 us (30%)
  starting transfers between devices  20.7 us (18%)
  blocking collectives  6.57 us (6%)
  other arithmetic  2.09 us (2%)
  local copies, waits for them, and re-layouts  1.45 us (1%)
    ppermute x9, waiting for transfers between devices, moved(): lax.ppermute(array, 'req', [(i, (i + by) % length) for i in range(length)])  46.7 us
    ppermute x9, starting transfers between devices, moved(): lax.ppermute(array, 'req', [(i, (i + by) % length) for i in range(length)])  20.7 us
    pallas_call x1, Pallas kernels, front(): pl.pallas_call(functools.partial(front_kernel, count, heads), grid=(tiles...  12.1 us
    pallas_call x2, Pallas kernels, finish(): pl.pallas_call(functools.partial(finish_kernel, offsets), in_specs=[in_sm...  7.57 us
    pallas_call x2, Pallas kernels, place(): pl.pallas_call(functools.partial(place_kernel, n, 1 if earlier else 0), i...  5.63 us
    pallas_call x2, Pallas kernels, merge(): pl.pallas_call(functools.partial(merge_kernel, n - 1), in_specs=[in_smem(...  5.53 us
    pallas_call x1, Pallas kernels, pick(): pl.pallas_call(functools.partial(pick_kernel, count, peers), in_specs=[in...  2.91 us
    all_gather x1, blocking collectives, local(): lax.all_gather(ready_ssm, 'head', axis=0, tiled=False)  2.49 us
  transfers between devices with their start and end apart: 9, of which 5 were waited for; matrix products, arithmetic and copies ran while one was open for 2% of the time, Pallas kernels for 25%

profile of v8, /device:TPU:0, one launch (start us, length us, event | category | flops | bytes accessed | tf_op | source)
XLA Modules:
  0.0 112.1 jit_solution(15858243061588542252)
XLA Ops:
  0.7 2.9 %pick.1 = (bf16[1536,128]{1,0:T(8,128)(2,1)}, bf16[1536,128]{1,0:T(8,128)(2,1)}, s32[4,8]{1,0:T(4,128)}) custom-call(s32[6]{0:T(128)} %destination.1, bf16[6,1536,128]{2,1,0:T(8,128)(2,1)} %bitcast.9), custom_call_target="tpu_custom_call" | custom-call | flops 1024 | bytes 1024 | tf_op jit(solution)/shard_map/pick/pallas_call | solution.py:347
  3.6 5.0 %collective-permute-start = (bf16[1536,128]{1,0:T(8,128)(2,1)}, bf16[1536,128]{1,0:T(8,128)(2,1)S(1)}, u32[]{:S(2)}, u32[]{:S(2)}) collective-permute-start(bf16[1536,128]{1,0:T(8,128)(2,1)} %get-tuple-element.51), channel_id=1, source_target_pairs={{0,14},{2,16},{4,18},{6,20},{8,22},{10,24},{12,26},{14,28},{16,30}... | collective-permute-start | bytes 1179656 | tf_op jit(solution)/shard_map/ppermute | solution.py:568
  8.6 1.5 %collective-permute-start.1 = (bf16[1536,128]{1,0:T(8,128)(2,1)}, bf16[1536,128]{1,0:T(8,128)(2,1)S(1)}, u32[]{:S(2)}, u32[]{:S(2)}) collective-permute-start(bf16[1536,128]{1,0:T(8,128)(2,1)} %get-tuple-element.52), channel_id=1, source_target_pairs={{0,4},{2,6},{4,8},{6,10},{8,12},{10,14},{12,16},{14,18},{16,20},{1... | collective-permute-start | bytes 1179656 | tf_op jit(solution)/shard_map/ppermute | solution.py:568
  10.2 2.0 %all-gather = bf16[96,768]{1,0:T(8,128)(2,1)} all-gather(bf16[48,768]{1,0:T(8,128)(2,1)S(1)} %copy-done.8), channel_id=2, replica_groups=mesh['req'=16,'head'=2] {'head'}, dimensions={0}, use_global_device_ids=true | all-gather | bytes 221184 | tf_op jit(solution)/shard_map/all_gather | solution.py:611
  12.2 0.6 pad_maximum_fusion.1.head_rows
  12.8 2.5 %all-gather.1 = bf16[3072,128]{1,0:T(8,128)(2,1)} all-gather(bf16[1536,128]{1,0:T(8,128)(2,1)S(1)} %copy-done.6), channel_id=3, replica_groups=mesh['req'=16,'head'=2] {'head'}, dimensions={0}, use_global_device_ids=true | all-gather | bytes 1179648 | tf_op jit(solution)/shard_map/all_gather | solution.py:616
  15.3 0.6 pad_maximum_fusion.vectors.vector_tile
  16.0 12.1 %front.1 = (f32[48,896]{1,0:T(8,128)}, f32[48,896]{1,0:T(8,128)}, bf16[16,1664]{1,0:T(8,128)(2,1)}, bf16[16,1664]{1,0:T(8,128)(2,1)}, bf16[16,1664]{1,0:T(8,128)...) custom-call(s32[4,8]{1,0:T(4,128)} %get-tuple-element.68.table.refs_, ...), custom_call_target="tpu_custom_call" | custom-call | flops 1024 | bytes 1024 | tf_op jit(solution)/shard_map/front/pallas_call | solution.py:287
  28.0 4.6 %finish.2 = (bf16[1600,128]{1,0:T(8,128)(2,1)}, bf16[1600,128]{1,0:T(8,128)(2,1)}, bf16[1600,128]{1,0:T(8,128)(2,1)}, bf16[1600,128]{1,0:T(8,128)(2,1)}) custom-call(s32[4,8]{1,0:T(4,128)} %get-tuple-element.68.table.refs_0_, bf16[6,1536,128]{2,1,0:T(8,128)(2,1)} %bitcast.11, bf16[16,1664]{1,0:T(8,128)(2,1)} %get-tuple-element.54.refs_2_, ...), custom_call_target="tpu_custom_call" | custom-call | flops 1024 | bytes 1024 | tf_op jit(solution)/shard_map/finish/pallas_call | solution.py:415
  32.6 0.0 collective-permute-done.refs_2_
  32.7 3.9 %collective-permute-start.2 = (bf16[1600,128]{1,0:T(8,128)(2,1)}, bf16[1600,128]{1,0:T(8,128)(2,1)S(1)}, u32[]{:S(2)}, u32[]{:S(2)}) collective-permute-start(bf16[1600,128]{1,0:T(8,128)(2,1)} %get-tuple-element.62), channel_id=1, source_target_pairs={{0,12},{2,14},{4,16},{6,18},{8,20},{10,22},{12,24},{14,26},{16,28}... | collective-permute-start | bytes 1228808 | tf_op jit(solution)/shard_map/ppermute | solution.py:568
  36.6 2.4 %collective-permute-start.4 = (bf16[1600,128]{1,0:T(8,128)(2,1)}, bf16[1600,128]{1,0:T(8,128)(2,1)S(1)}, u32[]{:S(2)}, u32[]{:S(2)}) collective-permute-start(bf16[1600,128]{1,0:T(8,128)(2,1)} %get-tuple-element.64), channel_id=1, source_target_pairs={{0,8},{2,10},{4,12},{6,14},{8,16},{10,18},{12,20},{14,22},{16,24},... | collective-permute-start | bytes 1228808 | tf_op jit(solution)/shard_map/ppermute | solution.py:568
  39.0 3.6 %collective-permute-start.5 = (bf16[1600,128]{1,0:T(8,128)(2,1)}, bf16[1600,128]{1,0:T(8,128)(2,1)S(1)}, u32[]{:S(2)}, u32[]{:S(2)}) collective-permute-start(bf16[1600,128]{1,0:T(8,128)(2,1)} %get-tuple-element.65), channel_id=1, source_target_pairs={{0,6},{2,8},{4,10},{6,12},{8,14},{10,16},{12,18},{14,20},{16,22},{... | collective-permute-start | bytes 1228808 | tf_op jit(solution)/shard_map/ppermute | solution.py:568
  42.6 2.5 %collective-permute-start.6 = (bf16[16,1664]{1,0:T(8,128)(2,1)S(1)}, bf16[16,1664]{1,0:T(8,128)(2,1)S(1)}, u32[]{:S(2)}, u32[]{:S(2)}) collective-permute-start(bf16[16,1664]{1,0:T(8,128)(2,1)S(1)} %copy-done.20), channel_id=1, source_target_pairs={{0,14},{2,16},{4,18},{6,20},{8,22},{10,24},{12,26},{14,28},{16,30}... | collective-permute-start | bytes 159752 | tf_op jit(solution)/shard_map/ppermute | solution.py:568
  45.1 2.0 %all-gather.2 = f32[96,896]{1,0:T(8,128)S(1)} all-gather(f32[48,896]{1,0:T(8,128)S(1)} %copy-done.12), channel_id=4, replica_groups=mesh['req'=16,'head'=2] {'head'}, dimensions={0}, use_global_device_ids=true | all-gather | bytes 516096 | tf_op jit(solution)/shard_map/all_gather | solution.py:641
  47.2 3.0 %finish.3 = bf16[1600,128]{1,0:T(8,128)(2,1)} custom-call(s32[4,8]{1,0:T(4,128)} %get-tuple-element.68.table.refs_0_, bf16[6,1536,128]{2,1,0:T(8,128)(2,1)} %bitcast.12, bf16[16,1664]{1,0:T(8,128)(2,1)} %get-tuple-element.69.refs_2_), custom_call_target="tpu_custom_call" | custom-call | flops 1024 | bytes 1024 | tf_op jit(solution)/shard_map/finish/pallas_call | solution.py:415
  50.2 27.6 %collective-permute-done.6.refs_5_.refs_3_ = bf16[16,1664]{1,0:T(8,128)(2,1)S(1)} collective-permute-done((bf16[16,1664]{1,0:T(8,128)(2,1)S(1)}, bf16[16,1664]{1,0:T(8,128)(2,1)S(1)}, u32[]{:S(2)}, u32[]{:S(2)}) %collective-permute-start.6) | collective-permute-done | bytes 53280 | tf_op jit(solution)/shard_map/ppermute | solution.py:568
  77.8 5.3 %collective-permute-done.2.refs_0_ = bf16[1600,128]{1,0:T(8,128)(2,1)S(1)} collective-permute-done((bf16[1600,128]{1,0:T(8,128)(2,1)}, bf16[1600,128]{1,0:T(8,128)(2,1)S(1)}, u32[]{:S(2)}, u32[]{:S(2)}) %collective-permute-start.2) | collective-permute-done | bytes 409632 | tf_op jit(solution)/shard_map/ppermute | solution.py:568
  83.1 9.5 %collective-permute-done.3.refs_1_ = bf16[1600,128]{1,0:T(8,128)(2,1)S(1)} collective-permute-done((bf16[1600,128]{1,0:T(8,128)(2,1)}, bf16[1600,128]{1,0:T(8,128)(2,1)S(1)}, u32[]{:S(2)}, u32[]{:S(2)}) %collective-permute-start.3) | collective-permute-done | bytes 409632 | tf_op jit(solution)/shard_map/ppermute | solution.py:568
  92.7 0.0 collective-permute-done.4.refs_2_
  92.7 0.1 collective-permute-start.7
  92.8 0.1 fusion.5
  92.9 1.7 %collective-permute-start.8 = (bf16[16,1664]{1,0:T(8,128)(2,1)S(1)}, bf16[16,1664]{1,0:T(8,128)(2,1)S(1)}, u32[]{:S(2)}, u32[]{:S(2)}) collective-permute-start(bf16[16,1664]{1,0:T(8,128)(2,1)S(1)} %copy-done.19), channel_id=1, source_target_pairs={{0,4},{2,6},{4,8},{6,10},{8,12},{10,14},{12,16},{14,18},{16,20},{1... | collective-permute-start | bytes 159752 | tf_op jit(solution)/shard_map/ppermute | solution.py:568
  94.6 0.7 fusion.2
  95.4 3.1 %place.2 = (bf16[6,1536,128]{2,1,0:T(8,128)(2,1)}, bf16[6,3,1536]{2,1,0:T(4,128)(2,1)}, bf16[6,3,256]{2,1,0:T(4,128)(2,1)}) custom-call(bf16[1600,128]{1,0:T(8,128)(2,1)} %copy-done, bf16[1600,128]{1,0:T(8,128)(2,1)} %copy-done.1, bf16[1600,128]{1,0:T(8,128)(2,1)} %copy-done.2, bf16[1600,128]{1,0:T(8,128)(2,1)} %copy-done.3, ...), custom_call_target="tpu_custom_call" | custom-call | flops 1024 | bytes 1024 | tf_op jit(solution)/shard_map/place/pallas_call | solution.py:549
  98.5 3.2 %merge.2.refs_4_ = bf16[6,1536,128]{2,1,0:T(8,128)(2,1)} custom-call(s32[4,8]{1,0:T(4,128)} %get-tuple-element.68.table.refs_0_, bf16[6,1536,128]{2,1,0:T(8,128)(2,1)} %bitcast.13, bf16[1536,128]{1,0:T(8,128)(2,1)} %copy-done.5, bf16[16,1664]{1,0:T(8,128)(2,1)} %copy-done.9, ...), custom_call_target="tpu_custom_call", output_to_operand_aliasing={{}: (5, {})} | custom-call | flops 1024 | bytes 1024 | tf_op jit(solution)/shard_map/merge/pallas_call | solution.py:466
  101.7 3.3 %collective-permute-done.8.refs_3_.refs_1_ = bf16[16,1664]{1,0:T(8,128)(2,1)S(1)} collective-permute-done((bf16[16,1664]{1,0:T(8,128)(2,1)S(1)}, bf16[16,1664]{1,0:T(8,128)(2,1)S(1)}, u32[]{:S(2)}, u32[]{:S(2)}) %collective-permute-start.8) | collective-permute-done | bytes 53280 | tf_op jit(solution)/shard_map/ppermute | solution.py:568
  105.0 0.6 copy-done.10
  105.6 2.3 %merge.3.refs_2_ = bf16[6,1536,128]{2,1,0:T(8,128)(2,1)} custom-call(s32[4,8]{1,0:T(4,128)} %get-tuple-element.68.table.refs_0_, bf16[6,1536,128]{2,1,0:T(8,128)(2,1)} %bitcast.14, bf16[1536,128]{1,0:T(8,128)(2,1)} %copy-done.7, bf16[16,1664]{1,0:T(8,128)(2,1)} %copy-done.10, bf16[6,1536,128]{2,1,0:T(8,128)(2,1)} %merge.2.refs_4_), custom_call_target="tpu_custom_call", output_to_operand_aliasing={{}: (4, {})} | custom-call | flops 1024 | bytes 1024 | tf_op jit(solution)/shard_map/merge/pallas_call | solution.py:466
  107.9 0.9 collective-permute-done.7.refs_0_
  108.8 0.7 copy-done.4
  109.6 2.6 %place.3 = (bf16[6,1536,128]{2,1,0:T(8,128)(2,1)}, bf16[6,3,1536]{2,1,0:T(4,128)(2,1)}, bf16[6,3,256]{2,1,0:T(4,128)(2,1)}) custom-call(bf16[1600,128]{1,0:T(8,128)(2,1)} %copy-done.4, bf16[16,1664]{1,0:T(8,128)(2,1)} %copy-done.10, bf16[6,1536,128]{2,1,0:T(8,128)(2,1)} %merge.3.refs_2_, ...), custom_call_target="tpu_custom_call", output_to_operand_aliasing={{0}: (2, {})} | custom-call | flops 1024 | bytes 1024 | tf_op jit(solution)/shard_map/place/pallas_call | solution.py:549
  (47 shorter events, 0.1 us)
Async XLA Ops:
  0.6 9.5 %copy-start.13 = (f32[1536]{0:T(1024)S(1)}, f32[1536]{0:T(1024)}, u32[]{:S(2)}) copy-start(f32[1536]{0:T(1024)} %param.22) | copy-start | bytes 18436
  0.6 9.5 %copy-start.14 = (f32[1536]{0:T(1024)S(1)}, f32[1536]{0:T(1024)}, u32[]{:S(2)}) copy-start(f32[1536]{0:T(1024)} %param.31) | copy-start | bytes 18436
  0.7 9.5 %copy-start.15 = (f32[1536]{0:T(1024)S(1)}, f32[1536]{0:T(1024)}, u32[]{:S(2)}) copy-start(f32[1536]{0:T(1024)} %param.34) | copy-start | bytes 18436
  0.7 9.5 %copy-start.8 = (bf16[48,768]{1,0:T(8,128)(2,1)S(1)}, bf16[48,768]{1,0:T(8,128)(2,1)}, u32[]{:S(2)}) copy-start(bf16[48,768]{1,0:T(8,128)(2,1)} %param.21) | copy-start | bytes 221188
  0.7 12.2 %copy-start.6 = (bf16[1536,128]{1,0:T(8,128)(2,1)S(1)}, bf16[1536,128]{1,0:T(8,128)(2,1)}, u32[]{:S(2)}) copy-start(bf16[1536,128]{1,0:T(8,128)(2,1)} %param.25) | copy-start | bytes 1179652
  0.7 11.5 %copy-start.16 = (f32[24]{0:T(128)S(1)}, f32[24]{0:T(128)}, u32[]{:S(2)}) copy-start(f32[24]{0:T(128)} %param.29) | copy-start | bytes 292
  0.7 11.5 %copy-start.17 = (f32[24]{0:T(128)S(1)}, f32[24]{0:T(128)}, u32[]{:S(2)}) copy-start(f32[24]{0:T(128)} %param.28) | copy-start | bytes 292
  0.7 11.5 %copy-start.18 = (f32[24]{0:T(128)S(1)}, f32[24]{0:T(128)}, u32[]{:S(2)}) copy-start(f32[24]{0:T(128)} %param.27) | copy-start | bytes 292
  3.6 29.0 %collective-permute-start = (bf16[1536,128]{1,0:T(8,128)(2,1)}, bf16[1536,128]{1,0:T(8,128)(2,1)S(1)}, u32[]{:S(2)}, u32[]{:S(2)}) collective-permute-start(bf16[1536,128]{1,0:T(8,128)(2,1)} %get-tuple-element.51), channel_id=1, source_target_pairs={{0,14},{2,16},{4,18},{6,20},{8,22},{10,24},{12,26},{14,28},{16,30}... | collective-permute-start | bytes 1179656 | tf_op jit(solution)/shard_map/ppermute | solution.py:568
  8.6 24.1 %collective-permute-start.1 = (bf16[1536,128]{1,0:T(8,128)(2,1)}, bf16[1536,128]{1,0:T(8,128)(2,1)S(1)}, u32[]{:S(2)}, u32[]{:S(2)}) collective-permute-start(bf16[1536,128]{1,0:T(8,128)(2,1)} %get-tuple-element.52), channel_id=1, source_target_pairs={{0,4},{2,6},{4,8},{6,10},{8,12},{10,14},{12,16},{14,18},{16,20},{1... | collective-permute-start | bytes 1179656 | tf_op jit(solution)/shard_map/ppermute | solution.py:568
  28.0 14.6 %copy-start.20 = (bf16[16,1664]{1,0:T(8,128)(2,1)S(1)}, bf16[16,1664]{1,0:T(8,128)(2,1)}, u32[]{:S(2)}) copy-start(bf16[16,1664]{1,0:T(8,128)(2,1)} %get-tuple-element.66) | copy-start | bytes 159748
  28.0 17.1 %copy-start.12 = (f32[48,896]{1,0:T(8,128)S(1)}, f32[48,896]{1,0:T(8,128)}, u32[]{:S(2)}) copy-start(f32[48,896]{1,0:T(8,128)} %get-tuple-element.50) | copy-start | bytes 516100
  28.0 64.7 %copy-start.11 = (f32[48,896]{1,0:T(8,128)S(1)}, f32[48,896]{1,0:T(8,128)}, u32[]{:S(2)}) copy-start(f32[48,896]{1,0:T(8,128)} %get-tuple-element.49) | copy-start | bytes 516100
  32.6 60.3 %copy-start.19 = (bf16[16,1664]{1,0:T(8,128)(2,1)S(1)}, bf16[16,1664]{1,0:T(8,128)(2,1)}, u32[]{:S(2)}) copy-start(bf16[16,1664]{1,0:T(8,128)(2,1)} %get-tuple-element.71) | copy-start | bytes 159748
  32.7 65.8 %copy-start.5 = (bf16[1536,128]{1,0:T(8,128)(2,1)}, bf16[1536,128]{1,0:T(8,128)(2,1)S(1)}, u32[]{:S(2)}) copy-start(bf16[1536,128]{1,0:T(8,128)(2,1)S(1)} %collective-permute-done.refs_2_) | copy-start | bytes 1179652
  32.7 65.8 %copy-start.7 = (bf16[1536,128]{1,0:T(8,128)(2,1)}, bf16[1536,128]{1,0:T(8,128)(2,1)S(1)}, u32[]{:S(2)}) copy-start(bf16[1536,128]{1,0:T(8,128)(2,1)S(1)} %collective-permute-done.1.refs_2_) | copy-start | bytes 1179652
  32.7 50.4 %collective-permute-start.2 = (bf16[1600,128]{1,0:T(8,128)(2,1)}, bf16[1600,128]{1,0:T(8,128)(2,1)S(1)}, u32[]{:S(2)}, u32[]{:S(2)}) collective-permute-start(bf16[1600,128]{1,0:T(8,128)(2,1)} %get-tuple-element.62), channel_id=1, source_target_pairs={{0,12},{2,14},{4,16},{6,18},{8,20},{10,22},{12,24},{14,26},{16,28}... | collective-permute-start | bytes 1228808 | tf_op jit(solution)/shard_map/ppermute | solution.py:568
  36.6 56.1 %collective-permute-start.3 = (bf16[1600,128]{1,0:T(8,128)(2,1)}, bf16[1600,128]{1,0:T(8,128)(2,1)S(1)}, u32[]{:S(2)}, u32[]{:S(2)}) collective-permute-start(bf16[1600,128]{1,0:T(8,128)(2,1)} %get-tuple-element.63), channel_id=1, source_target_pairs={{0,10},{2,12},{4,14},{6,16},{8,18},{10,20},{12,22},{14,24},{16,26}... | collective-permute-start | bytes 1228808 | tf_op jit(solution)/shard_map/ppermute | solution.py:568
  36.6 56.1 %collective-permute-start.4 = (bf16[1600,128]{1,0:T(8,128)(2,1)}, bf16[1600,128]{1,0:T(8,128)(2,1)S(1)}, u32[]{:S(2)}, u32[]{:S(2)}) collective-permute-start(bf16[1600,128]{1,0:T(8,128)(2,1)} %get-tuple-element.64), channel_id=1, source_target_pairs={{0,8},{2,10},{4,12},{6,14},{8,16},{10,18},{12,20},{14,22},{16,24},... | collective-permute-start | bytes 1228808 | tf_op jit(solution)/shard_map/ppermute | solution.py:568
  39.0 53.7 %collective-permute-start.5 = (bf16[1600,128]{1,0:T(8,128)(2,1)}, bf16[1600,128]{1,0:T(8,128)(2,1)S(1)}, u32[]{:S(2)}, u32[]{:S(2)}) collective-permute-start(bf16[1600,128]{1,0:T(8,128)(2,1)} %get-tuple-element.65), channel_id=1, source_target_pairs={{0,6},{2,8},{4,10},{6,12},{8,14},{10,16},{12,18},{14,20},{16,22},{... | collective-permute-start | bytes 1228808 | tf_op jit(solution)/shard_map/ppermute | solution.py:568
  42.6 35.2 %collective-permute-start.6 = (bf16[16,1664]{1,0:T(8,128)(2,1)S(1)}, bf16[16,1664]{1,0:T(8,128)(2,1)S(1)}, u32[]{:S(2)}, u32[]{:S(2)}) collective-permute-start(bf16[16,1664]{1,0:T(8,128)(2,1)S(1)} %copy-done.20), channel_id=1, source_target_pairs={{0,14},{2,16},{4,18},{6,20},{8,22},{10,24},{12,26},{14,28},{16,30}... | collective-permute-start | bytes 159752 | tf_op jit(solution)/shard_map/ppermute | solution.py:568
  77.8 17.5 %copy-start.9 = (bf16[16,1664]{1,0:T(8,128)(2,1)}, bf16[16,1664]{1,0:T(8,128)(2,1)S(1)}, u32[]{:S(2)}) copy-start(bf16[16,1664]{1,0:T(8,128)(2,1)S(1)} %collective-permute-done.6.refs_5_.refs_3_) | copy-start | bytes 159748
  83.1 12.2 %copy-start = (bf16[1600,128]{1,0:T(8,128)(2,1)}, bf16[1600,128]{1,0:T(8,128)(2,1)S(1)}, u32[]{:S(2)}) copy-start(bf16[1600,128]{1,0:T(8,128)(2,1)S(1)} %collective-permute-done.2.refs_0_) | copy-start | bytes 1228804
  92.7 2.7 %copy-start.1 = (bf16[1600,128]{1,0:T(8,128)(2,1)}, bf16[1600,128]{1,0:T(8,128)(2,1)S(1)}, u32[]{:S(2)}) copy-start(bf16[1600,128]{1,0:T(8,128)(2,1)S(1)} %collective-permute-done.3.refs_1_) | copy-start | bytes 1228804
  92.7 2.7 %copy-start.2 = (bf16[1600,128]{1,0:T(8,128)(2,1)}, bf16[1600,128]{1,0:T(8,128)(2,1)S(1)}, u32[]{:S(2)}) copy-start(bf16[1600,128]{1,0:T(8,128)(2,1)S(1)} %collective-permute-done.4.refs_2_) | copy-start | bytes 1228804
  92.7 2.7 %copy-start.3 = (bf16[1600,128]{1,0:T(8,128)(2,1)}, bf16[1600,128]{1,0:T(8,128)(2,1)S(1)}, u32[]{:S(2)}) copy-start(bf16[1600,128]{1,0:T(8,128)(2,1)S(1)} %collective-permute-done.5.refs_3_) | copy-start | bytes 1228804
  92.7 16.1 %collective-permute-start.7 = (bf16[1600,128]{1,0:T(8,128)(2,1)}, bf16[1600,128]{1,0:T(8,128)(2,1)S(1)}, u32[]{:S(2)}, u32[]{:S(2)}) collective-permute-start(bf16[1600,128]{1,0:T(8,128)(2,1)} %finish.3), channel_id=1, source_target_pairs={{0,2},{2,4},{4,6},{6,8},{8,10},{10,12},{12,14},{14,16},{16,18},{18... | collective-permute-start | bytes 1228808 | tf_op jit(solution)/shard_map/ppermute | solution.py:568
  92.9 12.0 %collective-permute-start.8 = (bf16[16,1664]{1,0:T(8,128)(2,1)S(1)}, bf16[16,1664]{1,0:T(8,128)(2,1)S(1)}, u32[]{:S(2)}, u32[]{:S(2)}) collective-permute-start(bf16[16,1664]{1,0:T(8,128)(2,1)S(1)} %copy-done.19), channel_id=1, source_target_pairs={{0,4},{2,6},{4,8},{6,10},{8,12},{10,14},{12,16},{14,18},{16,20},{1... | collective-permute-start | bytes 159752 | tf_op jit(solution)/shard_map/ppermute | solution.py:568
  105.0 0.6 copy-start.10
  108.8 0.7 copy-start.4

commit v9 on v8

--- a/solution.py
+++ b/solution.py
@@ -17,6 +17,7 @@
 EXTRA = NSTATE
 RAW = (7, 2)
 PARTS = 3
+ROOM = 12 * 1024 * 1024
 SMALL = pl.CostEstimate(flops=1024, bytes_accessed=1024, transcendentals=0)
 
 epsilon = 1e-05
@@ -422,6 +423,7 @@
             pltpu.SemaphoreType.DMA((n,)),
         ],
         cost_estimate=SMALL,
+        compiler_params=pltpu.CompilerParams(vmem_limit_bytes=ROOM),
         name="finish",
     )(table, states, *[corr[k] for k in offsets])
 
@@ -476,6 +478,7 @@
         ],
         input_output_aliases={3 + n: 0},
         cost_estimate=SMALL,
+        compiler_params=pltpu.CompilerParams(vmem_limit_bytes=ROOM),
         name="merge",
     )(table, states, raw, *corr, kept)
 
@@ -559,6 +562,7 @@
         input_output_aliases={len(inputs): 0} if earlier else {},
         scratch_shapes=[pltpu.SemaphoreType.DMA((n,))],
         cost_estimate=SMALL,
+        compiler_params=pltpu.CompilerParams(vmem_limit_bytes=ROOM),
         name="place",
     )(*inputs, *earlier)
 
@@ -645,10 +649,11 @@
     scale = lax.rsqrt(total[:, half : half + 1] / DINNER + epsilon)
     hidden_out = (hidden_in.astype(F32) + total[:, :half] * scale).astype(BF16)
 
-    sixth, fifth, fourth, third, corr[7], corr[2], first = lax.optimization_barrier(
-        (sixth, fifth, fourth, third, corr[7], corr[2], first)
-    )
+    corr[7], corr[2] = lax.optimization_barrier((corr[7], corr[2]))
     corr[2] = moved(corr[2], 2)
+    sixth, fifth, fourth, third, corr[7], first = lax.optimization_barrier(
+        (sixth, fifth, fourth, third, corr[7], first)
+    )
     first = moved(first, 1)
     kept, edges, edges_ssm = place(
         count, width, (sixth, fifth, fourth, third), (corr[0], corr[7])

time: 113 us -> 113 us (level)
  waiting for transfers between devices: 46.7 us -> 54.2 us
  Pallas kernels: 33.7 us -> 26.7 us
  starting transfers between devices: 20.7 us -> 17 us
  local copies, waits for them, and re-layouts: 1.45 us -> 4.82 us
    ppermute x9, waiting for transfers between devices: 46.7 us -> 54.2 us  [moved(): lax.ppermute(array, 'req', [(i, (i + by) % length) for i in range(length)])]
    ppermute x9, starting transfers between devices: 20.7 us -> 17 us  [moved(): lax.ppermute(array, 'req', [(i, (i + by) % length) for i in range(length)])]
    unnamed x42 -> x44, local copies, waits for them, and re-layouts: 1.43 us -> 4.8 us
    pallas_call x2, Pallas kernels: 5.53 us -> 2.78 us  [merge(): pl.pallas_call(functools.partial(merge_kernel, n - 1), in_specs=[in_smem(...]
    pallas_call x2, Pallas kernels: 7.57 us -> 5.16 us  [finish(): pl.pallas_call(functools.partial(finish_kernel, offsets), in_specs=[in_sm...]
    pallas_call x2, Pallas kernels: 5.63 us -> 3.94 us  [place(): pl.pallas_call(functools.partial(place_kernel, n, 1 if earlier else 0), i...]
  transfers between devices with their start and end apart: 9 -> 9, of which waited for: 5 -> 5; matrix products, arithmetic and copies ran while one was open for 2% -> 2% of each run, Pallas kernels for 25% -> 20%
where the time goes in v9:
time: 113 us; the launch traced here: 112 us
  waiting for transfers between devices  54.2 us (48%)
  Pallas kernels  26.7 us (24%)
  starting transfers between devices  17 us (15%)
  blocking collectives  6.78 us (6%)
  local copies, waits for them, and re-layouts  4.82 us (4%)
  other arithmetic  2.07 us (2%)
    ppermute x9, waiting for transfers between devices, moved(): lax.ppermute(array, 'req', [(i, (i + by) % length) for i in range(length)])  54.2 us
    ppermute x9, starting transfers between devices, moved(): lax.ppermute(array, 'req', [(i, (i + by) % length) for i in range(length)])  17 us
    pallas_call x1, Pallas kernels, front(): pl.pallas_call(functools.partial(front_kernel, count, heads), grid=(tiles...  11.9 us
    pallas_call x2, Pallas kernels, finish(): pl.pallas_call(functools.partial(finish_kernel, offsets), in_specs=[in_sm...  5.16 us
    unnamed x44, local copies, waits for them, and re-layouts  4.8 us
    pallas_call x2, Pallas kernels, place(): pl.pallas_call(functools.partial(place_kernel, n, 1 if earlier else 0), i...  3.94 us
    pallas_call x1, Pallas kernels, pick(): pl.pallas_call(functools.partial(pick_kernel, count, peers), in_specs=[in...  2.9 us
    pallas_call x2, Pallas kernels, merge(): pl.pallas_call(functools.partial(merge_kernel, n - 1), in_specs=[in_smem(...  2.78 us
  transfers between devices with their start and end apart: 9, of which 5 were waited for; matrix products, arithmetic and copies ran while one was open for 2% of the time, Pallas kernels for 20%

profile of v9, /device:TPU:0, one launch (start us, length us, event | category | flops | bytes accessed | tf_op | source)
XLA Modules:
  0.0 112.4 jit_solution(13646863566580686301)
XLA Ops:
  0.7 2.9 %pick.1 = (bf16[1536,128]{1,0:T(8,128)(2,1)}, bf16[1536,128]{1,0:T(8,128)(2,1)}, s32[4,8]{1,0:T(4,128)}) custom-call(s32[6]{0:T(128)} %destination.1, bf16[6,1536,128]{2,1,0:T(8,128)(2,1)} %bitcast.9), custom_call_target="tpu_custom_call" | custom-call | flops 1024 | bytes 1024 | tf_op jit(solution)/shard_map/pick/pallas_call | solution.py:348
  3.6 5.0 %collective-permute-start = (bf16[1536,128]{1,0:T(8,128)(2,1)}, bf16[1536,128]{1,0:T(8,128)(2,1)S(1)}, u32[]{:S(2)}, u32[]{:S(2)}) collective-permute-start(bf16[1536,128]{1,0:T(8,128)(2,1)} %get-tuple-element.52), channel_id=1, source_target_pairs={{0,14},{2,16},{4,18},{6,20},{8,22},{10,24},{12,26},{14,28},{16,30}... | collective-permute-start | bytes 1179656 | tf_op jit(solution)/shard_map/ppermute | solution.py:572
  8.6 1.5 %collective-permute-start.1 = (bf16[1536,128]{1,0:T(8,128)(2,1)}, bf16[1536,128]{1,0:T(8,128)(2,1)S(1)}, u32[]{:S(2)}, u32[]{:S(2)}) collective-permute-start(bf16[1536,128]{1,0:T(8,128)(2,1)} %get-tuple-element.53), channel_id=1, source_target_pairs={{0,4},{2,6},{4,8},{6,10},{8,12},{10,14},{12,16},{14,18},{16,20},{1... | collective-permute-start | bytes 1179656 | tf_op jit(solution)/shard_map/ppermute | solution.py:572
  10.2 2.0 %all-gather = bf16[96,768]{1,0:T(8,128)(2,1)} all-gather(bf16[48,768]{1,0:T(8,128)(2,1)S(1)} %copy-done.13), channel_id=2, replica_groups=mesh['req'=16,'head'=2] {'head'}, dimensions={0}, use_global_device_ids=true | all-gather | bytes 221184 | tf_op jit(solution)/shard_map/all_gather | solution.py:615
  12.2 0.6 pad_maximum_fusion.1.head_rows
  12.8 2.5 %all-gather.1 = bf16[3072,128]{1,0:T(8,128)(2,1)} all-gather(bf16[1536,128]{1,0:T(8,128)(2,1)S(1)} %copy-done.12), channel_id=3, replica_groups=mesh['req'=16,'head'=2] {'head'}, dimensions={0}, use_global_device_ids=true | all-gather | bytes 1179648 | tf_op jit(solution)/shard_map/all_gather | solution.py:620
  15.3 0.6 pad_maximum_fusion.vectors.vector_tile
  15.9 11.9 %front.1 = (f32[48,896]{1,0:T(8,128)}, f32[48,896]{1,0:T(8,128)}, bf16[16,1664]{1,0:T(8,128)(2,1)}, bf16[16,1664]{1,0:T(8,128)(2,1)}, bf16[16,1664]{1,0:T(8,128)...) custom-call(s32[4,8]{1,0:T(4,128)} %get-tuple-element.70.table.refs_, ...), custom_call_target="tpu_custom_call" | custom-call | flops 1024 | bytes 1024 | tf_op jit(solution)/shard_map/front/pallas_call | solution.py:288
  27.9 0.8 copy-done.7
  28.7 0.8 copy-done.8
  29.5 0.8 copy-done.9
  30.3 0.8 copy-done.10
  31.2 4.0 %finish.2 = (bf16[1600,128]{1,0:T(8,128)(2,1)}, bf16[1600,128]{1,0:T(8,128)(2,1)}, bf16[1600,128]{1,0:T(8,128)(2,1)}, bf16[1600,128]{1,0:T(8,128)(2,1)}) custom-call(s32[4,8]{1,0:T(4,128)S(1)} %copy-done.11, bf16[6,1536,128]{2,1,0:T(8,128)(2,1)S(1)} %bitcast.11, bf16[16,1664]{1,0:T(8,128)(2,1)S(1)} %copy-done.10, bf16[16,1664]{1,0:T(8,128)(2,1)S(1)} %copy-done.9, ...), custom_call_target="tpu_custom_call" | custom-call | flops 1024 | bytes 1024 | tf_op jit(solution)/shard_map/finish/pallas_call | solution.py:416
  35.2 0.7 copy-done.1
  35.9 0.8 copy-done.3
  36.7 2.5 %collective-permute-start.2 = (bf16[1600,128]{1,0:T(8,128)(2,1)}, bf16[1600,128]{1,0:T(8,128)(2,1)S(1)}, u32[]{:S(2)}, u32[]{:S(2)}) collective-permute-start(bf16[1600,128]{1,0:T(8,128)(2,1)} %get-tuple-element.63), channel_id=1, source_target_pairs={{0,12},{2,14},{4,16},{6,18},{8,20},{10,22},{12,24},{14,26},{16,28}... | collective-permute-start | bytes 1228808 | tf_op jit(solution)/shard_map/ppermute | solution.py:572
  39.2 1.8 %collective-permute-start.4 = (bf16[1600,128]{1,0:T(8,128)(2,1)}, bf16[1600,128]{1,0:T(8,128)(2,1)}, u32[]{:S(2)}, u32[]{:S(2)}) collective-permute-start(bf16[1600,128]{1,0:T(8,128)(2,1)} %get-tuple-element.65), channel_id=1, source_target_pairs={{0,8},{2,10},{4,12},{6,14},{8,16},{10,18},{12,20},{14,22},{16,24},... | collective-permute-start | bytes 1228808 | tf_op jit(solution)/shard_map/ppermute | solution.py:572
  41.0 3.3 %collective-permute-start.5 = (bf16[1600,128]{1,0:T(8,128)(2,1)}, bf16[1600,128]{1,0:T(8,128)(2,1)}, u32[]{:S(2)}, u32[]{:S(2)}) collective-permute-start(bf16[1600,128]{1,0:T(8,128)(2,1)} %get-tuple-element.66), channel_id=1, source_target_pairs={{0,6},{2,8},{4,10},{6,12},{8,14},{10,16},{12,18},{14,20},{16,22},{... | collective-permute-start | bytes 1228808 | tf_op jit(solution)/shard_map/ppermute | solution.py:572
  44.4 1.5 %collective-permute-start.6 = (bf16[16,1664]{1,0:T(8,128)(2,1)}, bf16[16,1664]{1,0:T(8,128)(2,1)S(1)}, u32[]{:S(2)}, u32[]{:S(2)}) collective-permute-start(bf16[16,1664]{1,0:T(8,128)(2,1)} %get-tuple-element.67), channel_id=1, source_target_pairs={{0,14},{2,16},{4,18},{6,20},{8,22},{10,24},{12,26},{14,28},{16,30}... | collective-permute-start | bytes 159752 | tf_op jit(solution)/shard_map/ppermute | solution.py:572
  45.9 2.3 %all-gather.2 = f32[96,896]{1,0:T(8,128)S(1)} all-gather(f32[48,896]{1,0:T(8,128)} %get-tuple-element.51), channel_id=4, replica_groups=mesh['req'=16,'head'=2] {'head'}, dimensions={0}, use_global_device_ids=true | all-gather | bytes 516096 | tf_op jit(solution)/shard_map/all_gather | solution.py:645
  48.2 1.2 %finish.3 = bf16[1600,128]{1,0:T(8,128)(2,1)S(1)} custom-call(s32[4,8]{1,0:T(4,128)S(1)} %copy-done.11, bf16[6,1536,128]{2,1,0:T(8,128)(2,1)S(1)} %bitcast.12, bf16[16,1664]{1,0:T(8,128)(2,1)S(1)} %copy-done.6), custom_call_target="tpu_custom_call" | custom-call | flops 1024 | bytes 1024 | tf_op jit(solution)/shard_map/finish/pallas_call | solution.py:416
  49.4 33.1 %collective-permute-done.6.refs_5_.refs_3_ = bf16[16,1664]{1,0:T(8,128)(2,1)S(1)} collective-permute-done((bf16[16,1664]{1,0:T(8,128)(2,1)}, bf16[16,1664]{1,0:T(8,128)(2,1)S(1)}, u32[]{:S(2)}, u32[]{:S(2)}) %collective-permute-start.6) | collective-permute-done | bytes 53280 | tf_op jit(solution)/shard_map/ppermute | solution.py:572
  82.4 4.7 %collective-permute-done.2.refs_0_ = bf16[1600,128]{1,0:T(8,128)(2,1)S(1)} collective-permute-done((bf16[1600,128]{1,0:T(8,128)(2,1)}, bf16[1600,128]{1,0:T(8,128)(2,1)S(1)}, u32[]{:S(2)}, u32[]{:S(2)}) %collective-permute-start.2) | collective-permute-done | bytes 409632 | tf_op jit(solution)/shard_map/ppermute | solution.py:572
  87.2 9.2 %collective-permute-done.3.refs_1_ = bf16[1600,128]{1,0:T(8,128)(2,1)S(1)} collective-permute-done((bf16[1600,128]{1,0:T(8,128)(2,1)}, bf16[1600,128]{1,0:T(8,128)(2,1)S(1)}, u32[]{:S(2)}, u32[]{:S(2)}) %collective-permute-start.3) | collective-permute-done | bytes 409632 | tf_op jit(solution)/shard_map/ppermute | solution.py:572
  96.5 1.3 %collective-permute-start.8 = (bf16[16,1664]{1,0:T(8,128)(2,1)S(1)}, bf16[16,1664]{1,0:T(8,128)(2,1)S(1)}, u32[]{:S(2)}, u32[]{:S(2)}) collective-permute-start(bf16[16,1664]{1,0:T(8,128)(2,1)S(1)} %copy-done.21), channel_id=1, source_target_pairs={{0,4},{2,6},{4,8},{6,10},{8,12},{10,14},{12,16},{14,18},{16,20},{1... | collective-permute-start | bytes 159752 | tf_op jit(solution)/shard_map/ppermute | solution.py:572
  97.8 0.7 fusion.2
  98.5 2.4 %place.2 = (bf16[6,1536,128]{2,1,0:T(8,128)(2,1)}, bf16[6,3,1536]{2,1,0:T(4,128)(2,1)S(1)}, bf16[6,3,256]{2,1,0:T(4,128)(2,1)S(1)}) custom-call(bf16[1600,128]{1,0:T(8,128)(2,1)S(1)} %collective-permute-done.2.refs_0_, bf16[1600,128]{1,0:T(8,128)(2,1)S(1)} %collective-permute-done.3.refs_1_, bf16[1600,128]{1,0:T(8,128)(2,1)} %collective-permute-done.4.refs_2_, ...), custom_call_target="tpu_custom_call" | custom-call | flops 1024 | bytes 1024 | tf_op jit(solution)/shard_map/place/pallas_call | solution.py:552
  101.0 0.9 merge.2.refs_4_
  101.9 5.0 %collective-permute-done.8.refs_3_.refs_1_ = bf16[16,1664]{1,0:T(8,128)(2,1)S(1)} collective-permute-done((bf16[16,1664]{1,0:T(8,128)(2,1)S(1)}, bf16[16,1664]{1,0:T(8,128)(2,1)S(1)}, u32[]{:S(2)}, u32[]{:S(2)}) %collective-permute-start.8) | collective-permute-done | bytes 53280 | tf_op jit(solution)/shard_map/ppermute | solution.py:572
  106.9 1.9 %merge.3.refs_2_ = bf16[6,1536,128]{2,1,0:T(8,128)(2,1)} custom-call(s32[4,8]{1,0:T(4,128)S(1)} %copy-done.11, bf16[6,1536,128]{2,1,0:T(8,128)(2,1)S(1)} %bitcast.14, bf16[1536,128]{1,0:T(8,128)(2,1)S(1)} %copy-done.4, bf16[16,1664]{1,0:T(8,128)(2,1)S(1)} %collective-permute-done.8.refs_3_.refs_1_, ...), custom_call_target="tpu_custom_call", output_to_operand_aliasing={{}: (4, {})} | custom-call | flops 1024 | bytes 1024 | tf_op jit(solution)/shard_map/merge/pallas_call | solution.py:468
  108.7 2.2 %collective-permute-done.7.refs_0_ = bf16[1600,128]{1,0:T(8,128)(2,1)S(1)} collective-permute-done((bf16[1600,128]{1,0:T(8,128)(2,1)S(1)}, bf16[1600,128]{1,0:T(8,128)(2,1)S(1)}, u32[]{:S(2)}, u32[]{:S(2)}) %collective-permute-start.7) | collective-permute-done | bytes 409632 | tf_op jit(solution)/shard_map/ppermute | solution.py:572
  110.9 1.5 %place.3 = (bf16[6,1536,128]{2,1,0:T(8,128)(2,1)}, bf16[6,3,1536]{2,1,0:T(4,128)(2,1)}, bf16[6,3,256]{2,1,0:T(4,128)(2,1)}) custom-call(bf16[1600,128]{1,0:T(8,128)(2,1)S(1)} %collective-permute-done.7.refs_0_, bf16[16,1664]{1,0:T(8,128)(2,1)S(1)} %collective-permute-done.8.refs_3_.refs_1_, ...), custom_call_target="tpu_custom_call", output_to_operand_aliasing={{0}: (2, {})} | custom-call | flops 1024 | bytes 1024 | tf_op jit(solution)/shard_map/place/pallas_call | solution.py:552
  (49 shorter events, 0.3 us)
Async XLA Ops:
  0.6 9.5 %copy-start.15 = (f32[1536]{0:T(1024)S(1)}, f32[1536]{0:T(1024)}, u32[]{:S(2)}) copy-start(f32[1536]{0:T(1024)} %param.22) | copy-start | bytes 18436
  0.6 9.5 %copy-start.16 = (f32[1536]{0:T(1024)S(1)}, f32[1536]{0:T(1024)}, u32[]{:S(2)}) copy-start(f32[1536]{0:T(1024)} %param.31) | copy-start | bytes 18436
  0.7 9.5 %copy-start.17 = (f32[1536]{0:T(1024)S(1)}, f32[1536]{0:T(1024)}, u32[]{:S(2)}) copy-start(f32[1536]{0:T(1024)} %param.34) | copy-start | bytes 18436
  0.7 9.5 %copy-start.13 = (bf16[48,768]{1,0:T(8,128)(2,1)S(1)}, bf16[48,768]{1,0:T(8,128)(2,1)}, u32[]{:S(2)}) copy-start(bf16[48,768]{1,0:T(8,128)(2,1)} %param.21) | copy-start | bytes 221188
  0.7 12.1 %copy-start.12 = (bf16[1536,128]{1,0:T(8,128)(2,1)S(1)}, bf16[1536,128]{1,0:T(8,128)(2,1)}, u32[]{:S(2)}) copy-start(bf16[1536,128]{1,0:T(8,128)(2,1)} %param.25) | copy-start | bytes 1179652
  0.7 11.5 %copy-start.18 = (f32[24]{0:T(128)S(1)}, f32[24]{0:T(128)}, u32[]{:S(2)}) copy-start(f32[24]{0:T(128)} %param.29) | copy-start | bytes 292
  0.7 11.5 %copy-start.19 = (f32[24]{0:T(128)S(1)}, f32[24]{0:T(128)}, u32[]{:S(2)}) copy-start(f32[24]{0:T(128)} %param.28) | copy-start | bytes 292
  0.7 11.5 %copy-start.20 = (f32[24]{0:T(128)S(1)}, f32[24]{0:T(128)}, u32[]{:S(2)}) copy-start(f32[24]{0:T(128)} %param.27) | copy-start | bytes 292
  3.6 31.5 %collective-permute-start = (bf16[1536,128]{1,0:T(8,128)(2,1)}, bf16[1536,128]{1,0:T(8,128)(2,1)S(1)}, u32[]{:S(2)}, u32[]{:S(2)}) collective-permute-start(bf16[1536,128]{1,0:T(8,128)(2,1)} %get-tuple-element.52), channel_id=1, source_target_pairs={{0,14},{2,16},{4,18},{6,20},{8,22},{10,24},{12,26},{14,28},{16,30}... | collective-permute-start | bytes 1179656 | tf_op jit(solution)/shard_map/ppermute | solution.py:572
  8.6 27.3 %collective-permute-start.1 = (bf16[1536,128]{1,0:T(8,128)(2,1)}, bf16[1536,128]{1,0:T(8,128)(2,1)S(1)}, u32[]{:S(2)}, u32[]{:S(2)}) collective-permute-start(bf16[1536,128]{1,0:T(8,128)(2,1)} %get-tuple-element.53), channel_id=1, source_target_pairs={{0,4},{2,6},{4,8},{6,10},{8,12},{10,14},{12,16},{14,18},{16,20},{1... | collective-permute-start | bytes 1179656 | tf_op jit(solution)/shard_map/ppermute | solution.py:572
  15.9 12.0 %copy-start = (bf16[6,24,64,128]{3,2,1,0:T(8,128)(2,1)S(1)}, bf16[6,24,64,128]{3,2,1,0:T(8,128)(2,1)}, u32[]{:S(2)}) copy-start(bf16[6,24,64,128]{3,2,1,0:T(8,128)(2,1)} %param.36) | copy-start | bytes 7077892
  15.9 12.0 %copy-start.11 = (s32[4,8]{1,0:T(4,128)S(1)}, s32[4,8]{1,0:T(4,128)}, u32[]{:S(2)}) copy-start(s32[4,8]{1,0:T(4,128)} %get-tuple-element.70.table.refs_0_) | copy-start | bytes 388
  27.9 20.3 %copy-start.6 = (bf16[16,1664]{1,0:T(8,128)(2,1)S(1)}, bf16[16,1664]{1,0:T(8,128)(2,1)}, u32[]{:S(2)}) copy-start(bf16[16,1664]{1,0:T(8,128)(2,1)} %get-tuple-element.71.refs_2_) | copy-start | bytes 159748
  27.9 0.8 copy-start.7
  28.7 0.8 copy-start.8
  29.5 0.8 copy-start.9
  30.3 0.8 copy-start.10
  31.2 65.2 %copy-start.14 = (f32[48,896]{1,0:T(8,128)S(1)}, f32[48,896]{1,0:T(8,128)}, u32[]{:S(2)}) copy-start(f32[48,896]{1,0:T(8,128)} %get-tuple-element.50) | copy-start | bytes 516100
  35.1 63.4 %copy-start.5 = (bf16[16,1664]{1,0:T(8,128)(2,1)S(1)}, bf16[16,1664]{1,0:T(8,128)(2,1)}, u32[]{:S(2)}) copy-start(bf16[16,1664]{1,0:T(8,128)(2,1)} %get-tuple-element.77.refs_4_) | copy-start | bytes 159748
  35.2 0.7 copy-start.1
  35.9 0.8 copy-start.3
  36.7 50.5 %collective-permute-start.2 = (bf16[1600,128]{1,0:T(8,128)(2,1)}, bf16[1600,128]{1,0:T(8,128)(2,1)S(1)}, u32[]{:S(2)}, u32[]{:S(2)}) collective-permute-start(bf16[1600,128]{1,0:T(8,128)(2,1)} %get-tuple-element.63), channel_id=1, source_target_pairs={{0,12},{2,14},{4,16},{6,18},{8,20},{10,22},{12,24},{14,26},{16,28}... | collective-permute-start | bytes 1228808 | tf_op jit(solution)/shard_map/ppermute | solution.py:572
  39.2 57.1 %collective-permute-start.3 = (bf16[1600,128]{1,0:T(8,128)(2,1)}, bf16[1600,128]{1,0:T(8,128)(2,1)S(1)}, u32[]{:S(2)}, u32[]{:S(2)}) collective-permute-start(bf16[1600,128]{1,0:T(8,128)(2,1)} %get-tuple-element.64), channel_id=1, source_target_pairs={{0,10},{2,12},{4,14},{6,16},{8,18},{10,20},{12,22},{14,24},{16,26}... | collective-permute-start | bytes 1228808 | tf_op jit(solution)/shard_map/ppermute | solution.py:572
  39.2 57.1 %collective-permute-start.4 = (bf16[1600,128]{1,0:T(8,128)(2,1)}, bf16[1600,128]{1,0:T(8,128)(2,1)}, u32[]{:S(2)}, u32[]{:S(2)}) collective-permute-start(bf16[1600,128]{1,0:T(8,128)(2,1)} %get-tuple-element.65), channel_id=1, source_target_pairs={{0,8},{2,10},{4,12},{6,14},{8,16},{10,18},{12,20},{14,22},{16,24},... | collective-permute-start | bytes 1228808 | tf_op jit(solution)/shard_map/ppermute | solution.py:572
  41.0 55.3 %collective-permute-start.5 = (bf16[1600,128]{1,0:T(8,128)(2,1)}, bf16[1600,128]{1,0:T(8,128)(2,1)}, u32[]{:S(2)}, u32[]{:S(2)}) collective-permute-start(bf16[1600,128]{1,0:T(8,128)(2,1)} %get-tuple-element.66), channel_id=1, source_target_pairs={{0,6},{2,8},{4,10},{6,12},{8,14},{10,16},{12,18},{14,20},{16,22},{... | collective-permute-start | bytes 1228808 | tf_op jit(solution)/shard_map/ppermute | solution.py:572
  44.4 52.1 %copy-start.21 = (bf16[16,1664]{1,0:T(8,128)(2,1)S(1)}, bf16[16,1664]{1,0:T(8,128)(2,1)}, u32[]{:S(2)}) copy-start(bf16[16,1664]{1,0:T(8,128)(2,1)} %get-tuple-element.73) | copy-start | bytes 159748
  44.4 38.0 %collective-permute-start.6 = (bf16[16,1664]{1,0:T(8,128)(2,1)}, bf16[16,1664]{1,0:T(8,128)(2,1)S(1)}, u32[]{:S(2)}, u32[]{:S(2)}) collective-permute-start(bf16[16,1664]{1,0:T(8,128)(2,1)} %get-tuple-element.67), channel_id=1, source_target_pairs={{0,14},{2,16},{4,18},{6,20},{8,22},{10,24},{12,26},{14,28},{16,30}... | collective-permute-start | bytes 159752 | tf_op jit(solution)/shard_map/ppermute | solution.py:572
  48.2 52.8 %copy-start.2 = (bf16[1536,128]{1,0:T(8,128)(2,1)S(1)}, bf16[1536,128]{1,0:T(8,128)(2,1)}, u32[]{:S(2)}) copy-start(bf16[1536,128]{1,0:T(8,128)(2,1)} %copy-done.1) | copy-start | bytes 1179652
  96.3 14.6 %collective-permute-start.7 = (bf16[1600,128]{1,0:T(8,128)(2,1)S(1)}, bf16[1600,128]{1,0:T(8,128)(2,1)S(1)}, u32[]{:S(2)}, u32[]{:S(2)}) collective-permute-start(bf16[1600,128]{1,0:T(8,128)(2,1)S(1)} %finish.3), channel_id=1, source_target_pairs={{0,2},{2,4},{4,6},{6,8},{8,10},{10,12},{12,14},{14,16},{16,18},{18... | collective-permute-start | bytes 1228808 | tf_op jit(solution)/shard_map/ppermute | solution.py:572
  96.5 10.3 %collective-permute-start.8 = (bf16[16,1664]{1,0:T(8,128)(2,1)S(1)}, bf16[16,1664]{1,0:T(8,128)(2,1)S(1)}, u32[]{:S(2)}, u32[]{:S(2)}) collective-permute-start(bf16[16,1664]{1,0:T(8,128)(2,1)S(1)} %copy-done.21), channel_id=1, source_target_pairs={{0,4},{2,6},{4,8},{6,10},{8,12},{10,14},{12,16},{14,18},{16,20},{1... | collective-permute-start | bytes 159752 | tf_op jit(solution)/shard_map/ppermute | solution.py:572
  100.9 5.9 %copy-start.4 = (bf16[1536,128]{1,0:T(8,128)(2,1)S(1)}, bf16[1536,128]{1,0:T(8,128)(2,1)}, u32[]{:S(2)}) copy-start(bf16[1536,128]{1,0:T(8,128)(2,1)} %copy-done.3) | copy-start | bytes 1179652

commit v10 on v9

--- a/solution.py
+++ b/solution.py
@@ -423,7 +423,6 @@
             pltpu.SemaphoreType.DMA((n,)),
         ],
         cost_estimate=SMALL,
-        compiler_params=pltpu.CompilerParams(vmem_limit_bytes=ROOM),
         name="finish",
     )(table, states, *[corr[k] for k in offsets])
 

time: 113 us -> 112 us (level)
  waiting for transfers between devices: 54.2 us -> 49.5 us
  local copies, waits for them, and re-layouts: 4.82 us -> 0.84 us
  starting transfers between devices: 17 us -> 20.7 us
  Pallas kernels: 26.7 us -> 29.7 us
    ppermute x9, waiting for transfers between devices: 54.2 us -> 49.5 us  [moved(): lax.ppermute(array, 'req', [(i, (i + by) % length) for i in range(length)])]
    unnamed x44 -> x34, local copies, waits for them, and re-layouts: 4.8 us -> 0.82 us
    ppermute x9, starting transfers between devices: 17 us -> 20.7 us  [moved(): lax.ppermute(array, 'req', [(i, (i + by) % length) for i in range(length)])]
    pallas_call x2, Pallas kernels: 5.16 us -> 7.71 us  [finish(): pl.pallas_call(functools.partial(finish_kernel, offsets), in_specs=[in_sm...]
  transfers between devices with their start and end apart: 9 -> 9, of which waited for: 5 -> 5; matrix products, arithmetic and copies ran while one was open for 2% -> 3% of each run, Pallas kernels for 20% -> 23%
where the time goes in v10:
time: 112 us; the launch traced here: 111 us
  waiting for transfers between devices  49.5 us (44%)
  Pallas kernels  29.7 us (27%)
  starting transfers between devices  20.7 us (18%)
  blocking collectives  6.71 us (6%)
  other arithmetic  3.08 us (3%)
    ppermute x9, waiting for transfers between devices, moved(): lax.ppermute(array, 'req', [(i, (i + by) % length) for i in range(length)])  49.5 us
    ppermute x9, starting transfers between devices, moved(): lax.ppermute(array, 'req', [(i, (i + by) % length) for i in range(length)])  20.7 us
    pallas_call x1, Pallas kernels, front(): pl.pallas_call(functools.partial(front_kernel, count, heads), grid=(tiles...  12 us
    pallas_call x2, Pallas kernels, finish(): pl.pallas_call(functools.partial(finish_kernel, offsets), in_specs=[in_sm...  7.71 us
    pallas_call x2, Pallas kernels, place(): pl.pallas_call(functools.partial(place_kernel, n, 1 if earlier else 0), i...  3.81 us
    pallas_call x2, Pallas kernels, merge(): pl.pallas_call(functools.partial(merge_kernel, n - 1), in_specs=[in_smem(...  3.19 us
    pallas_call x1, Pallas kernels, pick(): pl.pallas_call(functools.partial(pick_kernel, count, peers), in_specs=[in...  2.91 us
    all_gather x1, blocking collectives, local(): lax.all_gather(ready_ssm, 'head', axis=0, tiled=False)  2.49 us
  transfers between devices with their start and end apart: 9, of which 5 were waited for; matrix products, arithmetic and copies ran while one was open for 3% of the time, Pallas kernels for 23%

profile of v10, /device:TPU:0, one launch (start us, length us, event | category | flops | bytes accessed | tf_op | source)
XLA Modules:
  0.0 111.5 jit_solution(13759075899428284413)
XLA Ops:
  0.7 2.9 %pick.1 = (bf16[1536,128]{1,0:T(8,128)(2,1)}, bf16[1536,128]{1,0:T(8,128)(2,1)}, s32[4,8]{1,0:T(4,128)}) custom-call(s32[6]{0:T(128)} %destination.1, bf16[6,1536,128]{2,1,0:T(8,128)(2,1)} %bitcast.9), custom_call_target="tpu_custom_call" | custom-call | flops 1024 | bytes 1024 | tf_op jit(solution)/shard_map/pick/pallas_call | solution.py:348
  3.6 5.0 %collective-permute-start = (bf16[1536,128]{1,0:T(8,128)(2,1)}, bf16[1536,128]{1,0:T(8,128)(2,1)S(1)}, u32[]{:S(2)}, u32[]{:S(2)}) collective-permute-start(bf16[1536,128]{1,0:T(8,128)(2,1)} %get-tuple-element.52), channel_id=1, source_target_pairs={{0,14},{2,16},{4,18},{6,20},{8,22},{10,24},{12,26},{14,28},{16,30}... | collective-permute-start | bytes 1179656 | tf_op jit(solution)/shard_map/ppermute | solution.py:571
  8.6 1.5 %collective-permute-start.1 = (bf16[1536,128]{1,0:T(8,128)(2,1)}, bf16[1536,128]{1,0:T(8,128)(2,1)S(1)}, u32[]{:S(2)}, u32[]{:S(2)}) collective-permute-start(bf16[1536,128]{1,0:T(8,128)(2,1)} %get-tuple-element.53), channel_id=1, source_target_pairs={{0,4},{2,6},{4,8},{6,10},{8,12},{10,14},{12,16},{14,18},{16,20},{1... | collective-permute-start | bytes 1179656 | tf_op jit(solution)/shard_map/ppermute | solution.py:571
  10.2 2.0 %all-gather = bf16[96,768]{1,0:T(8,128)(2,1)} all-gather(bf16[48,768]{1,0:T(8,128)(2,1)S(1)} %copy-done.8), channel_id=2, replica_groups=mesh['req'=16,'head'=2] {'head'}, dimensions={0}, use_global_device_ids=true | all-gather | bytes 221184 | tf_op jit(solution)/shard_map/all_gather | solution.py:614
  12.2 0.6 pad_maximum_fusion.1.head_rows
  12.8 2.5 %all-gather.1 = bf16[3072,128]{1,0:T(8,128)(2,1)} all-gather(bf16[1536,128]{1,0:T(8,128)(2,1)S(1)} %copy-done.7), channel_id=3, replica_groups=mesh['req'=16,'head'=2] {'head'}, dimensions={0}, use_global_device_ids=true | all-gather | bytes 1179648 | tf_op jit(solution)/shard_map/all_gather | solution.py:619
  15.3 0.6 pad_maximum_fusion.vectors.vector_tile
  15.9 12.0 %front.1 = (f32[48,896]{1,0:T(8,128)}, f32[48,896]{1,0:T(8,128)}, bf16[16,1664]{1,0:T(8,128)(2,1)}, bf16[16,1664]{1,0:T(8,128)(2,1)}, bf16[16,1664]{1,0:T(8,128)...) custom-call(s32[4,8]{1,0:T(4,128)} %get-tuple-element.70.table.refs_, ...), custom_call_target="tpu_custom_call" | custom-call | flops 1024 | bytes 1024 | tf_op jit(solution)/shard_map/front/pallas_call | solution.py:288
  28.0 4.6 %finish.2 = (bf16[1600,128]{1,0:T(8,128)(2,1)}, bf16[1600,128]{1,0:T(8,128)(2,1)}, bf16[1600,128]{1,0:T(8,128)(2,1)}, bf16[1600,128]{1,0:T(8,128)(2,1)}) custom-call(s32[4,8]{1,0:T(4,128)} %get-tuple-element.70.table.refs_0_, bf16[6,1536,128]{2,1,0:T(8,128)(2,1)} %bitcast.11, bf16[16,1664]{1,0:T(8,128)(2,1)} %get-tuple-element.55.refs_2_, ...), custom_call_target="tpu_custom_call" | custom-call | flops 1024 | bytes 1024 | tf_op jit(solution)/shard_map/finish/pallas_call | solution.py:416
  32.6 0.0 copy-start.5
  32.6 0.0 collective-permute-done.refs_2_
  32.6 0.7 copy-done.3
  33.4 4.0 %collective-permute-start.2 = (bf16[1600,128]{1,0:T(8,128)(2,1)}, bf16[1600,128]{1,0:T(8,128)(2,1)S(1)}, u32[]{:S(2)}, u32[]{:S(2)}) collective-permute-start(bf16[1600,128]{1,0:T(8,128)(2,1)} %get-tuple-element.63), channel_id=1, source_target_pairs={{0,12},{2,14},{4,16},{6,18},{8,20},{10,22},{12,24},{14,26},{16,28}... | collective-permute-start | bytes 1228808 | tf_op jit(solution)/shard_map/ppermute | solution.py:571
  37.4 0.0 collective-permute-start.3
  37.4 2.4 %collective-permute-start.4 = (bf16[1600,128]{1,0:T(8,128)(2,1)}, bf16[1600,128]{1,0:T(8,128)(2,1)}, u32[]{:S(2)}, u32[]{:S(2)}) collective-permute-start(bf16[1600,128]{1,0:T(8,128)(2,1)} %get-tuple-element.65), channel_id=1, source_target_pairs={{0,8},{2,10},{4,12},{6,14},{8,16},{10,18},{12,20},{14,22},{16,24},... | collective-permute-start | bytes 1228808 | tf_op jit(solution)/shard_map/ppermute | solution.py:571
  39.7 3.6 %collective-permute-start.5 = (bf16[1600,128]{1,0:T(8,128)(2,1)}, bf16[1600,128]{1,0:T(8,128)(2,1)}, u32[]{:S(2)}, u32[]{:S(2)}) collective-permute-start(bf16[1600,128]{1,0:T(8,128)(2,1)} %get-tuple-element.66), channel_id=1, source_target_pairs={{0,6},{2,8},{4,10},{6,12},{8,14},{10,16},{12,18},{14,20},{16,22},{... | collective-permute-start | bytes 1228808 | tf_op jit(solution)/shard_map/ppermute | solution.py:571
  43.4 2.5 %collective-permute-start.6 = (bf16[16,1664]{1,0:T(8,128)(2,1)}, bf16[16,1664]{1,0:T(8,128)(2,1)S(1)}, u32[]{:S(2)}, u32[]{:S(2)}) collective-permute-start(bf16[16,1664]{1,0:T(8,128)(2,1)} %get-tuple-element.67), channel_id=1, source_target_pairs={{0,14},{2,16},{4,18},{6,20},{8,22},{10,24},{12,26},{14,28},{16,30}... | collective-permute-start | bytes 159752 | tf_op jit(solution)/shard_map/ppermute | solution.py:571
  45.9 2.2 %all-gather.2 = f32[96,896]{1,0:T(8,128)} all-gather(f32[48,896]{1,0:T(8,128)S(1)} %copy-done.10), channel_id=4, replica_groups=mesh['req'=16,'head'=2] {'head'}, dimensions={0}, use_global_device_ids=true | all-gather | bytes 516096 | tf_op jit(solution)/shard_map/all_gather | solution.py:644
  48.1 3.1 %finish.3 = bf16[1600,128]{1,0:T(8,128)(2,1)} custom-call(s32[4,8]{1,0:T(4,128)} %get-tuple-element.70.table.refs_0_, bf16[6,1536,128]{2,1,0:T(8,128)(2,1)} %bitcast.12, bf16[16,1664]{1,0:T(8,128)(2,1)} %get-tuple-element.71.refs_2_), custom_call_target="tpu_custom_call" | custom-call | flops 1024 | bytes 1024 | tf_op jit(solution)/shard_map/finish/pallas_call | solution.py:416
  51.3 27.2 %collective-permute-done.6.refs_5_.refs_3_ = bf16[16,1664]{1,0:T(8,128)(2,1)S(1)} collective-permute-done((bf16[16,1664]{1,0:T(8,128)(2,1)}, bf16[16,1664]{1,0:T(8,128)(2,1)S(1)}, u32[]{:S(2)}, u32[]{:S(2)}) %collective-permute-start.6) | collective-permute-done | bytes 53280 | tf_op jit(solution)/shard_map/ppermute | solution.py:571
  78.4 5.3 %collective-permute-done.2.refs_0_ = bf16[1600,128]{1,0:T(8,128)(2,1)S(1)} collective-permute-done((bf16[1600,128]{1,0:T(8,128)(2,1)}, bf16[1600,128]{1,0:T(8,128)(2,1)S(1)}, u32[]{:S(2)}, u32[]{:S(2)}) %collective-permute-start.2) | collective-permute-done | bytes 409632 | tf_op jit(solution)/shard_map/ppermute | solution.py:571
  83.8 9.5 %collective-permute-done.3.refs_1_ = bf16[1600,128]{1,0:T(8,128)(2,1)S(1)} collective-permute-done((bf16[1600,128]{1,0:T(8,128)(2,1)}, bf16[1600,128]{1,0:T(8,128)(2,1)S(1)}, u32[]{:S(2)}, u32[]{:S(2)}) %collective-permute-start.3) | collective-permute-done | bytes 409632 | tf_op jit(solution)/shard_map/ppermute | solution.py:571
  93.3 1.0 fusion
  94.4 0.1 fusion.5
  94.5 1.7 %collective-permute-start.8 = (bf16[16,1664]{1,0:T(8,128)(2,1)}, bf16[16,1664]{1,0:T(8,128)(2,1)S(1)}, u32[]{:S(2)}, u32[]{:S(2)}) collective-permute-start(bf16[16,1664]{1,0:T(8,128)(2,1)} %get-tuple-element.73), channel_id=1, source_target_pairs={{0,4},{2,6},{4,8},{6,10},{8,12},{10,14},{12,16},{14,18},{16,20},{1... | collective-permute-start | bytes 159752 | tf_op jit(solution)/shard_map/ppermute | solution.py:571
  96.2 0.7 fusion.2
  96.9 2.3 %place.2 = (bf16[6,1536,128]{2,1,0:T(8,128)(2,1)}, bf16[6,3,1536]{2,1,0:T(4,128)(2,1)S(1)}, bf16[6,3,256]{2,1,0:T(4,128)(2,1)S(1)}) custom-call(bf16[1600,128]{1,0:T(8,128)(2,1)S(1)} %collective-permute-done.2.refs_0_, bf16[1600,128]{1,0:T(8,128)(2,1)S(1)} %collective-permute-done.3.refs_1_, bf16[1600,128]{1,0:T(8,128)(2,1)} %collective-permute-done.4.refs_2_, ...), custom_call_target="tpu_custom_call" | custom-call | flops 1024 | bytes 1024 | tf_op jit(solution)/shard_map/place/pallas_call | solution.py:551
  99.3 2.5 %merge.2.refs_4_ = bf16[6,1536,128]{2,1,0:T(8,128)(2,1)} custom-call(s32[4,8]{1,0:T(4,128)S(1)} %copy-done.6, bf16[6,1536,128]{2,1,0:T(8,128)(2,1)S(1)} %bitcast.13, bf16[1536,128]{1,0:T(8,128)(2,1)S(1)} %copy-done.2, bf16[16,1664]{1,0:T(8,128)(2,1)S(1)} %collective-permute-done.6.refs_5_.refs_3_, ...), custom_call_target="tpu_custom_call", output_to_operand_aliasing={{}: (5, {})} | custom-call | flops 1024 | bytes 1024 | tf_op jit(solution)/shard_map/merge/pallas_call | solution.py:467
  101.8 4.4 %collective-permute-done.8.refs_3_.refs_1_ = bf16[16,1664]{1,0:T(8,128)(2,1)S(1)} collective-permute-done((bf16[16,1664]{1,0:T(8,128)(2,1)}, bf16[16,1664]{1,0:T(8,128)(2,1)S(1)}, u32[]{:S(2)}, u32[]{:S(2)}) %collective-permute-start.8) | collective-permute-done | bytes 53280 | tf_op jit(solution)/shard_map/ppermute | solution.py:571
  106.2 0.7 merge.3.refs_2_
  106.9 3.0 %collective-permute-done.7.refs_0_ = bf16[1600,128]{1,0:T(8,128)(2,1)S(1)} collective-permute-done((bf16[1600,128]{1,0:T(8,128)(2,1)}, bf16[1600,128]{1,0:T(8,128)(2,1)S(1)}, u32[]{:S(2)}, u32[]{:S(2)}) %collective-permute-start.7) | collective-permute-done | bytes 409632 | tf_op jit(solution)/shard_map/ppermute | solution.py:571
  110.0 1.5 %place.3 = (bf16[6,1536,128]{2,1,0:T(8,128)(2,1)}, bf16[6,3,1536]{2,1,0:T(4,128)(2,1)}, bf16[6,3,256]{2,1,0:T(4,128)(2,1)}) custom-call(bf16[1600,128]{1,0:T(8,128)(2,1)S(1)} %collective-permute-done.7.refs_0_, bf16[16,1664]{1,0:T(8,128)(2,1)S(1)} %collective-permute-done.8.refs_3_.refs_1_, ...), custom_call_target="tpu_custom_call", output_to_operand_aliasing={{0}: (2, {})} | custom-call | flops 1024 | bytes 1024 | tf_op jit(solution)/shard_map/place/pallas_call | solution.py:551
  (39 shorter events, 0.1 us)
Async XLA Ops:
  0.6 9.5 %copy-start.11 = (f32[1536]{0:T(1024)S(1)}, f32[1536]{0:T(1024)}, u32[]{:S(2)}) copy-start(f32[1536]{0:T(1024)} %param.22) | copy-start | bytes 18436
  0.6 9.5 %copy-start.12 = (f32[1536]{0:T(1024)S(1)}, f32[1536]{0:T(1024)}, u32[]{:S(2)}) copy-start(f32[1536]{0:T(1024)} %param.31) | copy-start | bytes 18436
  0.7 9.5 %copy-start.13 = (f32[1536]{0:T(1024)S(1)}, f32[1536]{0:T(1024)}, u32[]{:S(2)}) copy-start(f32[1536]{0:T(1024)} %param.34) | copy-start | bytes 18436
  0.7 9.5 %copy-start.8 = (bf16[48,768]{1,0:T(8,128)(2,1)S(1)}, bf16[48,768]{1,0:T(8,128)(2,1)}, u32[]{:S(2)}) copy-start(bf16[48,768]{1,0:T(8,128)(2,1)} %param.21) | copy-start | bytes 221188
  0.7 12.2 %copy-start.7 = (bf16[1536,128]{1,0:T(8,128)(2,1)S(1)}, bf16[1536,128]{1,0:T(8,128)(2,1)}, u32[]{:S(2)}) copy-start(bf16[1536,128]{1,0:T(8,128)(2,1)} %param.25) | copy-start | bytes 1179652
  0.7 11.5 %copy-start.14 = (f32[24]{0:T(128)S(1)}, f32[24]{0:T(128)}, u32[]{:S(2)}) copy-start(f32[24]{0:T(128)} %param.29) | copy-start | bytes 292
  0.7 11.5 %copy-start.15 = (f32[24]{0:T(128)S(1)}, f32[24]{0:T(128)}, u32[]{:S(2)}) copy-start(f32[24]{0:T(128)} %param.28) | copy-start | bytes 292
  0.7 11.5 %copy-start.16 = (f32[24]{0:T(128)S(1)}, f32[24]{0:T(128)}, u32[]{:S(2)}) copy-start(f32[24]{0:T(128)} %param.27) | copy-start | bytes 292
  3.6 29.0 %collective-permute-start = (bf16[1536,128]{1,0:T(8,128)(2,1)}, bf16[1536,128]{1,0:T(8,128)(2,1)S(1)}, u32[]{:S(2)}, u32[]{:S(2)}) collective-permute-start(bf16[1536,128]{1,0:T(8,128)(2,1)} %get-tuple-element.52), channel_id=1, source_target_pairs={{0,14},{2,16},{4,18},{6,20},{8,22},{10,24},{12,26},{14,28},{16,30}... | collective-permute-start | bytes 1179656 | tf_op jit(solution)/shard_map/ppermute | solution.py:571
  8.6 24.0 %collective-permute-start.1 = (bf16[1536,128]{1,0:T(8,128)(2,1)}, bf16[1536,128]{1,0:T(8,128)(2,1)S(1)}, u32[]{:S(2)}, u32[]{:S(2)}) collective-permute-start(bf16[1536,128]{1,0:T(8,128)(2,1)} %get-tuple-element.53), channel_id=1, source_target_pairs={{0,4},{2,6},{4,8},{6,10},{8,12},{10,14},{12,16},{14,18},{16,20},{1... | collective-permute-start | bytes 1179656 | tf_op jit(solution)/shard_map/ppermute | solution.py:571
  28.0 17.9 %copy-start.10 = (f32[48,896]{1,0:T(8,128)S(1)}, f32[48,896]{1,0:T(8,128)}, u32[]{:S(2)}) copy-start(f32[48,896]{1,0:T(8,128)} %get-tuple-element.51) | copy-start | bytes 516100
  28.0 65.3 %copy-start.9 = (f32[48,896]{1,0:T(8,128)S(1)}, f32[48,896]{1,0:T(8,128)}, u32[]{:S(2)}) copy-start(f32[48,896]{1,0:T(8,128)} %get-tuple-element.50) | copy-start | bytes 516100
  32.6 64.4 %copy-start.5 = (bf16[16,1664]{1,0:T(8,128)(2,1)S(1)}, bf16[16,1664]{1,0:T(8,128)(2,1)}, u32[]{:S(2)}) copy-start(bf16[16,1664]{1,0:T(8,128)(2,1)} %get-tuple-element.77.refs_4_) | copy-start | bytes 159748
  32.6 15.5 %copy-start.1 = (bf16[1536,128]{1,0:T(8,128)(2,1)}, bf16[1536,128]{1,0:T(8,128)(2,1)S(1)}, u32[]{:S(2)}) copy-start(bf16[1536,128]{1,0:T(8,128)(2,1)S(1)} %collective-permute-done.refs_2_) | copy-start | bytes 1179652
  32.6 0.8 copy-start.3
  33.4 50.4 %collective-permute-start.2 = (bf16[1600,128]{1,0:T(8,128)(2,1)}, bf16[1600,128]{1,0:T(8,128)(2,1)S(1)}, u32[]{:S(2)}, u32[]{:S(2)}) collective-permute-start(bf16[1600,128]{1,0:T(8,128)(2,1)} %get-tuple-element.63), channel_id=1, source_target_pairs={{0,12},{2,14},{4,16},{6,18},{8,20},{10,22},{12,24},{14,26},{16,28}... | collective-permute-start | bytes 1228808 | tf_op jit(solution)/shard_map/ppermute | solution.py:571
  37.4 55.9 %collective-permute-start.3 = (bf16[1600,128]{1,0:T(8,128)(2,1)}, bf16[1600,128]{1,0:T(8,128)(2,1)S(1)}, u32[]{:S(2)}, u32[]{:S(2)}) collective-permute-start(bf16[1600,128]{1,0:T(8,128)(2,1)} %get-tuple-element.64), channel_id=1, source_target_pairs={{0,10},{2,12},{4,14},{6,16},{8,18},{10,20},{12,22},{14,24},{16,26}... | collective-permute-start | bytes 1228808 | tf_op jit(solution)/shard_map/ppermute | solution.py:571
  37.4 55.9 %collective-permute-start.4 = (bf16[1600,128]{1,0:T(8,128)(2,1)}, bf16[1600,128]{1,0:T(8,128)(2,1)}, u32[]{:S(2)}, u32[]{:S(2)}) collective-permute-start(bf16[1600,128]{1,0:T(8,128)(2,1)} %get-tuple-element.65), channel_id=1, source_target_pairs={{0,8},{2,10},{4,12},{6,14},{8,16},{10,18},{12,20},{14,22},{16,24},... | collective-permute-start | bytes 1228808 | tf_op jit(solution)/shard_map/ppermute | solution.py:571
  39.7 53.6 %collective-permute-start.5 = (bf16[1600,128]{1,0:T(8,128)(2,1)}, bf16[1600,128]{1,0:T(8,128)(2,1)}, u32[]{:S(2)}, u32[]{:S(2)}) collective-permute-start(bf16[1600,128]{1,0:T(8,128)(2,1)} %get-tuple-element.66), channel_id=1, source_target_pairs={{0,6},{2,8},{4,10},{6,12},{8,14},{10,16},{12,18},{14,20},{16,22},{... | collective-permute-start | bytes 1228808 | tf_op jit(solution)/shard_map/ppermute | solution.py:571
  43.4 35.1 %collective-permute-start.6 = (bf16[16,1664]{1,0:T(8,128)(2,1)}, bf16[16,1664]{1,0:T(8,128)(2,1)S(1)}, u32[]{:S(2)}, u32[]{:S(2)}) collective-permute-start(bf16[16,1664]{1,0:T(8,128)(2,1)} %get-tuple-element.67), channel_id=1, source_target_pairs={{0,14},{2,16},{4,18},{6,20},{8,22},{10,24},{12,26},{14,28},{16,30}... | collective-permute-start | bytes 159752 | tf_op jit(solution)/shard_map/ppermute | solution.py:571
  48.1 51.2 %copy-start = (bf16[6,24,64,128]{3,2,1,0:T(8,128)(2,1)S(1)}, bf16[6,24,64,128]{3,2,1,0:T(8,128)(2,1)}, u32[]{:S(2)}) copy-start(bf16[6,24,64,128]{3,2,1,0:T(8,128)(2,1)} %param.36) | copy-start | bytes 7077892
  48.1 51.2 %copy-start.6 = (s32[4,8]{1,0:T(4,128)S(1)}, s32[4,8]{1,0:T(4,128)}, u32[]{:S(2)}) copy-start(s32[4,8]{1,0:T(4,128)} %get-tuple-element.70.table.refs_0_) | copy-start | bytes 388
  51.2 48.0 %copy-start.2 = (bf16[1536,128]{1,0:T(8,128)(2,1)S(1)}, bf16[1536,128]{1,0:T(8,128)(2,1)}, u32[]{:S(2)}) copy-start(bf16[1536,128]{1,0:T(8,128)(2,1)} %copy-done.1) | copy-start | bytes 1179652
  93.3 16.6 %collective-permute-start.7 = (bf16[1600,128]{1,0:T(8,128)(2,1)}, bf16[1600,128]{1,0:T(8,128)(2,1)S(1)}, u32[]{:S(2)}, u32[]{:S(2)}) collective-permute-start(bf16[1600,128]{1,0:T(8,128)(2,1)} %finish.3), channel_id=1, source_target_pairs={{0,2},{2,4},{4,6},{6,8},{8,10},{10,12},{12,14},{14,16},{16,18},{18... | collective-permute-start | bytes 1228808 | tf_op jit(solution)/shard_map/ppermute | solution.py:571
  94.5 11.7 %collective-permute-start.8 = (bf16[16,1664]{1,0:T(8,128)(2,1)}, bf16[16,1664]{1,0:T(8,128)(2,1)S(1)}, u32[]{:S(2)}, u32[]{:S(2)}) collective-permute-start(bf16[16,1664]{1,0:T(8,128)(2,1)} %get-tuple-element.73), channel_id=1, source_target_pairs={{0,4},{2,6},{4,8},{6,10},{8,12},{10,14},{12,16},{14,18},{16,20},{1... | collective-permute-start | bytes 159752 | tf_op jit(solution)/shard_map/ppermute | solution.py:571
  99.3 6.9 %copy-start.4 = (bf16[1536,128]{1,0:T(8,128)(2,1)S(1)}, bf16[1536,128]{1,0:T(8,128)(2,1)}, u32[]{:S(2)}) copy-start(bf16[1536,128]{1,0:T(8,128)(2,1)} %copy-done.3) | copy-start | bytes 1179652

commit v11 on v10

--- a/solution.py
+++ b/solution.py
@@ -423,6 +423,7 @@
             pltpu.SemaphoreType.DMA((n,)),
         ],
         cost_estimate=SMALL,
+        compiler_params=pltpu.CompilerParams(vmem_limit_bytes=ROOM if n == 1 else None),
         name="finish",
     )(table, states, *[corr[k] for k in offsets])
 

time: 112 us -> 112 us (level)
  waiting for transfers between devices: 49.5 us -> 51.8 us
    ppermute x9, waiting for transfers between devices: 49.5 us -> 51.8 us  [moved(): lax.ppermute(array, 'req', [(i, (i + by) % length) for i in range(length)])]
    pallas_call x2, Pallas kernels: 7.71 us -> 5.86 us  [finish(): pl.pallas_call(functools.partial(finish_kernel, offsets), in_specs=[in_sm...]
  transfers between devices with their start and end apart: 9 -> 9, of which waited for: 5 -> 5; matrix products, arithmetic and copies ran while one was open for 3% -> 2% of each run, Pallas kernels for 23% -> 22%
where the time goes in v11:
time: 112 us
  waiting for transfers between devices  51.8 us (46%)
  Pallas kernels  28.6 us (26%)
  starting transfers between devices  19.9 us (18%)
  blocking collectives  6.78 us (6%)
  other arithmetic  2.09 us (2%)
  local copies, waits for them, and re-layouts  1.59 us (1%)
    ppermute x9, waiting for transfers between devices, moved(): lax.ppermute(array, 'req', [(i, (i + by) % length) for i in range(length)])  51.8 us
    ppermute x9, starting transfers between devices, moved(): lax.ppermute(array, 'req', [(i, (i + by) % length) for i in range(length)])  19.9 us
    pallas_call x1, Pallas kernels, front(): pl.pallas_call(functools.partial(front_kernel, count, heads), grid=(tiles...  12 us
    pallas_call x2, Pallas kernels, finish(): pl.pallas_call(functools.partial(finish_kernel, offsets), in_specs=[in_sm...  5.86 us
    pallas_call x2, Pallas kernels, merge(): pl.pallas_call(functools.partial(merge_kernel, n - 1), in_specs=[in_smem(...  3.92 us
    pallas_call x2, Pallas kernels, place(): pl.pallas_call(functools.partial(place_kernel, n, 1 if earlier else 0), i...  3.81 us
    pallas_call x1, Pallas kernels, pick(): pl.pallas_call(functools.partial(pick_kernel, count, peers), in_specs=[in...  2.93 us
    all_gather x1, blocking collectives, local(): lax.all_gather(ready_ssm, 'head', axis=0, tiled=False)  2.49 us
  transfers between devices with their start and end apart: 9, of which 5 were waited for; matrix products, arithmetic and copies ran while one was open for 2% of the time, Pallas kernels for 22%

profile of v11, /device:TPU:0, one launch (start us, length us, event | category | flops | bytes accessed | tf_op | source)
XLA Modules:
  0.0 111.6 jit_solution(3491542880087080403)
XLA Ops:
  0.7 2.9 %pick.1 = (bf16[1536,128]{1,0:T(8,128)(2,1)}, bf16[1536,128]{1,0:T(8,128)(2,1)}, s32[4,8]{1,0:T(4,128)}) custom-call(s32[6]{0:T(128)} %destination.1, bf16[6,1536,128]{2,1,0:T(8,128)(2,1)} %bitcast.9), custom_call_target="tpu_custom_call" | custom-call | flops 1024 | bytes 1024 | tf_op jit(solution)/shard_map/pick/pallas_call | solution.py:348
  3.6 5.0 %collective-permute-start = (bf16[1536,128]{1,0:T(8,128)(2,1)}, bf16[1536,128]{1,0:T(8,128)(2,1)S(1)}, u32[]{:S(2)}, u32[]{:S(2)}) collective-permute-start(bf16[1536,128]{1,0:T(8,128)(2,1)} %get-tuple-element.52), channel_id=1, source_target_pairs={{0,14},{2,16},{4,18},{6,20},{8,22},{10,24},{12,26},{14,28},{16,30}... | collective-permute-start | bytes 1179656 | tf_op jit(solution)/shard_map/ppermute | solution.py:572
  8.6 1.5 %collective-permute-start.1 = (bf16[1536,128]{1,0:T(8,128)(2,1)}, bf16[1536,128]{1,0:T(8,128)(2,1)S(1)}, u32[]{:S(2)}, u32[]{:S(2)}) collective-permute-start(bf16[1536,128]{1,0:T(8,128)(2,1)} %get-tuple-element.53), channel_id=1, source_target_pairs={{0,4},{2,6},{4,8},{6,10},{8,12},{10,14},{12,16},{14,18},{16,20},{1... | collective-permute-start | bytes 1179656 | tf_op jit(solution)/shard_map/ppermute | solution.py:572
  10.2 2.0 %all-gather = bf16[96,768]{1,0:T(8,128)(2,1)} all-gather(bf16[48,768]{1,0:T(8,128)(2,1)S(1)} %copy-done.9), channel_id=2, replica_groups=mesh['req'=16,'head'=2] {'head'}, dimensions={0}, use_global_device_ids=true | all-gather | bytes 221184 | tf_op jit(solution)/shard_map/all_gather | solution.py:615
  12.3 0.6 pad_maximum_fusion.1.head_rows
  12.9 2.5 %all-gather.1 = bf16[3072,128]{1,0:T(8,128)(2,1)} all-gather(bf16[1536,128]{1,0:T(8,128)(2,1)S(1)} %copy-done.8), channel_id=3, replica_groups=mesh['req'=16,'head'=2] {'head'}, dimensions={0}, use_global_device_ids=true | all-gather | bytes 1179648 | tf_op jit(solution)/shard_map/all_gather | solution.py:620
  15.3 0.6 pad_maximum_fusion.vectors.vector_tile
  16.0 12.0 %front.1 = (f32[48,896]{1,0:T(8,128)}, f32[48,896]{1,0:T(8,128)}, bf16[16,1664]{1,0:T(8,128)(2,1)}, bf16[16,1664]{1,0:T(8,128)(2,1)}, bf16[16,1664]{1,0:T(8,128)...) custom-call(s32[4,8]{1,0:T(4,128)} %get-tuple-element.70.table.refs_, ...), custom_call_target="tpu_custom_call" | custom-call | flops 1024 | bytes 1024 | tf_op jit(solution)/shard_map/front/pallas_call | solution.py:288
  28.0 0.0 copy-start
  28.0 0.0 copy-start.7
  28.1 4.7 %finish.2 = (bf16[1600,128]{1,0:T(8,128)(2,1)}, bf16[1600,128]{1,0:T(8,128)(2,1)}, bf16[1600,128]{1,0:T(8,128)(2,1)}, bf16[1600,128]{1,0:T(8,128)(2,1)}) custom-call(s32[4,8]{1,0:T(4,128)} %get-tuple-element.70.table.refs_0_, bf16[6,1536,128]{2,1,0:T(8,128)(2,1)} %bitcast.11, bf16[16,1664]{1,0:T(8,128)(2,1)} %get-tuple-element.55.refs_2_, ...), custom_call_target="tpu_custom_call" | custom-call | flops 1024 | bytes 1024 | tf_op jit(solution)/shard_map/finish/pallas_call | solution.py:416
  32.8 0.7 copy-done.1
  33.5 0.8 copy-done.3
  34.3 3.1 %collective-permute-start.2 = (bf16[1600,128]{1,0:T(8,128)(2,1)}, bf16[1600,128]{1,0:T(8,128)(2,1)S(1)}, u32[]{:S(2)}, u32[]{:S(2)}) collective-permute-start(bf16[1600,128]{1,0:T(8,128)(2,1)} %get-tuple-element.63), channel_id=1, source_target_pairs={{0,12},{2,14},{4,16},{6,18},{8,20},{10,22},{12,24},{14,26},{16,28}... | collective-permute-start | bytes 1228808 | tf_op jit(solution)/shard_map/ppermute | solution.py:572
  37.4 0.2 collective-permute-start.3
  37.5 2.2 %collective-permute-start.4 = (bf16[1600,128]{1,0:T(8,128)(2,1)}, bf16[1600,128]{1,0:T(8,128)(2,1)}, u32[]{:S(2)}, u32[]{:S(2)}) collective-permute-start(bf16[1600,128]{1,0:T(8,128)(2,1)} %get-tuple-element.65), channel_id=1, source_target_pairs={{0,8},{2,10},{4,12},{6,14},{8,16},{10,18},{12,20},{14,22},{16,24},... | collective-permute-start | bytes 1228808 | tf_op jit(solution)/shard_map/ppermute | solution.py:572
  39.7 4.3 %collective-permute-start.5 = (bf16[1600,128]{1,0:T(8,128)(2,1)}, bf16[1600,128]{1,0:T(8,128)(2,1)}, u32[]{:S(2)}, u32[]{:S(2)}) collective-permute-start(bf16[1600,128]{1,0:T(8,128)(2,1)} %get-tuple-element.66), channel_id=1, source_target_pairs={{0,6},{2,8},{4,10},{6,12},{8,14},{10,16},{12,18},{14,20},{16,22},{... | collective-permute-start | bytes 1228808 | tf_op jit(solution)/shard_map/ppermute | solution.py:572
  44.1 1.8 %collective-permute-start.6 = (bf16[16,1664]{1,0:T(8,128)(2,1)}, bf16[16,1664]{1,0:T(8,128)(2,1)S(1)}, u32[]{:S(2)}, u32[]{:S(2)}) collective-permute-start(bf16[16,1664]{1,0:T(8,128)(2,1)} %get-tuple-element.67), channel_id=1, source_target_pairs={{0,14},{2,16},{4,18},{6,20},{8,22},{10,24},{12,26},{14,28},{16,30}... | collective-permute-start | bytes 159752 | tf_op jit(solution)/shard_map/ppermute | solution.py:572
  45.9 2.3 %all-gather.2 = f32[96,896]{1,0:T(8,128)S(1)} all-gather(f32[48,896]{1,0:T(8,128)} %get-tuple-element.51), channel_id=4, replica_groups=mesh['req'=16,'head'=2] {'head'}, dimensions={0}, use_global_device_ids=true | all-gather | bytes 516096 | tf_op jit(solution)/shard_map/all_gather | solution.py:645
  48.2 1.2 %finish.3 = bf16[1600,128]{1,0:T(8,128)(2,1)S(1)} custom-call(s32[4,8]{1,0:T(4,128)S(1)} %copy-done.7, bf16[6,1536,128]{2,1,0:T(8,128)(2,1)S(1)} %bitcast.12, bf16[16,1664]{1,0:T(8,128)(2,1)S(1)} %copy-done.6), custom_call_target="tpu_custom_call" | custom-call | flops 1024 | bytes 1024 | tf_op jit(solution)/shard_map/finish/pallas_call | solution.py:416
  49.4 30.0 %collective-permute-done.6.refs_5_.refs_3_ = bf16[16,1664]{1,0:T(8,128)(2,1)S(1)} collective-permute-done((bf16[16,1664]{1,0:T(8,128)(2,1)}, bf16[16,1664]{1,0:T(8,128)(2,1)S(1)}, u32[]{:S(2)}, u32[]{:S(2)}) %collective-permute-start.6) | collective-permute-done | bytes 53280 | tf_op jit(solution)/shard_map/ppermute | solution.py:572
  79.4 5.2 %collective-permute-done.2.refs_0_ = bf16[1600,128]{1,0:T(8,128)(2,1)S(1)} collective-permute-done((bf16[1600,128]{1,0:T(8,128)(2,1)}, bf16[1600,128]{1,0:T(8,128)(2,1)S(1)}, u32[]{:S(2)}, u32[]{:S(2)}) %collective-permute-start.2) | collective-permute-done | bytes 409632 | tf_op jit(solution)/shard_map/ppermute | solution.py:572
  84.7 9.6 %collective-permute-done.3.refs_1_ = bf16[1600,128]{1,0:T(8,128)(2,1)S(1)} collective-permute-done((bf16[1600,128]{1,0:T(8,128)(2,1)}, bf16[1600,128]{1,0:T(8,128)(2,1)S(1)}, u32[]{:S(2)}, u32[]{:S(2)}) %collective-permute-start.3) | collective-permute-done | bytes 409632 | tf_op jit(solution)/shard_map/ppermute | solution.py:572
  94.3 0.1 fusion.5
  94.4 1.7 %collective-permute-start.8 = (bf16[16,1664]{1,0:T(8,128)(2,1)S(1)}, bf16[16,1664]{1,0:T(8,128)(2,1)S(1)}, u32[]{:S(2)}, u32[]{:S(2)}) collective-permute-start(bf16[16,1664]{1,0:T(8,128)(2,1)S(1)} %copy-done.17), channel_id=1, source_target_pairs={{0,4},{2,6},{4,8},{6,10},{8,12},{10,14},{12,16},{14,18},{16,20},{1... | collective-permute-start | bytes 159752 | tf_op jit(solution)/shard_map/ppermute | solution.py:572
  96.1 0.7 fusion.2
  96.9 2.3 %place.2 = (bf16[6,1536,128]{2,1,0:T(8,128)(2,1)}, bf16[6,3,1536]{2,1,0:T(4,128)(2,1)S(1)}, bf16[6,3,256]{2,1,0:T(4,128)(2,1)S(1)}) custom-call(bf16[1600,128]{1,0:T(8,128)(2,1)S(1)} %collective-permute-done.2.refs_0_, bf16[1600,128]{1,0:T(8,128)(2,1)S(1)} %collective-permute-done.3.refs_1_, bf16[1600,128]{1,0:T(8,128)(2,1)} %collective-permute-done.4.refs_2_, ...), custom_call_target="tpu_custom_call" | custom-call | flops 1024 | bytes 1024 | tf_op jit(solution)/shard_map/place/pallas_call | solution.py:552
  99.2 2.1 %merge.2.refs_4_ = bf16[6,1536,128]{2,1,0:T(8,128)(2,1)} custom-call(s32[4,8]{1,0:T(4,128)S(1)} %copy-done.7, bf16[6,1536,128]{2,1,0:T(8,128)(2,1)S(1)} %bitcast.13, bf16[1536,128]{1,0:T(8,128)(2,1)S(1)} %copy-done.2, bf16[16,1664]{1,0:T(8,128)(2,1)S(1)} %collective-permute-done.6.refs_5_.refs_3_, ...), custom_call_target="tpu_custom_call", output_to_operand_aliasing={{}: (5, {})} | custom-call | flops 1024 | bytes 1024 | tf_op jit(solution)/shard_map/merge/pallas_call | solution.py:468
  101.3 5.0 %collective-permute-done.8.refs_3_.refs_1_ = bf16[16,1664]{1,0:T(8,128)(2,1)S(1)} collective-permute-done((bf16[16,1664]{1,0:T(8,128)(2,1)S(1)}, bf16[16,1664]{1,0:T(8,128)(2,1)S(1)}, u32[]{:S(2)}, u32[]{:S(2)}) %collective-permute-start.8) | collective-permute-done | bytes 53280 | tf_op jit(solution)/shard_map/ppermute | solution.py:572
  106.3 1.9 %merge.3.refs_2_ = bf16[6,1536,128]{2,1,0:T(8,128)(2,1)} custom-call(s32[4,8]{1,0:T(4,128)S(1)} %copy-done.7, bf16[6,1536,128]{2,1,0:T(8,128)(2,1)S(1)} %bitcast.14, bf16[1536,128]{1,0:T(8,128)(2,1)S(1)} %copy-done.4, bf16[16,1664]{1,0:T(8,128)(2,1)S(1)} %collective-permute-done.8.refs_3_.refs_1_, ...), custom_call_target="tpu_custom_call", output_to_operand_aliasing={{}: (4, {})} | custom-call | flops 1024 | bytes 1024 | tf_op jit(solution)/shard_map/merge/pallas_call | solution.py:468
  108.1 2.0 %collective-permute-done.7.refs_0_ = bf16[1600,128]{1,0:T(8,128)(2,1)S(1)} collective-permute-done((bf16[1600,128]{1,0:T(8,128)(2,1)S(1)}, bf16[1600,128]{1,0:T(8,128)(2,1)S(1)}, u32[]{:S(2)}, u32[]{:S(2)}) %collective-permute-start.7) | collective-permute-done | bytes 409632 | tf_op jit(solution)/shard_map/ppermute | solution.py:572
  110.1 1.5 %place.3 = (bf16[6,1536,128]{2,1,0:T(8,128)(2,1)}, bf16[6,3,1536]{2,1,0:T(4,128)(2,1)}, bf16[6,3,256]{2,1,0:T(4,128)(2,1)}) custom-call(bf16[1600,128]{1,0:T(8,128)(2,1)S(1)} %collective-permute-done.7.refs_0_, bf16[16,1664]{1,0:T(8,128)(2,1)S(1)} %collective-permute-done.8.refs_3_.refs_1_, ...), custom_call_target="tpu_custom_call", output_to_operand_aliasing={{0}: (2, {})} | custom-call | flops 1024 | bytes 1024 | tf_op jit(solution)/shard_map/place/pallas_call | solution.py:552
  (41 shorter events, 0.1 us)
Async XLA Ops:
  0.6 9.5 %copy-start.11 = (f32[1536]{0:T(1024)S(1)}, f32[1536]{0:T(1024)}, u32[]{:S(2)}) copy-start(f32[1536]{0:T(1024)} %param.22) | copy-start | bytes 18436
  0.6 9.5 %copy-start.12 = (f32[1536]{0:T(1024)S(1)}, f32[1536]{0:T(1024)}, u32[]{:S(2)}) copy-start(f32[1536]{0:T(1024)} %param.31) | copy-start | bytes 18436
  0.7 9.5 %copy-start.13 = (f32[1536]{0:T(1024)S(1)}, f32[1536]{0:T(1024)}, u32[]{:S(2)}) copy-start(f32[1536]{0:T(1024)} %param.34) | copy-start | bytes 18436
  0.7 9.5 %copy-start.9 = (bf16[48,768]{1,0:T(8,128)(2,1)S(1)}, bf16[48,768]{1,0:T(8,128)(2,1)}, u32[]{:S(2)}) copy-start(bf16[48,768]{1,0:T(8,128)(2,1)} %param.21) | copy-start | bytes 221188
  0.7 12.2 %copy-start.8 = (bf16[1536,128]{1,0:T(8,128)(2,1)S(1)}, bf16[1536,128]{1,0:T(8,128)(2,1)}, u32[]{:S(2)}) copy-start(bf16[1536,128]{1,0:T(8,128)(2,1)} %param.25) | copy-start | bytes 1179652
  0.7 11.6 %copy-start.14 = (f32[24]{0:T(128)S(1)}, f32[24]{0:T(128)}, u32[]{:S(2)}) copy-start(f32[24]{0:T(128)} %param.29) | copy-start | bytes 292
  0.7 11.6 %copy-start.15 = (f32[24]{0:T(128)S(1)}, f32[24]{0:T(128)}, u32[]{:S(2)}) copy-start(f32[24]{0:T(128)} %param.28) | copy-start | bytes 292
  0.7 11.5 %copy-start.16 = (f32[24]{0:T(128)S(1)}, f32[24]{0:T(128)}, u32[]{:S(2)}) copy-start(f32[24]{0:T(128)} %param.27) | copy-start | bytes 292
  3.6 29.1 %collective-permute-start = (bf16[1536,128]{1,0:T(8,128)(2,1)}, bf16[1536,128]{1,0:T(8,128)(2,1)S(1)}, u32[]{:S(2)}, u32[]{:S(2)}) collective-permute-start(bf16[1536,128]{1,0:T(8,128)(2,1)} %get-tuple-element.52), channel_id=1, source_target_pairs={{0,14},{2,16},{4,18},{6,20},{8,22},{10,24},{12,26},{14,28},{16,30}... | collective-permute-start | bytes 1179656 | tf_op jit(solution)/shard_map/ppermute | solution.py:572
  8.6 24.9 %collective-permute-start.1 = (bf16[1536,128]{1,0:T(8,128)(2,1)}, bf16[1536,128]{1,0:T(8,128)(2,1)S(1)}, u32[]{:S(2)}, u32[]{:S(2)}) collective-permute-start(bf16[1536,128]{1,0:T(8,128)(2,1)} %get-tuple-element.53), channel_id=1, source_target_pairs={{0,4},{2,6},{4,8},{6,10},{8,12},{10,14},{12,16},{14,18},{16,20},{1... | collective-permute-start | bytes 1179656 | tf_op jit(solution)/shard_map/ppermute | solution.py:572
  28.0 20.2 %copy-start = (bf16[6,24,64,128]{3,2,1,0:T(8,128)(2,1)S(1)}, bf16[6,24,64,128]{3,2,1,0:T(8,128)(2,1)}, u32[]{:S(2)}) copy-start(bf16[6,24,64,128]{3,2,1,0:T(8,128)(2,1)} %param.36) | copy-start | bytes 7077892
  28.0 20.1 %copy-start.6 = (bf16[16,1664]{1,0:T(8,128)(2,1)S(1)}, bf16[16,1664]{1,0:T(8,128)(2,1)}, u32[]{:S(2)}) copy-start(bf16[16,1664]{1,0:T(8,128)(2,1)} %get-tuple-element.71.refs_2_) | copy-start | bytes 159748
  28.0 20.1 %copy-start.7 = (s32[4,8]{1,0:T(4,128)S(1)}, s32[4,8]{1,0:T(4,128)}, u32[]{:S(2)}) copy-start(s32[4,8]{1,0:T(4,128)} %get-tuple-element.70.table.refs_0_) | copy-start | bytes 388
  28.1 66.2 %copy-start.10 = (f32[48,896]{1,0:T(8,128)S(1)}, f32[48,896]{1,0:T(8,128)}, u32[]{:S(2)}) copy-start(f32[48,896]{1,0:T(8,128)} %get-tuple-element.50) | copy-start | bytes 516100
  32.7 64.1 %copy-start.5 = (bf16[16,1664]{1,0:T(8,128)(2,1)S(1)}, bf16[16,1664]{1,0:T(8,128)(2,1)}, u32[]{:S(2)}) copy-start(bf16[16,1664]{1,0:T(8,128)(2,1)} %get-tuple-element.77.refs_4_) | copy-start | bytes 159748
  32.8 0.7 copy-start.1
  33.5 0.8 copy-start.3
  34.3 50.4 %collective-permute-start.2 = (bf16[1600,128]{1,0:T(8,128)(2,1)}, bf16[1600,128]{1,0:T(8,128)(2,1)S(1)}, u32[]{:S(2)}, u32[]{:S(2)}) collective-permute-start(bf16[1600,128]{1,0:T(8,128)(2,1)} %get-tuple-element.63), channel_id=1, source_target_pairs={{0,12},{2,14},{4,16},{6,18},{8,20},{10,22},{12,24},{14,26},{16,28}... | collective-permute-start | bytes 1228808 | tf_op jit(solution)/shard_map/ppermute | solution.py:572
  37.4 56.8 %collective-permute-start.3 = (bf16[1600,128]{1,0:T(8,128)(2,1)}, bf16[1600,128]{1,0:T(8,128)(2,1)S(1)}, u32[]{:S(2)}, u32[]{:S(2)}) collective-permute-start(bf16[1600,128]{1,0:T(8,128)(2,1)} %get-tuple-element.64), channel_id=1, source_target_pairs={{0,10},{2,12},{4,14},{6,16},{8,18},{10,20},{12,22},{14,24},{16,26}... | collective-permute-start | bytes 1228808 | tf_op jit(solution)/shard_map/ppermute | solution.py:572
  37.5 56.7 %collective-permute-start.4 = (bf16[1600,128]{1,0:T(8,128)(2,1)}, bf16[1600,128]{1,0:T(8,128)(2,1)}, u32[]{:S(2)}, u32[]{:S(2)}) collective-permute-start(bf16[1600,128]{1,0:T(8,128)(2,1)} %get-tuple-element.65), channel_id=1, source_target_pairs={{0,8},{2,10},{4,12},{6,14},{8,16},{10,18},{12,20},{14,22},{16,24},... | collective-permute-start | bytes 1228808 | tf_op jit(solution)/shard_map/ppermute | solution.py:572
  39.7 54.5 %collective-permute-start.5 = (bf16[1600,128]{1,0:T(8,128)(2,1)}, bf16[1600,128]{1,0:T(8,128)(2,1)}, u32[]{:S(2)}, u32[]{:S(2)}) collective-permute-start(bf16[1600,128]{1,0:T(8,128)(2,1)} %get-tuple-element.66), channel_id=1, source_target_pairs={{0,6},{2,8},{4,10},{6,12},{8,14},{10,16},{12,18},{14,20},{16,22},{... | collective-permute-start | bytes 1228808 | tf_op jit(solution)/shard_map/ppermute | solution.py:572
  44.1 50.3 %copy-start.17 = (bf16[16,1664]{1,0:T(8,128)(2,1)S(1)}, bf16[16,1664]{1,0:T(8,128)(2,1)}, u32[]{:S(2)}) copy-start(bf16[16,1664]{1,0:T(8,128)(2,1)} %get-tuple-element.73) | copy-start | bytes 159748
  44.1 35.3 %collective-permute-start.6 = (bf16[16,1664]{1,0:T(8,128)(2,1)}, bf16[16,1664]{1,0:T(8,128)(2,1)S(1)}, u32[]{:S(2)}, u32[]{:S(2)}) collective-permute-start(bf16[16,1664]{1,0:T(8,128)(2,1)} %get-tuple-element.67), channel_id=1, source_target_pairs={{0,14},{2,16},{4,18},{6,20},{8,22},{10,24},{12,26},{14,28},{16,30}... | collective-permute-start | bytes 159752 | tf_op jit(solution)/shard_map/ppermute | solution.py:572
  48.2 51.0 %copy-start.2 = (bf16[1536,128]{1,0:T(8,128)(2,1)S(1)}, bf16[1536,128]{1,0:T(8,128)(2,1)}, u32[]{:S(2)}) copy-start(bf16[1536,128]{1,0:T(8,128)(2,1)} %copy-done.1) | copy-start | bytes 1179652
  94.2 15.9 %collective-permute-start.7 = (bf16[1600,128]{1,0:T(8,128)(2,1)S(1)}, bf16[1600,128]{1,0:T(8,128)(2,1)S(1)}, u32[]{:S(2)}, u32[]{:S(2)}) collective-permute-start(bf16[1600,128]{1,0:T(8,128)(2,1)S(1)} %finish.3), channel_id=1, source_target_pairs={{0,2},{2,4},{4,6},{6,8},{8,10},{10,12},{12,14},{14,16},{16,18},{18... | collective-permute-start | bytes 1228808 | tf_op jit(solution)/shard_map/ppermute | solution.py:572
  94.4 11.9 %collective-permute-start.8 = (bf16[16,1664]{1,0:T(8,128)(2,1)S(1)}, bf16[16,1664]{1,0:T(8,128)(2,1)S(1)}, u32[]{:S(2)}, u32[]{:S(2)}) collective-permute-start(bf16[16,1664]{1,0:T(8,128)(2,1)S(1)} %copy-done.17), channel_id=1, source_target_pairs={{0,4},{2,6},{4,8},{6,10},{8,12},{10,14},{12,16},{14,18},{16,20},{1... | collective-permute-start | bytes 159752 | tf_op jit(solution)/shard_map/ppermute | solution.py:572
  99.2 7.1 %copy-start.4 = (bf16[1536,128]{1,0:T(8,128)(2,1)S(1)}, bf16[1536,128]{1,0:T(8,128)(2,1)}, u32[]{:S(2)}) copy-start(bf16[1536,128]{1,0:T(8,128)(2,1)} %copy-done.3) | copy-start | bytes 1179652
